TPU v7x, 32 devices: a whole 2x2x4 slice. The times are simulated.
32 devices in a mesh: runs: 2 (over x), space: 16 (over z, y, core).
Axes of the slice: x: 2, y: 2, z: 4, core: 2. Of those that a mesh axis runs over, the one named last changes fastest.
Arguments:
- fields: float32 [128, 512], P(('runs', 'space')), parts along dimension 0, may hold values from -3 to 3
- end_weights: bfloat16 [256, 128, 512], P(None, ('runs', 'space')), parts along dimension 1, may hold values from 0.5 to 1.5
- directions: float32 [3, 256], replicated, may hold values from -1 to 1
- analysis: bfloat16 [256, 256], replicated, may hold values from -0.375 to 0.375
- synthesis: bfloat16 [256, 256], replicated, may hold values from -0.375 to 0.375
- decay_rates: float32 [256], replicated, may hold values from 0.1 to 1
Outputs:
- density: float32 [128, 512], P(('runs', 'space')), parts along dimension 0
There are 2 independent parts, one for each index of `runs`. A program takes and returns all parts, laid end to end along the dimension named above; an argument that names none is the same for every part. Nothing has to cross between parts.
All inputs are finite; a program needn't handle non-finite values.
Results may differ from a plain program's by a relative error of at most 0.003.
Values may be sent and summed in bfloat16 or wider, within the bound.
No kernel may reach another device: no remote copies, remote signals or barrier semaphores. Data moves between devices by JAX's collectives and lax.ppermute only.
A program may use at most 64 MiB of HBM per device.

v0:
```python
import functools

import jax
import jax.numpy as jnp
from jax import lax
from jax.experimental import pallas as pl
from jax.experimental.pallas import tpu as pltpu
from jax.sharding import PartitionSpec as P

NZ = 16
STEPS = 4
LANES = 128
ROWS = 16
UNROLL = 4

courant = 0.3
slope = 0.6

BF16 = jnp.bfloat16
F32 = jnp.float32


def swap_species(block):
    count = lax.axis_size("space")
    return lax.ppermute(block, "space", [(i ^ 1, i) for i in range(count)])


def to_next_slab(block):
    count = lax.axis_size("space")
    return lax.ppermute(block, "space", [(i, (i + (2 if i % 2 == 0 else -2)) % count) for i in range(count)])


def rows_of(index):
    return pl.ds(pl.multiple_of(index * ROWS, ROWS), ROWS)


def each_row_block(orient):
    def run(body):
        def step(index, carry):
            body(index)
            return carry

        lax.fori_loop(0, orient // ROWS, step, 0, unroll=UNROLL)

    return run


def columns(tile):
    return slice(LANES * tile, LANES * (tile + 1))


def geometry(v_ref, rows, sign=1.0):
    lane = lax.broadcasted_iota(jnp.int32, (ROWS, LANES), 1)
    vx, vy, vz = (sign * v_ref[c, rows, :] for c in range(3))
    narrow = vx.astype(BF16)
    plus_x, narrow_plus, plus_y, plus_z = vx > 0, narrow > jnp.zeros_like(narrow), vy > 0, vz > 0
    rate_x, rate_y, rate_z = (courant * jnp.abs(t) for t in (vx, vy, vz))
    stay = 1.0 - (rate_x + rate_y + rate_z)
    z_from = (lane & (LANES - NZ)) | (jnp.where(plus_z, lane - 1, lane + 1) & (NZ - 1))
    y_from = jnp.where(plus_y, lane - NZ, lane + NZ) & (LANES - 1)
    y_edge = jnp.where(plus_y, lane, LANES - 1 - lane) < NZ
    return plus_x, narrow_plus, plus_y, stay, rate_x, rate_y, rate_z, z_from, y_from, y_edge


def pick(tile, index):
    return jnp.take_along_axis(tile, index, axis=1, mode="promise_in_bounds")


def load_plane(ref, plane, rows):
    return [ref[plane, rows, columns(t)] for t in range(ref.shape[2] // LANES)]


def drift(center, before, after, geo):
    plus_x, narrow_plus, plus_y, stay, rate_x, rate_y, rate_z, z_from, y_from, y_edge = geo
    tiles = len(center)
    center = [tile.astype(F32) for tile in center]
    turned = [pick(tile, y_from) for tile in center]
    moved = []
    for t in range(tiles):
        total = stay * center[t]
        if before is not None and after is not None:
            total = total + rate_x * jnp.where(narrow_plus, before[t], after[t]).astype(F32)
        elif before is not None:
            total = total + jnp.where(plus_x, rate_x, 0.0) * before[t].astype(F32)
        elif after is not None:
            total = total + jnp.where(plus_x, 0.0, rate_x) * after[t].astype(F32)
        over = jnp.where(plus_y, turned[t - 1], turned[(t + 1) % tiles])
        total = total + rate_y * jnp.where(y_edge, over, turned[t])
        total = total + rate_z * pick(center[t], z_from)
        moved.append(total)
    return moved


def store_plane(ref, plane, rows, tiles):
    for t, tile in enumerate(tiles):
        ref[plane, rows, columns(t)] = tile.astype(ref.dtype)


def mix(matrix, moved):
    return jnp.dot(matrix, moved, preferred_element_type=F32)


def boltzmann(field):
    return jnp.exp(-0.5 * field)


def prologue_kernel(core_ref, directions_ref, low_ref, high_ref, fields_ref, spread_ref, edge_ref):
    sign = 1.0 - 2.0 * core_ref[0].astype(F32)
    orient, cells = edge_ref.shape
    low = boltzmann(fields_ref[0:1])
    high = boltzmann(fields_ref[fields_ref.shape[0] - 1 :])
    for c in range(4):
        row = directions_ref[c % 3 : c % 3 + 1]
        column = jnp.broadcast_to(row, (LANES, orient)).T
        spread_ref[c] = column if c == 3 else sign * column

    @each_row_block(orient)
    def _(index):
        rows = rows_of(index)
        plus_x = spread_ref[0, rows, :] > 0
        for t in range(cells // LANES):
            at = rows, columns(t)
            chosen = jnp.where(
                plus_x, high[:, columns(t)] * high_ref[at].astype(F32), low[:, columns(t)] * low_ref[at].astype(F32)
            )
            edge_ref[at] = chosen.astype(BF16)


def write_edge(edges_ref, step, faces, rows, v_ref):
    narrow = v_ref[0, rows, :].astype(BF16)
    plus_x = narrow > jnp.zeros_like(narrow)
    for t in range(len(faces[0])):
        edges_ref[step, rows, columns(t)] = jnp.where(plus_x, faces[-1][t], faces[0][t])


def alone_step(source_ref, moved, targets, v_ref, edges_ref, step):
    planes, orient, _ = source_ref.shape

    @each_row_block(orient)
    def _(index):
        rows = rows_of(index)
        geo = geometry(v_ref, rows)
        loaded = [load_plane(source_ref, p, rows) for p in range(planes)]
        if edges_ref is not None:
            write_edge(edges_ref, step, loaded, rows, v_ref)
        for p in targets:
            before = loaded[p - 1] if p > 0 else None
            after = loaded[p + 1] if p < planes - 1 else None
            store_plane(moved, p, rows, drift(loaded[p], before, after, geo))


def first_alone_kernel(start_ref, first_ref, v_ref, m_ref, out_ref, edges_ref, held, moved):
    planes, orient, _ = start_ref.shape
    first = boltzmann(first_ref[...])
    for p in range(planes):
        held[p] = (first[p : p + 1] * start_ref[p].astype(F32)).astype(BF16)
    alone_step(held, moved, range(planes), v_ref, None, 0)
    for p in (0, planes - 1, *range(1, planes - 1)):
        out_ref[p] = (first[p : p + 1] * first[p : p + 1] * mix(m_ref[...], moved[p])).astype(BF16)

    @each_row_block(orient)
    def _(index):
        rows = rows_of(index)
        write_edge(edges_ref, 0, [load_plane(out_ref, p, rows) for p in (0, planes - 1)], rows, v_ref)


def next_alone_kernel(state_ref, first_ref, second_ref, v_ref, m_ref, edges_ref, held, moved):
    planes, orient, _ = state_ref.shape
    first = boltzmann(first_ref[...])
    second = boltzmann(second_ref[...])
    alone_step(state_ref, moved, range(planes), v_ref, None, 0)
    for p in range(planes):
        held[p] = (first[p : p + 1] * second[p : p + 1] * mix(m_ref[...], moved[p])).astype(BF16)
    alone_step(held, moved, (0, planes - 1), v_ref, edges_ref, 0)
    for p in (0, planes - 1):
        held[p] = (second[p : p + 1] * second[p : p + 1] * mix(m_ref[...], moved[p])).astype(BF16)

    @each_row_block(orient)
    def _(index):
        rows = rows_of(index)
        write_edge(edges_ref, 1, [load_plane(held, p, rows) for p in (0, planes - 1)], rows, v_ref)


def face_parts(v_ref, rows):
    vx = v_ref[0, rows, :]
    rate = courant * jnp.abs(vx)
    return v_ref[3, rows, :] > 0, jnp.where(vx > 0, rate, 0.0), jnp.where(vx > 0, 0.0, rate)


def face_drifts(v_ref, mine_ref, other_ref, moved, slots):
    @each_row_block(v_ref.shape[1])
    def _(index):
        rows = rows_of(index)
        ahead, rate_plus, rate_minus = face_parts(v_ref, rows)
        for t in range(mine_ref.shape[1] // LANES):
            mine = mine_ref[rows, columns(t)].astype(F32)
            other = other_ref[rows, columns(t)].astype(F32)
            face = jnp.where(ahead, mine, other)
            moved[slots[0], rows, columns(t)] = (rate_plus * face).astype(BF16)
            moved[slots[1], rows, columns(t)] = (rate_minus * face).astype(BF16)


def second_step_kernel(
    core_ref, alone_ref, edge_ref, mine_ref, other_ref, first_ref, second_ref, beyond_ref, v_ref, m_ref,
    out_ref, next_ref, sent_ref, held, moved,
):
    planes, orient, _ = alone_ref.shape
    matrix = m_ref[...]
    first, second = boltzmann(first_ref[...]), boltzmann(second_ref[...])
    beyond = boltzmann(beyond_ref[...])
    face_drifts(v_ref, mine_ref, other_ref, moved, (0, 1))

    @each_row_block(orient)
    def _(index):
        rows = rows_of(index)
        _, rate_plus, rate_minus = face_parts(v_ref, rows)
        for t in range(edge_ref.shape[1] // LANES):
            edge = edge_ref[rows, columns(t)].astype(F32)
            moved[2, rows, columns(t)] = (rate_minus * edge).astype(BF16)
            moved[3, rows, columns(t)] = (rate_plus * edge).astype(BF16)

    squared = first * first
    for p in range(planes):
        kept = alone_ref[p]
        if p in (0, planes - 1):
            arrived = squared[p : p + 1] * mix(matrix, moved[min(p, 1)])
            kept = (kept.astype(F32) + arrived).astype(BF16)
        held[p + 1] = kept
        out_ref[p] = kept
    held[0] = (beyond[0:1] * beyond[0:1] * mix(matrix, moved[2])).astype(BF16)
    held[planes + 1] = (beyond[2:3] * beyond[2:3] * mix(matrix, moved[3])).astype(BF16)
    count = planes + 2

    @each_row_block(orient)
    def _(index):
        rows = rows_of(index)
        geo = geometry(v_ref, rows)
        _, rate_plus, rate_minus = face_parts(v_ref, rows)
        loaded = [load_plane(held, p, rows) for p in range(count)]
        for p in range(count):
            before = loaded[p - 1] if p > 0 else None
            after = loaded[p + 1] if p < count - 1 else None
            store_plane(moved, p + 1, rows, drift(loaded[p], before, after, geo))
        store_plane(moved, 0, rows, [rate_minus * tile.astype(F32) for tile in loaded[0]])
        store_plane(moved, count + 1, rows, [rate_plus * tile.astype(F32) for tile in loaded[-1]])

    cross = first * second
    factors = [beyond[1:2] * beyond[5:6], beyond[0:1] * beyond[4:5]]
    factors += [cross[p : p + 1] for p in range(planes)]
    factors += [beyond[2:3] * beyond[6:7], beyond[3:4] * beyond[7:8]]
    for p, factor in enumerate(factors):
        next_ref[p] = (factor * mix(matrix, moved[p])).astype(BF16)
    core = core_ref[0]
    for p in range(planes // 2):
        sent_ref[p] = next_ref[2 + (planes - 1) * (1 - core) + (2 * core - 1) * p]


def middle_kernel(
    core_ref, own_ref, partner_ref, message_ref, first_ref, second_ref, v_ref, m_ref, out_ref, total_ref, moved
):
    orient, cells = message_ref.shape
    cross = boltzmann(first_ref[...]) * boltzmann(second_ref[...])
    core = core_ref[0]

    @each_row_block(orient)
    def _(index):
        rows = rows_of(index)
        ahead, rate_plus, rate_minus = face_parts(v_ref, rows)
        rate = rate_plus + rate_minus
        for t in range(cells // LANES):
            gained = rate * message_ref[rows, columns(t)].astype(F32)
            moved[0, rows, columns(t)] = jnp.where(ahead, gained, 0.0).astype(BF16)
            moved[1, rows, columns(t)] = jnp.where(ahead, 0.0, gained).astype(BF16)

    planes = own_ref.shape[0] - 4
    face_plane = 2 + (planes - 1) * core
    own_face = own_ref[face_plane].astype(F32) + cross[0:1] * mix(m_ref[...], moved[0])
    partner_face = partner_ref[0].astype(F32) + cross[0:1] * mix(m_ref[...], moved[1])
    face = jnp.sum(own_face * partner_face, axis=0, keepdims=True)
    total = jnp.zeros((1, 1), F32)
    for p in range(planes // 2):
        if p > 0:
            own = own_ref[face_plane + p - 2 * p * core].astype(F32)
            face = jnp.sum(own * partner_ref[p].astype(F32), axis=0, keepdims=True)
        met = face / (orient * cross[p : p + 1])
        out_ref[p : p + 1] = met
        total = total + jnp.sum(met, axis=1, keepdims=True)
    total_ref[...] = jnp.broadcast_to(total, total_ref.shape)


def third_step_kernel(
    held_ref, mine_ref, other_ref, first_ref, second_ref, beyond_ref, v_ref, m_ref, next_ref, held, moved
):
    planes, orient, _ = held.shape
    matrix = m_ref[...]
    first, second = boltzmann(first_ref[...]), boltzmann(second_ref[...])
    beyond = boltzmann(beyond_ref[...])
    face_drifts(v_ref, mine_ref, other_ref, moved, (0, 1))
    cross = first * second
    for p in range(planes):
        kept = held_ref[p + 2]
        if p in (0, planes - 1):
            arrived = cross[p : p + 1] * mix(matrix, moved[min(p, 1)])
            kept = (kept.astype(F32) + arrived).astype(BF16)
        held[p] = kept

    @each_row_block(orient)
    def _(index):
        rows = rows_of(index)
        geo = geometry(v_ref, rows)
        loaded = [load_plane(held_ref, p, rows) for p in (0, 1)]
        loaded += [load_plane(held, p, rows) for p in range(planes)]
        loaded += [load_plane(held_ref, p, rows) for p in (planes + 2, planes + 3)]
        for p in range(planes + 2):
            store_plane(moved, p, rows, drift(loaded[p + 1], loaded[p], loaded[p + 2], geo))

    squared = second * second
    factors = [beyond[4:5] * beyond[4:5]] + [squared[p : p + 1] for p in range(planes)] + [beyond[6:7] * beyond[6:7]]
    for p, factor in enumerate(factors):
        next_ref[p] = (factor * mix(matrix, moved[p])).astype(BF16)


def weight_kernel(core_ref, partner_ref, start_ref, turned_ref, weight_ref, own_ref):
    planes = partner_ref.shape[0]
    core = core_ref[0]
    for p in range(planes):
        weight_ref[p] = mix(turned_ref[...], partner_ref[p]).astype(BF16)
    for p in range(2):
        own_ref[p] = mix(turned_ref[...], start_ref[core * (planes - 1) + p - 2 * p * core]).astype(BF16)


def fold(value):
    return jnp.sum(value.reshape(ROWS // 8, 8, LANES), axis=0)


def pairing_kernel(held_ref, second_ref, v_ref, weight_ref, partner_ref, out_ref):
    planes, orient, cells = partner_ref.shape
    second = boltzmann(second_ref[...])
    tiles = cells // LANES

    def body(index, sums):
        rows = rows_of(index)
        geo = geometry(v_ref, rows)
        loaded = [load_plane(held_ref, p, rows) for p in range(planes + 2)]
        new = []
        for p in range(planes):
            moved_tiles = drift(loaded[p + 1], loaded[p], loaded[p + 2], geo)
            weights = load_plane(weight_ref, p, rows)
            partner = load_plane(partner_ref, p, rows)
            for t in range(tiles):
                last, third = sums[2 * (p * tiles + t)], sums[2 * (p * tiles + t) + 1]
                new.append(last + fold(moved_tiles[t] * weights[t].astype(F32)))
                new.append(third + fold(loaded[p + 1][t].astype(F32) * partner[t].astype(F32)))
        return tuple(new)

    zero = jnp.zeros((8, LANES), F32)
    sums = lax.fori_loop(0, orient // ROWS, body, (zero,) * (2 * planes * tiles))
    for p in range(planes):
        for t in range(tiles):
            last = jnp.sum(sums[2 * (p * tiles + t)], axis=0, keepdims=True)
            third = jnp.sum(sums[2 * (p * tiles + t) + 1], axis=0, keepdims=True)
            factor = second[p : p + 1, columns(t)]
            out_ref[p : p + 1, columns(t)] = (0.5 * factor * last + third / (factor * factor)) / orient


def last_kernel(
    core_ref, message_ref, weight_ref, own_weight_ref, own_state_ref, partner_state_ref, shared_ref, met_ref,
    own_ref, partner_ref, v_ref, m_ref, sent_ref, kept_ref, moved, gained,
):
    planes, cells = shared_ref.shape
    orient = m_ref.shape[0]
    tiles = cells // LANES
    core = core_ref[0]
    half = planes // 2
    face = core * (planes - 1)
    inner = face + 1 - 2 * core

    def at_face(ref, depth):
        return jnp.where(core == 0, boltzmann(ref[depth : depth + 1]), boltzmann(ref[planes - 1 - depth : planes - depth]))

    factors = [[at_face(ref, depth) for depth in range(2)] for ref in (partner_ref, own_ref)]

    @each_row_block(orient)
    def _(index):
        rows = rows_of(index)
        ahead, rate_plus, rate_minus = face_parts(v_ref, rows)
        rate = rate_plus + rate_minus
        for t in range(tiles):
            got = rate * message_ref[0, rows, columns(t)].astype(F32)
            moved[0, rows, columns(t)] = jnp.where(ahead, got, 0.0).astype(BF16)
            moved[1, rows, columns(t)] = jnp.where(ahead, 0.0, got).astype(BF16)

    for s in range(2):
        gained[s] = (factors[s][0] * factors[s][0] * mix(m_ref[...], moved[s])).astype(BF16)

    def body(index, sums):
        rows = rows_of(index)
        ahead, rate_plus, rate_minus = face_parts(v_ref, rows)
        rate = rate_plus + rate_minus
        sides = (jnp.where(ahead, rate, 0.0), jnp.where(ahead, 0.0, rate))
        message = load_plane(message_ref, 1, rows)
        new = []
        for s in range(2):
            change = load_plane(gained, s, rows)
            moved_tiles = drift(change, None, None, geometry(v_ref, rows, 1.0 - 2.0 * s))
            if s == 0:
                weights = [load_plane(weight_ref, p, rows) for p in (face, inner)]
            else:
                weights = [load_plane(own_weight_ref, p, rows) for p in (0, 1)]
            third = load_plane((partner_state_ref, own_state_ref)[s], face, rows)
            for t in range(tiles):
                on_face = moved_tiles[t] + sides[s] * message[t].astype(F32)
                wide = change[t].astype(F32)
                terms = (
                    on_face * weights[0][t].astype(F32),
                    sides[s] * wide * weights[1][t].astype(F32),
                    wide * third[t].astype(F32),
                )
                base = 3 * (s * tiles + t)
                new += [sums[base + k] + fold(term) for k, term in enumerate(terms)]
        return tuple(new)

    zero = jnp.zeros((8, LANES), F32)
    sums = lax.fori_loop(0, orient // ROWS, body, (zero,) * (6 * tiles))
    for t in range(tiles):
        shares = []
        for s in range(2):
            base = 3 * (s * tiles + t)
            last, onward, third = (jnp.sum(sums[base + k], axis=0, keepdims=True) / orient for k in range(3))
            near, far = (factors[s][depth][:, columns(t)] for depth in range(2))
            shares.append((0.5 * near * last + third / (near * near), 0.5 * far * onward))
        for p in range(planes):
            at = slice(p, p + 1), columns(t)
            mine = core == (0 if p < half else 1)
            depth = min(p, planes - 1 - p)
            met = jnp.where(mine, 0.5 * met_ref[depth : depth + 1, columns(t)], 0.0)
            sent, kept = shared_ref[at] + met, met
            if depth < 2:
                sent = sent + jnp.where(mine, shares[0][depth], 0.0)
                kept = kept + jnp.where(mine, shares[1][depth], 0.0)
            sent_ref[at] = sent
            kept_ref[at] = kept


def kernel_call(kernel, outs, scratch, args):
    vmem = pl.BlockSpec(memory_space=pltpu.VMEM)
    smem = pl.BlockSpec(memory_space=pltpu.SMEM)
    return pl.pallas_call(
        kernel,
        out_shape=outs,
        in_specs=[smem if arg.dtype == jnp.int32 else vmem for arg in args],
        out_specs=jax.tree.map(lambda _: vmem, outs),
        scratch_shapes=[pltpu.VMEM(shape, BF16) for shape in scratch],
        compiler_params=pltpu.CompilerParams(vmem_limit_bytes=12 << 20),
        cost_estimate=pl.CostEstimate(flops=0, bytes_accessed=0, transcendentals=0),
    )(*args)


def shards(fields, end_weights, directions, analysis, synthesis, decay_rates):
    device = lax.axis_index("space")
    core = device % 2
    is_first = core == 0
    planes, cells = fields.shape
    orient = end_weights.shape[0]
    plane_index = device // 2 * planes + lax.broadcasted_iota(jnp.int32, (planes, 1), 0)
    ramp = slope * plane_index.astype(F32) / (planes * lax.axis_size("space") // 2)
    own = fields + ramp
    partner = swap_species(fields) + ramp

    slab = jax.ShapeDtypeStruct((planes, orient, cells), BF16)
    plane = jax.ShapeDtypeStruct((orient, cells), BF16)
    wide = lambda extra: jax.ShapeDtypeStruct((planes + extra, orient, cells), BF16)
    core_word = jnp.reshape(core, (1,)).astype(jnp.int32)
    spread, edge0 = kernel_call(
        prologue_kernel,
        (jax.ShapeDtypeStruct((4, orient, LANES), F32), plane),
        (),
        (core_word, directions, end_weights[:, 0], end_weights[:, -1], own),
    )
    ahead = spread[3, :, :1] > 0

    def message(mine, other):
        return jnp.where(ahead, mine, other)

    near = jnp.where(is_first, jnp.stack([own[-1], own[-2]]), own[:2])
    near_other = jnp.where(is_first, jnp.stack([partner[-1], partner[-2]]), partner[:2])
    field_rows = jnp.concatenate([near, near_other])
    high = lax.reduce_precision(field_rows, 8, 7)
    coded = jnp.concatenate([high, field_rows - high, jnp.zeros((8, cells), F32)]).astype(BF16)
    message0 = jnp.concatenate([message(edge0, swap_species(edge0)), coded])

    scaled = synthesis.astype(F32) * decay_rates[None]
    mixing = jnp.dot(scaled, analysis.astype(F32), precision=lax.Precision.HIGHEST) + 1.0 / orient
    matrix = mixing.astype(BF16)

    raw, _ = lax.optimization_barrier((end_weights, edge0))
    start, _ = lax.optimization_barrier((jnp.transpose(raw, (1, 0, 2)), message0))
    arrived0 = to_next_slab(message0)
    alone, edges1 = kernel_call(
        first_alone_kernel,
        (slab, jax.ShapeDtypeStruct((1, orient, cells), BF16)),
        (slab.shape, slab.shape),
        (start, own, spread, matrix),
    )
    message1 = message(edges1, swap_species(edges1))
    edges = kernel_call(
        next_alone_kernel,
        jax.ShapeDtypeStruct((2, orient, cells), BF16),
        (slab.shape, slab.shape),
        (alone, own, partner, spread, matrix),
    )
    edges, arrived0 = lax.optimization_barrier((edges, arrived0))
    message2 = message(edges, swap_species(edges))
    arrived = [to_next_slab(message1)[0], to_next_slab(message2)]
    crossed0 = swap_species(arrived0)

    def near_fields(block):
        rows = block[orient : orient + 4].astype(F32) + block[orient + 4 : orient + 8].astype(F32)
        return rows[:2], rows[2:]

    mine_first, mine_second = near_fields(arrived0)
    other_second, other_first = near_fields(crossed0)
    low_first = jnp.where(is_first, mine_first, other_first)
    high_first = jnp.where(is_first, other_first, mine_first)
    low_second = jnp.where(is_first, mine_second, other_second)
    high_second = jnp.where(is_first, other_second, mine_second)
    beyond = jnp.concatenate([low_first, high_first, low_second, high_second])

    alone, *_ = lax.optimization_barrier((alone, message1, message2))
    half = planes // 2
    half_slab = jax.ShapeDtypeStruct((half, orient, cells), BF16)
    first_state, second_state, sent_half = kernel_call(
        second_step_kernel,
        (slab, wide(4), half_slab),
        (wide(2).shape, wide(4).shape),
        (core_word, alone, edge0, arrived0[:orient], crossed0[:orient], own, partner, beyond, spread, matrix),
    )
    arrived1, second_state = lax.optimization_barrier((arrived[0], second_state))
    sent_half, start, first_state, _ = lax.optimization_barrier((sent_half, start, first_state, arrived1))
    own_half_field = jnp.where(is_first, own[:half], own[half:][::-1])
    partner_half_field = jnp.where(is_first, partner[:half], partner[half:][::-1])
    met, partition = kernel_call(
        middle_kernel,
        (jax.ShapeDtypeStruct((half, cells), F32), jax.ShapeDtypeStruct((8, LANES), F32)),
        ((2, orient, cells),),
        (core_word, second_state, swap_species(sent_half), arrived1, own_half_field, partner_half_field, spread, matrix),
    )
    count = lax.axis_size("space")
    distance = 1
    while distance < count:
        partition = partition + lax.ppermute(partition, "space", [(i, i ^ distance) for i in range(count)])
        distance *= 2
    partition = partition[0, 0] / (count // 2 * planes * cells)

    crossed1 = swap_species(arrived1)
    third_state = kernel_call(
        third_step_kernel,
        wide(2),
        (slab.shape, wide(2).shape),
        (second_state, arrived1, crossed1, own, partner, beyond, spread, matrix),
    )
    weights, own_weights = kernel_call(
        weight_kernel,
        (slab, jax.ShapeDtypeStruct((2, orient, cells), BF16)),
        (),
        (core_word, swap_species(start), start, matrix.T),
    )
    partner_state = swap_species(first_state)
    density = jax.ShapeDtypeStruct((planes, cells), F32)
    shared = kernel_call(pairing_kernel, density, (), (third_state, partner, spread, weights, partner_state))
    arrived2, shared = lax.optimization_barrier((arrived[1], shared))
    sent, kept = kernel_call(
        last_kernel,
        (density, density),
        ((2, orient, cells), (2, orient, cells)),
        (
            core_word, arrived2, weights, own_weights, first_state, partner_state, shared, met,
            own, partner, spread, matrix,
        ),
    )
    return (kept + swap_species(sent)) / partition


def solution(mesh):
    return jax.shard_map(
        shards,
        mesh=mesh,
        in_specs=(P(("runs", "space"), None), P(None, ("runs", "space"), None), P(), P(), P(), P()),
        out_specs=P(("runs", "space"), None),
        check_vma=False,
    )
```

profile of v0, /device:TPU:0, one launch (start us, length us, event | category | flops | bytes accessed | tf_op | source)
XLA Modules:
  0.0 58.9 jit_solution(2539121882656406629)
XLA Ops:
  0.0 0.5 collective-permute-start.1
  0.5 2.5 %fusion.6 = (bf16[256,1,512]{2,1,0:T(2,128)(2,1)S(1)}, bf16[256,1,512]{2,1,0:T(2,128)(2,1)S(1)}) fusion(bf16[256,4,512]{2,1,0:T(4,128)(2,1)} %param.7), kind=kLoop, calls=%fused_computation.33 | loop fusion | bytes 1048576 | tf_op jit(solution)/shard_map/slice | solution.py:478
  4.3 1.4 %collective-permute-done = bf16[256,512]{1,0:T(8,128)(2,1)S(1)} collective-permute-done((bf16[256,512]{1,0:T(8,128)(2,1)S(1)}, bf16[256,512]{1,0:T(8,128)(2,1)S(1)}, u32[]{:S(2)}, u32[]{:S(2)}) %collective-permute-start) | collective-permute-done | bytes 262176 | tf_op jit(solution)/shard_map/ppermute | solution.py:25
  5.9 2.7 %collective-permute-start.2 = (bf16[272,512]{1,0:T(8,128)(2,1)S(1)}, bf16[272,512]{1,0:T(8,128)(2,1)S(1)}, u32[]{:S(2)}, u32[]{:S(2)}) collective-permute-start(bf16[272,512]{1,0:T(8,128)(2,1)S(1)} %maximum_maximum_fusion), channel_id=1, source_target_pairs={{0,2},{1,15},{2,4},{3,1},{4,6},{5,3},{6,8},{7,5},{8,10},{9,7},{10,... | collective-permute-start | bytes 835592 | tf_op jit(solution)/shard_map/ppermute | solution.py:30
  9.1 2.3 %shard_map.65 = (bf16[4,256,512]{2,1,0:T(8,128)(2,1)S(1)}, bf16[1,256,512]{2,1,0:T(8,128)(2,1)S(1)}) custom-call(bf16[4,256,512]{2,1,0:T(8,128)(2,1)S(1)} %bitcast.12, f32[4,512]{1,0:T(4,128)S(1)} %get-tuple-element.72.fields_ref.first_ref.own_ref, f32[4,256,128]{2,1,0:T(8,128)S(1)} %get-tuple-element.30.v_ref, bf16[256,256]{1,0:T(8,128)(2,1)S(1)} %fusion.m_ref), custom_call_target="tpu_custom_call" | custom-call | tf_op jit(solution)/shard_map/pallas_call | solution.py:448
  11.4 3.2 %collective-permute-start.5 = (bf16[1,256,512]{2,1,0:T(8,128)(2,1)S(1)}, bf16[1,256,512]{2,1,0:T(8,128)(2,1)S(1)}, u32[]{:S(2)}, u32[]{:S(2)}) collective-permute-start(bf16[1,256,512]{2,1,0:T(8,128)(2,1)S(1)} %get-tuple-element.36), channel_id=1, source_target_pairs={{1,0},{0,1},{3,2},{2,3},{5,4},{4,5},{7,6},{6,7},{9,8},{8,9},{11,10... | collective-permute-start | bytes 786440 | tf_op jit(solution)/shard_map/ppermute | solution.py:25
  14.6 3.3 %shard_map.66 = bf16[2,256,512]{2,1,0:T(8,128)(2,1)S(1)} custom-call(bf16[4,256,512]{2,1,0:T(8,128)(2,1)S(1)} %get-tuple-element.37.state_ref.alone_ref, f32[4,512]{1,0:T(4,128)S(1)} %get-tuple-element.72.fields_ref.first_ref.own_ref, f32[4,512]{1,0:T(4,128)S(1)} %get-tuple-element.71.second_ref.partner_ref, f32[4,256,128]{2,1,0:T(8,128)S(1)} %get-tuple-element.30.v_ref, ...), custom_call_target="tpu_custom_call" | custom-call | tf_op jit(solution)/shard_map/pallas_call | solution.py:448
  18.3 3.3 %collective-permute-start.3 = (bf16[2,256,512]{2,1,0:T(8,128)(2,1)S(1)}, bf16[2,256,512]{2,1,0:T(8,128)(2,1)S(1)}, u32[]{:S(2)}, u32[]{:S(2)}) collective-permute-start(bf16[2,256,512]{2,1,0:T(8,128)(2,1)S(1)} %shard_map.66), channel_id=1, source_target_pairs={{1,0},{0,1},{3,2},{2,3},{5,4},{4,5},{7,6},{6,7},{9,8},{8,9},{11,10... | collective-permute-start | bytes 1572872 | tf_op jit(solution)/shard_map/ppermute | solution.py:25
  21.8 1.4 %collective-permute-done.3 = bf16[2,256,512]{2,1,0:T(8,128)(2,1)S(1)} collective-permute-done((bf16[2,256,512]{2,1,0:T(8,128)(2,1)S(1)}, bf16[2,256,512]{2,1,0:T(8,128)(2,1)S(1)}, u32[]{:S(2)}, u32[]{:S(2)}) %collective-permute-start.3) | collective-permute-done | bytes 524320 | tf_op jit(solution)/shard_map/ppermute | solution.py:25
  23.2 0.9 %broadcast_select_fusion = bf16[2,256,512]{2,1,0:T(8,128)(2,1)} fusion(bf16[2,256,512]{2,1,0:T(8,128)(2,1)S(1)} %shard_map.66, bf16[2,256,512]{2,1,0:T(8,128)(2,1)S(1)} %collective-permute-done.3, pred[256]{0:T(512)(128)(4,1)S(1)} %fusion.4), kind=kLoop, calls=%fused_computation.3 | loop fusion | flops 262144 | bytes 1573120 | tf_op jit(solution)/shard_map/jit(_where)/select_n | solution.py:483
  24.1 3.8 %shard_map.67 = (bf16[4,256,512]{2,1,0:T(8,128)(2,1)}, bf16[8,256,512]{2,1,0:T(8,128)(2,1)S(1)}, bf16[2,256,512]{2,1,0:T(8,128)(2,1)S(1)}) custom-call(s32[1]{0:T(128)} %bitcast.core_ref, bf16[4,256,512]{2,1,0:T(8,128)(2,1)S(1)} %get-tuple-element.37.state_ref.alone_ref, bf16[256,512]{1,0:T(8,128)(2,1)S(1)} %get-tuple-element.31.edge_ref, ...), custom_call_target="tpu_custom_call" | custom-call | tf_op jit(solution)/shard_map/pallas_call | solution.py:448
  27.9 0.4 collective-permute-start.9
  28.5 0.4 collective-permute-start.11
  28.9 2.4 %collective-permute-start.8 = (bf16[256,512]{1,0:T(8,128)(2,1)S(1)}, bf16[256,512]{1,0:T(8,128)(2,1)S(1)}, u32[]{:S(2)}, u32[]{:S(2)}) collective-permute-start(bf16[256,512]{1,0:T(8,128)(2,1)S(1)} %bitcast.16), channel_id=1, source_target_pairs={{1,0},{0,1},{3,2},{2,3},{5,4},{4,5},{7,6},{6,7},{9,8},{8,9},{11,10... | collective-permute-start | bytes 786440 | tf_op jit(solution)/shard_map/ppermute | solution.py:25
  31.3 1.0 %collective-permute-done.11.partner_ref = bf16[2,256,512]{2,1,0:T(8,128)(2,1)S(1)} collective-permute-done((bf16[2,256,512]{2,1,0:T(8,128)(2,1)S(1)}, bf16[2,256,512]{2,1,0:T(8,128)(2,1)S(1)}, u32[]{:S(2)}, u32[]{:S(2)}) %collective-permute-start.11) | collective-permute-done | bytes 524320 | tf_op jit(solution)/shard_map/ppermute | solution.py:25
  32.3 0.6 %shard_map.71 = (f32[2,512]{1,0:T(2,128)S(1)}, f32[8,128]{1,0:T(8,128)S(1)}) custom-call(s32[1]{0:T(128)} %bitcast.core_ref, bf16[8,256,512]{2,1,0:T(8,128)(2,1)S(1)} %get-tuple-element.40.held_ref.own_ref, bf16[2,256,512]{2,1,0:T(8,128)(2,1)S(1)} %collective-permute-done.11.partner_ref, bf16[256,512]{1,0:T(8,128)(2,1)S(1)} %bitcast.17, ...), custom_call_target="tpu_custom_call" | custom-call | tf_op jit(solution)/shard_map/pallas_call | solution.py:448
  32.9 1.4 %copy-done.1 = bf16[8,256,512]{2,1,0:T(8,128)(2,1)} copy-done((bf16[8,256,512]{2,1,0:T(8,128)(2,1)}, bf16[8,256,512]{2,1,0:T(8,128)(2,1)S(1)}, u32[]{:S(2)}) %copy-start.1) | copy-done | bytes 2097176
  34.3 0.4 collective-permute-start.13
  34.6 0.8 %collective-permute-done.13 = f32[8,128]{1,0:T(8,128)S(1)} collective-permute-done((f32[8,128]{1,0:T(8,128)S(1)}, f32[8,128]{1,0:T(8,128)S(1)}, u32[]{:S(2)}, u32[]{:S(2)}) %collective-permute-start.13) | collective-permute-done | bytes 4128 | tf_op jit(solution)/shard_map/ppermute | solution.py:551
  35.4 0.6 %add.70 = f32[8,128]{1,0:T(8,128)} add(f32[8,128]{1,0:T(8,128)S(1)} %get-tuple-element.54, f32[8,128]{1,0:T(8,128)S(1)} %collective-permute-done.13) | non-fusion elementwise | flops 1024 | bytes 12288 | tf_op jit(solution)/shard_map/add | solution.py:551
  36.3 1.6 %copy-done.2 = bf16[8,256,512]{2,1,0:T(8,128)(2,1)S(1)} copy-done((bf16[8,256,512]{2,1,0:T(8,128)(2,1)S(1)}, bf16[8,256,512]{2,1,0:T(8,128)(2,1)}, u32[]{:S(2)}) %copy-start.2) | copy-done | bytes 2097176
  37.9 0.7 %copy-done.4 = f32[8,512]{1,0:T(8,128)S(1)} copy-done((f32[8,512]{1,0:T(8,128)S(1)}, f32[8,512]{1,0:T(8,128)}, u32[]{:S(2)}) %copy-start.4) | copy-done | bytes 16408
  38.6 3.3 %shard_map.68.held_ref = bf16[6,256,512]{2,1,0:T(8,128)(2,1)S(1)} custom-call(bf16[8,256,512]{2,1,0:T(8,128)(2,1)S(1)} %copy-done.2, bf16[256,512]{1,0:T(8,128)(2,1)S(1)} %bitcast.18, bf16[256,512]{1,0:T(8,128)(2,1)S(1)} %collective-permute-done.8.other_ref, f32[4,512]{1,0:T(4,128)S(1)} %get-tuple-element.72.fields_ref.first_ref.own_ref, ...), custom_call_target="tpu_custom_call" | custom-call | tf_op jit(solution)/shard_map/pallas_call | solution.py:448
  41.9 0.7 %add.71 = f32[8,128]{1,0:T(8,128)S(1)} add(f32[8,128]{1,0:T(8,128)} %add.70, f32[8,128]{1,0:T(8,128)} %collective-permute-done.14) | non-fusion elementwise | flops 1024 | bytes 12288 | tf_op jit(solution)/shard_map/add | solution.py:551
  42.6 1.6 %collective-permute-start.15 = (f32[8,128]{1,0:T(8,128)S(1)}, f32[8,128]{1,0:T(8,128)S(1)}, u32[]{:S(2)}, u32[]{:S(2)}) collective-permute-start(f32[8,128]{1,0:T(8,128)S(1)} %add.71), channel_id=1, source_target_pairs={{0,4},{1,5},{2,6},{3,7},{4,0},{5,1},{6,2},{7,3},{8,12},{9,13},{10,... | collective-permute-start | bytes 12296 | tf_op jit(solution)/shard_map/ppermute | solution.py:551
  44.2 1.8 %shard_map.69 = (bf16[4,256,512]{2,1,0:T(8,128)(2,1)S(1)}, bf16[2,256,512]{2,1,0:T(8,128)(2,1)S(1)}) custom-call(s32[1]{0:T(128)} %bitcast.core_ref, bf16[4,256,512]{2,1,0:T(8,128)(2,1)} %collective-permute-done.9.partner_ref, bf16[4,256,512]{2,1,0:T(8,128)(2,1)S(1)} %bitcast.14, bf16[256,256]{1,0:T(8,128)(2,1)S(1)} %copy.14.turned_ref), custom_call_target="tpu_custom_call" | custom-call | tf_op jit(solution)/shard_map/pallas_call | solution.py:448
  46.0 2.7 %shard_map.70.shared_ref = f32[4,512]{1,0:T(4,128)S(1)} custom-call(bf16[6,256,512]{2,1,0:T(8,128)(2,1)S(1)} %shard_map.68.held_ref, f32[4,512]{1,0:T(4,128)S(1)} %get-tuple-element.71.second_ref.partner_ref, f32[4,256,128]{2,1,0:T(8,128)S(1)} %get-tuple-element.30.v_ref, bf16[4,256,512]{2,1,0:T(8,128)(2,1)S(1)} %get-tuple-element.45.weight_ref, ...), custom_call_target="tpu_custom_call" | custom-call | tf_op jit(solution)/shard_map/pallas_call | solution.py:448
  48.7 3.8 %shard_map.72 = (f32[4,512]{1,0:T(4,128)S(1)}, f32[4,512]{1,0:T(4,128)S(1)}) custom-call(s32[1]{0:T(128)} %bitcast.core_ref, bf16[2,256,512]{2,1,0:T(8,128)(2,1)} %collective-permute-done.4.message_ref, bf16[4,256,512]{2,1,0:T(8,128)(2,1)S(1)} %get-tuple-element.45.weight_ref, bf16[2,256,512]{2,1,0:T(8,128)(2,1)S(1)} %get-tuple-element.48.own_weight_ref, ...), custom_call_target="tpu_custom_call" | custom-call | tf_op jit(solution)/shard_map/pallas_call | solution.py:448
  52.6 2.7 %collective-permute-start.16 = (f32[8,128]{1,0:T(8,128)S(1)}, f32[8,128]{1,0:T(8,128)S(1)}, u32[]{:S(2)}, u32[]{:S(2)}) collective-permute-start(f32[8,128]{1,0:T(8,128)S(1)} %add.72), channel_id=1, source_target_pairs={{0,8},{1,9},{2,10},{3,11},{4,12},{5,13},{6,14},{7,15},{8,0},{9,1},... | collective-permute-start | bytes 12296 | tf_op jit(solution)/shard_map/ppermute | solution.py:551
  55.2 1.9 %collective-permute-done.16 = f32[8,128]{1,0:T(8,128)S(1)} collective-permute-done((f32[8,128]{1,0:T(8,128)S(1)}, f32[8,128]{1,0:T(8,128)S(1)}, u32[]{:S(2)}, u32[]{:S(2)}) %collective-permute-start.16) | collective-permute-done | bytes 4128 | tf_op jit(solution)/shard_map/ppermute | solution.py:551
  57.1 0.5 slice.89
  58.3 0.6 %add_divide_fusion = f32[4,512]{1,0:T(4,128)} fusion(f32[4,512]{1,0:T(4,128)S(1)} %get-tuple-element.52, f32[4,512]{1,0:T(4,128)S(1)} %collective-permute-done.12, f32[]{:T(128)} %bitcast.6), kind=kLoop, calls=%fused_computation.19 | loop fusion | flops 4096 | bytes 24580 | tf_op jit(solution)/shard_map/div | solution.py:581
  (69 shorter events, 2.8 us)
Async XLA Ops:
  0.0 8.6 %copy-start = (bf16[256,256]{1,0:T(8,128)(2,1)S(1)}, bf16[256,256]{1,0:T(8,128)(2,1)}, u32[]{:S(2)}) copy-start(bf16[256,256]{1,0:T(8,128)(2,1)} %param.9) | copy-start | bytes 393220
  0.0 3.3 %copy-start.10 = (f32[4,512]{1,0:T(4,128)S(1)}, f32[4,512]{1,0:T(4,128)}, u32[]{:S(2)}) copy-start(f32[4,512]{1,0:T(4,128)} %param.6) | copy-start | bytes 24580
  0.0 3.7 %copy-start.5 = (f32[3,256]{1,0:T(4,128)S(1)}, f32[3,256]{1,0:T(4,128)}, u32[]{:S(2)}) copy-start(f32[3,256]{1,0:T(4,128)} %directions_ref.1) | copy-start | bytes 9220
  0.0 3.3 %collective-permute-start.1 = (f32[4,512]{1,0:T(4,128)}, f32[4,512]{1,0:T(4,128)S(1)}, u32[]{:S(2)}, u32[]{:S(2)}) collective-permute-start(f32[4,512]{1,0:T(4,128)} %param.6), channel_id=1, source_target_pairs={{1,0},{0,1},{3,2},{2,3},{5,4},{4,5},{7,6},{6,7},{9,8},{8,9},{11,10... | collective-permute-start | bytes 24584 | tf_op jit(solution)/shard_map/ppermute | solution.py:25
  3.0 5.6 %copy-start.9 = (bf16[256,256]{1,0:T(8,128)(2,1)S(1)}, bf16[256,256]{1,0:T(8,128)(2,1)}, u32[]{:S(2)}) copy-start(bf16[256,256]{1,0:T(8,128)(2,1)} %param.10) | copy-start | bytes 393220
  3.0 5.6 %copy-start.11 = (f32[256]{0:T(256)S(1)}, f32[256]{0:T(256)}, u32[]{:S(2)}) copy-start(f32[256]{0:T(256)} %param.11) | copy-start | bytes 3076
  3.0 5.9 %copy-start.8 = (bf16[256,4,512]{2,1,0:T(4,128)(2,1)S(1)}, bf16[256,4,512]{2,1,0:T(4,128)(2,1)}, u32[]{:S(2)}) copy-start(bf16[256,4,512]{2,1,0:T(4,128)(2,1)} %param.7) | copy-start | bytes 3145732
  4.1 1.6 %collective-permute-start = (bf16[256,512]{1,0:T(8,128)(2,1)S(1)}, bf16[256,512]{1,0:T(8,128)(2,1)S(1)}, u32[]{:S(2)}, u32[]{:S(2)}) collective-permute-start(bf16[256,512]{1,0:T(8,128)(2,1)S(1)} %get-tuple-element.31.edge_ref), channel_id=1, source_target_pairs={{1,0},{0,1},{3,2},{2,3},{5,4},{4,5},{7,6},{6,7},{9,8},{8,9},{11,10... | collective-permute-start | bytes 786440 | tf_op jit(solution)/shard_map/ppermute | solution.py:25
  5.9 12.0 %collective-permute-start.2 = (bf16[272,512]{1,0:T(8,128)(2,1)S(1)}, bf16[272,512]{1,0:T(8,128)(2,1)S(1)}, u32[]{:S(2)}, u32[]{:S(2)}) collective-permute-start(bf16[272,512]{1,0:T(8,128)(2,1)S(1)} %maximum_maximum_fusion), channel_id=1, source_target_pairs={{0,2},{1,15},{2,4},{3,1},{4,6},{5,3},{6,8},{7,5},{8,10},{9,7},{10,... | collective-permute-start | bytes 835592 | tf_op jit(solution)/shard_map/ppermute | solution.py:30
  11.4 6.6 %collective-permute-start.5 = (bf16[1,256,512]{2,1,0:T(8,128)(2,1)S(1)}, bf16[1,256,512]{2,1,0:T(8,128)(2,1)S(1)}, u32[]{:S(2)}, u32[]{:S(2)}) collective-permute-start(bf16[1,256,512]{2,1,0:T(8,128)(2,1)S(1)} %get-tuple-element.36), channel_id=1, source_target_pairs={{1,0},{0,1},{3,2},{2,3},{5,4},{4,5},{7,6},{6,7},{9,8},{8,9},{11,10... | collective-permute-start | bytes 786440 | tf_op jit(solution)/shard_map/ppermute | solution.py:25
  17.9 3.8 %collective-permute-start.7 = (bf16[272,512]{1,0:T(8,128)(2,1)S(1)}, bf16[272,512]{1,0:T(8,128)(2,1)S(1)}, u32[]{:S(2)}, u32[]{:S(2)}) collective-permute-start(bf16[272,512]{1,0:T(8,128)(2,1)S(1)} %collective-permute-done.2), channel_id=1, source_target_pairs={{1,0},{0,1},{3,2},{2,3},{5,4},{4,5},{7,6},{6,7},{9,8},{8,9},{11,10... | collective-permute-start | bytes 835592 | tf_op jit(solution)/shard_map/ppermute | solution.py:25
  18.1 9.8 %collective-permute-start.6 = (bf16[1,256,512]{2,1,0:T(8,128)(2,1)S(1)}, bf16[1,256,512]{2,1,0:T(8,128)(2,1)S(1)}, u32[]{:S(2)}, u32[]{:S(2)}) collective-permute-start(bf16[1,256,512]{2,1,0:T(8,128)(2,1)S(1)} %broadcast_select_fusion.1), channel_id=1, source_target_pairs={{0,2},{1,15},{2,4},{3,1},{4,6},{5,3},{6,8},{7,5},{8,10},{9,7},{10,... | collective-permute-start | bytes 786440 | tf_op jit(solution)/shard_map/ppermute | solution.py:30
  18.3 4.9 %collective-permute-start.3 = (bf16[2,256,512]{2,1,0:T(8,128)(2,1)S(1)}, bf16[2,256,512]{2,1,0:T(8,128)(2,1)S(1)}, u32[]{:S(2)}, u32[]{:S(2)}) collective-permute-start(bf16[2,256,512]{2,1,0:T(8,128)(2,1)S(1)} %shard_map.66), channel_id=1, source_target_pairs={{1,0},{0,1},{3,2},{2,3},{5,4},{4,5},{7,6},{6,7},{9,8},{8,9},{11,10... | collective-permute-start | bytes 1572872 | tf_op jit(solution)/shard_map/ppermute | solution.py:25
  21.8 11.1 %copy-start.3 = (f32[8,512]{1,0:T(8,128)}, f32[8,512]{1,0:T(8,128)S(1)}, u32[]{:S(2)}) copy-start(f32[8,512]{1,0:T(8,128)S(1)} %pad_maximum_fusion.beyond_ref) | copy-start | bytes 49156
  27.9 16.2 %collective-permute-start.9 = (bf16[4,256,512]{2,1,0:T(8,128)(2,1)S(1)}, bf16[4,256,512]{2,1,0:T(8,128)(2,1)}, u32[]{:S(2)}, u32[]{:S(2)}) collective-permute-start(bf16[4,256,512]{2,1,0:T(8,128)(2,1)S(1)} %bitcast.13), channel_id=1, source_target_pairs={{1,0},{0,1},{3,2},{2,3},{5,4},{4,5},{7,6},{6,7},{9,8},{8,9},{11,10... | collective-permute-start | bytes 3145736 | tf_op jit(solution)/shard_map/ppermute | solution.py:25
  28.3 17.6 %collective-permute-start.10 = (bf16[4,256,512]{2,1,0:T(8,128)(2,1)}, bf16[4,256,512]{2,1,0:T(8,128)(2,1)S(1)}, u32[]{:S(2)}, u32[]{:S(2)}) collective-permute-start(bf16[4,256,512]{2,1,0:T(8,128)(2,1)} %get-tuple-element.46.own_state_ref), channel_id=1, source_target_pairs={{1,0},{0,1},{3,2},{2,3},{5,4},{4,5},{7,6},{6,7},{9,8},{8,9},{11,10... | collective-permute-start | bytes 3145736 | tf_op jit(solution)/shard_map/ppermute | solution.py:25
  28.5 3.8 %collective-permute-start.11 = (bf16[2,256,512]{2,1,0:T(8,128)(2,1)S(1)}, bf16[2,256,512]{2,1,0:T(8,128)(2,1)S(1)}, u32[]{:S(2)}, u32[]{:S(2)}) collective-permute-start(bf16[2,256,512]{2,1,0:T(8,128)(2,1)S(1)} %get-tuple-element.50), channel_id=1, source_target_pairs={{1,0},{0,1},{3,2},{2,3},{5,4},{4,5},{7,6},{6,7},{9,8},{8,9},{11,10... | collective-permute-start | bytes 1572872 | tf_op jit(solution)/shard_map/ppermute | solution.py:25
  28.9 19.8 %collective-permute-start.4 = (bf16[2,256,512]{2,1,0:T(8,128)(2,1)}, bf16[2,256,512]{2,1,0:T(8,128)(2,1)}, u32[]{:S(2)}, u32[]{:S(2)}) collective-permute-start(bf16[2,256,512]{2,1,0:T(8,128)(2,1)} %broadcast_select_fusion), channel_id=1, source_target_pairs={{0,2},{1,15},{2,4},{3,1},{4,6},{5,3},{6,8},{7,5},{8,10},{9,7},{10,... | collective-permute-start | bytes 1572872 | tf_op jit(solution)/shard_map/ppermute | solution.py:30
  28.9 7.4 %collective-permute-start.8 = (bf16[256,512]{1,0:T(8,128)(2,1)S(1)}, bf16[256,512]{1,0:T(8,128)(2,1)S(1)}, u32[]{:S(2)}, u32[]{:S(2)}) collective-permute-start(bf16[256,512]{1,0:T(8,128)(2,1)S(1)} %bitcast.16), channel_id=1, source_target_pairs={{1,0},{0,1},{3,2},{2,3},{5,4},{4,5},{7,6},{6,7},{9,8},{8,9},{11,10... | collective-permute-start | bytes 786440 | tf_op jit(solution)/shard_map/ppermute | solution.py:25
  32.9 1.4 %copy-start.1 = (bf16[8,256,512]{2,1,0:T(8,128)(2,1)}, bf16[8,256,512]{2,1,0:T(8,128)(2,1)S(1)}, u32[]{:S(2)}) copy-start(bf16[8,256,512]{2,1,0:T(8,128)(2,1)S(1)} %get-tuple-element.40.held_ref.own_ref) | copy-start | bytes 6291460
  34.2 1.9 %copy-start.6 = (f32[2,512]{1,0:T(2,128)}, f32[2,512]{1,0:T(2,128)S(1)}, u32[]{:S(2)}) copy-start(f32[2,512]{1,0:T(2,128)S(1)} %get-tuple-element.51.met_ref) | copy-start | bytes 12292
  34.3 1.2 %collective-permute-start.13 = (f32[8,128]{1,0:T(8,128)S(1)}, f32[8,128]{1,0:T(8,128)S(1)}, u32[]{:S(2)}, u32[]{:S(2)}) collective-permute-start(f32[8,128]{1,0:T(8,128)S(1)} %get-tuple-element.54), channel_id=1, source_target_pairs={{0,1},{1,0},{2,3},{3,2},{4,5},{5,4},{6,7},{7,6},{8,9},{9,8},{10,11... | collective-permute-start | bytes 12296 | tf_op jit(solution)/shard_map/ppermute | solution.py:551
  36.0 5.8 %collective-permute-start.14 = (f32[8,128]{1,0:T(8,128)}, f32[8,128]{1,0:T(8,128)}, u32[]{:S(2)}, u32[]{:S(2)}) collective-permute-start(f32[8,128]{1,0:T(8,128)} %add.70), channel_id=1, source_target_pairs={{0,2},{1,3},{2,0},{3,1},{4,6},{5,7},{6,4},{7,5},{8,10},{9,11},{10,... | collective-permute-start | bytes 12296 | tf_op jit(solution)/shard_map/ppermute | solution.py:551
  36.3 1.6 %copy-start.2 = (bf16[8,256,512]{2,1,0:T(8,128)(2,1)S(1)}, bf16[8,256,512]{2,1,0:T(8,128)(2,1)}, u32[]{:S(2)}) copy-start(bf16[8,256,512]{2,1,0:T(8,128)(2,1)} %copy-done.1) | copy-start | bytes 6291460
  37.9 0.7 %copy-start.4 = (f32[8,512]{1,0:T(8,128)S(1)}, f32[8,512]{1,0:T(8,128)}, u32[]{:S(2)}) copy-start(f32[8,512]{1,0:T(8,128)} %copy-done.3) | copy-start | bytes 49156
  42.6 10.0 %collective-permute-start.15 = (f32[8,128]{1,0:T(8,128)S(1)}, f32[8,128]{1,0:T(8,128)S(1)}, u32[]{:S(2)}, u32[]{:S(2)}) collective-permute-start(f32[8,128]{1,0:T(8,128)S(1)} %add.71), channel_id=1, source_target_pairs={{0,4},{1,5},{2,6},{3,7},{4,0},{5,1},{6,2},{7,3},{8,12},{9,13},{10,... | collective-permute-start | bytes 12296 | tf_op jit(solution)/shard_map/ppermute | solution.py:551
  46.0 2.7 %copy-start.7 = (f32[2,512]{1,0:T(2,128)S(1)}, f32[2,512]{1,0:T(2,128)}, u32[]{:S(2)}) copy-start(f32[2,512]{1,0:T(2,128)} %copy-done.6) | copy-start | bytes 12292
  52.5 5.8 %collective-permute-start.12 = (f32[4,512]{1,0:T(4,128)S(1)}, f32[4,512]{1,0:T(4,128)S(1)}, u32[]{:S(2)}, u32[]{:S(2)}) collective-permute-start(f32[4,512]{1,0:T(4,128)S(1)} %get-tuple-element.53), channel_id=1, source_target_pairs={{1,0},{0,1},{3,2},{2,3},{5,4},{4,5},{7,6},{6,7},{9,8},{8,9},{11,10... | collective-permute-start | bytes 24584 | tf_op jit(solution)/shard_map/ppermute | solution.py:25
  52.6 4.6 %collective-permute-start.16 = (f32[8,128]{1,0:T(8,128)S(1)}, f32[8,128]{1,0:T(8,128)S(1)}, u32[]{:S(2)}, u32[]{:S(2)}) collective-permute-start(f32[8,128]{1,0:T(8,128)S(1)} %add.72), channel_id=1, source_target_pairs={{0,8},{1,9},{2,10},{3,11},{4,12},{5,13},{6,14},{7,15},{8,0},{9,1},... | collective-permute-start | bytes 12296 | tf_op jit(solution)/shard_map/ppermute | solution.py:551
where the time goes:
time: 59.2 us; the launch traced here: 58.9 us
  Pallas kernels  21.8 us (37%)
  starting transfers between devices  18.3 us (31%)
  local copies, waits for them, and re-layouts  7.52 us (13%)
  waiting for transfers between devices  6.56 us (11%)
  other arithmetic  3.41 us (6%)
  between operations  1.05 us (2%)
    pallas_call x9, Pallas kernels, kernel_call(): pl.pallas_call(kernel, out_shape=outs, in_specs=[smem if arg.dtype == jnp...  21.8 us
    ppermute x10, starting transfers between devices, swap_species(): return lax.ppermute(block, 'space', [(i ^ 1, i) for i in range(count)])  10.6 us
    ppermute x4, starting transfers between devices, shards(): lax.ppermute(partition, 'space', [(i, i ^ distance) for i in range(count)])  4.71 us
    ppermute x10, waiting for transfers between devices, swap_species(): return lax.ppermute(block, 'space', [(i ^ 1, i) for i in range(count)])  3.81 us
    unnamed x24, local copies, waits for them, and re-layouts  3.71 us
    ppermute x3, starting transfers between devices, to_next_slab(): lax.ppermute(block, 'space', [(i, (i + (2 if i % 2 == 0 else -2)) % count...  2.92 us
    ppermute x4, waiting for transfers between devices, shards(): lax.ppermute(partition, 'space', [(i, i ^ distance) for i in range(count)])  2.74 us
    slice x1, local copies, waits for them, and re-layouts, shards(): end_weights[:, -1]  2.48 us
  transfers between devices with their start and end apart: 17, of which 5 were waited for; matrix products, arithmetic and copies ran while one was open for 11% of the time, Pallas kernels for 36%

commit v1 on v0

--- a/solution.py
+++ b/solution.py
@@ -104,9 +104,9 @@
     return jnp.exp(-0.5 * field)
 
 
-def prologue_kernel(core_ref, directions_ref, low_ref, high_ref, fields_ref, spread_ref, edge_ref):
+def prologue_kernel(core_ref, directions_ref, start_ref, fields_ref, spread_ref, edge_ref):
     sign = 1.0 - 2.0 * core_ref[0].astype(F32)
-    orient, cells = edge_ref.shape
+    planes, orient, cells = start_ref.shape
     low = boltzmann(fields_ref[0:1])
     high = boltzmann(fields_ref[fields_ref.shape[0] - 1 :])
     for c in range(4):
@@ -121,7 +121,9 @@
         for t in range(cells // LANES):
             at = rows, columns(t)
             chosen = jnp.where(
-                plus_x, high[:, columns(t)] * high_ref[at].astype(F32), low[:, columns(t)] * low_ref[at].astype(F32)
+                plus_x,
+                high[:, columns(t)] * start_ref[planes - 1, *at].astype(F32),
+                low[:, columns(t)] * start_ref[0, *at].astype(F32),
             )
             edge_ref[at] = chosen.astype(BF16)
 
@@ -149,14 +151,17 @@
             store_plane(moved, p, rows, drift(loaded[p], before, after, geo))
 
 
-def first_alone_kernel(start_ref, first_ref, v_ref, m_ref, out_ref, edges_ref, held, moved):
+def first_alone_kernel(start_ref, first_ref, v_ref, m_ref, out_ref, inner_ref, edges_ref, held, moved):
     planes, orient, _ = start_ref.shape
     first = boltzmann(first_ref[...])
     for p in range(planes):
         held[p] = (first[p : p + 1] * start_ref[p].astype(F32)).astype(BF16)
     alone_step(held, moved, range(planes), v_ref, None, 0)
     for p in (0, planes - 1, *range(1, planes - 1)):
-        out_ref[p] = (first[p : p + 1] * first[p : p + 1] * mix(m_ref[...], moved[p])).astype(BF16)
+        state = (first[p : p + 1] * first[p : p + 1] * mix(m_ref[...], moved[p])).astype(BF16)
+        out_ref[p] = state
+        if 0 < p < planes - 1:
+            inner_ref[p - 1] = state
 
     @each_row_block(orient)
     def _(index):
@@ -202,7 +207,7 @@
 
 def second_step_kernel(
     core_ref, alone_ref, edge_ref, mine_ref, other_ref, first_ref, second_ref, beyond_ref, v_ref, m_ref,
-    out_ref, next_ref, sent_ref, held, moved,
+    out_ref, next_ref, sent_ref, kept_ref, outer_ref, held, moved,
 ):
     planes, orient, _ = alone_ref.shape
     matrix = m_ref[...]
@@ -225,8 +230,8 @@
         if p in (0, planes - 1):
             arrived = squared[p : p + 1] * mix(matrix, moved[min(p, 1)])
             kept = (kept.astype(F32) + arrived).astype(BF16)
+            out_ref[min(p, 1)] = kept
         held[p + 1] = kept
-        out_ref[p] = kept
     held[0] = (beyond[0:1] * beyond[0:1] * mix(matrix, moved[2])).astype(BF16)
     held[planes + 1] = (beyond[2:3] * beyond[2:3] * mix(matrix, moved[3])).astype(BF16)
     count = planes + 2
@@ -253,14 +258,16 @@
     core = core_ref[0]
     for p in range(planes // 2):
         sent_ref[p] = next_ref[2 + (planes - 1) * (1 - core) + (2 * core - 1) * p]
+        kept_ref[p] = next_ref[2 + (planes - 1) * core + (1 - 2 * core) * p]
+    outer_ref[0:1] = beyond[4:5] * beyond[4:5]
+    outer_ref[1:2] = beyond[6:7] * beyond[6:7]
 
 
 def middle_kernel(
-    core_ref, own_ref, partner_ref, message_ref, first_ref, second_ref, v_ref, m_ref, out_ref, total_ref, moved
+    own_ref, partner_ref, message_ref, first_ref, second_ref, v_ref, m_ref, out_ref, total_ref, moved
 ):
     orient, cells = message_ref.shape
     cross = boltzmann(first_ref[...]) * boltzmann(second_ref[...])
-    core = core_ref[0]
 
     @each_row_block(orient)
     def _(index):
@@ -272,16 +279,13 @@
             moved[0, rows, columns(t)] = jnp.where(ahead, gained, 0.0).astype(BF16)
             moved[1, rows, columns(t)] = jnp.where(ahead, 0.0, gained).astype(BF16)
 
-    planes = own_ref.shape[0] - 4
-    face_plane = 2 + (planes - 1) * core
-    own_face = own_ref[face_plane].astype(F32) + cross[0:1] * mix(m_ref[...], moved[0])
+    own_face = own_ref[0].astype(F32) + cross[0:1] * mix(m_ref[...], moved[0])
     partner_face = partner_ref[0].astype(F32) + cross[0:1] * mix(m_ref[...], moved[1])
     face = jnp.sum(own_face * partner_face, axis=0, keepdims=True)
     total = jnp.zeros((1, 1), F32)
-    for p in range(planes // 2):
+    for p in range(own_ref.shape[0]):
         if p > 0:
-            own = own_ref[face_plane + p - 2 * p * core].astype(F32)
-            face = jnp.sum(own * partner_ref[p].astype(F32), axis=0, keepdims=True)
+            face = jnp.sum(own_ref[p].astype(F32) * partner_ref[p].astype(F32), axis=0, keepdims=True)
         met = face / (orient * cross[p : p + 1])
         out_ref[p : p + 1] = met
         total = total + jnp.sum(met, axis=1, keepdims=True)
@@ -289,12 +293,11 @@
 
 
 def third_step_kernel(
-    held_ref, mine_ref, other_ref, first_ref, second_ref, beyond_ref, v_ref, m_ref, next_ref, held, moved
+    held_ref, mine_ref, other_ref, first_ref, second_ref, outer_ref, v_ref, m_ref, next_ref, held, moved
 ):
     planes, orient, _ = held.shape
     matrix = m_ref[...]
     first, second = boltzmann(first_ref[...]), boltzmann(second_ref[...])
-    beyond = boltzmann(beyond_ref[...])
     face_drifts(v_ref, mine_ref, other_ref, moved, (0, 1))
     cross = first * second
     for p in range(planes):
@@ -315,7 +318,7 @@
             store_plane(moved, p, rows, drift(loaded[p + 1], loaded[p], loaded[p + 2], geo))
 
     squared = second * second
-    factors = [beyond[4:5] * beyond[4:5]] + [squared[p : p + 1] for p in range(planes)] + [beyond[6:7] * beyond[6:7]]
+    factors = [outer_ref[0:1]] + [squared[p : p + 1] for p in range(planes)] + [outer_ref[1:2]]
     for p, factor in enumerate(factors):
         next_ref[p] = (factor * mix(matrix, moved[p])).astype(BF16)
 
@@ -333,8 +336,8 @@
     return jnp.sum(value.reshape(ROWS // 8, 8, LANES), axis=0)
 
 
-def pairing_kernel(held_ref, second_ref, v_ref, weight_ref, partner_ref, out_ref):
-    planes, orient, cells = partner_ref.shape
+def pairing_kernel(held_ref, second_ref, v_ref, weight_ref, faces_ref, inner_ref, out_ref):
+    planes, orient, cells = weight_ref.shape
     second = boltzmann(second_ref[...])
     tiles = cells // LANES
 
@@ -346,7 +349,8 @@
         for p in range(planes):
             moved_tiles = drift(loaded[p + 1], loaded[p], loaded[p + 2], geo)
             weights = load_plane(weight_ref, p, rows)
-            partner = load_plane(partner_ref, p, rows)
+            on_face = p in (0, planes - 1)
+            partner = load_plane(faces_ref, min(p, 1), rows) if on_face else load_plane(inner_ref, p - 1, rows)
             for t in range(tiles):
                 last, third = sums[2 * (p * tiles + t)], sums[2 * (p * tiles + t) + 1]
                 new.append(last + fold(moved_tiles[t] * weights[t].astype(F32)))
@@ -354,7 +358,7 @@
         return tuple(new)
 
     zero = jnp.zeros((8, LANES), F32)
-    sums = lax.fori_loop(0, orient // ROWS, body, (zero,) * (2 * planes * tiles))
+    sums = lax.fori_loop(0, orient // ROWS, body, (zero,) * (2 * planes * tiles), unroll=UNROLL)
     for p in range(planes):
         for t in range(tiles):
             last = jnp.sum(sums[2 * (p * tiles + t)], axis=0, keepdims=True)
@@ -364,7 +368,7 @@
 
 
 def last_kernel(
-    core_ref, message_ref, weight_ref, own_weight_ref, own_state_ref, partner_state_ref, shared_ref, met_ref,
+    core_ref, message_ref, weight_ref, own_weight_ref, own_faces_ref, partner_faces_ref, shared_ref, met_ref,
     own_ref, partner_ref, v_ref, m_ref, sent_ref, kept_ref, moved, gained,
 ):
     planes, cells = shared_ref.shape
@@ -407,7 +411,7 @@
                 weights = [load_plane(weight_ref, p, rows) for p in (face, inner)]
             else:
                 weights = [load_plane(own_weight_ref, p, rows) for p in (0, 1)]
-            third = load_plane((partner_state_ref, own_state_ref)[s], face, rows)
+            third = load_plane((partner_faces_ref, own_faces_ref)[s], core, rows)
             for t in range(tiles):
                 on_face = moved_tiles[t] + sides[s] * message[t].astype(F32)
                 wide = change[t].astype(F32)
@@ -421,7 +425,7 @@
         return tuple(new)
 
     zero = jnp.zeros((8, LANES), F32)
-    sums = lax.fori_loop(0, orient // ROWS, body, (zero,) * (6 * tiles))
+    sums = lax.fori_loop(0, orient // ROWS, body, (zero,) * (6 * tiles), unroll=UNROLL)
     for t in range(tiles):
         shares = []
         for s in range(2):
@@ -451,7 +455,7 @@
         in_specs=[smem if arg.dtype == jnp.int32 else vmem for arg in args],
         out_specs=jax.tree.map(lambda _: vmem, outs),
         scratch_shapes=[pltpu.VMEM(shape, BF16) for shape in scratch],
-        compiler_params=pltpu.CompilerParams(vmem_limit_bytes=12 << 20),
+        compiler_params=pltpu.CompilerParams(vmem_limit_bytes=8 << 20),
         cost_estimate=pl.CostEstimate(flops=0, bytes_accessed=0, transcendentals=0),
     )(*args)
 
@@ -471,11 +475,12 @@
     plane = jax.ShapeDtypeStruct((orient, cells), BF16)
     wide = lambda extra: jax.ShapeDtypeStruct((planes + extra, orient, cells), BF16)
     core_word = jnp.reshape(core, (1,)).astype(jnp.int32)
+    start = jnp.transpose(end_weights, (1, 0, 2))
     spread, edge0 = kernel_call(
         prologue_kernel,
         (jax.ShapeDtypeStruct((4, orient, LANES), F32), plane),
         (),
-        (core_word, directions, end_weights[:, 0], end_weights[:, -1], own),
+        (core_word, directions, start, own),
     )
     ahead = spread[3, :, :1] > 0
 
@@ -493,12 +498,11 @@
     mixing = jnp.dot(scaled, analysis.astype(F32), precision=lax.Precision.HIGHEST) + 1.0 / orient
     matrix = mixing.astype(BF16)
 
-    raw, _ = lax.optimization_barrier((end_weights, edge0))
-    start, _ = lax.optimization_barrier((jnp.transpose(raw, (1, 0, 2)), message0))
+    start, _ = lax.optimization_barrier((start, message0))
     arrived0 = to_next_slab(message0)
-    alone, edges1 = kernel_call(
+    alone, inner, edges1 = kernel_call(
         first_alone_kernel,
-        (slab, jax.ShapeDtypeStruct((1, orient, cells), BF16)),
+        (slab, wide(-2), jax.ShapeDtypeStruct((1, orient, cells), BF16)),
         (slab.shape, slab.shape),
         (start, own, spread, matrix),
     )
@@ -509,7 +513,14 @@
         (slab.shape, slab.shape),
         (alone, own, partner, spread, matrix),
     )
-    edges, arrived0 = lax.optimization_barrier((edges, arrived0))
+    weights, own_weights = kernel_call(
+        weight_kernel,
+        (slab, jax.ShapeDtypeStruct((2, orient, cells), BF16)),
+        (),
+        (core_word, swap_species(start), start, matrix.T),
+    )
+    edges, arrived0, weights, inner = lax.optimization_barrier((edges, arrived0, weights, inner))
+    partner_inner = swap_species(inner)
     message2 = message(edges, swap_species(edges))
     arrived = [to_next_slab(message1)[0], to_next_slab(message2)]
     crossed0 = swap_species(arrived0)
@@ -526,55 +537,58 @@
     high_second = jnp.where(is_first, other_second, mine_second)
     beyond = jnp.concatenate([low_first, high_first, low_second, high_second])
 
-    alone, *_ = lax.optimization_barrier((alone, message1, message2))
+    alone, *_ = lax.optimization_barrier((alone, message1, message2, partner_inner))
     half = planes // 2
     half_slab = jax.ShapeDtypeStruct((half, orient, cells), BF16)
-    first_state, second_state, sent_half = kernel_call(
+    first_faces, second_state, sent_half, kept_half, outer = kernel_call(
         second_step_kernel,
-        (slab, wide(4), half_slab),
+        (wide(2 - planes), wide(4), half_slab, half_slab, jax.ShapeDtypeStruct((2, cells), F32)),
         (wide(2).shape, wide(4).shape),
         (core_word, alone, edge0, arrived0[:orient], crossed0[:orient], own, partner, beyond, spread, matrix),
     )
     arrived1, second_state = lax.optimization_barrier((arrived[0], second_state))
-    sent_half, start, first_state, _ = lax.optimization_barrier((sent_half, start, first_state, arrived1))
+    sent_half, first_faces, _ = lax.optimization_barrier((sent_half, first_faces, arrived1))
+    partner_faces = swap_species(first_faces)
+    partner_half, crossed1 = lax.optimization_barrier((swap_species(sent_half), swap_species(arrived1)))
     own_half_field = jnp.where(is_first, own[:half], own[half:][::-1])
     partner_half_field = jnp.where(is_first, partner[:half], partner[half:][::-1])
+    density = jax.ShapeDtypeStruct((planes, cells), F32)
     met, partition = kernel_call(
         middle_kernel,
-        (jax.ShapeDtypeStruct((half, cells), F32), jax.ShapeDtypeStruct((8, LANES), F32)),
+        (jax.ShapeDtypeStruct((half, cells), F32), density),
         ((2, orient, cells),),
-        (core_word, second_state, swap_species(sent_half), arrived1, own_half_field, partner_half_field, spread, matrix),
+        (kept_half, partner_half, arrived1, own_half_field, partner_half_field, spread, matrix),
     )
     count = lax.axis_size("space")
-    distance = 1
-    while distance < count:
-        partition = partition + lax.ppermute(partition, "space", [(i, i ^ distance) for i in range(count)])
-        distance *= 2
-    partition = partition[0, 0] / (count // 2 * planes * cells)
-
-    crossed1 = swap_species(arrived1)
+
+    def gathered(value, distance, after):
+        received = lax.ppermute(value, "space", [(i, i ^ distance) for i in range(count)])
+        received, after = lax.optimization_barrier((received, after))
+        return value + received, after
+
+    partition, second_state = gathered(partition, 1, second_state)
+    second_state, _ = lax.optimization_barrier((second_state, partition))
     third_state = kernel_call(
         third_step_kernel,
         wide(2),
         (slab.shape, wide(2).shape),
-        (second_state, arrived1, crossed1, own, partner, beyond, spread, matrix),
-    )
-    weights, own_weights = kernel_call(
-        weight_kernel,
-        (slab, jax.ShapeDtypeStruct((2, orient, cells), BF16)),
-        (),
-        (core_word, swap_species(start), start, matrix.T),
-    )
-    partner_state = swap_species(first_state)
-    density = jax.ShapeDtypeStruct((planes, cells), F32)
-    shared = kernel_call(pairing_kernel, density, (), (third_state, partner, spread, weights, partner_state))
+        (second_state, arrived1, crossed1, own, partner, outer, spread, matrix),
+    )
+    partition, third_state = gathered(partition, 2, third_state)
+    third_state, _ = lax.optimization_barrier((third_state, partition))
+    shared = kernel_call(pairing_kernel, density, (), (third_state, partner, spread, weights, partner_faces, partner_inner))
+    distance = 4
+    while distance < count:
+        partition, shared = gathered(partition, distance, shared)
+        distance *= 2
+    partition = partition / (count // 2 * planes * cells)
     arrived2, shared = lax.optimization_barrier((arrived[1], shared))
     sent, kept = kernel_call(
         last_kernel,
         (density, density),
         ((2, orient, cells), (2, orient, cells)),
         (
-            core_word, arrived2, weights, own_weights, first_state, partner_state, shared, met,
+            core_word, arrived2, weights, own_weights, first_faces, partner_faces, shared, met,
             own, partner, spread, matrix,
         ),
     )

time: 59.2 us -> 55.9 us (0.944)
  waiting for transfers between devices: 6.56 us -> 13 us
  local copies, waits for them, and re-layouts: 7.52 us -> 3.74 us
  starting transfers between devices: 18.3 us -> 15 us
  Pallas kernels: 21.8 us -> 18.9 us
  other arithmetic: 3.41 us -> 4.33 us
  between operations: 1.05 us -> 0.34 us
    ppermute x4, waiting for transfers between devices: 2.74 us -> 8.25 us  [gathered(): lax.ppermute(value, 'space', [(i, i ^ distance) for i in range(count)])]
    slice x2 -> x0, local copies, waits for them, and re-layouts: 2.99 us -> none  [the longest x1 2.48 us: shards(): end_weights[:, -1]]
    pallas_call x9, Pallas kernels: 21.8 us -> 18.9 us  [kernel_call(): pl.pallas_call(kernel, out_shape=outs, in_specs=[smem if arg.dtype == jnp...]
    ppermute x10 -> x11, starting transfers between devices: 10.6 us -> 8.63 us  [swap_species(): return lax.ppermute(block, 'space', [(i ^ 1, i) for i in range(count)])]
    ppermute x4, starting transfers between devices: 4.71 us -> 2.89 us  [gathered(): lax.ppermute(value, 'space', [(i, i ^ distance) for i in range(count)])]
    unnamed x24 -> x23, local copies, waits for them, and re-layouts: 3.71 us -> 2.29 us
    add x5 -> x4, other arithmetic: 1.37 us -> 0.08 us  [the longest x1 0.07 us: shards(): own = fields + ramp]
    slice x1, local copies, waits for them, and re-layouts: 0.02 us -> 0.97 us  [shards(): arrived0[:orient]]
  transfers between devices with their start and end apart: 17 -> 18, of which waited for: 5 -> 9; matrix products, arithmetic and copies ran while one was open for 11% -> 10% of each run, Pallas kernels for 36% -> 30%
where the time goes in v1:
time: 55.9 us; the launch traced here: 55.6 us
  Pallas kernels  18.9 us (34%)
  starting transfers between devices  15 us (27%)
  waiting for transfers between devices  13 us (23%)
  other arithmetic  4.33 us (8%)
  local copies, waits for them, and re-layouts  3.74 us (7%)
    pallas_call x9, Pallas kernels, kernel_call(): pl.pallas_call(kernel, out_shape=outs, in_specs=[smem if arg.dtype == jnp...  18.9 us
    ppermute x11, starting transfers between devices, swap_species(): return lax.ppermute(block, 'space', [(i ^ 1, i) for i in range(count)])  8.63 us
    ppermute x4, waiting for transfers between devices, gathered(): lax.ppermute(value, 'space', [(i, i ^ distance) for i in range(count)])  8.25 us
    ppermute x11, waiting for transfers between devices, swap_species(): return lax.ppermute(block, 'space', [(i ^ 1, i) for i in range(count)])  4.39 us
    ppermute x3, starting transfers between devices, to_next_slab(): lax.ppermute(block, 'space', [(i, (i + (2 if i % 2 == 0 else -2)) % count...  3.44 us
    ppermute x4, starting transfers between devices, gathered(): lax.ppermute(value, 'space', [(i, i ^ distance) for i in range(count)])  2.89 us
    unnamed x23, local copies, waits for them, and re-layouts  2.29 us
    select_n x3, other arithmetic, message(): return jnp.where(ahead, mine, other)  1.27 us
  transfers between devices with their start and end apart: 18, of which 9 were waited for; matrix products, arithmetic and copies ran while one was open for 10% of the time, Pallas kernels for 30%

profile of v1, /device:TPU:0, one launch (start us, length us, event | category | flops | bytes accessed | tf_op | source)
XLA Modules:
  0.0 55.6 jit_solution(5817340507078942332)
XLA Ops:
  0.0 0.5 collective-permute-start.1
  0.5 1.5 %copy.12 = bf16[256,4,512]{2,0,1:T(8,128)(2,1)S(1)} copy(bf16[256,4,512]{2,1,0:T(4,128)(2,1)} %param.7) | data formatting | bytes 2097152 | tf_op args[1]
  3.0 0.6 %broadcast_select_fusion.3 = (f32[2,512]{1,0:T(2,128)}, f32[2,512]{1,0:T(2,128)S(1)}, f32[2,512]{1,0:T(2,128)S(1)}, f32[2,512]{1,0:T(2,128)}) fusion(f32[2,512]{1,0:T(2,128)S(1)} %rev.7, pred[]{:T(512)S(6)} %eq.5, f32[4,512]{1,0:T(4,128)S(1)} %get-tuple-element.100.second_ref.partner_ref, f32[1,512]{1,0:T(1,128)S(1)} %get-tuple-element.98, ...), kind=kLoop, calls=%fused_computation.24 | loop fusion | flops 6144 | bytes 40961 | tf_op jit(solution)/shard_map/jit(_where)/select_n | solution.py:554
  3.7 0.7 %collective-permute-done = bf16[256,512]{1,0:T(8,128)(2,1)S(1)} collective-permute-done((bf16[256,512]{1,0:T(8,128)(2,1)S(1)}, bf16[256,512]{1,0:T(8,128)(2,1)S(1)}, u32[]{:S(2)}, u32[]{:S(2)}) %collective-permute-start) | collective-permute-done | bytes 262176 | tf_op jit(solution)/shard_map/ppermute | solution.py:25
  4.6 0.8 %maximum_maximum_fusion = bf16[272,512]{1,0:T(8,128)(2,1)} fusion(bf16[4,512]{1,0:T(4,128)(2,1)S(1)} %get-tuple-element.94, bf16[4,512]{1,0:T(4,128)(2,1)S(1)} %get-tuple-element.93, bf16[256,512]{1,0:T(8,128)(2,1)S(1)} %broadcast_select_fusion.2, bf16[272]{0:T(512)(128)(2,1)S(1)} %pad.7.clone), kind=kLoop, calls=%fused_computation.4 | loop fusion | flops 1114112 | bytes 549408 | tf_op jit(solution)/shard_map/concatenate | solution.py:495
  5.5 2.9 %collective-permute-start.2 = (bf16[272,512]{1,0:T(8,128)(2,1)}, bf16[272,512]{1,0:T(8,128)(2,1)}, u32[]{:S(2)}, u32[]{:S(2)}) collective-permute-start(bf16[272,512]{1,0:T(8,128)(2,1)} %maximum_maximum_fusion), channel_id=1, source_target_pairs={{0,2},{1,15},{2,4},{3,1},{4,6},{5,3},{6,8},{7,5},{8,10},{9,7},{10,... | collective-permute-start | bytes 835592 | tf_op jit(solution)/shard_map/ppermute | solution.py:30
  8.7 2.3 %shard_map.65 = (bf16[4,256,512]{2,1,0:T(8,128)(2,1)S(1)}, bf16[2,256,512]{2,1,0:T(8,128)(2,1)S(1)}, bf16[1,256,512]{2,1,0:T(8,128)(2,1)S(1)}) custom-call(bf16[4,256,512]{2,1,0:T(8,128)(2,1)S(1)} %bitcast.9, f32[4,512]{1,0:T(4,128)S(1)} %get-tuple-element.99.fields_ref.first_ref.own_ref, f32[4,256,128]{2,1,0:T(8,128)S(1)} %get-tuple-element.45.v_ref, ...), custom_call_target="tpu_custom_call" | custom-call | tf_op jit(solution)/shard_map/pallas_call | solution.py:452
  11.0 0.8 %copy-done.4 = bf16[2,256,512]{2,1,0:T(8,128)(2,1)} copy-done((bf16[2,256,512]{2,1,0:T(8,128)(2,1)}, bf16[2,256,512]{2,1,0:T(8,128)(2,1)S(1)}, u32[]{:S(2)}) %copy-start.4) | copy-done | bytes 524312
  11.8 2.9 %collective-permute-start.6 = (bf16[1,256,512]{2,1,0:T(8,128)(2,1)S(1)}, bf16[1,256,512]{2,1,0:T(8,128)(2,1)}, u32[]{:S(2)}, u32[]{:S(2)}) collective-permute-start(bf16[1,256,512]{2,1,0:T(8,128)(2,1)S(1)} %get-tuple-element.52), channel_id=1, source_target_pairs={{1,0},{0,1},{3,2},{2,3},{5,4},{4,5},{7,6},{6,7},{9,8},{8,9},{11,10... | collective-permute-start | bytes 786440 | tf_op jit(solution)/shard_map/ppermute | solution.py:25
  14.8 3.3 %shard_map.66 = bf16[2,256,512]{2,1,0:T(8,128)(2,1)S(1)} custom-call(bf16[4,256,512]{2,1,0:T(8,128)(2,1)S(1)} %get-tuple-element.54.state_ref.alone_ref, f32[4,512]{1,0:T(4,128)S(1)} %get-tuple-element.99.fields_ref.first_ref.own_ref, f32[4,512]{1,0:T(4,128)S(1)} %get-tuple-element.100.second_ref.partner_ref, f32[4,256,128]{2,1,0:T(8,128)S(1)} %get-tuple-element.45.v_ref, ...), custom_call_target="tpu_custom_call" | custom-call | tf_op jit(solution)/shard_map/pallas_call | solution.py:452
  18.1 1.9 %shard_map.67 = (bf16[4,256,512]{2,1,0:T(8,128)(2,1)S(1)}, bf16[2,256,512]{2,1,0:T(8,128)(2,1)S(1)}) custom-call(s32[1]{0:T(128)} %bitcast.core_ref, bf16[4,256,512]{2,1,0:T(8,128)(2,1)} %collective-permute-done.3.partner_ref, bf16[4,256,512]{2,1,0:T(8,128)(2,1)S(1)} %bitcast.10, bf16[256,256]{1,0:T(8,128)(2,1)S(1)} %copy.10.turned_ref), custom_call_target="tpu_custom_call" | custom-call | tf_op jit(solution)/shard_map/pallas_call | solution.py:452
  20.1 1.1 %broadcast_select_fusion.1 = bf16[1,256,512]{2,1,0:T(8,128)(2,1)S(1)} fusion(bf16[1,256,512]{2,1,0:T(8,128)(2,1)S(1)} %get-tuple-element.52, bf16[1,256,512]{2,1,0:T(8,128)(2,1)} %collective-permute-done.6, pred[256]{0:T(512)(128)(4,1)S(1)} %copy-done.9), kind=kLoop, calls=%fused_computation.7 | loop fusion | flops 131072 | bytes 786688 | tf_op jit(solution)/shard_map/jit(_where)/select_n | solution.py:488
  21.2 1.0 %slice.66.mine_ref = bf16[256,512]{1,0:T(8,128)(2,1)S(1)} slice(bf16[272,512]{1,0:T(8,128)(2,1)} %collective-permute-done.2), slice={[0:256], [0:512]} | slice | bytes 524288 | tf_op jit(solution)/shard_map/slice | solution.py:547
  22.2 1.5 %collective-permute-start.7 = (bf16[2,256,512]{2,1,0:T(8,128)(2,1)S(1)}, bf16[2,256,512]{2,1,0:T(8,128)(2,1)S(1)}, u32[]{:S(2)}, u32[]{:S(2)}) collective-permute-start(bf16[2,256,512]{2,1,0:T(8,128)(2,1)S(1)} %copy-done.5), channel_id=1, source_target_pairs={{1,0},{0,1},{3,2},{2,3},{5,4},{4,5},{7,6},{6,7},{9,8},{8,9},{11,10... | collective-permute-start | bytes 1572872 | tf_op jit(solution)/shard_map/ppermute | solution.py:25
  23.8 0.8 %convert_add_fusion.1 = f32[4,512]{1,0:T(4,128)S(1)} fusion(bf16[272,512]{1,0:T(8,128)(2,1)} %collective-permute-done.2), kind=kLoop, calls=%fused_computation.19 | loop fusion | flops 6144 | bytes 16384 | tf_op jit(solution)/shard_map/add | solution.py:529
  24.7 1.3 %collective-permute-done.4 = bf16[2,256,512]{2,1,0:T(8,128)(2,1)S(1)} collective-permute-done((bf16[2,256,512]{2,1,0:T(8,128)(2,1)S(1)}, bf16[2,256,512]{2,1,0:T(8,128)(2,1)S(1)}, u32[]{:S(2)}, u32[]{:S(2)}) %collective-permute-start.4) | collective-permute-done | bytes 524320 | tf_op jit(solution)/shard_map/ppermute | solution.py:25
  26.1 3.8 %shard_map.68 = (bf16[2,256,512]{2,1,0:T(8,128)(2,1)S(1)}, bf16[8,256,512]{2,1,0:T(8,128)(2,1)S(1)}, bf16[2,256,512]{2,1,0:T(8,128)(2,1)S(1)}, bf16[2,256,512]{2,1,0:T(8,128)(2,1)S(1)}, f32[2,512]{1,0:T(2,128)S(1)}) custom-call(s32[1]{0:T(128)} %bitcast.core_ref, bf16[4,256,512]{2,1,0:T(8,128)(2,1)S(1)} %get-tuple-element.54.state_ref.alone_ref, ...), custom_call_target="tpu_custom_call" | custom-call | tf_op jit(solution)/shard_map/pallas_call | solution.py:452
  30.4 0.4 collective-permute-start.15
  30.8 0.5 collective-permute-start.5
  31.3 2.7 %collective-permute-start.11 = (bf16[256,512]{1,0:T(8,128)(2,1)S(1)}, bf16[256,512]{1,0:T(8,128)(2,1)S(1)}, u32[]{:S(2)}, u32[]{:S(2)}) collective-permute-start(bf16[256,512]{1,0:T(8,128)(2,1)S(1)} %bitcast.12), channel_id=1, source_target_pairs={{1,0},{0,1},{3,2},{2,3},{5,4},{4,5},{7,6},{6,7},{9,8},{8,9},{11,10... | collective-permute-start | bytes 786440 | tf_op jit(solution)/shard_map/ppermute | solution.py:25
  34.0 1.2 %collective-permute-done.11.other_ref = bf16[256,512]{1,0:T(8,128)(2,1)S(1)} collective-permute-done((bf16[256,512]{1,0:T(8,128)(2,1)S(1)}, bf16[256,512]{1,0:T(8,128)(2,1)S(1)}, u32[]{:S(2)}, u32[]{:S(2)}) %collective-permute-start.11) | collective-permute-done | bytes 262176 | tf_op jit(solution)/shard_map/ppermute | solution.py:25
  35.2 0.6 %shard_map.69 = (f32[2,512]{1,0:T(2,128)S(1)}, f32[4,512]{1,0:T(4,128)S(1)}) custom-call(bf16[2,256,512]{2,1,0:T(8,128)(2,1)S(1)} %get-tuple-element.56.own_ref, bf16[2,256,512]{2,1,0:T(8,128)(2,1)S(1)} %collective-permute-done.10.partner_ref, bf16[256,512]{1,0:T(8,128)(2,1)S(1)} %bitcast.13, f32[2,512]{1,0:T(2,128)S(1)} %copy-done.2, ...), custom_call_target="tpu_custom_call" | custom-call | tf_op jit(solution)/shard_map/pallas_call | solution.py:452
  36.2 0.8 %collective-permute-done.12 = f32[4,512]{1,0:T(4,128)S(1)} collective-permute-done((f32[4,512]{1,0:T(4,128)S(1)}, f32[4,512]{1,0:T(4,128)S(1)}, u32[]{:S(2)}, u32[]{:S(2)}) %collective-permute-start.12) | collective-permute-done | bytes 8224 | tf_op jit(solution)/shard_map/ppermute | solution.py:565
  37.0 3.3 %shard_map.70.held_ref = bf16[6,256,512]{2,1,0:T(8,128)(2,1)S(1)} custom-call(bf16[8,256,512]{2,1,0:T(8,128)(2,1)S(1)} %get-tuple-element.67.held_ref, bf16[256,512]{1,0:T(8,128)(2,1)S(1)} %bitcast.14, bf16[256,512]{1,0:T(8,128)(2,1)S(1)} %collective-permute-done.11.other_ref, f32[4,512]{1,0:T(4,128)S(1)} %get-tuple-element.99.fields_ref.first_ref.own_ref, ...), custom_call_target="tpu_custom_call" | custom-call | tf_op jit(solution)/shard_map/pallas_call | solution.py:452
  40.3 3.4 %collective-permute-done.13 = f32[4,512]{1,0:T(4,128)S(1)} collective-permute-done((f32[4,512]{1,0:T(4,128)S(1)}, f32[4,512]{1,0:T(4,128)S(1)}, u32[]{:S(2)}, u32[]{:S(2)}) %collective-permute-start.13) | collective-permute-done | bytes 8224 | tf_op jit(solution)/shard_map/ppermute | solution.py:565
  44.1 1.8 %shard_map.71.shared_ref = f32[4,512]{1,0:T(4,128)S(1)} custom-call(bf16[6,256,512]{2,1,0:T(8,128)(2,1)S(1)} %shard_map.70.held_ref, f32[4,512]{1,0:T(4,128)S(1)} %get-tuple-element.100.second_ref.partner_ref, f32[4,256,128]{2,1,0:T(8,128)S(1)} %get-tuple-element.45.v_ref, bf16[4,256,512]{2,1,0:T(8,128)(2,1)S(1)} %get-tuple-element.73.weight_ref, ...), custom_call_target="tpu_custom_call" | custom-call | tf_op jit(solution)/shard_map/pallas_call | solution.py:452
  45.9 1.6 %collective-permute-done.14 = f32[4,512]{1,0:T(4,128)S(1)} collective-permute-done((f32[4,512]{1,0:T(4,128)S(1)}, f32[4,512]{1,0:T(4,128)S(1)}, u32[]{:S(2)}, u32[]{:S(2)}) %collective-permute-start.14) | collective-permute-done | bytes 8224 | tf_op jit(solution)/shard_map/ppermute | solution.py:565
  47.5 2.2 %collective-permute-start.16 = (f32[4,512]{1,0:T(4,128)S(1)}, f32[4,512]{1,0:T(4,128)S(1)}, u32[]{:S(2)}, u32[]{:S(2)}) collective-permute-start(f32[4,512]{1,0:T(4,128)S(1)} %add.71), channel_id=1, source_target_pairs={{0,8},{1,9},{2,10},{3,11},{4,12},{5,13},{6,14},{7,15},{8,0},{9,1},... | collective-permute-start | bytes 24584 | tf_op jit(solution)/shard_map/ppermute | solution.py:565
  49.6 2.4 %collective-permute-done.16 = f32[4,512]{1,0:T(4,128)S(1)} collective-permute-done((f32[4,512]{1,0:T(4,128)S(1)}, f32[4,512]{1,0:T(4,128)S(1)}, u32[]{:S(2)}, u32[]{:S(2)}) %collective-permute-start.16) | collective-permute-done | bytes 8224 | tf_op jit(solution)/shard_map/ppermute | solution.py:565
  52.0 1.7 %shard_map.72 = (f32[4,512]{1,0:T(4,128)S(1)}, f32[4,512]{1,0:T(4,128)S(1)}) custom-call(s32[1]{0:T(128)} %bitcast.core_ref, bf16[2,256,512]{2,1,0:T(8,128)(2,1)S(1)} %collective-permute-done.5.message_ref, bf16[4,256,512]{2,1,0:T(8,128)(2,1)S(1)} %get-tuple-element.73.weight_ref, bf16[2,256,512]{2,1,0:T(8,128)(2,1)S(1)} %get-tuple-element.79.own_weight_ref, ...), custom_call_target="tpu_custom_call" | custom-call | tf_op jit(solution)/shard_map/pallas_call | solution.py:452
  53.8 1.2 %collective-permute-done.17 = f32[4,512]{1,0:T(4,128)S(1)} collective-permute-done((f32[4,512]{1,0:T(4,128)S(1)}, f32[4,512]{1,0:T(4,128)S(1)}, u32[]{:S(2)}, u32[]{:S(2)}) %collective-permute-start.17) | collective-permute-done | bytes 8224 | tf_op jit(solution)/shard_map/ppermute | solution.py:25
  55.0 0.6 %multiply_divide_fusion = f32[4,512]{1,0:T(4,128)} fusion(f32[4,512]{1,0:T(4,128)S(1)} %add.71, f32[4,512]{1,0:T(4,128)S(1)} %collective-permute-done.16, f32[4,512]{1,0:T(4,128)S(1)} %get-tuple-element.82, f32[4,512]{1,0:T(4,128)S(1)} %collective-permute-done.17), kind=kLoop, calls=%fused_computation.17 | loop fusion | flops 8192 | bytes 40960 | tf_op jit(solution)/shard_map/div | solution.py:595
  (65 shorter events, 3.3 us)
Async XLA Ops:
  0.0 8.4 %copy-start = (bf16[256,256]{1,0:T(8,128)(2,1)S(1)}, bf16[256,256]{1,0:T(8,128)(2,1)}, u32[]{:S(2)}) copy-start(bf16[256,256]{1,0:T(8,128)(2,1)} %param.9) | copy-start | bytes 393220
  0.0 2.1 %copy-start.7 = (f32[4,512]{1,0:T(4,128)S(1)}, f32[4,512]{1,0:T(4,128)}, u32[]{:S(2)}) copy-start(f32[4,512]{1,0:T(4,128)} %param.6) | copy-start | bytes 24580
  0.0 2.5 %copy-start.3 = (f32[3,256]{1,0:T(4,128)S(1)}, f32[3,256]{1,0:T(4,128)}, u32[]{:S(2)}) copy-start(f32[3,256]{1,0:T(4,128)} %directions_ref.1) | copy-start | bytes 9220
  0.0 2.1 %collective-permute-start.1 = (f32[4,512]{1,0:T(4,128)}, f32[4,512]{1,0:T(4,128)S(1)}, u32[]{:S(2)}, u32[]{:S(2)}) collective-permute-start(f32[4,512]{1,0:T(4,128)} %param.6), channel_id=1, source_target_pairs={{1,0},{0,1},{3,2},{2,3},{5,4},{4,5},{7,6},{6,7},{9,8},{8,9},{11,10... | collective-permute-start | bytes 24584 | tf_op jit(solution)/shard_map/ppermute | solution.py:25
  0.5 7.9 %copy-start.6 = (bf16[256,256]{1,0:T(8,128)(2,1)S(1)}, bf16[256,256]{1,0:T(8,128)(2,1)}, u32[]{:S(2)}) copy-start(bf16[256,256]{1,0:T(8,128)(2,1)} %param.10) | copy-start | bytes 393220
  0.5 7.9 %copy-start.10 = (f32[256]{0:T(256)S(1)}, f32[256]{0:T(256)}, u32[]{:S(2)}) copy-start(f32[256]{0:T(256)} %param.11) | copy-start | bytes 3076
  2.8 1.6 %collective-permute-start = (bf16[256,512]{1,0:T(8,128)(2,1)S(1)}, bf16[256,512]{1,0:T(8,128)(2,1)S(1)}, u32[]{:S(2)}, u32[]{:S(2)}) collective-permute-start(bf16[256,512]{1,0:T(8,128)(2,1)S(1)} %get-tuple-element.46.edge_ref), channel_id=1, source_target_pairs={{1,0},{0,1},{3,2},{2,3},{5,4},{4,5},{7,6},{6,7},{9,8},{8,9},{11,10... | collective-permute-start | bytes 786440 | tf_op jit(solution)/shard_map/ppermute | solution.py:25
  3.7 11.0 %copy-start.8 = (pred[256]{0:T(512)(128)(4,1)}, pred[256]{0:T(512)(128)(4,1)S(1)}, u32[]{:S(2)}) copy-start(pred[256]{0:T(512)(128)(4,1)S(1)} %fusion.4) | copy-start | bytes 772
  5.4 12.7 %collective-permute-start.3 = (bf16[4,256,512]{2,1,0:T(8,128)(2,1)S(1)}, bf16[4,256,512]{2,1,0:T(8,128)(2,1)}, u32[]{:S(2)}, u32[]{:S(2)}) collective-permute-start(bf16[4,256,512]{2,1,0:T(8,128)(2,1)S(1)} %bitcast.8), channel_id=1, source_target_pairs={{1,0},{0,1},{3,2},{2,3},{5,4},{4,5},{7,6},{6,7},{9,8},{8,9},{11,10... | collective-permute-start | bytes 3145736 | tf_op jit(solution)/shard_map/ppermute | solution.py:25
  5.5 14.5 %collective-permute-start.2 = (bf16[272,512]{1,0:T(8,128)(2,1)}, bf16[272,512]{1,0:T(8,128)(2,1)}, u32[]{:S(2)}, u32[]{:S(2)}) collective-permute-start(bf16[272,512]{1,0:T(8,128)(2,1)} %maximum_maximum_fusion), channel_id=1, source_target_pairs={{0,2},{1,15},{2,4},{3,1},{4,6},{5,3},{6,8},{7,5},{8,10},{9,7},{10,... | collective-permute-start | bytes 835592 | tf_op jit(solution)/shard_map/ppermute | solution.py:30
  11.0 0.8 %copy-start.4 = (bf16[2,256,512]{2,1,0:T(8,128)(2,1)}, bf16[2,256,512]{2,1,0:T(8,128)(2,1)S(1)}, u32[]{:S(2)}) copy-start(bf16[2,256,512]{2,1,0:T(8,128)(2,1)S(1)} %get-tuple-element.53) | copy-start | bytes 1572868
  11.8 8.3 %collective-permute-start.6 = (bf16[1,256,512]{2,1,0:T(8,128)(2,1)S(1)}, bf16[1,256,512]{2,1,0:T(8,128)(2,1)}, u32[]{:S(2)}, u32[]{:S(2)}) collective-permute-start(bf16[1,256,512]{2,1,0:T(8,128)(2,1)S(1)} %get-tuple-element.52), channel_id=1, source_target_pairs={{1,0},{0,1},{3,2},{2,3},{5,4},{4,5},{7,6},{6,7},{9,8},{8,9},{11,10... | collective-permute-start | bytes 786440 | tf_op jit(solution)/shard_map/ppermute | solution.py:25
  14.8 5.3 %copy-start.9 = (pred[256]{0:T(512)(128)(4,1)S(1)}, pred[256]{0:T(512)(128)(4,1)}, u32[]{:S(2)}) copy-start(pred[256]{0:T(512)(128)(4,1)} %copy-done.8) | copy-start | bytes 772
  18.1 4.1 %copy-start.5 = (bf16[2,256,512]{2,1,0:T(8,128)(2,1)S(1)}, bf16[2,256,512]{2,1,0:T(8,128)(2,1)}, u32[]{:S(2)}) copy-start(bf16[2,256,512]{2,1,0:T(8,128)(2,1)} %copy-done.4) | copy-start | bytes 1572868
  20.0 4.6 %collective-permute-start.8 = (bf16[272,512]{1,0:T(8,128)(2,1)}, bf16[272,512]{1,0:T(8,128)(2,1)S(1)}, u32[]{:S(2)}, u32[]{:S(2)}) collective-permute-start(bf16[272,512]{1,0:T(8,128)(2,1)} %collective-permute-done.2), channel_id=1, source_target_pairs={{1,0},{0,1},{3,2},{2,3},{5,4},{4,5},{7,6},{6,7},{9,8},{8,9},{11,10... | collective-permute-start | bytes 835592 | tf_op jit(solution)/shard_map/ppermute | solution.py:25
  21.1 9.1 %collective-permute-start.9 = (bf16[1,256,512]{2,1,0:T(8,128)(2,1)S(1)}, bf16[1,256,512]{2,1,0:T(8,128)(2,1)S(1)}, u32[]{:S(2)}, u32[]{:S(2)}) collective-permute-start(bf16[1,256,512]{2,1,0:T(8,128)(2,1)S(1)} %broadcast_select_fusion.1), channel_id=1, source_target_pairs={{0,2},{1,15},{2,4},{3,1},{4,6},{5,3},{6,8},{7,5},{8,10},{9,7},{10,... | collective-permute-start | bytes 786440 | tf_op jit(solution)/shard_map/ppermute | solution.py:30
  22.2 3.9 %collective-permute-start.7 = (bf16[2,256,512]{2,1,0:T(8,128)(2,1)S(1)}, bf16[2,256,512]{2,1,0:T(8,128)(2,1)S(1)}, u32[]{:S(2)}, u32[]{:S(2)}) collective-permute-start(bf16[2,256,512]{2,1,0:T(8,128)(2,1)S(1)} %copy-done.5), channel_id=1, source_target_pairs={{1,0},{0,1},{3,2},{2,3},{5,4},{4,5},{7,6},{6,7},{9,8},{8,9},{11,10... | collective-permute-start | bytes 1572872 | tf_op jit(solution)/shard_map/ppermute | solution.py:25
  23.7 2.3 %collective-permute-start.4 = (bf16[2,256,512]{2,1,0:T(8,128)(2,1)S(1)}, bf16[2,256,512]{2,1,0:T(8,128)(2,1)S(1)}, u32[]{:S(2)}, u32[]{:S(2)}) collective-permute-start(bf16[2,256,512]{2,1,0:T(8,128)(2,1)S(1)} %shard_map.66), channel_id=1, source_target_pairs={{1,0},{0,1},{3,2},{2,3},{5,4},{4,5},{7,6},{6,7},{9,8},{8,9},{11,10... | collective-permute-start | bytes 1572872 | tf_op jit(solution)/shard_map/ppermute | solution.py:25
  24.6 10.6 %copy-start.1 = (f32[2,512]{1,0:T(2,128)S(1)}, f32[2,512]{1,0:T(2,128)}, u32[]{:S(2)}) copy-start(f32[2,512]{1,0:T(2,128)} %get-tuple-element.89.second_ref) | copy-start | bytes 12292
  24.6 10.6 %copy-start.2 = (f32[2,512]{1,0:T(2,128)S(1)}, f32[2,512]{1,0:T(2,128)}, u32[]{:S(2)}) copy-start(f32[2,512]{1,0:T(2,128)} %get-tuple-element.102.first_ref) | copy-start | bytes 12292
  30.3 4.9 %collective-permute-start.10 = (bf16[2,256,512]{2,1,0:T(8,128)(2,1)S(1)}, bf16[2,256,512]{2,1,0:T(8,128)(2,1)S(1)}, u32[]{:S(2)}, u32[]{:S(2)}) collective-permute-start(bf16[2,256,512]{2,1,0:T(8,128)(2,1)S(1)} %get-tuple-element.61), channel_id=1, source_target_pairs={{1,0},{0,1},{3,2},{2,3},{5,4},{4,5},{7,6},{6,7},{9,8},{8,9},{11,10... | collective-permute-start | bytes 1572872 | tf_op jit(solution)/shard_map/ppermute | solution.py:25
  30.4 13.8 %collective-permute-start.15 = (bf16[2,256,512]{2,1,0:T(8,128)(2,1)S(1)}, bf16[2,256,512]{2,1,0:T(8,128)(2,1)S(1)}, u32[]{:S(2)}, u32[]{:S(2)}) collective-permute-start(bf16[2,256,512]{2,1,0:T(8,128)(2,1)S(1)} %get-tuple-element.74.own_faces_ref), channel_id=1, source_target_pairs={{1,0},{0,1},{3,2},{2,3},{5,4},{4,5},{7,6},{6,7},{9,8},{8,9},{11,10... | collective-permute-start | bytes 1572872 | tf_op jit(solution)/shard_map/ppermute | solution.py:25
  30.8 21.3 %collective-permute-start.5 = (bf16[2,256,512]{2,1,0:T(8,128)(2,1)S(1)}, bf16[2,256,512]{2,1,0:T(8,128)(2,1)S(1)}, u32[]{:S(2)}, u32[]{:S(2)}) collective-permute-start(bf16[2,256,512]{2,1,0:T(8,128)(2,1)S(1)} %broadcast_select_fusion), channel_id=1, source_target_pairs={{0,2},{1,15},{2,4},{3,1},{4,6},{5,3},{6,8},{7,5},{8,10},{9,7},{10,... | collective-permute-start | bytes 1572872 | tf_op jit(solution)/shard_map/ppermute | solution.py:30
  31.3 3.9 %collective-permute-start.11 = (bf16[256,512]{1,0:T(8,128)(2,1)S(1)}, bf16[256,512]{1,0:T(8,128)(2,1)S(1)}, u32[]{:S(2)}, u32[]{:S(2)}) collective-permute-start(bf16[256,512]{1,0:T(8,128)(2,1)S(1)} %bitcast.12), channel_id=1, source_target_pairs={{1,0},{0,1},{3,2},{2,3},{5,4},{4,5},{7,6},{6,7},{9,8},{8,9},{11,10... | collective-permute-start | bytes 786440 | tf_op jit(solution)/shard_map/ppermute | solution.py:25
  35.8 1.2 %collective-permute-start.12 = (f32[4,512]{1,0:T(4,128)S(1)}, f32[4,512]{1,0:T(4,128)S(1)}, u32[]{:S(2)}, u32[]{:S(2)}) collective-permute-start(f32[4,512]{1,0:T(4,128)S(1)} %get-tuple-element.63), channel_id=1, source_target_pairs={{0,1},{1,0},{2,3},{3,2},{4,5},{5,4},{6,7},{7,6},{8,9},{9,8},{10,11... | collective-permute-start | bytes 24584 | tf_op jit(solution)/shard_map/ppermute | solution.py:565
  37.0 6.8 %collective-permute-start.13 = (f32[4,512]{1,0:T(4,128)S(1)}, f32[4,512]{1,0:T(4,128)S(1)}, u32[]{:S(2)}, u32[]{:S(2)}) collective-permute-start(f32[4,512]{1,0:T(4,128)S(1)} %add.69), channel_id=1, source_target_pairs={{0,2},{1,3},{2,0},{3,1},{4,6},{5,7},{6,4},{7,5},{8,10},{9,11},{10,... | collective-permute-start | bytes 24584 | tf_op jit(solution)/shard_map/ppermute | solution.py:565
  43.8 3.7 %collective-permute-start.14 = (f32[4,512]{1,0:T(4,128)S(1)}, f32[4,512]{1,0:T(4,128)S(1)}, u32[]{:S(2)}, u32[]{:S(2)}) collective-permute-start(f32[4,512]{1,0:T(4,128)S(1)} %add.70), channel_id=1, source_target_pairs={{0,4},{1,5},{2,6},{3,7},{4,0},{5,1},{6,2},{7,3},{8,12},{9,13},{10,... | collective-permute-start | bytes 24584 | tf_op jit(solution)/shard_map/ppermute | solution.py:565
  47.5 4.5 %collective-permute-start.16 = (f32[4,512]{1,0:T(4,128)S(1)}, f32[4,512]{1,0:T(4,128)S(1)}, u32[]{:S(2)}, u32[]{:S(2)}) collective-permute-start(f32[4,512]{1,0:T(4,128)S(1)} %add.71), channel_id=1, source_target_pairs={{0,8},{1,9},{2,10},{3,11},{4,12},{5,13},{6,14},{7,15},{8,0},{9,1},... | collective-permute-start | bytes 24584 | tf_op jit(solution)/shard_map/ppermute | solution.py:565
  53.8 1.2 %collective-permute-start.17 = (f32[4,512]{1,0:T(4,128)S(1)}, f32[4,512]{1,0:T(4,128)S(1)}, u32[]{:S(2)}, u32[]{:S(2)}) collective-permute-start(f32[4,512]{1,0:T(4,128)S(1)} %get-tuple-element.83), channel_id=1, source_target_pairs={{1,0},{0,1},{3,2},{2,3},{5,4},{4,5},{7,6},{6,7},{9,8},{8,9},{11,10... | collective-permute-start | bytes 24584 | tf_op jit(solution)/shard_map/ppermute | solution.py:25

commit v2 on v1

--- a/solution.py
+++ b/solution.py
@@ -23,6 +23,10 @@
 def swap_species(block):
     count = lax.axis_size("space")
     return lax.ppermute(block, "space", [(i ^ 1, i) for i in range(count)])
+
+
+def swap_each(blocks):
+    return jnp.concatenate([swap_species(blocks[k : k + 1]) for k in range(blocks.shape[0])])
 
 
 def to_next_slab(block):
@@ -104,7 +108,9 @@
     return jnp.exp(-0.5 * field)
 
 
-def prologue_kernel(core_ref, directions_ref, start_ref, fields_ref, spread_ref, edge_ref):
+def prologue_kernel(
+    core_ref, directions_ref, start_ref, fields_ref, partner_ref, spread_ref, edge_ref, coded_ref, near
+):
     sign = 1.0 - 2.0 * core_ref[0].astype(F32)
     planes, orient, cells = start_ref.shape
     low = boltzmann(fields_ref[0:1])
@@ -125,7 +131,38 @@
                 high[:, columns(t)] * start_ref[planes - 1, *at].astype(F32),
                 low[:, columns(t)] * start_ref[0, *at].astype(F32),
             )
-            edge_ref[at] = chosen.astype(BF16)
+            edge_ref[0, *at] = chosen.astype(BF16)
+
+    near[...] = jnp.zeros_like(near)
+    for s, ref in enumerate((fields_ref, partner_ref)):
+        for depth in range(2):
+            high_row, low_row = (ref[p : p + 1] for p in (planes - 1 - depth, depth))
+            row = jnp.where(core_ref[0] == 0, high_row, low_row)
+            coarse = row.astype(BF16).astype(F32)
+            at = 2 * s + depth
+            near[at : at + 1] = coarse
+            near[at + 4 : at + 5] = row - coarse
+    coded_ref[...] = near[...].astype(BF16)
+
+
+def message_kernel(mine_ref, other_ref, v_ref, out_ref):
+    orient, cells = mine_ref.shape[1:]
+
+    @each_row_block(orient)
+    def _(index):
+        rows = rows_of(index)
+        narrow = v_ref[3, rows, :].astype(BF16)
+        ahead = narrow > jnp.zeros_like(narrow)
+        for p in range(mine_ref.shape[0]):
+            for t in range(cells // LANES):
+                at = p, rows, columns(t)
+                out_ref[at] = jnp.where(ahead, mine_ref[at], other_ref[at])
+
+
+def first_message_kernel(mine_ref, other_ref, coded_ref, v_ref, out_ref):
+    message_kernel(mine_ref, other_ref, v_ref, out_ref)
+    orient = mine_ref.shape[1]
+    out_ref[0, orient:] = coded_ref[...]
 
 
 def write_edge(edges_ref, step, faces, rows, v_ref):
@@ -197,30 +234,36 @@
     def _(index):
         rows = rows_of(index)
         ahead, rate_plus, rate_minus = face_parts(v_ref, rows)
-        for t in range(mine_ref.shape[1] // LANES):
-            mine = mine_ref[rows, columns(t)].astype(F32)
-            other = other_ref[rows, columns(t)].astype(F32)
+        for t in range(mine_ref.shape[2] // LANES):
+            mine = mine_ref[0, rows, columns(t)].astype(F32)
+            other = other_ref[0, rows, columns(t)].astype(F32)
             face = jnp.where(ahead, mine, other)
             moved[slots[0], rows, columns(t)] = (rate_plus * face).astype(BF16)
             moved[slots[1], rows, columns(t)] = (rate_minus * face).astype(BF16)
 
 
 def second_step_kernel(
-    core_ref, alone_ref, edge_ref, mine_ref, other_ref, first_ref, second_ref, beyond_ref, v_ref, m_ref,
+    core_ref, alone_ref, edge_ref, mine_ref, other_ref, first_ref, second_ref, v_ref, m_ref,
     out_ref, next_ref, sent_ref, kept_ref, outer_ref, held, moved,
 ):
     planes, orient, _ = alone_ref.shape
     matrix = m_ref[...]
     first, second = boltzmann(first_ref[...]), boltzmann(second_ref[...])
-    beyond = boltzmann(beyond_ref[...])
+    core = core_ref[0]
+    mine, other = (block[:4] + block[4:8] for block in (ref[0, orient:].astype(F32) for ref in (mine_ref, other_ref)))
+    other = (other[2:4], other[0:2])
+    mine = (mine[0:2], mine[2:4])
+    low = [jnp.where(core == 0, mine[k], other[k]) for k in range(2)]
+    high = [jnp.where(core == 0, other[k], mine[k]) for k in range(2)]
+    beyond = [boltzmann(block[k : k + 1]) for block in (low[0], high[0], low[1], high[1]) for k in range(2)]
     face_drifts(v_ref, mine_ref, other_ref, moved, (0, 1))
 
     @each_row_block(orient)
     def _(index):
         rows = rows_of(index)
         _, rate_plus, rate_minus = face_parts(v_ref, rows)
-        for t in range(edge_ref.shape[1] // LANES):
-            edge = edge_ref[rows, columns(t)].astype(F32)
+        for t in range(edge_ref.shape[2] // LANES):
+            edge = edge_ref[0, rows, columns(t)].astype(F32)
             moved[2, rows, columns(t)] = (rate_minus * edge).astype(BF16)
             moved[3, rows, columns(t)] = (rate_plus * edge).astype(BF16)
 
@@ -232,8 +275,8 @@
             kept = (kept.astype(F32) + arrived).astype(BF16)
             out_ref[min(p, 1)] = kept
         held[p + 1] = kept
-    held[0] = (beyond[0:1] * beyond[0:1] * mix(matrix, moved[2])).astype(BF16)
-    held[planes + 1] = (beyond[2:3] * beyond[2:3] * mix(matrix, moved[3])).astype(BF16)
+    held[0] = (beyond[0] * beyond[0] * mix(matrix, moved[2])).astype(BF16)
+    held[planes + 1] = (beyond[2] * beyond[2] * mix(matrix, moved[3])).astype(BF16)
     count = planes + 2
 
     @each_row_block(orient)
@@ -250,23 +293,22 @@
         store_plane(moved, count + 1, rows, [rate_plus * tile.astype(F32) for tile in loaded[-1]])
 
     cross = first * second
-    factors = [beyond[1:2] * beyond[5:6], beyond[0:1] * beyond[4:5]]
+    factors = [beyond[1] * beyond[5], beyond[0] * beyond[4]]
     factors += [cross[p : p + 1] for p in range(planes)]
-    factors += [beyond[2:3] * beyond[6:7], beyond[3:4] * beyond[7:8]]
+    factors += [beyond[2] * beyond[6], beyond[3] * beyond[7]]
     for p, factor in enumerate(factors):
         next_ref[p] = (factor * mix(matrix, moved[p])).astype(BF16)
-    core = core_ref[0]
     for p in range(planes // 2):
         sent_ref[p] = next_ref[2 + (planes - 1) * (1 - core) + (2 * core - 1) * p]
         kept_ref[p] = next_ref[2 + (planes - 1) * core + (1 - 2 * core) * p]
-    outer_ref[0:1] = beyond[4:5] * beyond[4:5]
-    outer_ref[1:2] = beyond[6:7] * beyond[6:7]
+    outer_ref[0:1] = beyond[4] * beyond[4]
+    outer_ref[1:2] = beyond[6] * beyond[6]
 
 
 def middle_kernel(
     own_ref, partner_ref, message_ref, first_ref, second_ref, v_ref, m_ref, out_ref, total_ref, moved
 ):
-    orient, cells = message_ref.shape
+    _, orient, cells = own_ref.shape
     cross = boltzmann(first_ref[...]) * boltzmann(second_ref[...])
 
     @each_row_block(orient)
@@ -275,7 +317,7 @@
         ahead, rate_plus, rate_minus = face_parts(v_ref, rows)
         rate = rate_plus + rate_minus
         for t in range(cells // LANES):
-            gained = rate * message_ref[rows, columns(t)].astype(F32)
+            gained = rate * message_ref[0, rows, columns(t)].astype(F32)
             moved[0, rows, columns(t)] = jnp.where(ahead, gained, 0.0).astype(BF16)
             moved[1, rows, columns(t)] = jnp.where(ahead, 0.0, gained).astype(BF16)
 
@@ -454,7 +496,7 @@
         out_shape=outs,
         in_specs=[smem if arg.dtype == jnp.int32 else vmem for arg in args],
         out_specs=jax.tree.map(lambda _: vmem, outs),
-        scratch_shapes=[pltpu.VMEM(shape, BF16) for shape in scratch],
+        scratch_shapes=[pltpu.VMEM(*s) if len(s) == 2 else pltpu.VMEM(s, BF16) for s in scratch],
         compiler_params=pltpu.CompilerParams(vmem_limit_bytes=8 << 20),
         cost_estimate=pl.CostEstimate(flops=0, bytes_accessed=0, transcendentals=0),
     )(*args)
@@ -471,28 +513,26 @@
     own = fields + ramp
     partner = swap_species(fields) + ramp
 
-    slab = jax.ShapeDtypeStruct((planes, orient, cells), BF16)
-    plane = jax.ShapeDtypeStruct((orient, cells), BF16)
     wide = lambda extra: jax.ShapeDtypeStruct((planes + extra, orient, cells), BF16)
+    slab, plane = wide(0), wide(1 - planes)
     core_word = jnp.reshape(core, (1,)).astype(jnp.int32)
     start = jnp.transpose(end_weights, (1, 0, 2))
-    spread, edge0 = kernel_call(
+    spread, edge0, coded = kernel_call(
         prologue_kernel,
-        (jax.ShapeDtypeStruct((4, orient, LANES), F32), plane),
+        (jax.ShapeDtypeStruct((4, orient, LANES), F32), plane, jax.ShapeDtypeStruct((16, cells), BF16)),
+        (((16, cells), F32),),
+        (core_word, directions, start, own, partner),
+    )
+    message0 = kernel_call(
+        first_message_kernel,
+        jax.ShapeDtypeStruct((1, orient + 16, cells), BF16),
         (),
-        (core_word, directions, start, own),
-    )
-    ahead = spread[3, :, :1] > 0
-
-    def message(mine, other):
-        return jnp.where(ahead, mine, other)
-
-    near = jnp.where(is_first, jnp.stack([own[-1], own[-2]]), own[:2])
-    near_other = jnp.where(is_first, jnp.stack([partner[-1], partner[-2]]), partner[:2])
-    field_rows = jnp.concatenate([near, near_other])
-    high = lax.reduce_precision(field_rows, 8, 7)
-    coded = jnp.concatenate([high, field_rows - high, jnp.zeros((8, cells), F32)]).astype(BF16)
-    message0 = jnp.concatenate([message(edge0, swap_species(edge0)), coded])
+        (edge0, swap_species(edge0), coded, spread),
+    )
+
+    def message(mine):
+        shape = jax.ShapeDtypeStruct(mine.shape, BF16)
+        return kernel_call(message_kernel, shape, (), (mine, swap_each(mine), spread))
 
     scaled = synthesis.astype(F32) * decay_rates[None]
     mixing = jnp.dot(scaled, analysis.astype(F32), precision=lax.Precision.HIGHEST) + 1.0 / orient
@@ -506,50 +546,40 @@
         (slab.shape, slab.shape),
         (start, own, spread, matrix),
     )
-    message1 = message(edges1, swap_species(edges1))
+    weights, own_weights = kernel_call(
+        weight_kernel,
+        (slab, wide(2 - planes)),
+        (),
+        (core_word, swap_species(start), start, matrix.T),
+    )
+    edges1, _ = lax.optimization_barrier((edges1, alone))
+    message1 = message(edges1)
+    state, *_ = lax.optimization_barrier((alone, message1, weights))
     edges = kernel_call(
         next_alone_kernel,
         jax.ShapeDtypeStruct((2, orient, cells), BF16),
         (slab.shape, slab.shape),
-        (alone, own, partner, spread, matrix),
-    )
-    weights, own_weights = kernel_call(
-        weight_kernel,
-        (slab, jax.ShapeDtypeStruct((2, orient, cells), BF16)),
-        (),
-        (core_word, swap_species(start), start, matrix.T),
-    )
-    edges, arrived0, weights, inner = lax.optimization_barrier((edges, arrived0, weights, inner))
+        (state, own, partner, spread, matrix),
+    )
+    edges, arrived0 = lax.optimization_barrier((edges, arrived0))
+    message2 = message(edges)
+    arrived = [to_next_slab(message1), to_next_slab(message2)]
+    crossed0 = swap_species(arrived0)
+    inner, _ = lax.optimization_barrier((inner, arrived0))
     partner_inner = swap_species(inner)
-    message2 = message(edges, swap_species(edges))
-    arrived = [to_next_slab(message1)[0], to_next_slab(message2)]
-    crossed0 = swap_species(arrived0)
-
-    def near_fields(block):
-        rows = block[orient : orient + 4].astype(F32) + block[orient + 4 : orient + 8].astype(F32)
-        return rows[:2], rows[2:]
-
-    mine_first, mine_second = near_fields(arrived0)
-    other_second, other_first = near_fields(crossed0)
-    low_first = jnp.where(is_first, mine_first, other_first)
-    high_first = jnp.where(is_first, other_first, mine_first)
-    low_second = jnp.where(is_first, mine_second, other_second)
-    high_second = jnp.where(is_first, other_second, mine_second)
-    beyond = jnp.concatenate([low_first, high_first, low_second, high_second])
-
-    alone, *_ = lax.optimization_barrier((alone, message1, message2, partner_inner))
+    alone, *_ = lax.optimization_barrier((alone, message1, message2))
     half = planes // 2
     half_slab = jax.ShapeDtypeStruct((half, orient, cells), BF16)
     first_faces, second_state, sent_half, kept_half, outer = kernel_call(
         second_step_kernel,
         (wide(2 - planes), wide(4), half_slab, half_slab, jax.ShapeDtypeStruct((2, cells), F32)),
         (wide(2).shape, wide(4).shape),
-        (core_word, alone, edge0, arrived0[:orient], crossed0[:orient], own, partner, beyond, spread, matrix),
-    )
-    arrived1, second_state = lax.optimization_barrier((arrived[0], second_state))
+        (core_word, alone, edge0, arrived0, crossed0, own, partner, spread, matrix),
+    )
+    arrived1, second_state, partner_inner = lax.optimization_barrier((arrived[0], second_state, partner_inner))
     sent_half, first_faces, _ = lax.optimization_barrier((sent_half, first_faces, arrived1))
-    partner_faces = swap_species(first_faces)
-    partner_half, crossed1 = lax.optimization_barrier((swap_species(sent_half), swap_species(arrived1)))
+    partner_faces = swap_each(first_faces)
+    partner_half, crossed1 = lax.optimization_barrier((swap_each(sent_half), swap_species(arrived1)))
     own_half_field = jnp.where(is_first, own[:half], own[half:][::-1])
     partner_half_field = jnp.where(is_first, partner[:half], partner[half:][::-1])
     density = jax.ShapeDtypeStruct((planes, cells), F32)
@@ -574,15 +604,16 @@
         (slab.shape, wide(2).shape),
         (second_state, arrived1, crossed1, own, partner, outer, spread, matrix),
     )
-    partition, third_state = gathered(partition, 2, third_state)
+    partition, third_state = gathered(partition, 4, third_state)
     third_state, _ = lax.optimization_barrier((third_state, partition))
     shared = kernel_call(pairing_kernel, density, (), (third_state, partner, spread, weights, partner_faces, partner_inner))
-    distance = 4
+    arrived2, shared = lax.optimization_barrier((arrived[1], shared))
+    distance = 8
     while distance < count:
         partition, shared = gathered(partition, distance, shared)
         distance *= 2
+    partition, shared = gathered(partition, 2, shared)
     partition = partition / (count // 2 * planes * cells)
-    arrived2, shared = lax.optimization_barrier((arrived[1], shared))
     sent, kept = kernel_call(
         last_kernel,
         (density, density),

time: 55.9 us -> 60.5 us (1.082)
  local copies, waits for them, and re-layouts: 3.74 us -> 9.97 us
  other arithmetic: 4.33 us -> 1.76 us
  Pallas kernels: 18.9 us -> 21.3 us
  waiting for transfers between devices: 13 us -> 11.8 us
    unnamed x23 -> x42, local copies, waits for them, and re-layouts: 2.29 us -> 8.57 us
    ppermute x4, waiting for transfers between devices: 8.25 us -> 4.65 us  [gathered(): lax.ppermute(value, 'space', [(i, i ^ distance) for i in range(count)])]
    ppermute x11 -> x14, waiting for transfers between devices: 4.39 us -> 7.05 us  [swap_species(): return lax.ppermute(block, 'space', [(i ^ 1, i) for i in range(count)])]
    pallas_call x9 -> x12, Pallas kernels: 18.9 us -> 21.3 us  [kernel_call(): pl.pallas_call(kernel, out_shape=outs, in_specs=[smem if arg.dtype == jnp...]
    select_n x4 -> x0, other arithmetic: 1.28 us -> none  [the longest x3 1.27 us: message(): return jnp.where(ahead, mine, other)]
    add x3 -> x1, other arithmetic: 0.86 us -> 0.07 us  [shards(): partner = swap_species(fields) + ramp]
    ppermute x11 -> x14, starting transfers between devices: 8.63 us -> 8.59 us  [swap_species(): return lax.ppermute(block, 'space', [(i ^ 1, i) for i in range(count)])]
  transfers between devices with their start and end apart: 18 -> 21, of which waited for: 9 -> 11; matrix products, arithmetic and copies ran while one was open for 10% -> 5% of each run, Pallas kernels for 30% -> 31%
where the time goes in v2:
time: 60.5 us; the launch traced here: 60.2 us
  Pallas kernels  21.3 us (35%)
  starting transfers between devices  14.8 us (24%)
  waiting for transfers between devices  11.8 us (20%)
  local copies, waits for them, and re-layouts  9.97 us (16%)
  other arithmetic  1.76 us (3%)
    pallas_call x12, Pallas kernels, kernel_call(): pl.pallas_call(kernel, out_shape=outs, in_specs=[smem if arg.dtype == jnp...  21.3 us
    ppermute x14, starting transfers between devices, swap_species(): return lax.ppermute(block, 'space', [(i ^ 1, i) for i in range(count)])  8.59 us
    unnamed x42, local copies, waits for them, and re-layouts  8.57 us
    ppermute x14, waiting for transfers between devices, swap_species(): return lax.ppermute(block, 'space', [(i ^ 1, i) for i in range(count)])  7.05 us
    ppermute x4, waiting for transfers between devices, gathered(): lax.ppermute(value, 'space', [(i, i ^ distance) for i in range(count)])  4.65 us
    ppermute x4, starting transfers between devices, gathered(): lax.ppermute(value, 'space', [(i, i ^ distance) for i in range(count)])  3.27 us
    ppermute x3, starting transfers between devices, to_next_slab(): lax.ppermute(block, 'space', [(i, (i + (2 if i % 2 == 0 else -2)) % count...  2.95 us
  transfers between devices with their start and end apart: 21, of which 11 were waited for; matrix products, arithmetic and copies ran while one was open for 5% of the time, Pallas kernels for 31%

profile of v2, /device:TPU:0, one launch (start us, length us, event | category | flops | bytes accessed | tf_op | source)
XLA Modules:
  0.0 60.2 jit_solution(2303749728194257787)
XLA Ops:
  0.5 1.5 %copy.10 = bf16[256,4,512]{2,0,1:T(8,128)(2,1)S(1)} copy(bf16[256,4,512]{2,1,0:T(4,128)(2,1)} %param.7) | data formatting | bytes 2097152 | tf_op args[1]
  2.6 1.5 %collective-permute-done.1.other_ref = bf16[1,256,512]{2,1,0:T(8,128)(2,1)S(1)} collective-permute-done((bf16[1,256,512]{2,1,0:T(8,128)(2,1)S(1)}, bf16[1,256,512]{2,1,0:T(8,128)(2,1)S(1)}, u32[]{:S(2)}, u32[]{:S(2)}) %collective-permute-start.1) | collective-permute-done | bytes 262176 | tf_op jit(solution)/shard_map/ppermute | solution.py:25
  4.1 0.8 %shard_map.65 = bf16[1,272,512]{2,1,0:T(8,128)(2,1)} custom-call(bf16[1,256,512]{2,1,0:T(8,128)(2,1)S(1)} %get-tuple-element.48.mine_ref.edge_ref, bf16[1,256,512]{2,1,0:T(8,128)(2,1)S(1)} %collective-permute-done.1.other_ref, bf16[16,512]{1,0:T(8,128)(2,1)S(1)} %get-tuple-element.49.coded_ref, f32[4,256,128]{2,1,0:T(8,128)S(1)} %get-tuple-element.50.v_ref), custom_call_target="tpu_custom_call" | custom-call | tf_op jit(solution)/shard_map/pallas_call | solution.py:494
  5.0 2.9 %collective-permute-start.4 = (bf16[1,272,512]{2,1,0:T(8,128)(2,1)}, bf16[1,272,512]{2,1,0:T(8,128)(2,1)}, u32[]{:S(2)}, u32[]{:S(2)}) collective-permute-start(bf16[1,272,512]{2,1,0:T(8,128)(2,1)} %shard_map.65), channel_id=1, source_target_pairs={{0,2},{1,15},{2,4},{3,1},{4,6},{5,3},{6,8},{7,5},{8,10},{9,7},{10,... | collective-permute-start | bytes 835592 | tf_op jit(solution)/shard_map/ppermute | solution.py:34
  8.2 3.0 %shard_map.66 = (bf16[4,256,512]{2,1,0:T(8,128)(2,1)S(1)}, bf16[2,256,512]{2,1,0:T(8,128)(2,1)S(1)}, bf16[1,256,512]{2,1,0:T(8,128)(2,1)}) custom-call(bf16[4,256,512]{2,1,0:T(8,128)(2,1)S(1)} %bitcast.8, f32[4,512]{1,0:T(4,128)S(1)} %get-tuple-element.98.fields_ref.first_ref.own_ref, f32[4,256,128]{2,1,0:T(8,128)S(1)} %get-tuple-element.50.v_ref, ...), custom_call_target="tpu_custom_call" | custom-call | tf_op jit(solution)/shard_map/pallas_call | solution.py:494
  11.1 1.0 %copy-done.1 = bf16[4,256,512]{2,1,0:T(8,128)(2,1)} copy-done((bf16[4,256,512]{2,1,0:T(8,128)(2,1)}, bf16[4,256,512]{2,1,0:T(8,128)(2,1)S(1)}, u32[]{:S(2)}) %copy-start.1) | copy-done | bytes 1048600
  12.1 0.8 %copy-done.15 = bf16[2,256,512]{2,1,0:T(8,128)(2,1)} copy-done((bf16[2,256,512]{2,1,0:T(8,128)(2,1)}, bf16[2,256,512]{2,1,0:T(8,128)(2,1)S(1)}, u32[]{:S(2)}) %copy-start.15) | copy-done | bytes 524312
  12.9 2.9 %collective-permute-start.2 = (bf16[1,256,512]{2,1,0:T(8,128)(2,1)}, bf16[1,256,512]{2,1,0:T(8,128)(2,1)}, u32[]{:S(2)}, u32[]{:S(2)}) collective-permute-start(bf16[1,256,512]{2,1,0:T(8,128)(2,1)} %get-tuple-element.54.mine_ref), channel_id=1, source_target_pairs={{1,0},{0,1},{3,2},{2,3},{5,4},{4,5},{7,6},{6,7},{9,8},{8,9},{11,10... | collective-permute-start | bytes 786440 | tf_op jit(solution)/shard_map/ppermute | solution.py:25
  15.9 1.4 %collective-permute-done.2.other_ref = bf16[1,256,512]{2,1,0:T(8,128)(2,1)} collective-permute-done((bf16[1,256,512]{2,1,0:T(8,128)(2,1)}, bf16[1,256,512]{2,1,0:T(8,128)(2,1)}, u32[]{:S(2)}, u32[]{:S(2)}) %collective-permute-start.2) | collective-permute-done | bytes 262176 | tf_op jit(solution)/shard_map/ppermute | solution.py:25
  17.3 1.1 %shard_map.67 = bf16[1,256,512]{2,1,0:T(8,128)(2,1)S(1)} custom-call(bf16[1,256,512]{2,1,0:T(8,128)(2,1)} %get-tuple-element.54.mine_ref, bf16[1,256,512]{2,1,0:T(8,128)(2,1)} %collective-permute-done.2.other_ref, f32[4,256,128]{2,1,0:T(8,128)S(1)} %get-tuple-element.50.v_ref), custom_call_target="tpu_custom_call" | custom-call | tf_op jit(solution)/shard_map/pallas_call | solution.py:494
  18.4 1.0 %copy-done.5 = bf16[4,256,512]{2,1,0:T(8,128)(2,1)} copy-done((bf16[4,256,512]{2,1,0:T(8,128)(2,1)}, bf16[4,256,512]{2,1,0:T(8,128)(2,1)S(1)}, u32[]{:S(2)}) %copy-start.5) | copy-done | bytes 1048600
  19.4 1.2 %copy-done.6 = bf16[4,256,512]{2,1,0:T(8,128)(2,1)S(1)} copy-done((bf16[4,256,512]{2,1,0:T(8,128)(2,1)S(1)}, bf16[4,256,512]{2,1,0:T(8,128)(2,1)}, u32[]{:S(2)}) %copy-start.6) | copy-done | bytes 1048600
  21.2 0.8 %copy-done.7 = bf16[2,256,512]{2,1,0:T(8,128)(2,1)} copy-done((bf16[2,256,512]{2,1,0:T(8,128)(2,1)}, bf16[2,256,512]{2,1,0:T(8,128)(2,1)S(1)}, u32[]{:S(2)}) %copy-start.7) | copy-done | bytes 524312
  22.0 3.3 %shard_map.69.mine_ref = bf16[2,256,512]{2,1,0:T(8,128)(2,1)S(1)} custom-call(bf16[4,256,512]{2,1,0:T(8,128)(2,1)S(1)} %copy-done.2, f32[4,512]{1,0:T(4,128)S(1)} %get-tuple-element.98.fields_ref.first_ref.own_ref, f32[4,512]{1,0:T(4,128)S(1)} %get-tuple-element.97.partner_ref.second_ref, f32[4,256,128]{2,1,0:T(8,128)S(1)} %get-tuple-element.50.v_ref, ...), custom_call_target="tpu_custom_call" | custom-call | tf_op jit(solution)/shard_map/pallas_call | solution.py:494
  26.6 1.2 %collective-permute-done.5 = bf16[1,256,512]{2,1,0:T(8,128)(2,1)S(1)} collective-permute-done((bf16[1,256,512]{2,1,0:T(8,128)(2,1)S(1)}, bf16[1,256,512]{2,1,0:T(8,128)(2,1)S(1)}, u32[]{:S(2)}, u32[]{:S(2)}) %collective-permute-start.5) | collective-permute-done | bytes 262176 | tf_op jit(solution)/shard_map/ppermute | solution.py:25
  27.7 0.7 %collective-permute-done.6 = bf16[1,256,512]{2,1,0:T(8,128)(2,1)S(1)} collective-permute-done((bf16[1,256,512]{2,1,0:T(8,128)(2,1)S(1)}, bf16[1,256,512]{2,1,0:T(8,128)(2,1)S(1)}, u32[]{:S(2)}, u32[]{:S(2)}) %collective-permute-start.6) | collective-permute-done | bytes 262176 | tf_op jit(solution)/shard_map/ppermute | solution.py:25
  28.7 0.8 %copy-done.9 = bf16[2,256,512]{2,1,0:T(8,128)(2,1)} copy-done((bf16[2,256,512]{2,1,0:T(8,128)(2,1)}, bf16[2,256,512]{2,1,0:T(8,128)(2,1)S(1)}, u32[]{:S(2)}) %copy-start.9) | copy-done | bytes 524312
  29.5 4.7 %shard_map.71 = (bf16[2,256,512]{2,1,0:T(8,128)(2,1)S(1)}, bf16[8,256,512]{2,1,0:T(8,128)(2,1)S(1)}, bf16[2,256,512]{2,1,0:T(8,128)(2,1)S(1)}, bf16[2,256,512]{2,1,0:T(8,128)(2,1)S(1)}, f32[2,512]{1,0:T(2,128)S(1)}) custom-call(s32[1]{0:T(128)} %bitcast.core_ref, bf16[4,256,512]{2,1,0:T(8,128)(2,1)S(1)} %copy-done.2, ...), custom_call_target="tpu_custom_call" | custom-call | tf_op jit(solution)/shard_map/pallas_call | solution.py:494
  34.2 1.3 %copy-done.3 = bf16[8,256,512]{2,1,0:T(8,128)(2,1)} copy-done((bf16[8,256,512]{2,1,0:T(8,128)(2,1)}, bf16[8,256,512]{2,1,0:T(8,128)(2,1)S(1)}, u32[]{:S(2)}) %copy-start.3) | copy-done | bytes 2097176
  35.6 0.9 %fusion.5 = (bf16[1,256,512]{2,1,0:T(8,128)(2,1)}, bf16[1,256,512]{2,1,0:T(8,128)(2,1)}) fusion(bf16[2,256,512]{2,1,0:T(8,128)(2,1)S(1)} %get-tuple-element.67), kind=kLoop, calls=%fused_computation.17 | loop fusion | bytes 1048576 | tf_op jit(solution)/shard_map/slice | solution.py:29
  37.5 2.7 %collective-permute-start.13 = (bf16[1,256,512]{2,1,0:T(8,128)(2,1)S(1)}, bf16[1,256,512]{2,1,0:T(8,128)(2,1)S(1)}, u32[]{:S(2)}, u32[]{:S(2)}) collective-permute-start(bf16[1,256,512]{2,1,0:T(8,128)(2,1)S(1)} %collective-permute-done.9.message_ref.mine_ref), channel_id=1, source_target_pairs={{1,0},{0,1},{3,2},{2,3},{5,4},{4,5},{7,6},{6,7},{9,8},{8,9},{11,10... | collective-permute-start | bytes 786440 | tf_op jit(solution)/shard_map/ppermute | solution.py:25
  40.9 1.1 %collective-permute-done.12 = bf16[1,256,512]{2,1,0:T(8,128)(2,1)S(1)} collective-permute-done((bf16[1,256,512]{2,1,0:T(8,128)(2,1)}, bf16[1,256,512]{2,1,0:T(8,128)(2,1)S(1)}, u32[]{:S(2)}, u32[]{:S(2)}) %collective-permute-start.12) | collective-permute-done | bytes 262176 | tf_op jit(solution)/shard_map/ppermute | solution.py:25
  42.0 1.0 %pad_maximum_fusion.1.partner_ref = bf16[2,256,512]{2,1,0:T(8,128)(2,1)S(1)} fusion(bf16[1,256,512]{2,1,0:T(8,128)(2,1)S(1)} %collective-permute-done.12, bf16[1,256,512]{2,1,0:T(8,128)(2,1)} %collective-permute-done.11), kind=kLoop, calls=%fused_computation.4 | loop fusion | flops 262144 | bytes 1048576 | tf_op jit(solution)/shard_map/concatenate | solution.py:29
  44.0 0.8 %collective-permute-done.14 = f32[4,512]{1,0:T(4,128)S(1)} collective-permute-done((f32[4,512]{1,0:T(4,128)S(1)}, f32[4,512]{1,0:T(4,128)S(1)}, u32[]{:S(2)}, u32[]{:S(2)}) %collective-permute-start.14) | collective-permute-done | bytes 8224 | tf_op jit(solution)/shard_map/ppermute | solution.py:595
  44.9 3.3 %shard_map.73.held_ref = bf16[6,256,512]{2,1,0:T(8,128)(2,1)S(1)} custom-call(bf16[8,256,512]{2,1,0:T(8,128)(2,1)S(1)} %copy-done.4, bf16[1,256,512]{2,1,0:T(8,128)(2,1)S(1)} %collective-permute-done.9.message_ref.mine_ref, bf16[1,256,512]{2,1,0:T(8,128)(2,1)S(1)} %collective-permute-done.13.other_ref, ...), custom_call_target="tpu_custom_call" | custom-call | tf_op jit(solution)/shard_map/pallas_call | solution.py:494
  48.5 1.0 %collective-permute-start.18 = (f32[4,512]{1,0:T(4,128)S(1)}, f32[4,512]{1,0:T(4,128)S(1)}, u32[]{:S(2)}, u32[]{:S(2)}) collective-permute-start(f32[4,512]{1,0:T(4,128)S(1)} %add.62), channel_id=1, source_target_pairs={{0,8},{1,9},{2,10},{3,11},{4,12},{5,13},{6,14},{7,15},{8,0},{9,1},... | collective-permute-start | bytes 24584 | tf_op jit(solution)/shard_map/ppermute | solution.py:595
  49.5 1.7 %shard_map.74.shared_ref = f32[4,512]{1,0:T(4,128)S(1)} custom-call(bf16[6,256,512]{2,1,0:T(8,128)(2,1)S(1)} %shard_map.73.held_ref, f32[4,512]{1,0:T(4,128)S(1)} %get-tuple-element.97.partner_ref.second_ref, f32[4,256,128]{2,1,0:T(8,128)S(1)} %get-tuple-element.50.v_ref, bf16[4,256,512]{2,1,0:T(8,128)(2,1)S(1)} %get-tuple-element.55.weight_ref, ...), custom_call_target="tpu_custom_call" | custom-call | tf_op jit(solution)/shard_map/pallas_call | solution.py:494
  51.3 1.7 %collective-permute-done.18 = f32[4,512]{1,0:T(4,128)S(1)} collective-permute-done((f32[4,512]{1,0:T(4,128)S(1)}, f32[4,512]{1,0:T(4,128)S(1)}, u32[]{:S(2)}, u32[]{:S(2)}) %collective-permute-start.18) | collective-permute-done | bytes 8224 | tf_op jit(solution)/shard_map/ppermute | solution.py:595
  53.0 1.9 %collective-permute-start.19 = (f32[4,512]{1,0:T(4,128)S(1)}, f32[4,512]{1,0:T(4,128)S(1)}, u32[]{:S(2)}, u32[]{:S(2)}) collective-permute-start(f32[4,512]{1,0:T(4,128)S(1)} %add.63), channel_id=1, source_target_pairs={{0,2},{1,3},{2,0},{3,1},{4,6},{5,7},{6,4},{7,5},{8,10},{9,11},{10,... | collective-permute-start | bytes 24584 | tf_op jit(solution)/shard_map/ppermute | solution.py:595
  54.9 1.8 %collective-permute-done.19 = f32[4,512]{1,0:T(4,128)S(1)} collective-permute-done((f32[4,512]{1,0:T(4,128)S(1)}, f32[4,512]{1,0:T(4,128)S(1)}, u32[]{:S(2)}, u32[]{:S(2)}) %collective-permute-start.19) | collective-permute-done | bytes 8224 | tf_op jit(solution)/shard_map/ppermute | solution.py:595
  56.7 1.7 %shard_map.75 = (f32[4,512]{1,0:T(4,128)S(1)}, f32[4,512]{1,0:T(4,128)S(1)}) custom-call(s32[1]{0:T(128)} %bitcast.core_ref, bf16[2,256,512]{2,1,0:T(8,128)(2,1)S(1)} %collective-permute-done.7.message_ref, bf16[4,256,512]{2,1,0:T(8,128)(2,1)S(1)} %get-tuple-element.55.weight_ref, bf16[2,256,512]{2,1,0:T(8,128)(2,1)S(1)} %copy-done.8, ...), custom_call_target="tpu_custom_call" | custom-call | tf_op jit(solution)/shard_map/pallas_call | solution.py:494
  58.5 1.2 %collective-permute-done.20 = f32[4,512]{1,0:T(4,128)S(1)} collective-permute-done((f32[4,512]{1,0:T(4,128)S(1)}, f32[4,512]{1,0:T(4,128)S(1)}, u32[]{:S(2)}, u32[]{:S(2)}) %collective-permute-start.20) | collective-permute-done | bytes 8224 | tf_op jit(solution)/shard_map/ppermute | solution.py:25
  (83 shorter events, 7.3 us)
Async XLA Ops:
  0.0 7.9 %copy-start = (bf16[256,256]{1,0:T(8,128)(2,1)S(1)}, bf16[256,256]{1,0:T(8,128)(2,1)}, u32[]{:S(2)}) copy-start(bf16[256,256]{1,0:T(8,128)(2,1)} %param.9) | copy-start | bytes 393220
  0.0 2.0 %copy-start.18 = (f32[4,512]{1,0:T(4,128)S(1)}, f32[4,512]{1,0:T(4,128)}, u32[]{:S(2)}) copy-start(f32[4,512]{1,0:T(4,128)} %param.6) | copy-start | bytes 24580
  0.0 2.1 %copy-start.14 = (f32[3,256]{1,0:T(4,128)S(1)}, f32[3,256]{1,0:T(4,128)}, u32[]{:S(2)}) copy-start(f32[3,256]{1,0:T(4,128)} %directions_ref.1) | copy-start | bytes 9220
  0.0 2.0 %collective-permute-start = (f32[4,512]{1,0:T(4,128)}, f32[4,512]{1,0:T(4,128)S(1)}, u32[]{:S(2)}, u32[]{:S(2)}) collective-permute-start(f32[4,512]{1,0:T(4,128)} %param.6), channel_id=1, source_target_pairs={{1,0},{0,1},{3,2},{2,3},{5,4},{4,5},{7,6},{6,7},{9,8},{8,9},{11,10... | collective-permute-start | bytes 24584 | tf_op jit(solution)/shard_map/ppermute | solution.py:25
  0.5 7.3 %copy-start.17 = (bf16[256,256]{1,0:T(8,128)(2,1)S(1)}, bf16[256,256]{1,0:T(8,128)(2,1)}, u32[]{:S(2)}) copy-start(bf16[256,256]{1,0:T(8,128)(2,1)} %param.10) | copy-start | bytes 393220
  0.5 7.3 %copy-start.19 = (f32[256]{0:T(256)S(1)}, f32[256]{0:T(256)}, u32[]{:S(2)}) copy-start(f32[256]{0:T(256)} %param.11) | copy-start | bytes 3076
  2.5 1.6 %collective-permute-start.1 = (bf16[1,256,512]{2,1,0:T(8,128)(2,1)S(1)}, bf16[1,256,512]{2,1,0:T(8,128)(2,1)S(1)}, u32[]{:S(2)}, u32[]{:S(2)}) collective-permute-start(bf16[1,256,512]{2,1,0:T(8,128)(2,1)S(1)} %get-tuple-element.48.mine_ref.edge_ref), channel_id=1, source_target_pairs={{1,0},{0,1},{3,2},{2,3},{5,4},{4,5},{7,6},{6,7},{9,8},{8,9},{11,10... | collective-permute-start | bytes 786440 | tf_op jit(solution)/shard_map/ppermute | solution.py:25
  4.8 13.6 %collective-permute-start.3 = (bf16[4,256,512]{2,1,0:T(8,128)(2,1)S(1)}, bf16[4,256,512]{2,1,0:T(8,128)(2,1)S(1)}, u32[]{:S(2)}, u32[]{:S(2)}) collective-permute-start(bf16[4,256,512]{2,1,0:T(8,128)(2,1)S(1)} %bitcast.7), channel_id=1, source_target_pairs={{1,0},{0,1},{3,2},{2,3},{5,4},{4,5},{7,6},{6,7},{9,8},{8,9},{11,10... | collective-permute-start | bytes 3145736 | tf_op jit(solution)/shard_map/ppermute | solution.py:25
  5.0 20.4 %collective-permute-start.4 = (bf16[1,272,512]{2,1,0:T(8,128)(2,1)}, bf16[1,272,512]{2,1,0:T(8,128)(2,1)}, u32[]{:S(2)}, u32[]{:S(2)}) collective-permute-start(bf16[1,272,512]{2,1,0:T(8,128)(2,1)} %shard_map.65), channel_id=1, source_target_pairs={{0,2},{1,15},{2,4},{3,1},{4,6},{5,3},{6,8},{7,5},{8,10},{9,7},{10,... | collective-permute-start | bytes 835592 | tf_op jit(solution)/shard_map/ppermute | solution.py:34
  12.9 4.4 %collective-permute-start.2 = (bf16[1,256,512]{2,1,0:T(8,128)(2,1)}, bf16[1,256,512]{2,1,0:T(8,128)(2,1)}, u32[]{:S(2)}, u32[]{:S(2)}) collective-permute-start(bf16[1,256,512]{2,1,0:T(8,128)(2,1)} %get-tuple-element.54.mine_ref), channel_id=1, source_target_pairs={{1,0},{0,1},{3,2},{2,3},{5,4},{4,5},{7,6},{6,7},{9,8},{8,9},{11,10... | collective-permute-start | bytes 786440 | tf_op jit(solution)/shard_map/ppermute | solution.py:25
  15.9 6.1 %copy-start.2 = (bf16[4,256,512]{2,1,0:T(8,128)(2,1)S(1)}, bf16[4,256,512]{2,1,0:T(8,128)(2,1)}, u32[]{:S(2)}) copy-start(bf16[4,256,512]{2,1,0:T(8,128)(2,1)} %copy-done.1) | copy-start | bytes 3145732
  20.6 4.7 %copy-start.16 = (bf16[2,256,512]{2,1,0:T(8,128)(2,1)S(1)}, bf16[2,256,512]{2,1,0:T(8,128)(2,1)}, u32[]{:S(2)}) copy-start(bf16[2,256,512]{2,1,0:T(8,128)(2,1)} %copy-done.15) | copy-start | bytes 1572868
  25.4 10.3 %collective-permute-start.10 = (bf16[2,256,512]{2,1,0:T(8,128)(2,1)S(1)}, bf16[2,256,512]{2,1,0:T(8,128)(2,1)S(1)}, u32[]{:S(2)}, u32[]{:S(2)}) collective-permute-start(bf16[2,256,512]{2,1,0:T(8,128)(2,1)S(1)} %copy-done.16), channel_id=1, source_target_pairs={{1,0},{0,1},{3,2},{2,3},{5,4},{4,5},{7,6},{6,7},{9,8},{8,9},{11,10... | collective-permute-start | bytes 1572872 | tf_op jit(solution)/shard_map/ppermute | solution.py:25
  25.8 1.9 %collective-permute-start.5 = (bf16[1,256,512]{2,1,0:T(8,128)(2,1)S(1)}, bf16[1,256,512]{2,1,0:T(8,128)(2,1)S(1)}, u32[]{:S(2)}, u32[]{:S(2)}) collective-permute-start(bf16[1,256,512]{2,1,0:T(8,128)(2,1)S(1)} %get-tuple-element.95), channel_id=1, source_target_pairs={{1,0},{0,1},{3,2},{2,3},{5,4},{4,5},{7,6},{6,7},{9,8},{8,9},{11,10... | collective-permute-start | bytes 786440 | tf_op jit(solution)/shard_map/ppermute | solution.py:25
  26.0 2.4 %collective-permute-start.6 = (bf16[1,256,512]{2,1,0:T(8,128)(2,1)S(1)}, bf16[1,256,512]{2,1,0:T(8,128)(2,1)S(1)}, u32[]{:S(2)}, u32[]{:S(2)}) collective-permute-start(bf16[1,256,512]{2,1,0:T(8,128)(2,1)S(1)} %get-tuple-element.96), channel_id=1, source_target_pairs={{1,0},{0,1},{3,2},{2,3},{5,4},{4,5},{7,6},{6,7},{9,8},{8,9},{11,10... | collective-permute-start | bytes 786440 | tf_op jit(solution)/shard_map/ppermute | solution.py:25
  26.4 3.0 %collective-permute-start.8 = (bf16[1,272,512]{2,1,0:T(8,128)(2,1)}, bf16[1,272,512]{2,1,0:T(8,128)(2,1)S(1)}, u32[]{:S(2)}, u32[]{:S(2)}) collective-permute-start(bf16[1,272,512]{2,1,0:T(8,128)(2,1)} %collective-permute-done.4.mine_ref), channel_id=1, source_target_pairs={{1,0},{0,1},{3,2},{2,3},{5,4},{4,5},{7,6},{6,7},{9,8},{8,9},{11,10... | collective-permute-start | bytes 835592 | tf_op jit(solution)/shard_map/ppermute | solution.py:25
  26.6 9.1 %collective-permute-start.9 = (bf16[1,256,512]{2,1,0:T(8,128)(2,1)S(1)}, bf16[1,256,512]{2,1,0:T(8,128)(2,1)S(1)}, u32[]{:S(2)}, u32[]{:S(2)}) collective-permute-start(bf16[1,256,512]{2,1,0:T(8,128)(2,1)S(1)} %shard_map.67), channel_id=1, source_target_pairs={{0,2},{1,15},{2,4},{3,1},{4,6},{5,3},{6,8},{7,5},{8,10},{9,7},{10,... | collective-permute-start | bytes 786440 | tf_op jit(solution)/shard_map/ppermute | solution.py:34
  36.7 4.0 %collective-permute-start.11 = (bf16[1,256,512]{2,1,0:T(8,128)(2,1)}, bf16[1,256,512]{2,1,0:T(8,128)(2,1)}, u32[]{:S(2)}, u32[]{:S(2)}) collective-permute-start(bf16[1,256,512]{2,1,0:T(8,128)(2,1)} %get-tuple-element.93), channel_id=1, source_target_pairs={{1,0},{0,1},{3,2},{2,3},{5,4},{4,5},{7,6},{6,7},{9,8},{8,9},{11,10... | collective-permute-start | bytes 786440 | tf_op jit(solution)/shard_map/ppermute | solution.py:25
  37.4 5.6 %copy-start.11 = (bf16[2,256,512]{2,1,0:T(8,128)(2,1)S(1)}, bf16[2,256,512]{2,1,0:T(8,128)(2,1)}, u32[]{:S(2)}) copy-start(bf16[2,256,512]{2,1,0:T(8,128)(2,1)} %copy-done.10) | copy-start | bytes 1572868
  37.4 13.9 %collective-permute-start.7 = (bf16[2,256,512]{2,1,0:T(8,128)(2,1)}, bf16[2,256,512]{2,1,0:T(8,128)(2,1)S(1)}, u32[]{:S(2)}, u32[]{:S(2)}) collective-permute-start(bf16[2,256,512]{2,1,0:T(8,128)(2,1)} %copy-done.9), channel_id=1, source_target_pairs={{0,2},{1,15},{2,4},{3,1},{4,6},{5,3},{6,8},{7,5},{8,10},{9,7},{10,... | collective-permute-start | bytes 1572872 | tf_op jit(solution)/shard_map/ppermute | solution.py:34
  37.5 5.5 %collective-permute-start.13 = (bf16[1,256,512]{2,1,0:T(8,128)(2,1)S(1)}, bf16[1,256,512]{2,1,0:T(8,128)(2,1)S(1)}, u32[]{:S(2)}, u32[]{:S(2)}) collective-permute-start(bf16[1,256,512]{2,1,0:T(8,128)(2,1)S(1)} %collective-permute-done.9.message_ref.mine_ref), channel_id=1, source_target_pairs={{1,0},{0,1},{3,2},{2,3},{5,4},{4,5},{7,6},{6,7},{9,8},{8,9},{11,10... | collective-permute-start | bytes 786440 | tf_op jit(solution)/shard_map/ppermute | solution.py:25
  40.1 4.7 %copy-start.4 = (bf16[8,256,512]{2,1,0:T(8,128)(2,1)S(1)}, bf16[8,256,512]{2,1,0:T(8,128)(2,1)}, u32[]{:S(2)}) copy-start(bf16[8,256,512]{2,1,0:T(8,128)(2,1)} %copy-done.3) | copy-start | bytes 6291460
  40.1 1.8 %collective-permute-start.12 = (bf16[1,256,512]{2,1,0:T(8,128)(2,1)}, bf16[1,256,512]{2,1,0:T(8,128)(2,1)S(1)}, u32[]{:S(2)}, u32[]{:S(2)}) collective-permute-start(bf16[1,256,512]{2,1,0:T(8,128)(2,1)} %get-tuple-element.94), channel_id=1, source_target_pairs={{1,0},{0,1},{3,2},{2,3},{5,4},{4,5},{7,6},{6,7},{9,8},{8,9},{11,10... | collective-permute-start | bytes 786440 | tf_op jit(solution)/shard_map/ppermute | solution.py:25
  40.2 4.6 %collective-permute-start.16 = (bf16[1,256,512]{2,1,0:T(8,128)(2,1)S(1)}, bf16[1,256,512]{2,1,0:T(8,128)(2,1)S(1)}, u32[]{:S(2)}, u32[]{:S(2)}) collective-permute-start(bf16[1,256,512]{2,1,0:T(8,128)(2,1)S(1)} %get-tuple-element.92), channel_id=1, source_target_pairs={{1,0},{0,1},{3,2},{2,3},{5,4},{4,5},{7,6},{6,7},{9,8},{8,9},{11,10... | collective-permute-start | bytes 786440 | tf_op jit(solution)/shard_map/ppermute | solution.py:25
  40.8 8.7 %collective-permute-start.17 = (bf16[1,256,512]{2,1,0:T(8,128)(2,1)S(1)}, bf16[1,256,512]{2,1,0:T(8,128)(2,1)S(1)}, u32[]{:S(2)}, u32[]{:S(2)}) collective-permute-start(bf16[1,256,512]{2,1,0:T(8,128)(2,1)S(1)} %get-tuple-element.91), channel_id=1, source_target_pairs={{1,0},{0,1},{3,2},{2,3},{5,4},{4,5},{7,6},{6,7},{9,8},{8,9},{11,10... | collective-permute-start | bytes 786440 | tf_op jit(solution)/shard_map/ppermute | solution.py:25
  43.6 1.2 %collective-permute-start.14 = (f32[4,512]{1,0:T(4,128)S(1)}, f32[4,512]{1,0:T(4,128)S(1)}, u32[]{:S(2)}, u32[]{:S(2)}) collective-permute-start(f32[4,512]{1,0:T(4,128)S(1)} %get-tuple-element.69), channel_id=1, source_target_pairs={{0,1},{1,0},{2,3},{3,2},{4,5},{5,4},{6,7},{7,6},{8,9},{9,8},{10,11... | collective-permute-start | bytes 24584 | tf_op jit(solution)/shard_map/ppermute | solution.py:595
  44.8 3.7 %collective-permute-start.15 = (f32[4,512]{1,0:T(4,128)S(1)}, f32[4,512]{1,0:T(4,128)S(1)}, u32[]{:S(2)}, u32[]{:S(2)}) collective-permute-start(f32[4,512]{1,0:T(4,128)S(1)} %add.61), channel_id=1, source_target_pairs={{0,4},{1,5},{2,6},{3,7},{4,0},{5,1},{6,2},{7,3},{8,12},{9,13},{10,... | collective-permute-start | bytes 24584 | tf_op jit(solution)/shard_map/ppermute | solution.py:595
  44.9 4.6 %copy-start.13 = (bf16[2,256,512]{2,1,0:T(8,128)(2,1)S(1)}, bf16[2,256,512]{2,1,0:T(8,128)(2,1)}, u32[]{:S(2)}) copy-start(bf16[2,256,512]{2,1,0:T(8,128)(2,1)} %copy-done.12) | copy-start | bytes 1572868
  48.5 4.5 %collective-permute-start.18 = (f32[4,512]{1,0:T(4,128)S(1)}, f32[4,512]{1,0:T(4,128)S(1)}, u32[]{:S(2)}, u32[]{:S(2)}) collective-permute-start(f32[4,512]{1,0:T(4,128)S(1)} %add.62), channel_id=1, source_target_pairs={{0,8},{1,9},{2,10},{3,11},{4,12},{5,13},{6,14},{7,15},{8,0},{9,1},... | collective-permute-start | bytes 24584 | tf_op jit(solution)/shard_map/ppermute | solution.py:595
  49.5 7.2 %copy-start.8 = (bf16[2,256,512]{2,1,0:T(8,128)(2,1)S(1)}, bf16[2,256,512]{2,1,0:T(8,128)(2,1)}, u32[]{:S(2)}) copy-start(bf16[2,256,512]{2,1,0:T(8,128)(2,1)} %copy-done.7) | copy-start | bytes 1572868
  53.0 3.7 %collective-permute-start.19 = (f32[4,512]{1,0:T(4,128)S(1)}, f32[4,512]{1,0:T(4,128)S(1)}, u32[]{:S(2)}, u32[]{:S(2)}) collective-permute-start(f32[4,512]{1,0:T(4,128)S(1)} %add.63), channel_id=1, source_target_pairs={{0,2},{1,3},{2,0},{3,1},{4,6},{5,7},{6,4},{7,5},{8,10},{9,11},{10,... | collective-permute-start | bytes 24584 | tf_op jit(solution)/shard_map/ppermute | solution.py:595
  58.4 1.2 %collective-permute-start.20 = (f32[4,512]{1,0:T(4,128)S(1)}, f32[4,512]{1,0:T(4,128)S(1)}, u32[]{:S(2)}, u32[]{:S(2)}) collective-permute-start(f32[4,512]{1,0:T(4,128)S(1)} %get-tuple-element.89), channel_id=1, source_target_pairs={{1,0},{0,1},{3,2},{2,3},{5,4},{4,5},{7,6},{6,7},{9,8},{8,9},{11,10... | collective-permute-start | bytes 24584 | tf_op jit(solution)/shard_map/ppermute | solution.py:25
  (9 other events, 9.1 us)

commit v3 on v2

--- a/solution.py
+++ b/solution.py
@@ -23,10 +23,6 @@
 def swap_species(block):
     count = lax.axis_size("space")
     return lax.ppermute(block, "space", [(i ^ 1, i) for i in range(count)])
-
-
-def swap_each(blocks):
-    return jnp.concatenate([swap_species(blocks[k : k + 1]) for k in range(blocks.shape[0])])
 
 
 def to_next_slab(block):
@@ -145,18 +141,39 @@
     coded_ref[...] = near[...].astype(BF16)
 
 
-def message_kernel(mine_ref, other_ref, v_ref, out_ref):
-    orient, cells = mine_ref.shape[1:]
+def matrix_kernel(synthesis_ref, decay_ref, analysis_ref, out_ref, turned_ref):
+    rest = synthesis_ref[...].astype(F32) * decay_ref[...]
+    total = jnp.full(out_ref.shape, 1.0 / out_ref.shape[1], F32)
+    for _ in range(3):
+        part = rest.astype(BF16)
+        rest = rest - part.astype(F32)
+        total = total + jnp.dot(part, analysis_ref[...], preferred_element_type=F32)
+    out_ref[...] = total.astype(BF16)
+    turned_ref[...] = total.T.astype(BF16)
+
+
+def add_kernel(one_ref, two_ref, out_ref):
+    out_ref[...] = one_ref[...] + two_ref[...]
+
+
+def divide_kernel(cells, kept_ref, arrived_ref, one_ref, two_ref, out_ref):
+    out_ref[...] = (kept_ref[...] + arrived_ref[...]) * (cells / (one_ref[...] + two_ref[...]))
+
+
+def message_kernel(*refs):
+    count = (len(refs) - 2) // 2
+    v_ref, out_ref = refs[-2:]
+    orient, cells = refs[0].shape[1:]
 
     @each_row_block(orient)
     def _(index):
         rows = rows_of(index)
         narrow = v_ref[3, rows, :].astype(BF16)
         ahead = narrow > jnp.zeros_like(narrow)
-        for p in range(mine_ref.shape[0]):
+        for p in range(count):
             for t in range(cells // LANES):
-                at = p, rows, columns(t)
-                out_ref[at] = jnp.where(ahead, mine_ref[at], other_ref[at])
+                at = 0, rows, columns(t)
+                out_ref[p, rows, columns(t)] = jnp.where(ahead, refs[p][at], refs[count + p][at])
 
 
 def first_message_kernel(mine_ref, other_ref, coded_ref, v_ref, out_ref):
@@ -206,21 +223,21 @@
         write_edge(edges_ref, 0, [load_plane(out_ref, p, rows) for p in (0, planes - 1)], rows, v_ref)
 
 
-def next_alone_kernel(state_ref, first_ref, second_ref, v_ref, m_ref, edges_ref, held, moved):
+def next_alone_kernel(state_ref, first_ref, second_ref, v_ref, m_ref, edges2_ref, edges3_ref, held, moved):
     planes, orient, _ = state_ref.shape
     first = boltzmann(first_ref[...])
     second = boltzmann(second_ref[...])
     alone_step(state_ref, moved, range(planes), v_ref, None, 0)
     for p in range(planes):
         held[p] = (first[p : p + 1] * second[p : p + 1] * mix(m_ref[...], moved[p])).astype(BF16)
-    alone_step(held, moved, (0, planes - 1), v_ref, edges_ref, 0)
+    alone_step(held, moved, (0, planes - 1), v_ref, edges2_ref, 0)
     for p in (0, planes - 1):
         held[p] = (second[p : p + 1] * second[p : p + 1] * mix(m_ref[...], moved[p])).astype(BF16)
 
     @each_row_block(orient)
     def _(index):
         rows = rows_of(index)
-        write_edge(edges_ref, 1, [load_plane(held, p, rows) for p in (0, planes - 1)], rows, v_ref)
+        write_edge(edges3_ref, 0, [load_plane(held, p, rows) for p in (0, planes - 1)], rows, v_ref)
 
 
 def face_parts(v_ref, rows):
@@ -244,7 +261,7 @@
 
 def second_step_kernel(
     core_ref, alone_ref, edge_ref, mine_ref, other_ref, first_ref, second_ref, v_ref, m_ref,
-    out_ref, next_ref, sent_ref, kept_ref, outer_ref, held, moved,
+    face_low_ref, face_high_ref, next_ref, sent_near_ref, sent_far_ref, kept_ref, outer_ref, held, moved,
 ):
     planes, orient, _ = alone_ref.shape
     matrix = m_ref[...]
@@ -273,7 +290,7 @@
         if p in (0, planes - 1):
             arrived = squared[p : p + 1] * mix(matrix, moved[min(p, 1)])
             kept = (kept.astype(F32) + arrived).astype(BF16)
-            out_ref[min(p, 1)] = kept
+            (face_high_ref if p else face_low_ref)[0] = kept
         held[p + 1] = kept
     held[0] = (beyond[0] * beyond[0] * mix(matrix, moved[2])).astype(BF16)
     held[planes + 1] = (beyond[2] * beyond[2] * mix(matrix, moved[3])).astype(BF16)
@@ -299,17 +316,26 @@
     for p, factor in enumerate(factors):
         next_ref[p] = (factor * mix(matrix, moved[p])).astype(BF16)
     for p in range(planes // 2):
-        sent_ref[p] = next_ref[2 + (planes - 1) * (1 - core) + (2 * core - 1) * p]
+        sent_ref = (sent_near_ref, sent_far_ref)[p]
+        sent_ref[0] = next_ref[2 + (planes - 1) * (1 - core) + (2 * core - 1) * p]
         kept_ref[p] = next_ref[2 + (planes - 1) * core + (1 - 2 * core) * p]
     outer_ref[0:1] = beyond[4] * beyond[4]
     outer_ref[1:2] = beyond[6] * beyond[6]
 
 
 def middle_kernel(
-    own_ref, partner_ref, message_ref, first_ref, second_ref, v_ref, m_ref, out_ref, total_ref, moved
+    core_ref, own_ref, near_ref, far_ref, message_ref, first_ref, second_ref, v_ref, m_ref, out_ref, total_ref, moved
 ):
     _, orient, cells = own_ref.shape
-    cross = boltzmann(first_ref[...]) * boltzmann(second_ref[...])
+    planes = first_ref.shape[0]
+
+    def cross_of(depth):
+        low, high = (
+            boltzmann(first_ref[p : p + 1]) * boltzmann(second_ref[p : p + 1]) for p in (depth, planes - 1 - depth)
+        )
+        return jnp.where(core_ref[0] == 0, low, high)
+
+    cross = [cross_of(depth) for depth in range(2)]
 
     @each_row_block(orient)
     def _(index):
@@ -321,14 +347,14 @@
             moved[0, rows, columns(t)] = jnp.where(ahead, gained, 0.0).astype(BF16)
             moved[1, rows, columns(t)] = jnp.where(ahead, 0.0, gained).astype(BF16)
 
-    own_face = own_ref[0].astype(F32) + cross[0:1] * mix(m_ref[...], moved[0])
-    partner_face = partner_ref[0].astype(F32) + cross[0:1] * mix(m_ref[...], moved[1])
+    own_face = own_ref[0].astype(F32) + cross[0] * mix(m_ref[...], moved[0])
+    partner_face = near_ref[0].astype(F32) + cross[0] * mix(m_ref[...], moved[1])
     face = jnp.sum(own_face * partner_face, axis=0, keepdims=True)
     total = jnp.zeros((1, 1), F32)
     for p in range(own_ref.shape[0]):
         if p > 0:
-            face = jnp.sum(own_ref[p].astype(F32) * partner_ref[p].astype(F32), axis=0, keepdims=True)
-        met = face / (orient * cross[p : p + 1])
+            face = jnp.sum(own_ref[p].astype(F32) * far_ref[0].astype(F32), axis=0, keepdims=True)
+        met = face / (orient * cross[p])
         out_ref[p : p + 1] = met
         total = total + jnp.sum(met, axis=1, keepdims=True)
     total_ref[...] = jnp.broadcast_to(total, total_ref.shape)
@@ -378,7 +404,7 @@
     return jnp.sum(value.reshape(ROWS // 8, 8, LANES), axis=0)
 
 
-def pairing_kernel(held_ref, second_ref, v_ref, weight_ref, faces_ref, inner_ref, out_ref):
+def pairing_kernel(held_ref, second_ref, v_ref, weight_ref, low_ref, inner_ref, high_ref, out_ref):
     planes, orient, cells = weight_ref.shape
     second = boltzmann(second_ref[...])
     tiles = cells // LANES
@@ -391,8 +417,8 @@
         for p in range(planes):
             moved_tiles = drift(loaded[p + 1], loaded[p], loaded[p + 2], geo)
             weights = load_plane(weight_ref, p, rows)
-            on_face = p in (0, planes - 1)
-            partner = load_plane(faces_ref, min(p, 1), rows) if on_face else load_plane(inner_ref, p - 1, rows)
+            partner_refs = [(low_ref, 0)] + [(inner_ref, k) for k in range(planes - 2)] + [(high_ref, 0)]
+            partner = load_plane(*partner_refs[p], rows)
             for t in range(tiles):
                 last, third = sums[2 * (p * tiles + t)], sums[2 * (p * tiles + t) + 1]
                 new.append(last + fold(moved_tiles[t] * weights[t].astype(F32)))
@@ -410,8 +436,8 @@
 
 
 def last_kernel(
-    core_ref, message_ref, weight_ref, own_weight_ref, own_faces_ref, partner_faces_ref, shared_ref, met_ref,
-    own_ref, partner_ref, v_ref, m_ref, sent_ref, kept_ref, moved, gained,
+    core_ref, message_ref, weight_ref, own_weight_ref, own_low_ref, own_high_ref, partner_low_ref, partner_high_ref,
+    shared_ref, met_ref,    own_ref, partner_ref, v_ref, m_ref, sent_ref, kept_ref, moved, gained,
 ):
     planes, cells = shared_ref.shape
     orient = m_ref.shape[0]
@@ -453,7 +479,8 @@
                 weights = [load_plane(weight_ref, p, rows) for p in (face, inner)]
             else:
                 weights = [load_plane(own_weight_ref, p, rows) for p in (0, 1)]
-            third = load_plane((partner_faces_ref, own_faces_ref)[s], core, rows)
+            pair = ((partner_low_ref, partner_high_ref), (own_low_ref, own_high_ref))[s]
+            third = [jnp.where(core == 0, low, high) for low, high in zip(*(load_plane(ref, 0, rows) for ref in pair))]
             for t in range(tiles):
                 on_face = moved_tiles[t] + sides[s] * message[t].astype(F32)
                 wide = change[t].astype(F32)
@@ -488,6 +515,11 @@
             kept_ref[at] = kept
 
 
+def split_outputs(outs):
+    low, high, state, near, far, kept, outer = outs
+    return (low, high), state, (near, far), kept, outer
+
+
 def kernel_call(kernel, outs, scratch, args):
     vmem = pl.BlockSpec(memory_space=pltpu.VMEM)
     smem = pl.BlockSpec(memory_space=pltpu.SMEM)
@@ -497,7 +529,7 @@
         in_specs=[smem if arg.dtype == jnp.int32 else vmem for arg in args],
         out_specs=jax.tree.map(lambda _: vmem, outs),
         scratch_shapes=[pltpu.VMEM(*s) if len(s) == 2 else pltpu.VMEM(s, BF16) for s in scratch],
-        compiler_params=pltpu.CompilerParams(vmem_limit_bytes=8 << 20),
+        compiler_params=pltpu.CompilerParams(vmem_limit_bytes=7 << 20),
         cost_estimate=pl.CostEstimate(flops=0, bytes_accessed=0, transcendentals=0),
     )(*args)
 
@@ -523,78 +555,75 @@
         (((16, cells), F32),),
         (core_word, directions, start, own, partner),
     )
+    matrix, turned = kernel_call(
+        matrix_kernel,
+        (jax.ShapeDtypeStruct((orient, orient), BF16),) * 2,
+        (),
+        (synthesis, decay_rates[None], analysis),
+    )
+    other0, matrix = lax.optimization_barrier((swap_species(edge0), matrix))
     message0 = kernel_call(
         first_message_kernel,
         jax.ShapeDtypeStruct((1, orient + 16, cells), BF16),
         (),
-        (edge0, swap_species(edge0), coded, spread),
-    )
-
-    def message(mine):
-        shape = jax.ShapeDtypeStruct(mine.shape, BF16)
-        return kernel_call(message_kernel, shape, (), (mine, swap_each(mine), spread))
-
-    scaled = synthesis.astype(F32) * decay_rates[None]
-    mixing = jnp.dot(scaled, analysis.astype(F32), precision=lax.Precision.HIGHEST) + 1.0 / orient
-    matrix = mixing.astype(BF16)
+        (edge0, other0, coded, spread),
+    )
+
+    def message(blocks, others):
+        shape = jax.ShapeDtypeStruct((len(blocks),) + blocks[0].shape[1:], BF16)
+        return kernel_call(message_kernel, shape, (), (*blocks, *others, spread))
 
     start, _ = lax.optimization_barrier((start, message0))
     arrived0 = to_next_slab(message0)
     alone, inner, edges1 = kernel_call(
-        first_alone_kernel,
-        (slab, wide(-2), jax.ShapeDtypeStruct((1, orient, cells), BF16)),
-        (slab.shape, slab.shape),
-        (start, own, spread, matrix),
+        first_alone_kernel, (slab, wide(-2), plane), (slab.shape, slab.shape), (start, own, spread, matrix)
     )
     weights, own_weights = kernel_call(
-        weight_kernel,
-        (slab, wide(2 - planes)),
-        (),
-        (core_word, swap_species(start), start, matrix.T),
-    )
-    edges1, _ = lax.optimization_barrier((edges1, alone))
-    message1 = message(edges1)
+        weight_kernel, (slab, wide(2 - planes)), (), (core_word, swap_species(start), start, turned)
+    )
+    others1, weights = lax.optimization_barrier((swap_species(edges1), weights))
+    message1 = message([edges1], [others1])
     state, *_ = lax.optimization_barrier((alone, message1, weights))
-    edges = kernel_call(
-        next_alone_kernel,
-        jax.ShapeDtypeStruct((2, orient, cells), BF16),
-        (slab.shape, slab.shape),
-        (state, own, partner, spread, matrix),
-    )
-    edges, arrived0 = lax.optimization_barrier((edges, arrived0))
-    message2 = message(edges)
+    edges2, edges3 = kernel_call(
+        next_alone_kernel, (plane, plane), (slab.shape, slab.shape), (state, own, partner, spread, matrix)
+    )
+    edges2, edges3, arrived0 = lax.optimization_barrier((edges2, edges3, arrived0))
+    message2 = message([edges2, edges3], [swap_species(edges2), swap_species(edges3)])
     arrived = [to_next_slab(message1), to_next_slab(message2)]
     crossed0 = swap_species(arrived0)
     inner, _ = lax.optimization_barrier((inner, arrived0))
     partner_inner = swap_species(inner)
+
     alone, *_ = lax.optimization_barrier((alone, message1, message2))
     half = planes // 2
-    half_slab = jax.ShapeDtypeStruct((half, orient, cells), BF16)
-    first_faces, second_state, sent_half, kept_half, outer = kernel_call(
-        second_step_kernel,
-        (wide(2 - planes), wide(4), half_slab, half_slab, jax.ShapeDtypeStruct((2, cells), F32)),
-        (wide(2).shape, wide(4).shape),
-        (core_word, alone, edge0, arrived0, crossed0, own, partner, spread, matrix),
+    faces, second_state, sent_half, kept_half, outer = split_outputs(
+        kernel_call(
+            second_step_kernel,
+            (plane, plane, wide(4), plane, plane, wide(half - planes), jax.ShapeDtypeStruct((2, cells), F32)),
+            (wide(2).shape, wide(4).shape),
+            (core_word, alone, edge0, arrived0, crossed0, own, partner, spread, matrix),
+        )
     )
     arrived1, second_state, partner_inner = lax.optimization_barrier((arrived[0], second_state, partner_inner))
-    sent_half, first_faces, _ = lax.optimization_barrier((sent_half, first_faces, arrived1))
-    partner_faces = swap_each(first_faces)
-    partner_half, crossed1 = lax.optimization_barrier((swap_each(sent_half), swap_species(arrived1)))
-    own_half_field = jnp.where(is_first, own[:half], own[half:][::-1])
-    partner_half_field = jnp.where(is_first, partner[:half], partner[half:][::-1])
+    *moving, _ = lax.optimization_barrier((*sent_half, *faces, arrived1))
+    partner_faces = [swap_species(block) for block in moving[2:]]
+    *partner_half, crossed1 = lax.optimization_barrier((*map(swap_species, moving[:2]), swap_species(arrived1)))
     density = jax.ShapeDtypeStruct((planes, cells), F32)
     met, partition = kernel_call(
         middle_kernel,
         (jax.ShapeDtypeStruct((half, cells), F32), density),
         ((2, orient, cells),),
-        (kept_half, partner_half, arrived1, own_half_field, partner_half_field, spread, matrix),
+        (core_word, kept_half, *partner_half, arrived1, own, partner, spread, matrix),
     )
     count = lax.axis_size("space")
 
+    def received(value, distance, after):
+        block = lax.ppermute(value, "space", [(i, i ^ distance) for i in range(count)])
+        return lax.optimization_barrier((block, after))
+
     def gathered(value, distance, after):
-        received = lax.ppermute(value, "space", [(i, i ^ distance) for i in range(count)])
-        received, after = lax.optimization_barrier((received, after))
-        return value + received, after
+        block, after = received(value, distance, after)
+        return kernel_call(add_kernel, density, (), (value, block)), after
 
     partition, second_state = gathered(partition, 1, second_state)
     second_state, _ = lax.optimization_barrier((second_state, partition))
@@ -606,24 +635,33 @@
     )
     partition, third_state = gathered(partition, 4, third_state)
     third_state, _ = lax.optimization_barrier((third_state, partition))
-    shared = kernel_call(pairing_kernel, density, (), (third_state, partner, spread, weights, partner_faces, partner_inner))
+    shared = kernel_call(
+        pairing_kernel,
+        density,
+        (),
+        (third_state, partner, spread, weights, partner_faces[0], partner_inner, partner_faces[1]),
+    )
     arrived2, shared = lax.optimization_barrier((arrived[1], shared))
     distance = 8
     while distance < count:
         partition, shared = gathered(partition, distance, shared)
         distance *= 2
-    partition, shared = gathered(partition, 2, shared)
-    partition = partition / (count // 2 * planes * cells)
+    beside, shared = received(partition, 2, shared)
     sent, kept = kernel_call(
         last_kernel,
         (density, density),
         ((2, orient, cells), (2, orient, cells)),
         (
-            core_word, arrived2, weights, own_weights, first_faces, partner_faces, shared, met,
+            core_word, arrived2, weights, own_weights, *faces, *partner_faces, shared, met,
             own, partner, spread, matrix,
         ),
     )
-    return (kept + swap_species(sent)) / partition
+    return kernel_call(
+        functools.partial(divide_kernel, count // 2 * planes * cells),
+        density,
+        (),
+        (kept, swap_species(sent), partition, beside),
+    )
 
 
 def solution(mesh):

time: 60.5 us -> 49.8 us (0.82)
  local copies, waits for them, and re-layouts: 9.97 us -> 1.44 us
  Pallas kernels: 21.3 us -> 19.1 us
  waiting for transfers between devices: 11.8 us -> 13.5 us
  other arithmetic: 1.76 us -> 0.08 us
    unnamed x42 -> x11, local copies, waits for them, and re-layouts: 8.57 us -> 1.44 us
    ppermute x3, waiting for transfers between devices: 0.07 us -> 3.06 us  [to_next_slab(): lax.ppermute(block, 'space', [(i, (i + (2 if i % 2 == 0 else -2)) % count...]
    pallas_call x12 -> x17, Pallas kernels: 21.3 us -> 19.1 us  [kernel_call(): pl.pallas_call(kernel, out_shape=outs, in_specs=[smem if arg.dtype == jnp...]
    ppermute x14, waiting for transfers between devices: 7.05 us -> 5.91 us  [swap_species(): return lax.ppermute(block, 'space', [(i ^ 1, i) for i in range(count)])]
    concatenate x2 -> x0, other arithmetic: 1.05 us -> none  [swap_each(): jnp.concatenate([swap_species(blocks[k:k + 1]) for k in range(blocks.shap...]
    slice x5 -> x0, local copies, waits for them, and re-layouts: 1.03 us -> none  [the longest x3 1.02 us: swap_each(): blocks[k:k + 1]]
    ppermute x4, starting transfers between devices: 3.27 us -> 4 us  [received(): lax.ppermute(value, 'space', [(i, i ^ distance) for i in range(count)])]
    div x1 -> x0, other arithmetic: 0.61 us -> none  [shards(): return (kept + swap_species(sent)) / partition]
  transfers between devices with their start and end apart: 21 -> 21, of which waited for: 11 -> 12; matrix products, arithmetic and copies ran while one was open for 5% -> 3% of each run, Pallas kernels for 31% -> 33%
where the time goes in v3:
time: 49.8 us; the launch traced here: 49.7 us
  Pallas kernels  19.1 us (38%)
  starting transfers between devices  15.4 us (31%)
  waiting for transfers between devices  13.5 us (27%)
  local copies, waits for them, and re-layouts  1.44 us (3%)
    pallas_call x17, Pallas kernels, kernel_call(): pl.pallas_call(kernel, out_shape=outs, in_specs=[smem if arg.dtype == jnp...  19.1 us
    ppermute x14, starting transfers between devices, swap_species(): return lax.ppermute(block, 'space', [(i ^ 1, i) for i in range(count)])  8.51 us
    ppermute x14, waiting for transfers between devices, swap_species(): return lax.ppermute(block, 'space', [(i ^ 1, i) for i in range(count)])  5.91 us
    ppermute x4, waiting for transfers between devices, received(): lax.ppermute(value, 'space', [(i, i ^ distance) for i in range(count)])  4.56 us
    ppermute x4, starting transfers between devices, received(): lax.ppermute(value, 'space', [(i, i ^ distance) for i in range(count)])  4 us
    ppermute x3, waiting for transfers between devices, to_next_slab(): lax.ppermute(block, 'space', [(i, (i + (2 if i % 2 == 0 else -2)) % count...  3.06 us
    ppermute x3, starting transfers between devices, to_next_slab(): lax.ppermute(block, 'space', [(i, (i + (2 if i % 2 == 0 else -2)) % count...  2.89 us
    unnamed x11, local copies, waits for them, and re-layouts  1.44 us
  transfers between devices with their start and end apart: 21, of which 12 were waited for; matrix products, arithmetic and copies ran while one was open for 3% of the time, Pallas kernels for 33%

profile of v3, /device:TPU:0, one launch (start us, length us, event | category | flops | bytes accessed | tf_op | source)
XLA Modules:
  0.0 49.7 jit_solution(17747485231748187967)
XLA Ops:
  0.0 0.5 %collective-permute-start = (f32[4,512]{1,0:T(4,128)}, f32[4,512]{1,0:T(4,128)S(1)}, u32[]{:S(2)}, u32[]{:S(2)}) collective-permute-start(f32[4,512]{1,0:T(4,128)} %param.6), channel_id=1, source_target_pairs={{1,0},{0,1},{3,2},{2,3},{5,4},{4,5},{7,6},{6,7},{9,8},{8,9},{11,10... | collective-permute-start | bytes 24584 | tf_op jit(solution)/shard_map/ppermute | solution.py:25
  0.6 1.4 %copy.9 = bf16[256,4,512]{2,0,1:T(8,128)(2,1)S(1)} copy(bf16[256,4,512]{2,1,0:T(4,128)(2,1)} %param.7) | data formatting | bytes 2097152 | tf_op args[1]
  2.1 0.4 shard_map.64
  3.0 1.1 %collective-permute-done.1.other_ref = bf16[1,256,512]{2,1,0:T(8,128)(2,1)S(1)} collective-permute-done((bf16[1,256,512]{2,1,0:T(8,128)(2,1)S(1)}, bf16[1,256,512]{2,1,0:T(8,128)(2,1)S(1)}, u32[]{:S(2)}, u32[]{:S(2)}) %collective-permute-start.1) | collective-permute-done | bytes 262176 | tf_op jit(solution)/shard_map/ppermute | solution.py:25
  4.3 2.9 %collective-permute-start.4 = (bf16[1,272,512]{2,1,0:T(8,128)(2,1)S(1)}, bf16[1,272,512]{2,1,0:T(8,128)(2,1)S(1)}, u32[]{:S(2)}, u32[]{:S(2)}) collective-permute-start(bf16[1,272,512]{2,1,0:T(8,128)(2,1)S(1)} %shard_map.66), channel_id=1, source_target_pairs={{0,2},{1,15},{2,4},{3,1},{4,6},{5,3},{6,8},{7,5},{8,10},{9,7},{10,... | collective-permute-start | bytes 835592 | tf_op jit(solution)/shard_map/ppermute | solution.py:30
  7.2 2.3 %shard_map.67 = (bf16[4,256,512]{2,1,0:T(8,128)(2,1)S(1)}, bf16[2,256,512]{2,1,0:T(8,128)(2,1)S(1)}, bf16[1,256,512]{2,1,0:T(8,128)(2,1)S(1)}) custom-call(bf16[4,256,512]{2,1,0:T(8,128)(2,1)S(1)} %bitcast.7, f32[4,512]{1,0:T(4,128)S(1)} %get-tuple-element.118.fields_ref.first_ref.own_ref, f32[4,256,128]{2,1,0:T(8,128)S(1)} %get-tuple-element.65.v_ref.refs_2_.refs_4_, ...), custom_call_target="tpu_custom_call" | custom-call | tf_op jit(solution)/shard_map/pallas_call | solution.py:526
  9.5 3.0 %collective-permute-start.2 = (bf16[1,256,512]{2,1,0:T(8,128)(2,1)S(1)}, bf16[1,256,512]{2,1,0:T(8,128)(2,1)S(1)}, u32[]{:S(2)}, u32[]{:S(2)}) collective-permute-start(bf16[1,256,512]{2,1,0:T(8,128)(2,1)S(1)} %get-tuple-element.69.refs_0_), channel_id=1, source_target_pairs={{1,0},{0,1},{3,2},{2,3},{5,4},{4,5},{7,6},{6,7},{9,8},{8,9},{11,10... | collective-permute-start | bytes 786440 | tf_op jit(solution)/shard_map/ppermute | solution.py:25
  12.4 0.6 %shard_map.68 = (bf16[4,256,512]{2,1,0:T(8,128)(2,1)S(1)}, bf16[2,256,512]{2,1,0:T(8,128)(2,1)S(1)}) custom-call(s32[1]{0:T(128)} %bitcast.core_ref, bf16[4,256,512]{2,1,0:T(8,128)(2,1)S(1)} %collective-permute-done.3.partner_ref, bf16[4,256,512]{2,1,0:T(8,128)(2,1)S(1)} %bitcast.8, bf16[256,256]{1,0:T(8,128)(2,1)S(1)} %get-tuple-element.70.turned_ref), custom_call_target="tpu_custom_call" | custom-call | tf_op jit(solution)/shard_map/pallas_call | solution.py:526
  13.0 0.6 %collective-permute-done.2.refs_1_ = bf16[1,256,512]{2,1,0:T(8,128)(2,1)S(1)} collective-permute-done((bf16[1,256,512]{2,1,0:T(8,128)(2,1)S(1)}, bf16[1,256,512]{2,1,0:T(8,128)(2,1)S(1)}, u32[]{:S(2)}, u32[]{:S(2)}) %collective-permute-start.2) | collective-permute-done | bytes 262176 | tf_op jit(solution)/shard_map/ppermute | solution.py:25
  13.7 3.3 %shard_map.70 = (bf16[1,256,512]{2,1,0:T(8,128)(2,1)S(1)}, bf16[1,256,512]{2,1,0:T(8,128)(2,1)S(1)}) custom-call(bf16[4,256,512]{2,1,0:T(8,128)(2,1)S(1)} %get-tuple-element.79.state_ref.alone_ref, f32[4,512]{1,0:T(4,128)S(1)} %get-tuple-element.118.fields_ref.first_ref.own_ref, f32[4,512]{1,0:T(4,128)S(1)} %get-tuple-element.117.partner_ref.second_ref, ...), custom_call_target="tpu_custom_call" | custom-call | tf_op jit(solution)/shard_map/pallas_call | solution.py:526
  17.1 0.4 collective-permute-start.10
  17.6 0.4 collective-permute-start.5
  18.1 1.7 %collective-permute-done.5.refs_2_ = bf16[1,256,512]{2,1,0:T(8,128)(2,1)S(1)} collective-permute-done((bf16[1,256,512]{2,1,0:T(8,128)(2,1)S(1)}, bf16[1,256,512]{2,1,0:T(8,128)(2,1)S(1)}, u32[]{:S(2)}, u32[]{:S(2)}) %collective-permute-start.5) | collective-permute-done | bytes 262176 | tf_op jit(solution)/shard_map/ppermute | solution.py:25
  19.8 0.4 collective-permute-done.6.refs_3_
  20.3 3.8 %shard_map.72 = (bf16[1,256,512]{2,1,0:T(8,128)(2,1)S(1)}, bf16[1,256,512]{2,1,0:T(8,128)(2,1)S(1)}, bf16[8,256,512]{2,1,0:T(8,128)(2,1)S(1)}, bf16[1,256,512]{2...) custom-call(s32[1]{0:T(128)} %bitcast.core_ref, ...), custom_call_target="tpu_custom_call" | custom-call | tf_op jit(solution)/shard_map/pallas_call | solution.py:526
  24.1 3.1 %collective-permute-done.9.message_ref.mine_ref = bf16[1,256,512]{2,1,0:T(8,128)(2,1)S(1)} collective-permute-done((bf16[1,256,512]{2,1,0:T(8,128)(2,1)S(1)}, bf16[1,256,512]{2,1,0:T(8,128)(2,1)S(1)}, u32[]{:S(2)}, u32[]{:S(2)}) %collective-permute-start.9) | collective-permute-done | bytes 262176 | tf_op jit(solution)/shard_map/ppermute | solution.py:30
  27.2 3.0 %collective-permute-start.12 = (bf16[1,256,512]{2,1,0:T(8,128)(2,1)S(1)}, bf16[1,256,512]{2,1,0:T(8,128)(2,1)S(1)}, u32[]{:S(2)}, u32[]{:S(2)}) collective-permute-start(bf16[1,256,512]{2,1,0:T(8,128)(2,1)S(1)} %get-tuple-element.91), channel_id=1, source_target_pairs={{1,0},{0,1},{3,2},{2,3},{5,4},{4,5},{7,6},{6,7},{9,8},{8,9},{11,10... | collective-permute-start | bytes 786440 | tf_op jit(solution)/shard_map/ppermute | solution.py:25
  30.2 0.5 %collective-permute-start.16 = (bf16[1,256,512]{2,1,0:T(8,128)(2,1)S(1)}, bf16[1,256,512]{2,1,0:T(8,128)(2,1)S(1)}, u32[]{:S(2)}, u32[]{:S(2)}) collective-permute-start(bf16[1,256,512]{2,1,0:T(8,128)(2,1)S(1)} %get-tuple-element.104.own_low_ref), channel_id=1, source_target_pairs={{1,0},{0,1},{3,2},{2,3},{5,4},{4,5},{7,6},{6,7},{9,8},{8,9},{11,10... | collective-permute-start | bytes 786440 | tf_op jit(solution)/shard_map/ppermute | solution.py:25
  30.7 0.6 %collective-permute-done.12.far_ref = bf16[1,256,512]{2,1,0:T(8,128)(2,1)S(1)} collective-permute-done((bf16[1,256,512]{2,1,0:T(8,128)(2,1)S(1)}, bf16[1,256,512]{2,1,0:T(8,128)(2,1)S(1)}, u32[]{:S(2)}, u32[]{:S(2)}) %collective-permute-start.12) | collective-permute-done | bytes 262176 | tf_op jit(solution)/shard_map/ppermute | solution.py:25
  31.4 0.4 collective-permute-done.13.other_ref
  31.8 0.6 %shard_map.73 = (f32[2,512]{1,0:T(2,128)S(1)}, f32[4,512]{1,0:T(4,128)S(1)}) custom-call(s32[1]{0:T(128)} %bitcast.core_ref, bf16[2,256,512]{2,1,0:T(8,128)(2,1)S(1)} %get-tuple-element.81.own_ref, bf16[1,256,512]{2,1,0:T(8,128)(2,1)S(1)} %collective-permute-done.11.near_ref, bf16[1,256,512]{2,1,0:T(8,128)(2,1)S(1)} %collective-permute-done.12.far_ref, ...), custom_call_target="tpu_custom_call" | custom-call | tf_op jit(solution)/shard_map/pallas_call | solution.py:526
  32.4 0.4 collective-permute-start.14
  32.8 0.8 %collective-permute-done.14.two_ref = f32[4,512]{1,0:T(4,128)S(1)} collective-permute-done((f32[4,512]{1,0:T(4,128)S(1)}, f32[4,512]{1,0:T(4,128)S(1)}, u32[]{:S(2)}, u32[]{:S(2)}) %collective-permute-start.14) | collective-permute-done | bytes 8224 | tf_op jit(solution)/shard_map/ppermute | solution.py:621
  33.6 3.3 %shard_map.75.held_ref = bf16[6,256,512]{2,1,0:T(8,128)(2,1)S(1)} custom-call(bf16[8,256,512]{2,1,0:T(8,128)(2,1)S(1)} %get-tuple-element.98.held_ref, bf16[1,256,512]{2,1,0:T(8,128)(2,1)S(1)} %collective-permute-done.9.message_ref.mine_ref, bf16[1,256,512]{2,1,0:T(8,128)(2,1)S(1)} %collective-permute-done.13.other_ref, ...), custom_call_target="tpu_custom_call" | custom-call | tf_op jit(solution)/shard_map/pallas_call | solution.py:526
  37.2 1.0 %collective-permute-start.18 = (f32[4,512]{1,0:T(4,128)S(1)}, f32[4,512]{1,0:T(4,128)S(1)}, u32[]{:S(2)}, u32[]{:S(2)}) collective-permute-start(f32[4,512]{1,0:T(4,128)S(1)} %shard_map.76.one_ref), channel_id=1, source_target_pairs={{0,8},{1,9},{2,10},{3,11},{4,12},{5,13},{6,14},{7,15},{8,0},{9,1},... | collective-permute-start | bytes 24584 | tf_op jit(solution)/shard_map/ppermute | solution.py:621
  38.2 1.8 %shard_map.77.shared_ref = f32[4,512]{1,0:T(4,128)S(1)} custom-call(bf16[6,256,512]{2,1,0:T(8,128)(2,1)S(1)} %shard_map.75.held_ref, f32[4,512]{1,0:T(4,128)S(1)} %get-tuple-element.117.partner_ref.second_ref, f32[4,256,128]{2,1,0:T(8,128)S(1)} %get-tuple-element.65.v_ref.refs_2_.refs_4_, bf16[4,256,512]{2,1,0:T(8,128)(2,1)S(1)} %get-tuple-element.73.weight_ref, ...), custom_call_target="tpu_custom_call" | custom-call | tf_op jit(solution)/shard_map/pallas_call | solution.py:526
  40.0 1.8 %collective-permute-done.18.two_ref = f32[4,512]{1,0:T(4,128)S(1)} collective-permute-done((f32[4,512]{1,0:T(4,128)S(1)}, f32[4,512]{1,0:T(4,128)S(1)}, u32[]{:S(2)}, u32[]{:S(2)}) %collective-permute-start.18) | collective-permute-done | bytes 8224 | tf_op jit(solution)/shard_map/ppermute | solution.py:621
  41.8 2.6 %collective-permute-start.19 = (f32[4,512]{1,0:T(4,128)S(1)}, f32[4,512]{1,0:T(4,128)S(1)}, u32[]{:S(2)}, u32[]{:S(2)}) collective-permute-start(f32[4,512]{1,0:T(4,128)S(1)} %shard_map.78.one_ref), channel_id=1, source_target_pairs={{0,2},{1,3},{2,0},{3,1},{4,6},{5,7},{6,4},{7,5},{8,10},{9,11},{10,... | collective-permute-start | bytes 24584 | tf_op jit(solution)/shard_map/ppermute | solution.py:621
  44.4 1.6 %collective-permute-done.19.two_ref = f32[4,512]{1,0:T(4,128)S(1)} collective-permute-done((f32[4,512]{1,0:T(4,128)S(1)}, f32[4,512]{1,0:T(4,128)S(1)}, u32[]{:S(2)}, u32[]{:S(2)}) %collective-permute-start.19) | collective-permute-done | bytes 8224 | tf_op jit(solution)/shard_map/ppermute | solution.py:621
  46.1 1.8 %shard_map.79 = (f32[4,512]{1,0:T(4,128)S(1)}, f32[4,512]{1,0:T(4,128)S(1)}) custom-call(s32[1]{0:T(128)} %bitcast.core_ref, bf16[2,256,512]{2,1,0:T(8,128)(2,1)S(1)} %collective-permute-done.7.message_ref, bf16[4,256,512]{2,1,0:T(8,128)(2,1)S(1)} %get-tuple-element.73.weight_ref, bf16[2,256,512]{2,1,0:T(8,128)(2,1)S(1)} %get-tuple-element.108.own_weight_ref, ...), custom_call_target="tpu_custom_call" | custom-call | tf_op jit(solution)/shard_map/pallas_call | solution.py:526
  47.9 1.2 %collective-permute-done.20.arrived_ref = f32[4,512]{1,0:T(4,128)S(1)} collective-permute-done((f32[4,512]{1,0:T(4,128)S(1)}, f32[4,512]{1,0:T(4,128)S(1)}, u32[]{:S(2)}, u32[]{:S(2)}) %collective-permute-start.20) | collective-permute-done | bytes 8224 | tf_op jit(solution)/shard_map/ppermute | solution.py:25
  49.1 0.6 %shard_map.80 = f32[4,512]{1,0:T(4,128)} custom-call(f32[4,512]{1,0:T(4,128)S(1)} %get-tuple-element.114.kept_ref, f32[4,512]{1,0:T(4,128)S(1)} %collective-permute-done.20.arrived_ref, f32[4,512]{1,0:T(4,128)S(1)} %shard_map.78.one_ref, f32[4,512]{1,0:T(4,128)S(1)} %collective-permute-done.19.two_ref), custom_call_target="tpu_custom_call" | custom-call | tf_op jit(solution)/shard_map/pallas_call | solution.py:526
  (40 shorter events, 1.8 us)
Async XLA Ops:
  0.0 2.0 %copy-start.4 = (f32[4,512]{1,0:T(4,128)S(1)}, f32[4,512]{1,0:T(4,128)}, u32[]{:S(2)}) copy-start(f32[4,512]{1,0:T(4,128)} %param.6) | copy-start | bytes 24580
  0.0 2.1 %copy-start.2 = (f32[3,256]{1,0:T(4,128)S(1)}, f32[3,256]{1,0:T(4,128)}, u32[]{:S(2)}) copy-start(f32[3,256]{1,0:T(4,128)} %directions_ref.1) | copy-start | bytes 9220
  0.0 2.6 %copy-start.3 = (f32[256]{0:T(256)S(1)}, f32[256]{0:T(256)}, u32[]{:S(2)}) copy-start(f32[256]{0:T(256)} %param.11) | copy-start | bytes 3076
  0.0 2.6 %copy-start = (bf16[256,256]{1,0:T(8,128)(2,1)S(1)}, bf16[256,256]{1,0:T(8,128)(2,1)}, u32[]{:S(2)}) copy-start(bf16[256,256]{1,0:T(8,128)(2,1)} %synthesis_ref.1) | copy-start | bytes 393220
  0.0 2.6 %copy-start.1 = (bf16[256,256]{1,0:T(8,128)(2,1)S(1)}, bf16[256,256]{1,0:T(8,128)(2,1)}, u32[]{:S(2)}) copy-start(bf16[256,256]{1,0:T(8,128)(2,1)} %analysis_ref.1) | copy-start | bytes 393220
  0.0 2.0 %collective-permute-start = (f32[4,512]{1,0:T(4,128)}, f32[4,512]{1,0:T(4,128)S(1)}, u32[]{:S(2)}, u32[]{:S(2)}) collective-permute-start(f32[4,512]{1,0:T(4,128)} %param.6), channel_id=1, source_target_pairs={{1,0},{0,1},{3,2},{2,3},{5,4},{4,5},{7,6},{6,7},{9,8},{8,9},{11,10... | collective-permute-start | bytes 24584 | tf_op jit(solution)/shard_map/ppermute | solution.py:25
  2.4 1.6 %collective-permute-start.1 = (bf16[1,256,512]{2,1,0:T(8,128)(2,1)S(1)}, bf16[1,256,512]{2,1,0:T(8,128)(2,1)S(1)}, u32[]{:S(2)}, u32[]{:S(2)}) collective-permute-start(bf16[1,256,512]{2,1,0:T(8,128)(2,1)S(1)} %get-tuple-element.61.mine_ref.edge_ref), channel_id=1, source_target_pairs={{1,0},{0,1},{3,2},{2,3},{5,4},{4,5},{7,6},{6,7},{9,8},{8,9},{11,10... | collective-permute-start | bytes 786440 | tf_op jit(solution)/shard_map/ppermute | solution.py:25
  4.1 8.3 %collective-permute-start.3 = (bf16[4,256,512]{2,1,0:T(8,128)(2,1)S(1)}, bf16[4,256,512]{2,1,0:T(8,128)(2,1)S(1)}, u32[]{:S(2)}, u32[]{:S(2)}) collective-permute-start(bf16[4,256,512]{2,1,0:T(8,128)(2,1)S(1)} %bitcast.6), channel_id=1, source_target_pairs={{1,0},{0,1},{3,2},{2,3},{5,4},{4,5},{7,6},{6,7},{9,8},{8,9},{11,10... | collective-permute-start | bytes 3145736 | tf_op jit(solution)/shard_map/ppermute | solution.py:25
  4.3 12.7 %collective-permute-start.4 = (bf16[1,272,512]{2,1,0:T(8,128)(2,1)S(1)}, bf16[1,272,512]{2,1,0:T(8,128)(2,1)S(1)}, u32[]{:S(2)}, u32[]{:S(2)}) collective-permute-start(bf16[1,272,512]{2,1,0:T(8,128)(2,1)S(1)} %shard_map.66), channel_id=1, source_target_pairs={{0,2},{1,15},{2,4},{3,1},{4,6},{5,3},{6,8},{7,5},{8,10},{9,7},{10,... | collective-permute-start | bytes 835592 | tf_op jit(solution)/shard_map/ppermute | solution.py:30
  9.5 4.1 %collective-permute-start.2 = (bf16[1,256,512]{2,1,0:T(8,128)(2,1)S(1)}, bf16[1,256,512]{2,1,0:T(8,128)(2,1)S(1)}, u32[]{:S(2)}, u32[]{:S(2)}) collective-permute-start(bf16[1,256,512]{2,1,0:T(8,128)(2,1)S(1)} %get-tuple-element.69.refs_0_), channel_id=1, source_target_pairs={{1,0},{0,1},{3,2},{2,3},{5,4},{4,5},{7,6},{6,7},{9,8},{8,9},{11,10... | collective-permute-start | bytes 786440 | tf_op jit(solution)/shard_map/ppermute | solution.py:25
  17.1 10.2 %collective-permute-start.10 = (bf16[2,256,512]{2,1,0:T(8,128)(2,1)S(1)}, bf16[2,256,512]{2,1,0:T(8,128)(2,1)S(1)}, u32[]{:S(2)}, u32[]{:S(2)}) collective-permute-start(bf16[2,256,512]{2,1,0:T(8,128)(2,1)S(1)} %get-tuple-element.88), channel_id=1, source_target_pairs={{1,0},{0,1},{3,2},{2,3},{5,4},{4,5},{7,6},{6,7},{9,8},{8,9},{11,10... | collective-permute-start | bytes 1572872 | tf_op jit(solution)/shard_map/ppermute | solution.py:25
  17.5 2.8 %collective-permute-start.8 = (bf16[1,272,512]{2,1,0:T(8,128)(2,1)S(1)}, bf16[1,272,512]{2,1,0:T(8,128)(2,1)S(1)}, u32[]{:S(2)}, u32[]{:S(2)}) collective-permute-start(bf16[1,272,512]{2,1,0:T(8,128)(2,1)S(1)} %collective-permute-done.4.mine_ref), channel_id=1, source_target_pairs={{1,0},{0,1},{3,2},{2,3},{5,4},{4,5},{7,6},{6,7},{9,8},{8,9},{11,10... | collective-permute-start | bytes 835592 | tf_op jit(solution)/shard_map/ppermute | solution.py:25
  17.6 2.2 %collective-permute-start.5 = (bf16[1,256,512]{2,1,0:T(8,128)(2,1)S(1)}, bf16[1,256,512]{2,1,0:T(8,128)(2,1)S(1)}, u32[]{:S(2)}, u32[]{:S(2)}) collective-permute-start(bf16[1,256,512]{2,1,0:T(8,128)(2,1)S(1)} %get-tuple-element.77.refs_0_), channel_id=1, source_target_pairs={{1,0},{0,1},{3,2},{2,3},{5,4},{4,5},{7,6},{6,7},{9,8},{8,9},{11,10... | collective-permute-start | bytes 786440 | tf_op jit(solution)/shard_map/ppermute | solution.py:25
  18.0 2.2 %collective-permute-start.6 = (bf16[1,256,512]{2,1,0:T(8,128)(2,1)S(1)}, bf16[1,256,512]{2,1,0:T(8,128)(2,1)S(1)}, u32[]{:S(2)}, u32[]{:S(2)}) collective-permute-start(bf16[1,256,512]{2,1,0:T(8,128)(2,1)S(1)} %get-tuple-element.78.refs_1_), channel_id=1, source_target_pairs={{1,0},{0,1},{3,2},{2,3},{5,4},{4,5},{7,6},{6,7},{9,8},{8,9},{11,10... | collective-permute-start | bytes 786440 | tf_op jit(solution)/shard_map/ppermute | solution.py:25
  18.1 9.1 %collective-permute-start.9 = (bf16[1,256,512]{2,1,0:T(8,128)(2,1)S(1)}, bf16[1,256,512]{2,1,0:T(8,128)(2,1)S(1)}, u32[]{:S(2)}, u32[]{:S(2)}) collective-permute-start(bf16[1,256,512]{2,1,0:T(8,128)(2,1)S(1)} %shard_map.69), channel_id=1, source_target_pairs={{0,2},{1,15},{2,4},{3,1},{4,6},{5,3},{6,8},{7,5},{8,10},{9,7},{10,... | collective-permute-start | bytes 786440 | tf_op jit(solution)/shard_map/ppermute | solution.py:30
  27.2 3.5 %collective-permute-start.11 = (bf16[1,256,512]{2,1,0:T(8,128)(2,1)S(1)}, bf16[1,256,512]{2,1,0:T(8,128)(2,1)S(1)}, u32[]{:S(2)}, u32[]{:S(2)}) collective-permute-start(bf16[1,256,512]{2,1,0:T(8,128)(2,1)S(1)} %get-tuple-element.90), channel_id=1, source_target_pairs={{1,0},{0,1},{3,2},{2,3},{5,4},{4,5},{7,6},{6,7},{9,8},{8,9},{11,10... | collective-permute-start | bytes 786440 | tf_op jit(solution)/shard_map/ppermute | solution.py:25
  27.2 12.8 %collective-permute-start.7 = (bf16[2,256,512]{2,1,0:T(8,128)(2,1)S(1)}, bf16[2,256,512]{2,1,0:T(8,128)(2,1)S(1)}, u32[]{:S(2)}, u32[]{:S(2)}) collective-permute-start(bf16[2,256,512]{2,1,0:T(8,128)(2,1)S(1)} %shard_map.71), channel_id=1, source_target_pairs={{0,2},{1,15},{2,4},{3,1},{4,6},{5,3},{6,8},{7,5},{8,10},{9,7},{10,... | collective-permute-start | bytes 1572872 | tf_op jit(solution)/shard_map/ppermute | solution.py:30
  27.2 4.2 %collective-permute-start.12 = (bf16[1,256,512]{2,1,0:T(8,128)(2,1)S(1)}, bf16[1,256,512]{2,1,0:T(8,128)(2,1)S(1)}, u32[]{:S(2)}, u32[]{:S(2)}) collective-permute-start(bf16[1,256,512]{2,1,0:T(8,128)(2,1)S(1)} %get-tuple-element.91), channel_id=1, source_target_pairs={{1,0},{0,1},{3,2},{2,3},{5,4},{4,5},{7,6},{6,7},{9,8},{8,9},{11,10... | collective-permute-start | bytes 786440 | tf_op jit(solution)/shard_map/ppermute | solution.py:25
  30.2 1.5 %collective-permute-start.13 = (bf16[1,256,512]{2,1,0:T(8,128)(2,1)S(1)}, bf16[1,256,512]{2,1,0:T(8,128)(2,1)S(1)}, u32[]{:S(2)}, u32[]{:S(2)}) collective-permute-start(bf16[1,256,512]{2,1,0:T(8,128)(2,1)S(1)} %collective-permute-done.9.message_ref.mine_ref), channel_id=1, source_target_pairs={{1,0},{0,1},{3,2},{2,3},{5,4},{4,5},{7,6},{6,7},{9,8},{8,9},{11,10... | collective-permute-start | bytes 786440 | tf_op jit(solution)/shard_map/ppermute | solution.py:25
  30.2 8.0 %collective-permute-start.16 = (bf16[1,256,512]{2,1,0:T(8,128)(2,1)S(1)}, bf16[1,256,512]{2,1,0:T(8,128)(2,1)S(1)}, u32[]{:S(2)}, u32[]{:S(2)}) collective-permute-start(bf16[1,256,512]{2,1,0:T(8,128)(2,1)S(1)} %get-tuple-element.104.own_low_ref), channel_id=1, source_target_pairs={{1,0},{0,1},{3,2},{2,3},{5,4},{4,5},{7,6},{6,7},{9,8},{8,9},{11,10... | collective-permute-start | bytes 786440 | tf_op jit(solution)/shard_map/ppermute | solution.py:25
  30.7 7.5 %collective-permute-start.17 = (bf16[1,256,512]{2,1,0:T(8,128)(2,1)S(1)}, bf16[1,256,512]{2,1,0:T(8,128)(2,1)S(1)}, u32[]{:S(2)}, u32[]{:S(2)}) collective-permute-start(bf16[1,256,512]{2,1,0:T(8,128)(2,1)S(1)} %get-tuple-element.106.own_high_ref), channel_id=1, source_target_pairs={{1,0},{0,1},{3,2},{2,3},{5,4},{4,5},{7,6},{6,7},{9,8},{8,9},{11,10... | collective-permute-start | bytes 786440 | tf_op jit(solution)/shard_map/ppermute | solution.py:25
  32.4 1.2 %collective-permute-start.14 = (f32[4,512]{1,0:T(4,128)S(1)}, f32[4,512]{1,0:T(4,128)S(1)}, u32[]{:S(2)}, u32[]{:S(2)}) collective-permute-start(f32[4,512]{1,0:T(4,128)S(1)} %get-tuple-element.94.one_ref), channel_id=1, source_target_pairs={{0,1},{1,0},{2,3},{3,2},{4,5},{5,4},{6,7},{7,6},{8,9},{9,8},{10,11... | collective-permute-start | bytes 24584 | tf_op jit(solution)/shard_map/ppermute | solution.py:621
  33.6 3.7 %collective-permute-start.15 = (f32[4,512]{1,0:T(4,128)S(1)}, f32[4,512]{1,0:T(4,128)S(1)}, u32[]{:S(2)}, u32[]{:S(2)}) collective-permute-start(f32[4,512]{1,0:T(4,128)S(1)} %shard_map.74.one_ref), channel_id=1, source_target_pairs={{0,4},{1,5},{2,6},{3,7},{4,0},{5,1},{6,2},{7,3},{8,12},{9,13},{10,... | collective-permute-start | bytes 24584 | tf_op jit(solution)/shard_map/ppermute | solution.py:621
  37.2 4.5 %collective-permute-start.18 = (f32[4,512]{1,0:T(4,128)S(1)}, f32[4,512]{1,0:T(4,128)S(1)}, u32[]{:S(2)}, u32[]{:S(2)}) collective-permute-start(f32[4,512]{1,0:T(4,128)S(1)} %shard_map.76.one_ref), channel_id=1, source_target_pairs={{0,8},{1,9},{2,10},{3,11},{4,12},{5,13},{6,14},{7,15},{8,0},{9,1},... | collective-permute-start | bytes 24584 | tf_op jit(solution)/shard_map/ppermute | solution.py:621
  41.8 4.3 %collective-permute-start.19 = (f32[4,512]{1,0:T(4,128)S(1)}, f32[4,512]{1,0:T(4,128)S(1)}, u32[]{:S(2)}, u32[]{:S(2)}) collective-permute-start(f32[4,512]{1,0:T(4,128)S(1)} %shard_map.78.one_ref), channel_id=1, source_target_pairs={{0,2},{1,3},{2,0},{3,1},{4,6},{5,7},{6,4},{7,5},{8,10},{9,11},{10,... | collective-permute-start | bytes 24584 | tf_op jit(solution)/shard_map/ppermute | solution.py:621
  47.8 1.2 %collective-permute-start.20 = (f32[4,512]{1,0:T(4,128)S(1)}, f32[4,512]{1,0:T(4,128)S(1)}, u32[]{:S(2)}, u32[]{:S(2)}) collective-permute-start(f32[4,512]{1,0:T(4,128)S(1)} %get-tuple-element.115), channel_id=1, source_target_pairs={{1,0},{0,1},{3,2},{2,3},{5,4},{4,5},{7,6},{6,7},{9,8},{8,9},{11,10... | collective-permute-start | bytes 24584 | tf_op jit(solution)/shard_map/ppermute | solution.py:25

commit v4 on v3

--- a/solution.py
+++ b/solution.py
@@ -25,9 +25,13 @@
     return lax.ppermute(block, "space", [(i ^ 1, i) for i in range(count)])
 
 
-def to_next_slab(block):
+def exchange_faces(block):
     count = lax.axis_size("space")
-    return lax.ppermute(block, "space", [(i, (i + (2 if i % 2 == 0 else -2)) % count) for i in range(count)])
+    route = []
+    for slab in range(count // 2):
+        beside = ((slab + 1) ^ 1) - 1
+        route += [(2 * slab, 2 * (slab ^ 1)), (2 * slab + 1, 2 * beside % count + 1)]
+    return lax.ppermute(block, "space", route)
 
 
 def rows_of(index):
@@ -107,14 +111,15 @@
 def prologue_kernel(
     core_ref, directions_ref, start_ref, fields_ref, partner_ref, spread_ref, edge_ref, coded_ref, near
 ):
-    sign = 1.0 - 2.0 * core_ref[0].astype(F32)
+    sign = 1.0 - 2.0 * core_ref[1].astype(F32)
+    toward = sign * (1.0 - 2.0 * core_ref[0].astype(F32))
     planes, orient, cells = start_ref.shape
     low = boltzmann(fields_ref[0:1])
     high = boltzmann(fields_ref[fields_ref.shape[0] - 1 :])
     for c in range(4):
         row = directions_ref[c % 3 : c % 3 + 1]
         column = jnp.broadcast_to(row, (LANES, orient)).T
-        spread_ref[c] = column if c == 3 else sign * column
+        spread_ref[c] = (toward if c == 3 else sign) * column
 
     @each_row_block(orient)
     def _(index):
@@ -133,7 +138,7 @@
     for s, ref in enumerate((fields_ref, partner_ref)):
         for depth in range(2):
             high_row, low_row = (ref[p : p + 1] for p in (planes - 1 - depth, depth))
-            row = jnp.where(core_ref[0] == 0, high_row, low_row)
+            row = jnp.where(core_ref[0] == 1, high_row, low_row)
             coarse = row.astype(BF16).astype(F32)
             at = 2 * s + depth
             near[at : at + 1] = coarse
@@ -169,11 +174,11 @@
     def _(index):
         rows = rows_of(index)
         narrow = v_ref[3, rows, :].astype(BF16)
-        ahead = narrow > jnp.zeros_like(narrow)
+        leaves = narrow < jnp.zeros_like(narrow)
         for p in range(count):
             for t in range(cells // LANES):
                 at = 0, rows, columns(t)
-                out_ref[p, rows, columns(t)] = jnp.where(ahead, refs[p][at], refs[count + p][at])
+                out_ref[p, rows, columns(t)] = jnp.where(leaves, refs[p][at], refs[count + p][at])
 
 
 def first_message_kernel(mine_ref, other_ref, coded_ref, v_ref, out_ref):
@@ -537,7 +542,6 @@
 def shards(fields, end_weights, directions, analysis, synthesis, decay_rates):
     device = lax.axis_index("space")
     core = device % 2
-    is_first = core == 0
     planes, cells = fields.shape
     orient = end_weights.shape[0]
     plane_index = device // 2 * planes + lax.broadcasted_iota(jnp.int32, (planes, 1), 0)
@@ -547,7 +551,8 @@
 
     wide = lambda extra: jax.ShapeDtypeStruct((planes + extra, orient, cells), BF16)
     slab, plane = wide(0), wide(1 - planes)
-    core_word = jnp.reshape(core, (1,)).astype(jnp.int32)
+    face = core ^ (1 - device // 2 % 2)
+    core_word = jnp.stack([face, core]).astype(jnp.int32)
     start = jnp.transpose(end_weights, (1, 0, 2))
     spread, edge0, coded = kernel_call(
         prologue_kernel,
@@ -574,7 +579,7 @@
         return kernel_call(message_kernel, shape, (), (*blocks, *others, spread))
 
     start, _ = lax.optimization_barrier((start, message0))
-    arrived0 = to_next_slab(message0)
+    arrived0 = exchange_faces(message0)
     alone, inner, edges1 = kernel_call(
         first_alone_kernel, (slab, wide(-2), plane), (slab.shape, slab.shape), (start, own, spread, matrix)
     )
@@ -589,7 +594,7 @@
     )
     edges2, edges3, arrived0 = lax.optimization_barrier((edges2, edges3, arrived0))
     message2 = message([edges2, edges3], [swap_species(edges2), swap_species(edges3)])
-    arrived = [to_next_slab(message1), to_next_slab(message2)]
+    arrived = [exchange_faces(message1), exchange_faces(message2)]
     crossed0 = swap_species(arrived0)
     inner, _ = lax.optimization_barrier((inner, arrived0))
     partner_inner = swap_species(inner)

time: 49.8 us -> 50.9 us (1.022)
  Pallas kernels: 19.1 us -> 21.7 us
  starting transfers between devices: 15.4 us -> 14.4 us
  waiting for transfers between devices: 13.5 us -> 12.9 us
    pallas_call x17, Pallas kernels: 19.1 us -> 21.7 us  [kernel_call(): pl.pallas_call(kernel, out_shape=outs, in_specs=[smem if arg.dtype == jnp...]
    ppermute x4, waiting for transfers between devices: 4.56 us -> 3.33 us  [received(): lax.ppermute(value, 'space', [(i, i ^ distance) for i in range(count)])]
    ppermute x3, waiting for transfers between devices: 3.06 us -> 4.21 us  [exchange_faces(): return lax.ppermute(block, 'space', route)]
    ppermute x4, starting transfers between devices: 4 us -> 3.08 us  [received(): lax.ppermute(value, 'space', [(i, i ^ distance) for i in range(count)])]
    ppermute x14, waiting for transfers between devices: 5.91 us -> 5.38 us  [swap_species(): return lax.ppermute(block, 'space', [(i ^ 1, i) for i in range(count)])]
  transfers between devices with their start and end apart: 21 -> 21, of which waited for: 12 -> 12; matrix products, arithmetic and copies ran while one was open for 3% -> 3% of each run, Pallas kernels for 33% -> 35%
where the time goes in v4:
time: 50.9 us; the launch traced here: 50.8 us
  Pallas kernels  21.7 us (43%)
  starting transfers between devices  14.4 us (28%)
  waiting for transfers between devices  12.9 us (25%)
  local copies, waits for them, and re-layouts  1.44 us (3%)
    pallas_call x17, Pallas kernels, kernel_call(): pl.pallas_call(kernel, out_shape=outs, in_specs=[smem if arg.dtype == jnp...  21.7 us
    ppermute x14, starting transfers between devices, swap_species(): return lax.ppermute(block, 'space', [(i ^ 1, i) for i in range(count)])  8.4 us
    ppermute x14, waiting for transfers between devices, swap_species(): return lax.ppermute(block, 'space', [(i ^ 1, i) for i in range(count)])  5.38 us
    ppermute x3, waiting for transfers between devices, exchange_faces(): return lax.ppermute(block, 'space', route)  4.21 us
    ppermute x4, waiting for transfers between devices, received(): lax.ppermute(value, 'space', [(i, i ^ distance) for i in range(count)])  3.33 us
    ppermute x4, starting transfers between devices, received(): lax.ppermute(value, 'space', [(i, i ^ distance) for i in range(count)])  3.08 us
    ppermute x3, starting transfers between devices, exchange_faces(): return lax.ppermute(block, 'space', route)  2.89 us
    unnamed x11, local copies, waits for them, and re-layouts  1.44 us
  transfers between devices with their start and end apart: 21, of which 12 were waited for; matrix products, arithmetic and copies ran while one was open for 3% of the time, Pallas kernels for 35%

profile of v4, /device:TPU:0, one launch (start us, length us, event | category | flops | bytes accessed | tf_op | source)
XLA Modules:
  0.0 50.8 jit_solution(1416464191015425913)
XLA Ops:
  0.0 0.5 %collective-permute-start = (f32[4,512]{1,0:T(4,128)}, f32[4,512]{1,0:T(4,128)S(1)}, u32[]{:S(2)}, u32[]{:S(2)}) collective-permute-start(f32[4,512]{1,0:T(4,128)} %param.6), channel_id=1, source_target_pairs={{1,0},{0,1},{3,2},{2,3},{5,4},{4,5},{7,6},{6,7},{9,8},{8,9},{11,10... | collective-permute-start | bytes 24584 | tf_op jit(solution)/shard_map/ppermute | solution.py:25
  0.6 1.4 %copy.9 = bf16[256,4,512]{2,0,1:T(8,128)(2,1)S(1)} copy(bf16[256,4,512]{2,1,0:T(4,128)(2,1)} %param.7) | data formatting | bytes 2097152 | tf_op args[1]
  2.1 0.9 %shard_map.64 = (f32[4,256,128]{2,1,0:T(8,128)S(1)}, bf16[1,256,512]{2,1,0:T(8,128)(2,1)S(1)}, bf16[16,512]{1,0:T(8,128)(2,1)S(1)}) custom-call(s32[2]{0:T(128)S(1)} %pad_add_fusion.core_ref, f32[3,256]{1,0:T(4,128)S(1)} %copy-done.2, bf16[4,256,512]{2,1,0:T(8,128)(2,1)S(1)} %bitcast.6, f32[4,512]{1,0:T(4,128)S(1)} %get-tuple-element.118.fields_ref.first_ref.own_ref, ...), custom_call_target="tpu_custom_call" | custom-call | tf_op jit(solution)/shard_map/pallas_call | solution.py:531
  3.5 1.1 %collective-permute-done.1.other_ref = bf16[1,256,512]{2,1,0:T(8,128)(2,1)S(1)} collective-permute-done((bf16[1,256,512]{2,1,0:T(8,128)(2,1)S(1)}, bf16[1,256,512]{2,1,0:T(8,128)(2,1)S(1)}, u32[]{:S(2)}, u32[]{:S(2)}) %collective-permute-start.1) | collective-permute-done | bytes 262176 | tf_op jit(solution)/shard_map/ppermute | solution.py:25
  4.9 2.9 %collective-permute-start.4 = (bf16[1,272,512]{2,1,0:T(8,128)(2,1)S(1)}, bf16[1,272,512]{2,1,0:T(8,128)(2,1)S(1)}, u32[]{:S(2)}, u32[]{:S(2)}) collective-permute-start(bf16[1,272,512]{2,1,0:T(8,128)(2,1)S(1)} %shard_map.66), channel_id=1, source_target_pairs={{0,2},{1,15},{2,0},{3,5},{4,6},{5,3},{6,4},{7,9},{8,10},{9,7},{10,... | collective-permute-start | bytes 835592 | tf_op jit(solution)/shard_map/ppermute | solution.py:34
  7.8 2.3 %shard_map.67 = (bf16[4,256,512]{2,1,0:T(8,128)(2,1)S(1)}, bf16[2,256,512]{2,1,0:T(8,128)(2,1)S(1)}, bf16[1,256,512]{2,1,0:T(8,128)(2,1)S(1)}) custom-call(bf16[4,256,512]{2,1,0:T(8,128)(2,1)S(1)} %bitcast.8, f32[4,512]{1,0:T(4,128)S(1)} %get-tuple-element.118.fields_ref.first_ref.own_ref, f32[4,256,128]{2,1,0:T(8,128)S(1)} %get-tuple-element.65.v_ref.refs_2_.refs_4_, ...), custom_call_target="tpu_custom_call" | custom-call | tf_op jit(solution)/shard_map/pallas_call | solution.py:531
  10.1 3.0 %collective-permute-start.2 = (bf16[1,256,512]{2,1,0:T(8,128)(2,1)S(1)}, bf16[1,256,512]{2,1,0:T(8,128)(2,1)S(1)}, u32[]{:S(2)}, u32[]{:S(2)}) collective-permute-start(bf16[1,256,512]{2,1,0:T(8,128)(2,1)S(1)} %get-tuple-element.69.refs_0_), channel_id=1, source_target_pairs={{1,0},{0,1},{3,2},{2,3},{5,4},{4,5},{7,6},{6,7},{9,8},{8,9},{11,10... | collective-permute-start | bytes 786440 | tf_op jit(solution)/shard_map/ppermute | solution.py:25
  13.1 1.1 %shard_map.68 = (bf16[4,256,512]{2,1,0:T(8,128)(2,1)S(1)}, bf16[2,256,512]{2,1,0:T(8,128)(2,1)S(1)}) custom-call(s32[2]{0:T(128)S(1)} %pad_add_fusion.core_ref, bf16[4,256,512]{2,1,0:T(8,128)(2,1)S(1)} %collective-permute-done.3.partner_ref, bf16[4,256,512]{2,1,0:T(8,128)(2,1)S(1)} %bitcast.9, bf16[256,256]{1,0:T(8,128)(2,1)S(1)} %get-tuple-element.70.turned_ref), custom_call_target="tpu_custom_call" | custom-call | tf_op jit(solution)/shard_map/pallas_call | solution.py:531
  14.3 3.3 %shard_map.70 = (bf16[1,256,512]{2,1,0:T(8,128)(2,1)S(1)}, bf16[1,256,512]{2,1,0:T(8,128)(2,1)S(1)}) custom-call(bf16[4,256,512]{2,1,0:T(8,128)(2,1)S(1)} %get-tuple-element.79.state_ref.alone_ref, f32[4,512]{1,0:T(4,128)S(1)} %get-tuple-element.118.fields_ref.first_ref.own_ref, f32[4,512]{1,0:T(4,128)S(1)} %get-tuple-element.117.partner_ref.second_ref, ...), custom_call_target="tpu_custom_call" | custom-call | tf_op jit(solution)/shard_map/pallas_call | solution.py:531
  17.7 0.4 collective-permute-start.10
  18.2 0.4 collective-permute-start.5
  18.7 1.7 %collective-permute-done.5.refs_2_ = bf16[1,256,512]{2,1,0:T(8,128)(2,1)S(1)} collective-permute-done((bf16[1,256,512]{2,1,0:T(8,128)(2,1)S(1)}, bf16[1,256,512]{2,1,0:T(8,128)(2,1)S(1)}, u32[]{:S(2)}, u32[]{:S(2)}) %collective-permute-start.5) | collective-permute-done | bytes 262176 | tf_op jit(solution)/shard_map/ppermute | solution.py:25
  20.4 0.4 collective-permute-done.6.refs_3_
  20.9 4.4 %shard_map.72 = (bf16[1,256,512]{2,1,0:T(8,128)(2,1)S(1)}, bf16[1,256,512]{2,1,0:T(8,128)(2,1)S(1)}, bf16[8,256,512]{2,1,0:T(8,128)(2,1)S(1)}, bf16[1,256,512]{2...) custom-call(s32[2]{0:T(128)S(1)} %pad_add_fusion.core_ref, ...), custom_call_target="tpu_custom_call" | custom-call | tf_op jit(solution)/shard_map/pallas_call | solution.py:531
  25.3 2.6 %collective-permute-done.9.message_ref.mine_ref = bf16[1,256,512]{2,1,0:T(8,128)(2,1)S(1)} collective-permute-done((bf16[1,256,512]{2,1,0:T(8,128)(2,1)S(1)}, bf16[1,256,512]{2,1,0:T(8,128)(2,1)S(1)}, u32[]{:S(2)}, u32[]{:S(2)}) %collective-permute-start.9) | collective-permute-done | bytes 262176 | tf_op jit(solution)/shard_map/ppermute | solution.py:34
  27.9 2.9 %collective-permute-start.12 = (bf16[1,256,512]{2,1,0:T(8,128)(2,1)S(1)}, bf16[1,256,512]{2,1,0:T(8,128)(2,1)S(1)}, u32[]{:S(2)}, u32[]{:S(2)}) collective-permute-start(bf16[1,256,512]{2,1,0:T(8,128)(2,1)S(1)} %get-tuple-element.91), channel_id=1, source_target_pairs={{1,0},{0,1},{3,2},{2,3},{5,4},{4,5},{7,6},{6,7},{9,8},{8,9},{11,10... | collective-permute-start | bytes 786440 | tf_op jit(solution)/shard_map/ppermute | solution.py:25
  30.8 0.5 collective-permute-start.16
  31.4 0.6 %collective-permute-done.12.far_ref = bf16[1,256,512]{2,1,0:T(8,128)(2,1)S(1)} collective-permute-done((bf16[1,256,512]{2,1,0:T(8,128)(2,1)S(1)}, bf16[1,256,512]{2,1,0:T(8,128)(2,1)S(1)}, u32[]{:S(2)}, u32[]{:S(2)}) %collective-permute-start.12) | collective-permute-done | bytes 262176 | tf_op jit(solution)/shard_map/ppermute | solution.py:25
  32.0 0.4 collective-permute-done.13.other_ref
  32.4 1.2 %shard_map.73 = (f32[2,512]{1,0:T(2,128)S(1)}, f32[4,512]{1,0:T(4,128)S(1)}) custom-call(s32[2]{0:T(128)S(1)} %pad_add_fusion.core_ref, bf16[2,256,512]{2,1,0:T(8,128)(2,1)S(1)} %get-tuple-element.81.own_ref, bf16[1,256,512]{2,1,0:T(8,128)(2,1)S(1)} %collective-permute-done.11.near_ref, bf16[1,256,512]{2,1,0:T(8,128)(2,1)S(1)} %collective-permute-done.12.far_ref, ...), custom_call_target="tpu_custom_call" | custom-call | tf_op jit(solution)/shard_map/pallas_call | solution.py:531
  33.5 0.4 collective-permute-start.14
  33.9 0.8 %collective-permute-done.14.two_ref = f32[4,512]{1,0:T(4,128)S(1)} collective-permute-done((f32[4,512]{1,0:T(4,128)S(1)}, f32[4,512]{1,0:T(4,128)S(1)}, u32[]{:S(2)}, u32[]{:S(2)}) %collective-permute-start.14) | collective-permute-done | bytes 8224 | tf_op jit(solution)/shard_map/ppermute | solution.py:626
  34.8 3.3 %shard_map.75.held_ref = bf16[6,256,512]{2,1,0:T(8,128)(2,1)S(1)} custom-call(bf16[8,256,512]{2,1,0:T(8,128)(2,1)S(1)} %get-tuple-element.98.held_ref, bf16[1,256,512]{2,1,0:T(8,128)(2,1)S(1)} %collective-permute-done.9.message_ref.mine_ref, bf16[1,256,512]{2,1,0:T(8,128)(2,1)S(1)} %collective-permute-done.13.other_ref, ...), custom_call_target="tpu_custom_call" | custom-call | tf_op jit(solution)/shard_map/pallas_call | solution.py:531
  38.0 0.4 collective-permute-done.15.two_ref
  38.4 1.0 %collective-permute-start.18 = (f32[4,512]{1,0:T(4,128)S(1)}, f32[4,512]{1,0:T(4,128)S(1)}, u32[]{:S(2)}, u32[]{:S(2)}) collective-permute-start(f32[4,512]{1,0:T(4,128)S(1)} %shard_map.76.one_ref), channel_id=1, source_target_pairs={{0,8},{1,9},{2,10},{3,11},{4,12},{5,13},{6,14},{7,15},{8,0},{9,1},... | collective-permute-start | bytes 24584 | tf_op jit(solution)/shard_map/ppermute | solution.py:626
  39.4 1.8 %shard_map.77.shared_ref = f32[4,512]{1,0:T(4,128)S(1)} custom-call(bf16[6,256,512]{2,1,0:T(8,128)(2,1)S(1)} %shard_map.75.held_ref, f32[4,512]{1,0:T(4,128)S(1)} %get-tuple-element.117.partner_ref.second_ref, f32[4,256,128]{2,1,0:T(8,128)S(1)} %get-tuple-element.65.v_ref.refs_2_.refs_4_, bf16[4,256,512]{2,1,0:T(8,128)(2,1)S(1)} %get-tuple-element.73.weight_ref, ...), custom_call_target="tpu_custom_call" | custom-call | tf_op jit(solution)/shard_map/pallas_call | solution.py:531
  41.2 1.6 %collective-permute-done.7.message_ref = bf16[2,256,512]{2,1,0:T(8,128)(2,1)S(1)} collective-permute-done((bf16[2,256,512]{2,1,0:T(8,128)(2,1)S(1)}, bf16[2,256,512]{2,1,0:T(8,128)(2,1)S(1)}, u32[]{:S(2)}, u32[]{:S(2)}) %collective-permute-start.7) | collective-permute-done | bytes 524320 | tf_op jit(solution)/shard_map/ppermute | solution.py:34
  43.0 1.7 %collective-permute-start.19 = (f32[4,512]{1,0:T(4,128)S(1)}, f32[4,512]{1,0:T(4,128)S(1)}, u32[]{:S(2)}, u32[]{:S(2)}) collective-permute-start(f32[4,512]{1,0:T(4,128)S(1)} %shard_map.78.one_ref), channel_id=1, source_target_pairs={{0,2},{1,3},{2,0},{3,1},{4,6},{5,7},{6,4},{7,5},{8,10},{9,11},{10,... | collective-permute-start | bytes 24584 | tf_op jit(solution)/shard_map/ppermute | solution.py:626
  44.7 1.9 %collective-permute-done.19.two_ref = f32[4,512]{1,0:T(4,128)S(1)} collective-permute-done((f32[4,512]{1,0:T(4,128)S(1)}, f32[4,512]{1,0:T(4,128)S(1)}, u32[]{:S(2)}, u32[]{:S(2)}) %collective-permute-start.19) | collective-permute-done | bytes 8224 | tf_op jit(solution)/shard_map/ppermute | solution.py:626
  46.6 2.3 %shard_map.79 = (f32[4,512]{1,0:T(4,128)S(1)}, f32[4,512]{1,0:T(4,128)S(1)}) custom-call(s32[2]{0:T(128)S(1)} %pad_add_fusion.core_ref, bf16[2,256,512]{2,1,0:T(8,128)(2,1)S(1)} %collective-permute-done.7.message_ref, bf16[4,256,512]{2,1,0:T(8,128)(2,1)S(1)} %get-tuple-element.73.weight_ref, bf16[2,256,512]{2,1,0:T(8,128)(2,1)S(1)} %get-tuple-element.108.own_weight_ref, ...), custom_call_target="tpu_custom_call" | custom-call | tf_op jit(solution)/shard_map/pallas_call | solution.py:531
  49.0 1.2 %collective-permute-done.20.arrived_ref = f32[4,512]{1,0:T(4,128)S(1)} collective-permute-done((f32[4,512]{1,0:T(4,128)S(1)}, f32[4,512]{1,0:T(4,128)S(1)}, u32[]{:S(2)}, u32[]{:S(2)}) %collective-permute-start.20) | collective-permute-done | bytes 8224 | tf_op jit(solution)/shard_map/ppermute | solution.py:25
  50.1 0.6 %shard_map.80 = f32[4,512]{1,0:T(4,128)} custom-call(f32[4,512]{1,0:T(4,128)S(1)} %get-tuple-element.114.kept_ref, f32[4,512]{1,0:T(4,128)S(1)} %collective-permute-done.20.arrived_ref, f32[4,512]{1,0:T(4,128)S(1)} %shard_map.78.one_ref, f32[4,512]{1,0:T(4,128)S(1)} %collective-permute-done.19.two_ref), custom_call_target="tpu_custom_call" | custom-call | tf_op jit(solution)/shard_map/pallas_call | solution.py:531
  (41 shorter events, 1.8 us)
Async XLA Ops:
  0.0 2.1 %copy-start.4 = (f32[4,512]{1,0:T(4,128)S(1)}, f32[4,512]{1,0:T(4,128)}, u32[]{:S(2)}) copy-start(f32[4,512]{1,0:T(4,128)} %param.6) | copy-start | bytes 24580
  0.0 2.1 %copy-start.2 = (f32[3,256]{1,0:T(4,128)S(1)}, f32[3,256]{1,0:T(4,128)}, u32[]{:S(2)}) copy-start(f32[3,256]{1,0:T(4,128)} %directions_ref.1) | copy-start | bytes 9220
  0.0 3.2 %copy-start.3 = (f32[256]{0:T(256)S(1)}, f32[256]{0:T(256)}, u32[]{:S(2)}) copy-start(f32[256]{0:T(256)} %param.11) | copy-start | bytes 3076
  0.0 3.2 %copy-start = (bf16[256,256]{1,0:T(8,128)(2,1)S(1)}, bf16[256,256]{1,0:T(8,128)(2,1)}, u32[]{:S(2)}) copy-start(bf16[256,256]{1,0:T(8,128)(2,1)} %synthesis_ref.1) | copy-start | bytes 393220
  0.0 3.2 %copy-start.1 = (bf16[256,256]{1,0:T(8,128)(2,1)S(1)}, bf16[256,256]{1,0:T(8,128)(2,1)}, u32[]{:S(2)}) copy-start(bf16[256,256]{1,0:T(8,128)(2,1)} %analysis_ref.1) | copy-start | bytes 393220
  0.0 2.0 %collective-permute-start = (f32[4,512]{1,0:T(4,128)}, f32[4,512]{1,0:T(4,128)S(1)}, u32[]{:S(2)}, u32[]{:S(2)}) collective-permute-start(f32[4,512]{1,0:T(4,128)} %param.6), channel_id=1, source_target_pairs={{1,0},{0,1},{3,2},{2,3},{5,4},{4,5},{7,6},{6,7},{9,8},{8,9},{11,10... | collective-permute-start | bytes 24584 | tf_op jit(solution)/shard_map/ppermute | solution.py:25
  3.1 1.6 %collective-permute-start.1 = (bf16[1,256,512]{2,1,0:T(8,128)(2,1)S(1)}, bf16[1,256,512]{2,1,0:T(8,128)(2,1)S(1)}, u32[]{:S(2)}, u32[]{:S(2)}) collective-permute-start(bf16[1,256,512]{2,1,0:T(8,128)(2,1)S(1)} %get-tuple-element.61.mine_ref.edge_ref), channel_id=1, source_target_pairs={{1,0},{0,1},{3,2},{2,3},{5,4},{4,5},{7,6},{6,7},{9,8},{8,9},{11,10... | collective-permute-start | bytes 786440 | tf_op jit(solution)/shard_map/ppermute | solution.py:25
  4.7 8.3 %collective-permute-start.3 = (bf16[4,256,512]{2,1,0:T(8,128)(2,1)S(1)}, bf16[4,256,512]{2,1,0:T(8,128)(2,1)S(1)}, u32[]{:S(2)}, u32[]{:S(2)}) collective-permute-start(bf16[4,256,512]{2,1,0:T(8,128)(2,1)S(1)} %bitcast.7), channel_id=1, source_target_pairs={{1,0},{0,1},{3,2},{2,3},{5,4},{4,5},{7,6},{6,7},{9,8},{8,9},{11,10... | collective-permute-start | bytes 3145736 | tf_op jit(solution)/shard_map/ppermute | solution.py:25
  4.9 12.7 %collective-permute-start.4 = (bf16[1,272,512]{2,1,0:T(8,128)(2,1)S(1)}, bf16[1,272,512]{2,1,0:T(8,128)(2,1)S(1)}, u32[]{:S(2)}, u32[]{:S(2)}) collective-permute-start(bf16[1,272,512]{2,1,0:T(8,128)(2,1)S(1)} %shard_map.66), channel_id=1, source_target_pairs={{0,2},{1,15},{2,0},{3,5},{4,6},{5,3},{6,4},{7,9},{8,10},{9,7},{10,... | collective-permute-start | bytes 835592 | tf_op jit(solution)/shard_map/ppermute | solution.py:34
  10.1 4.1 %collective-permute-start.2 = (bf16[1,256,512]{2,1,0:T(8,128)(2,1)S(1)}, bf16[1,256,512]{2,1,0:T(8,128)(2,1)S(1)}, u32[]{:S(2)}, u32[]{:S(2)}) collective-permute-start(bf16[1,256,512]{2,1,0:T(8,128)(2,1)S(1)} %get-tuple-element.69.refs_0_), channel_id=1, source_target_pairs={{1,0},{0,1},{3,2},{2,3},{5,4},{4,5},{7,6},{6,7},{9,8},{8,9},{11,10... | collective-permute-start | bytes 786440 | tf_op jit(solution)/shard_map/ppermute | solution.py:25
  17.7 10.3 %collective-permute-start.10 = (bf16[2,256,512]{2,1,0:T(8,128)(2,1)S(1)}, bf16[2,256,512]{2,1,0:T(8,128)(2,1)S(1)}, u32[]{:S(2)}, u32[]{:S(2)}) collective-permute-start(bf16[2,256,512]{2,1,0:T(8,128)(2,1)S(1)} %get-tuple-element.88), channel_id=1, source_target_pairs={{1,0},{0,1},{3,2},{2,3},{5,4},{4,5},{7,6},{6,7},{9,8},{8,9},{11,10... | collective-permute-start | bytes 1572872 | tf_op jit(solution)/shard_map/ppermute | solution.py:25
  18.1 2.8 %collective-permute-start.8 = (bf16[1,272,512]{2,1,0:T(8,128)(2,1)S(1)}, bf16[1,272,512]{2,1,0:T(8,128)(2,1)S(1)}, u32[]{:S(2)}, u32[]{:S(2)}) collective-permute-start(bf16[1,272,512]{2,1,0:T(8,128)(2,1)S(1)} %collective-permute-done.4.mine_ref), channel_id=1, source_target_pairs={{1,0},{0,1},{3,2},{2,3},{5,4},{4,5},{7,6},{6,7},{9,8},{8,9},{11,10... | collective-permute-start | bytes 835592 | tf_op jit(solution)/shard_map/ppermute | solution.py:25
  18.2 2.2 %collective-permute-start.5 = (bf16[1,256,512]{2,1,0:T(8,128)(2,1)S(1)}, bf16[1,256,512]{2,1,0:T(8,128)(2,1)S(1)}, u32[]{:S(2)}, u32[]{:S(2)}) collective-permute-start(bf16[1,256,512]{2,1,0:T(8,128)(2,1)S(1)} %get-tuple-element.77.refs_0_), channel_id=1, source_target_pairs={{1,0},{0,1},{3,2},{2,3},{5,4},{4,5},{7,6},{6,7},{9,8},{8,9},{11,10... | collective-permute-start | bytes 786440 | tf_op jit(solution)/shard_map/ppermute | solution.py:25
  18.6 2.2 %collective-permute-start.6 = (bf16[1,256,512]{2,1,0:T(8,128)(2,1)S(1)}, bf16[1,256,512]{2,1,0:T(8,128)(2,1)S(1)}, u32[]{:S(2)}, u32[]{:S(2)}) collective-permute-start(bf16[1,256,512]{2,1,0:T(8,128)(2,1)S(1)} %get-tuple-element.78.refs_1_), channel_id=1, source_target_pairs={{1,0},{0,1},{3,2},{2,3},{5,4},{4,5},{7,6},{6,7},{9,8},{8,9},{11,10... | collective-permute-start | bytes 786440 | tf_op jit(solution)/shard_map/ppermute | solution.py:25
  18.7 9.2 %collective-permute-start.9 = (bf16[1,256,512]{2,1,0:T(8,128)(2,1)S(1)}, bf16[1,256,512]{2,1,0:T(8,128)(2,1)S(1)}, u32[]{:S(2)}, u32[]{:S(2)}) collective-permute-start(bf16[1,256,512]{2,1,0:T(8,128)(2,1)S(1)} %shard_map.69), channel_id=1, source_target_pairs={{0,2},{1,15},{2,0},{3,5},{4,6},{5,3},{6,4},{7,9},{8,10},{9,7},{10,... | collective-permute-start | bytes 786440 | tf_op jit(solution)/shard_map/ppermute | solution.py:34
  27.9 3.4 %collective-permute-start.11 = (bf16[1,256,512]{2,1,0:T(8,128)(2,1)S(1)}, bf16[1,256,512]{2,1,0:T(8,128)(2,1)S(1)}, u32[]{:S(2)}, u32[]{:S(2)}) collective-permute-start(bf16[1,256,512]{2,1,0:T(8,128)(2,1)S(1)} %get-tuple-element.90), channel_id=1, source_target_pairs={{1,0},{0,1},{3,2},{2,3},{5,4},{4,5},{7,6},{6,7},{9,8},{8,9},{11,10... | collective-permute-start | bytes 786440 | tf_op jit(solution)/shard_map/ppermute | solution.py:25
  27.9 14.8 %collective-permute-start.7 = (bf16[2,256,512]{2,1,0:T(8,128)(2,1)S(1)}, bf16[2,256,512]{2,1,0:T(8,128)(2,1)S(1)}, u32[]{:S(2)}, u32[]{:S(2)}) collective-permute-start(bf16[2,256,512]{2,1,0:T(8,128)(2,1)S(1)} %shard_map.71), channel_id=1, source_target_pairs={{0,2},{1,15},{2,0},{3,5},{4,6},{5,3},{6,4},{7,9},{8,10},{9,7},{10,... | collective-permute-start | bytes 1572872 | tf_op jit(solution)/shard_map/ppermute | solution.py:34
  27.9 4.1 %collective-permute-start.12 = (bf16[1,256,512]{2,1,0:T(8,128)(2,1)S(1)}, bf16[1,256,512]{2,1,0:T(8,128)(2,1)S(1)}, u32[]{:S(2)}, u32[]{:S(2)}) collective-permute-start(bf16[1,256,512]{2,1,0:T(8,128)(2,1)S(1)} %get-tuple-element.91), channel_id=1, source_target_pairs={{1,0},{0,1},{3,2},{2,3},{5,4},{4,5},{7,6},{6,7},{9,8},{8,9},{11,10... | collective-permute-start | bytes 786440 | tf_op jit(solution)/shard_map/ppermute | solution.py:25
  30.8 1.5 %collective-permute-start.13 = (bf16[1,256,512]{2,1,0:T(8,128)(2,1)S(1)}, bf16[1,256,512]{2,1,0:T(8,128)(2,1)S(1)}, u32[]{:S(2)}, u32[]{:S(2)}) collective-permute-start(bf16[1,256,512]{2,1,0:T(8,128)(2,1)S(1)} %collective-permute-done.9.message_ref.mine_ref), channel_id=1, source_target_pairs={{1,0},{0,1},{3,2},{2,3},{5,4},{4,5},{7,6},{6,7},{9,8},{8,9},{11,10... | collective-permute-start | bytes 786440 | tf_op jit(solution)/shard_map/ppermute | solution.py:25
  30.8 8.5 %collective-permute-start.16 = (bf16[1,256,512]{2,1,0:T(8,128)(2,1)S(1)}, bf16[1,256,512]{2,1,0:T(8,128)(2,1)S(1)}, u32[]{:S(2)}, u32[]{:S(2)}) collective-permute-start(bf16[1,256,512]{2,1,0:T(8,128)(2,1)S(1)} %get-tuple-element.104.own_low_ref), channel_id=1, source_target_pairs={{1,0},{0,1},{3,2},{2,3},{5,4},{4,5},{7,6},{6,7},{9,8},{8,9},{11,10... | collective-permute-start | bytes 786440 | tf_op jit(solution)/shard_map/ppermute | solution.py:25
  31.4 8.0 %collective-permute-start.17 = (bf16[1,256,512]{2,1,0:T(8,128)(2,1)S(1)}, bf16[1,256,512]{2,1,0:T(8,128)(2,1)S(1)}, u32[]{:S(2)}, u32[]{:S(2)}) collective-permute-start(bf16[1,256,512]{2,1,0:T(8,128)(2,1)S(1)} %get-tuple-element.106.own_high_ref), channel_id=1, source_target_pairs={{1,0},{0,1},{3,2},{2,3},{5,4},{4,5},{7,6},{6,7},{9,8},{8,9},{11,10... | collective-permute-start | bytes 786440 | tf_op jit(solution)/shard_map/ppermute | solution.py:25
  33.5 1.2 %collective-permute-start.14 = (f32[4,512]{1,0:T(4,128)S(1)}, f32[4,512]{1,0:T(4,128)S(1)}, u32[]{:S(2)}, u32[]{:S(2)}) collective-permute-start(f32[4,512]{1,0:T(4,128)S(1)} %get-tuple-element.94.one_ref), channel_id=1, source_target_pairs={{0,1},{1,0},{2,3},{3,2},{4,5},{5,4},{6,7},{7,6},{8,9},{9,8},{10,11... | collective-permute-start | bytes 24584 | tf_op jit(solution)/shard_map/ppermute | solution.py:626
  34.7 3.7 %collective-permute-start.15 = (f32[4,512]{1,0:T(4,128)S(1)}, f32[4,512]{1,0:T(4,128)S(1)}, u32[]{:S(2)}, u32[]{:S(2)}) collective-permute-start(f32[4,512]{1,0:T(4,128)S(1)} %shard_map.74.one_ref), channel_id=1, source_target_pairs={{0,4},{1,5},{2,6},{3,7},{4,0},{5,1},{6,2},{7,3},{8,12},{9,13},{10,... | collective-permute-start | bytes 24584 | tf_op jit(solution)/shard_map/ppermute | solution.py:626
  38.4 4.5 %collective-permute-start.18 = (f32[4,512]{1,0:T(4,128)S(1)}, f32[4,512]{1,0:T(4,128)S(1)}, u32[]{:S(2)}, u32[]{:S(2)}) collective-permute-start(f32[4,512]{1,0:T(4,128)S(1)} %shard_map.76.one_ref), channel_id=1, source_target_pairs={{0,8},{1,9},{2,10},{3,11},{4,12},{5,13},{6,14},{7,15},{8,0},{9,1},... | collective-permute-start | bytes 24584 | tf_op jit(solution)/shard_map/ppermute | solution.py:626
  43.0 3.7 %collective-permute-start.19 = (f32[4,512]{1,0:T(4,128)S(1)}, f32[4,512]{1,0:T(4,128)S(1)}, u32[]{:S(2)}, u32[]{:S(2)}) collective-permute-start(f32[4,512]{1,0:T(4,128)S(1)} %shard_map.78.one_ref), channel_id=1, source_target_pairs={{0,2},{1,3},{2,0},{3,1},{4,6},{5,7},{6,4},{7,5},{8,10},{9,11},{10,... | collective-permute-start | bytes 24584 | tf_op jit(solution)/shard_map/ppermute | solution.py:626
  48.9 1.2 %collective-permute-start.20 = (f32[4,512]{1,0:T(4,128)S(1)}, f32[4,512]{1,0:T(4,128)S(1)}, u32[]{:S(2)}, u32[]{:S(2)}) collective-permute-start(f32[4,512]{1,0:T(4,128)S(1)} %get-tuple-element.115), channel_id=1, source_target_pairs={{1,0},{0,1},{3,2},{2,3},{5,4},{4,5},{7,6},{6,7},{9,8},{8,9},{11,10... | collective-permute-start | bytes 24584 | tf_op jit(solution)/shard_map/ppermute | solution.py:25

commit v5 on v4

--- a/solution.py
+++ b/solution.py
@@ -109,9 +109,9 @@
 
 
 def prologue_kernel(
-    core_ref, directions_ref, start_ref, fields_ref, partner_ref, spread_ref, edge_ref, coded_ref, near
+    core_ref, species_ref, directions_ref, start_ref, fields_ref, partner_ref, spread_ref, edge_ref, coded_ref, near
 ):
-    sign = 1.0 - 2.0 * core_ref[1].astype(F32)
+    sign = 1.0 - 2.0 * species_ref[0].astype(F32)
     toward = sign * (1.0 - 2.0 * core_ref[0].astype(F32))
     planes, orient, cells = start_ref.shape
     low = boltzmann(fields_ref[0:1])
@@ -552,13 +552,14 @@
     wide = lambda extra: jax.ShapeDtypeStruct((planes + extra, orient, cells), BF16)
     slab, plane = wide(0), wide(1 - planes)
     face = core ^ (1 - device // 2 % 2)
-    core_word = jnp.stack([face, core]).astype(jnp.int32)
+    core_word = jnp.reshape(face, (1,)).astype(jnp.int32)
+    species_word = jnp.reshape(core, (1,)).astype(jnp.int32)
     start = jnp.transpose(end_weights, (1, 0, 2))
     spread, edge0, coded = kernel_call(
         prologue_kernel,
         (jax.ShapeDtypeStruct((4, orient, LANES), F32), plane, jax.ShapeDtypeStruct((16, cells), BF16)),
         (((16, cells), F32),),
-        (core_word, directions, start, own, partner),
+        (core_word, species_word, directions, start, own, partner),
     )
     matrix, turned = kernel_call(
         matrix_kernel,

time: 50.9 us -> 49.6 us (0.974)
  Pallas kernels: 21.7 us -> 19.1 us
  waiting for transfers between devices: 12.9 us -> 14 us
    pallas_call x17, Pallas kernels: 21.7 us -> 19.1 us  [kernel_call(): pl.pallas_call(kernel, out_shape=outs, in_specs=[smem if arg.dtype == jnp...]
    ppermute x3, waiting for transfers between devices: 4.21 us -> 5.27 us  [exchange_faces(): return lax.ppermute(block, 'space', route)]
    ppermute x14, waiting for transfers between devices: 5.38 us -> 5.89 us  [swap_species(): return lax.ppermute(block, 'space', [(i ^ 1, i) for i in range(count)])]
  transfers between devices with their start and end apart: 21 -> 21, of which waited for: 12 -> 12; matrix products, arithmetic and copies ran while one was open for 3% -> 3% of each run, Pallas kernels for 35% -> 33%
where the time goes in v5:
time: 49.6 us; the launch traced here: 49.4 us
  Pallas kernels  19.1 us (39%)
  starting transfers between devices  14.6 us (29%)
  waiting for transfers between devices  14 us (28%)
  local copies, waits for them, and re-layouts  1.44 us (3%)
    pallas_call x17, Pallas kernels, kernel_call(): pl.pallas_call(kernel, out_shape=outs, in_specs=[smem if arg.dtype == jnp...  19.1 us
    ppermute x14, starting transfers between devices, swap_species(): return lax.ppermute(block, 'space', [(i ^ 1, i) for i in range(count)])  8.41 us
    ppermute x14, waiting for transfers between devices, swap_species(): return lax.ppermute(block, 'space', [(i ^ 1, i) for i in range(count)])  5.89 us
    ppermute x3, waiting for transfers between devices, exchange_faces(): return lax.ppermute(block, 'space', route)  5.27 us
    ppermute x4, starting transfers between devices, received(): lax.ppermute(value, 'space', [(i, i ^ distance) for i in range(count)])  3.32 us
    ppermute x3, starting transfers between devices, exchange_faces(): return lax.ppermute(block, 'space', route)  2.89 us
    ppermute x4, waiting for transfers between devices, received(): lax.ppermute(value, 'space', [(i, i ^ distance) for i in range(count)])  2.87 us
    unnamed x11, local copies, waits for them, and re-layouts  1.44 us
  transfers between devices with their start and end apart: 21, of which 12 were waited for; matrix products, arithmetic and copies ran while one was open for 3% of the time, Pallas kernels for 33%

profile of v5, /device:TPU:0, one launch (start us, length us, event | category | flops | bytes accessed | tf_op | source)
XLA Modules:
  0.0 49.4 jit_solution(4740426553064700985)
XLA Ops:
  0.0 0.5 %collective-permute-start = (f32[4,512]{1,0:T(4,128)}, f32[4,512]{1,0:T(4,128)S(1)}, u32[]{:S(2)}, u32[]{:S(2)}) collective-permute-start(f32[4,512]{1,0:T(4,128)} %param.6), channel_id=1, source_target_pairs={{1,0},{0,1},{3,2},{2,3},{5,4},{4,5},{7,6},{6,7},{9,8},{8,9},{11,10... | collective-permute-start | bytes 24584 | tf_op jit(solution)/shard_map/ppermute | solution.py:25
  0.6 1.4 %copy.9 = bf16[256,4,512]{2,0,1:T(8,128)(2,1)S(1)} copy(bf16[256,4,512]{2,1,0:T(4,128)(2,1)} %param.7) | data formatting | bytes 2097152 | tf_op args[1]
  2.1 0.4 shard_map.64
  3.0 1.1 %collective-permute-done.1.other_ref = bf16[1,256,512]{2,1,0:T(8,128)(2,1)S(1)} collective-permute-done((bf16[1,256,512]{2,1,0:T(8,128)(2,1)S(1)}, bf16[1,256,512]{2,1,0:T(8,128)(2,1)S(1)}, u32[]{:S(2)}, u32[]{:S(2)}) %collective-permute-start.1) | collective-permute-done | bytes 262176 | tf_op jit(solution)/shard_map/ppermute | solution.py:25
  4.3 2.9 %collective-permute-start.4 = (bf16[1,272,512]{2,1,0:T(8,128)(2,1)S(1)}, bf16[1,272,512]{2,1,0:T(8,128)(2,1)S(1)}, u32[]{:S(2)}, u32[]{:S(2)}) collective-permute-start(bf16[1,272,512]{2,1,0:T(8,128)(2,1)S(1)} %shard_map.66), channel_id=1, source_target_pairs={{0,2},{1,15},{2,0},{3,5},{4,6},{5,3},{6,4},{7,9},{8,10},{9,7},{10,... | collective-permute-start | bytes 835592 | tf_op jit(solution)/shard_map/ppermute | solution.py:34
  7.2 2.3 %shard_map.67 = (bf16[4,256,512]{2,1,0:T(8,128)(2,1)S(1)}, bf16[2,256,512]{2,1,0:T(8,128)(2,1)S(1)}, bf16[1,256,512]{2,1,0:T(8,128)(2,1)S(1)}) custom-call(bf16[4,256,512]{2,1,0:T(8,128)(2,1)S(1)} %bitcast.8, f32[4,512]{1,0:T(4,128)S(1)} %get-tuple-element.118.fields_ref.first_ref.own_ref, f32[4,256,128]{2,1,0:T(8,128)S(1)} %get-tuple-element.65.v_ref.refs_2_.refs_4_, ...), custom_call_target="tpu_custom_call" | custom-call | tf_op jit(solution)/shard_map/pallas_call | solution.py:531
  9.5 3.0 %collective-permute-start.2 = (bf16[1,256,512]{2,1,0:T(8,128)(2,1)S(1)}, bf16[1,256,512]{2,1,0:T(8,128)(2,1)S(1)}, u32[]{:S(2)}, u32[]{:S(2)}) collective-permute-start(bf16[1,256,512]{2,1,0:T(8,128)(2,1)S(1)} %get-tuple-element.69.refs_0_), channel_id=1, source_target_pairs={{1,0},{0,1},{3,2},{2,3},{5,4},{4,5},{7,6},{6,7},{9,8},{8,9},{11,10... | collective-permute-start | bytes 786440 | tf_op jit(solution)/shard_map/ppermute | solution.py:25
  12.5 0.6 %shard_map.68 = (bf16[4,256,512]{2,1,0:T(8,128)(2,1)S(1)}, bf16[2,256,512]{2,1,0:T(8,128)(2,1)S(1)}) custom-call(s32[1]{0:T(128)} %bitcast.core_ref, bf16[4,256,512]{2,1,0:T(8,128)(2,1)S(1)} %collective-permute-done.3.partner_ref, bf16[4,256,512]{2,1,0:T(8,128)(2,1)S(1)} %bitcast.9, bf16[256,256]{1,0:T(8,128)(2,1)S(1)} %get-tuple-element.70.turned_ref), custom_call_target="tpu_custom_call" | custom-call | tf_op jit(solution)/shard_map/pallas_call | solution.py:531
  13.0 0.6 %collective-permute-done.2.refs_1_ = bf16[1,256,512]{2,1,0:T(8,128)(2,1)S(1)} collective-permute-done((bf16[1,256,512]{2,1,0:T(8,128)(2,1)S(1)}, bf16[1,256,512]{2,1,0:T(8,128)(2,1)S(1)}, u32[]{:S(2)}, u32[]{:S(2)}) %collective-permute-start.2) | collective-permute-done | bytes 262176 | tf_op jit(solution)/shard_map/ppermute | solution.py:25
  13.7 3.3 %shard_map.70 = (bf16[1,256,512]{2,1,0:T(8,128)(2,1)S(1)}, bf16[1,256,512]{2,1,0:T(8,128)(2,1)S(1)}) custom-call(bf16[4,256,512]{2,1,0:T(8,128)(2,1)S(1)} %get-tuple-element.79.state_ref.alone_ref, f32[4,512]{1,0:T(4,128)S(1)} %get-tuple-element.118.fields_ref.first_ref.own_ref, f32[4,512]{1,0:T(4,128)S(1)} %get-tuple-element.117.partner_ref.second_ref, ...), custom_call_target="tpu_custom_call" | custom-call | tf_op jit(solution)/shard_map/pallas_call | solution.py:531
  17.1 0.4 collective-permute-start.10
  17.6 0.4 collective-permute-start.5
  18.1 1.7 %collective-permute-done.5.refs_2_ = bf16[1,256,512]{2,1,0:T(8,128)(2,1)S(1)} collective-permute-done((bf16[1,256,512]{2,1,0:T(8,128)(2,1)S(1)}, bf16[1,256,512]{2,1,0:T(8,128)(2,1)S(1)}, u32[]{:S(2)}, u32[]{:S(2)}) %collective-permute-start.5) | collective-permute-done | bytes 262176 | tf_op jit(solution)/shard_map/ppermute | solution.py:25
  19.8 0.4 collective-permute-done.6.refs_3_
  20.3 3.8 %shard_map.72 = (bf16[1,256,512]{2,1,0:T(8,128)(2,1)S(1)}, bf16[1,256,512]{2,1,0:T(8,128)(2,1)S(1)}, bf16[8,256,512]{2,1,0:T(8,128)(2,1)S(1)}, bf16[1,256,512]{2...) custom-call(s32[1]{0:T(128)} %bitcast.core_ref, ...), custom_call_target="tpu_custom_call" | custom-call | tf_op jit(solution)/shard_map/pallas_call | solution.py:531
  24.2 3.2 %collective-permute-done.9.message_ref.mine_ref = bf16[1,256,512]{2,1,0:T(8,128)(2,1)S(1)} collective-permute-done((bf16[1,256,512]{2,1,0:T(8,128)(2,1)S(1)}, bf16[1,256,512]{2,1,0:T(8,128)(2,1)S(1)}, u32[]{:S(2)}, u32[]{:S(2)}) %collective-permute-start.9) | collective-permute-done | bytes 262176 | tf_op jit(solution)/shard_map/ppermute | solution.py:34
  27.3 2.9 %collective-permute-start.12 = (bf16[1,256,512]{2,1,0:T(8,128)(2,1)S(1)}, bf16[1,256,512]{2,1,0:T(8,128)(2,1)S(1)}, u32[]{:S(2)}, u32[]{:S(2)}) collective-permute-start(bf16[1,256,512]{2,1,0:T(8,128)(2,1)S(1)} %get-tuple-element.91), channel_id=1, source_target_pairs={{1,0},{0,1},{3,2},{2,3},{5,4},{4,5},{7,6},{6,7},{9,8},{8,9},{11,10... | collective-permute-start | bytes 786440 | tf_op jit(solution)/shard_map/ppermute | solution.py:25
  30.2 0.5 %collective-permute-start.16 = (bf16[1,256,512]{2,1,0:T(8,128)(2,1)S(1)}, bf16[1,256,512]{2,1,0:T(8,128)(2,1)S(1)}, u32[]{:S(2)}, u32[]{:S(2)}) collective-permute-start(bf16[1,256,512]{2,1,0:T(8,128)(2,1)S(1)} %get-tuple-element.104.own_low_ref), channel_id=1, source_target_pairs={{1,0},{0,1},{3,2},{2,3},{5,4},{4,5},{7,6},{6,7},{9,8},{8,9},{11,10... | collective-permute-start | bytes 786440 | tf_op jit(solution)/shard_map/ppermute | solution.py:25
  30.8 0.6 %collective-permute-done.12.far_ref = bf16[1,256,512]{2,1,0:T(8,128)(2,1)S(1)} collective-permute-done((bf16[1,256,512]{2,1,0:T(8,128)(2,1)S(1)}, bf16[1,256,512]{2,1,0:T(8,128)(2,1)S(1)}, u32[]{:S(2)}, u32[]{:S(2)}) %collective-permute-start.12) | collective-permute-done | bytes 262176 | tf_op jit(solution)/shard_map/ppermute | solution.py:25
  31.4 0.4 collective-permute-done.13.other_ref
  31.8 0.6 %shard_map.73 = (f32[2,512]{1,0:T(2,128)S(1)}, f32[4,512]{1,0:T(4,128)S(1)}) custom-call(s32[1]{0:T(128)} %bitcast.core_ref, bf16[2,256,512]{2,1,0:T(8,128)(2,1)S(1)} %get-tuple-element.81.own_ref, bf16[1,256,512]{2,1,0:T(8,128)(2,1)S(1)} %collective-permute-done.11.near_ref, bf16[1,256,512]{2,1,0:T(8,128)(2,1)S(1)} %collective-permute-done.12.far_ref, ...), custom_call_target="tpu_custom_call" | custom-call | tf_op jit(solution)/shard_map/pallas_call | solution.py:531
  32.4 0.4 collective-permute-start.14
  32.8 0.8 %collective-permute-done.14.two_ref = f32[4,512]{1,0:T(4,128)S(1)} collective-permute-done((f32[4,512]{1,0:T(4,128)S(1)}, f32[4,512]{1,0:T(4,128)S(1)}, u32[]{:S(2)}, u32[]{:S(2)}) %collective-permute-start.14) | collective-permute-done | bytes 8224 | tf_op jit(solution)/shard_map/ppermute | solution.py:627
  33.6 3.3 %shard_map.75.held_ref = bf16[6,256,512]{2,1,0:T(8,128)(2,1)S(1)} custom-call(bf16[8,256,512]{2,1,0:T(8,128)(2,1)S(1)} %get-tuple-element.98.held_ref, bf16[1,256,512]{2,1,0:T(8,128)(2,1)S(1)} %collective-permute-done.9.message_ref.mine_ref, bf16[1,256,512]{2,1,0:T(8,128)(2,1)S(1)} %collective-permute-done.13.other_ref, ...), custom_call_target="tpu_custom_call" | custom-call | tf_op jit(solution)/shard_map/pallas_call | solution.py:531
  37.3 1.0 %collective-permute-start.18 = (f32[4,512]{1,0:T(4,128)S(1)}, f32[4,512]{1,0:T(4,128)S(1)}, u32[]{:S(2)}, u32[]{:S(2)}) collective-permute-start(f32[4,512]{1,0:T(4,128)S(1)} %shard_map.76.one_ref), channel_id=1, source_target_pairs={{0,8},{1,9},{2,10},{3,11},{4,12},{5,13},{6,14},{7,15},{8,0},{9,1},... | collective-permute-start | bytes 24584 | tf_op jit(solution)/shard_map/ppermute | solution.py:627
  38.2 1.8 %shard_map.77.shared_ref = f32[4,512]{1,0:T(4,128)S(1)} custom-call(bf16[6,256,512]{2,1,0:T(8,128)(2,1)S(1)} %shard_map.75.held_ref, f32[4,512]{1,0:T(4,128)S(1)} %get-tuple-element.117.partner_ref.second_ref, f32[4,256,128]{2,1,0:T(8,128)S(1)} %get-tuple-element.65.v_ref.refs_2_.refs_4_, bf16[4,256,512]{2,1,0:T(8,128)(2,1)S(1)} %get-tuple-element.73.weight_ref, ...), custom_call_target="tpu_custom_call" | custom-call | tf_op jit(solution)/shard_map/pallas_call | solution.py:531
  40.0 2.1 %collective-permute-done.7.message_ref = bf16[2,256,512]{2,1,0:T(8,128)(2,1)S(1)} collective-permute-done((bf16[2,256,512]{2,1,0:T(8,128)(2,1)S(1)}, bf16[2,256,512]{2,1,0:T(8,128)(2,1)S(1)}, u32[]{:S(2)}, u32[]{:S(2)}) %collective-permute-start.7) | collective-permute-done | bytes 524320 | tf_op jit(solution)/shard_map/ppermute | solution.py:34
  42.1 2.0 %collective-permute-start.19 = (f32[4,512]{1,0:T(4,128)S(1)}, f32[4,512]{1,0:T(4,128)S(1)}, u32[]{:S(2)}, u32[]{:S(2)}) collective-permute-start(f32[4,512]{1,0:T(4,128)S(1)} %shard_map.78.one_ref), channel_id=1, source_target_pairs={{0,2},{1,3},{2,0},{3,1},{4,6},{5,7},{6,4},{7,5},{8,10},{9,11},{10,... | collective-permute-start | bytes 24584 | tf_op jit(solution)/shard_map/ppermute | solution.py:627
  44.1 1.7 %collective-permute-done.19.two_ref = f32[4,512]{1,0:T(4,128)S(1)} collective-permute-done((f32[4,512]{1,0:T(4,128)S(1)}, f32[4,512]{1,0:T(4,128)S(1)}, u32[]{:S(2)}, u32[]{:S(2)}) %collective-permute-start.19) | collective-permute-done | bytes 8224 | tf_op jit(solution)/shard_map/ppermute | solution.py:627
  45.8 1.8 %shard_map.79 = (f32[4,512]{1,0:T(4,128)S(1)}, f32[4,512]{1,0:T(4,128)S(1)}) custom-call(s32[1]{0:T(128)} %bitcast.core_ref, bf16[2,256,512]{2,1,0:T(8,128)(2,1)S(1)} %collective-permute-done.7.message_ref, bf16[4,256,512]{2,1,0:T(8,128)(2,1)S(1)} %get-tuple-element.73.weight_ref, bf16[2,256,512]{2,1,0:T(8,128)(2,1)S(1)} %get-tuple-element.108.own_weight_ref, ...), custom_call_target="tpu_custom_call" | custom-call | tf_op jit(solution)/shard_map/pallas_call | solution.py:531
  47.6 1.2 %collective-permute-done.20.arrived_ref = f32[4,512]{1,0:T(4,128)S(1)} collective-permute-done((f32[4,512]{1,0:T(4,128)S(1)}, f32[4,512]{1,0:T(4,128)S(1)}, u32[]{:S(2)}, u32[]{:S(2)}) %collective-permute-start.20) | collective-permute-done | bytes 8224 | tf_op jit(solution)/shard_map/ppermute | solution.py:25
  48.8 0.6 %shard_map.80 = f32[4,512]{1,0:T(4,128)} custom-call(f32[4,512]{1,0:T(4,128)S(1)} %get-tuple-element.114.kept_ref, f32[4,512]{1,0:T(4,128)S(1)} %collective-permute-done.20.arrived_ref, f32[4,512]{1,0:T(4,128)S(1)} %shard_map.78.one_ref, f32[4,512]{1,0:T(4,128)S(1)} %collective-permute-done.19.two_ref), custom_call_target="tpu_custom_call" | custom-call | tf_op jit(solution)/shard_map/pallas_call | solution.py:531
  (40 shorter events, 1.8 us)
Async XLA Ops:
  0.0 2.0 %copy-start.4 = (f32[4,512]{1,0:T(4,128)S(1)}, f32[4,512]{1,0:T(4,128)}, u32[]{:S(2)}) copy-start(f32[4,512]{1,0:T(4,128)} %param.6) | copy-start | bytes 24580
  0.0 2.1 %copy-start.2 = (f32[3,256]{1,0:T(4,128)S(1)}, f32[3,256]{1,0:T(4,128)}, u32[]{:S(2)}) copy-start(f32[3,256]{1,0:T(4,128)} %directions_ref.1) | copy-start | bytes 9220
  0.0 2.6 %copy-start.3 = (f32[256]{0:T(256)S(1)}, f32[256]{0:T(256)}, u32[]{:S(2)}) copy-start(f32[256]{0:T(256)} %param.11) | copy-start | bytes 3076
  0.0 2.6 %copy-start = (bf16[256,256]{1,0:T(8,128)(2,1)S(1)}, bf16[256,256]{1,0:T(8,128)(2,1)}, u32[]{:S(2)}) copy-start(bf16[256,256]{1,0:T(8,128)(2,1)} %synthesis_ref.1) | copy-start | bytes 393220
  0.0 2.6 %copy-start.1 = (bf16[256,256]{1,0:T(8,128)(2,1)S(1)}, bf16[256,256]{1,0:T(8,128)(2,1)}, u32[]{:S(2)}) copy-start(bf16[256,256]{1,0:T(8,128)(2,1)} %analysis_ref.1) | copy-start | bytes 393220
  0.0 2.0 %collective-permute-start = (f32[4,512]{1,0:T(4,128)}, f32[4,512]{1,0:T(4,128)S(1)}, u32[]{:S(2)}, u32[]{:S(2)}) collective-permute-start(f32[4,512]{1,0:T(4,128)} %param.6), channel_id=1, source_target_pairs={{1,0},{0,1},{3,2},{2,3},{5,4},{4,5},{7,6},{6,7},{9,8},{8,9},{11,10... | collective-permute-start | bytes 24584 | tf_op jit(solution)/shard_map/ppermute | solution.py:25
  2.5 1.6 %collective-permute-start.1 = (bf16[1,256,512]{2,1,0:T(8,128)(2,1)S(1)}, bf16[1,256,512]{2,1,0:T(8,128)(2,1)S(1)}, u32[]{:S(2)}, u32[]{:S(2)}) collective-permute-start(bf16[1,256,512]{2,1,0:T(8,128)(2,1)S(1)} %get-tuple-element.61.mine_ref.edge_ref), channel_id=1, source_target_pairs={{1,0},{0,1},{3,2},{2,3},{5,4},{4,5},{7,6},{6,7},{9,8},{8,9},{11,10... | collective-permute-start | bytes 786440 | tf_op jit(solution)/shard_map/ppermute | solution.py:25
  4.1 8.3 %collective-permute-start.3 = (bf16[4,256,512]{2,1,0:T(8,128)(2,1)S(1)}, bf16[4,256,512]{2,1,0:T(8,128)(2,1)S(1)}, u32[]{:S(2)}, u32[]{:S(2)}) collective-permute-start(bf16[4,256,512]{2,1,0:T(8,128)(2,1)S(1)} %bitcast.7), channel_id=1, source_target_pairs={{1,0},{0,1},{3,2},{2,3},{5,4},{4,5},{7,6},{6,7},{9,8},{8,9},{11,10... | collective-permute-start | bytes 3145736 | tf_op jit(solution)/shard_map/ppermute | solution.py:25
  4.3 12.7 %collective-permute-start.4 = (bf16[1,272,512]{2,1,0:T(8,128)(2,1)S(1)}, bf16[1,272,512]{2,1,0:T(8,128)(2,1)S(1)}, u32[]{:S(2)}, u32[]{:S(2)}) collective-permute-start(bf16[1,272,512]{2,1,0:T(8,128)(2,1)S(1)} %shard_map.66), channel_id=1, source_target_pairs={{0,2},{1,15},{2,0},{3,5},{4,6},{5,3},{6,4},{7,9},{8,10},{9,7},{10,... | collective-permute-start | bytes 835592 | tf_op jit(solution)/shard_map/ppermute | solution.py:34
  9.5 4.1 %collective-permute-start.2 = (bf16[1,256,512]{2,1,0:T(8,128)(2,1)S(1)}, bf16[1,256,512]{2,1,0:T(8,128)(2,1)S(1)}, u32[]{:S(2)}, u32[]{:S(2)}) collective-permute-start(bf16[1,256,512]{2,1,0:T(8,128)(2,1)S(1)} %get-tuple-element.69.refs_0_), channel_id=1, source_target_pairs={{1,0},{0,1},{3,2},{2,3},{5,4},{4,5},{7,6},{6,7},{9,8},{8,9},{11,10... | collective-permute-start | bytes 786440 | tf_op jit(solution)/shard_map/ppermute | solution.py:25
  17.1 10.3 %collective-permute-start.10 = (bf16[2,256,512]{2,1,0:T(8,128)(2,1)S(1)}, bf16[2,256,512]{2,1,0:T(8,128)(2,1)S(1)}, u32[]{:S(2)}, u32[]{:S(2)}) collective-permute-start(bf16[2,256,512]{2,1,0:T(8,128)(2,1)S(1)} %get-tuple-element.88), channel_id=1, source_target_pairs={{1,0},{0,1},{3,2},{2,3},{5,4},{4,5},{7,6},{6,7},{9,8},{8,9},{11,10... | collective-permute-start | bytes 1572872 | tf_op jit(solution)/shard_map/ppermute | solution.py:25
  17.5 2.8 %collective-permute-start.8 = (bf16[1,272,512]{2,1,0:T(8,128)(2,1)S(1)}, bf16[1,272,512]{2,1,0:T(8,128)(2,1)S(1)}, u32[]{:S(2)}, u32[]{:S(2)}) collective-permute-start(bf16[1,272,512]{2,1,0:T(8,128)(2,1)S(1)} %collective-permute-done.4.mine_ref), channel_id=1, source_target_pairs={{1,0},{0,1},{3,2},{2,3},{5,4},{4,5},{7,6},{6,7},{9,8},{8,9},{11,10... | collective-permute-start | bytes 835592 | tf_op jit(solution)/shard_map/ppermute | solution.py:25
  17.6 2.2 %collective-permute-start.5 = (bf16[1,256,512]{2,1,0:T(8,128)(2,1)S(1)}, bf16[1,256,512]{2,1,0:T(8,128)(2,1)S(1)}, u32[]{:S(2)}, u32[]{:S(2)}) collective-permute-start(bf16[1,256,512]{2,1,0:T(8,128)(2,1)S(1)} %get-tuple-element.77.refs_0_), channel_id=1, source_target_pairs={{1,0},{0,1},{3,2},{2,3},{5,4},{4,5},{7,6},{6,7},{9,8},{8,9},{11,10... | collective-permute-start | bytes 786440 | tf_op jit(solution)/shard_map/ppermute | solution.py:25
  18.0 2.2 %collective-permute-start.6 = (bf16[1,256,512]{2,1,0:T(8,128)(2,1)S(1)}, bf16[1,256,512]{2,1,0:T(8,128)(2,1)S(1)}, u32[]{:S(2)}, u32[]{:S(2)}) collective-permute-start(bf16[1,256,512]{2,1,0:T(8,128)(2,1)S(1)} %get-tuple-element.78.refs_1_), channel_id=1, source_target_pairs={{1,0},{0,1},{3,2},{2,3},{5,4},{4,5},{7,6},{6,7},{9,8},{8,9},{11,10... | collective-permute-start | bytes 786440 | tf_op jit(solution)/shard_map/ppermute | solution.py:25
  18.1 9.2 %collective-permute-start.9 = (bf16[1,256,512]{2,1,0:T(8,128)(2,1)S(1)}, bf16[1,256,512]{2,1,0:T(8,128)(2,1)S(1)}, u32[]{:S(2)}, u32[]{:S(2)}) collective-permute-start(bf16[1,256,512]{2,1,0:T(8,128)(2,1)S(1)} %shard_map.69), channel_id=1, source_target_pairs={{0,2},{1,15},{2,0},{3,5},{4,6},{5,3},{6,4},{7,9},{8,10},{9,7},{10,... | collective-permute-start | bytes 786440 | tf_op jit(solution)/shard_map/ppermute | solution.py:34
  27.3 3.4 %collective-permute-start.11 = (bf16[1,256,512]{2,1,0:T(8,128)(2,1)S(1)}, bf16[1,256,512]{2,1,0:T(8,128)(2,1)S(1)}, u32[]{:S(2)}, u32[]{:S(2)}) collective-permute-start(bf16[1,256,512]{2,1,0:T(8,128)(2,1)S(1)} %get-tuple-element.90), channel_id=1, source_target_pairs={{1,0},{0,1},{3,2},{2,3},{5,4},{4,5},{7,6},{6,7},{9,8},{8,9},{11,10... | collective-permute-start | bytes 786440 | tf_op jit(solution)/shard_map/ppermute | solution.py:25
  27.3 14.8 %collective-permute-start.7 = (bf16[2,256,512]{2,1,0:T(8,128)(2,1)S(1)}, bf16[2,256,512]{2,1,0:T(8,128)(2,1)S(1)}, u32[]{:S(2)}, u32[]{:S(2)}) collective-permute-start(bf16[2,256,512]{2,1,0:T(8,128)(2,1)S(1)} %shard_map.71), channel_id=1, source_target_pairs={{0,2},{1,15},{2,0},{3,5},{4,6},{5,3},{6,4},{7,9},{8,10},{9,7},{10,... | collective-permute-start | bytes 1572872 | tf_op jit(solution)/shard_map/ppermute | solution.py:34
  27.3 4.1 %collective-permute-start.12 = (bf16[1,256,512]{2,1,0:T(8,128)(2,1)S(1)}, bf16[1,256,512]{2,1,0:T(8,128)(2,1)S(1)}, u32[]{:S(2)}, u32[]{:S(2)}) collective-permute-start(bf16[1,256,512]{2,1,0:T(8,128)(2,1)S(1)} %get-tuple-element.91), channel_id=1, source_target_pairs={{1,0},{0,1},{3,2},{2,3},{5,4},{4,5},{7,6},{6,7},{9,8},{8,9},{11,10... | collective-permute-start | bytes 786440 | tf_op jit(solution)/shard_map/ppermute | solution.py:25
  30.2 1.5 %collective-permute-start.13 = (bf16[1,256,512]{2,1,0:T(8,128)(2,1)S(1)}, bf16[1,256,512]{2,1,0:T(8,128)(2,1)S(1)}, u32[]{:S(2)}, u32[]{:S(2)}) collective-permute-start(bf16[1,256,512]{2,1,0:T(8,128)(2,1)S(1)} %collective-permute-done.9.message_ref.mine_ref), channel_id=1, source_target_pairs={{1,0},{0,1},{3,2},{2,3},{5,4},{4,5},{7,6},{6,7},{9,8},{8,9},{11,10... | collective-permute-start | bytes 786440 | tf_op jit(solution)/shard_map/ppermute | solution.py:25
  30.2 8.0 %collective-permute-start.16 = (bf16[1,256,512]{2,1,0:T(8,128)(2,1)S(1)}, bf16[1,256,512]{2,1,0:T(8,128)(2,1)S(1)}, u32[]{:S(2)}, u32[]{:S(2)}) collective-permute-start(bf16[1,256,512]{2,1,0:T(8,128)(2,1)S(1)} %get-tuple-element.104.own_low_ref), channel_id=1, source_target_pairs={{1,0},{0,1},{3,2},{2,3},{5,4},{4,5},{7,6},{6,7},{9,8},{8,9},{11,10... | collective-permute-start | bytes 786440 | tf_op jit(solution)/shard_map/ppermute | solution.py:25
  30.7 7.5 %collective-permute-start.17 = (bf16[1,256,512]{2,1,0:T(8,128)(2,1)S(1)}, bf16[1,256,512]{2,1,0:T(8,128)(2,1)S(1)}, u32[]{:S(2)}, u32[]{:S(2)}) collective-permute-start(bf16[1,256,512]{2,1,0:T(8,128)(2,1)S(1)} %get-tuple-element.106.own_high_ref), channel_id=1, source_target_pairs={{1,0},{0,1},{3,2},{2,3},{5,4},{4,5},{7,6},{6,7},{9,8},{8,9},{11,10... | collective-permute-start | bytes 786440 | tf_op jit(solution)/shard_map/ppermute | solution.py:25
  32.4 1.2 %collective-permute-start.14 = (f32[4,512]{1,0:T(4,128)S(1)}, f32[4,512]{1,0:T(4,128)S(1)}, u32[]{:S(2)}, u32[]{:S(2)}) collective-permute-start(f32[4,512]{1,0:T(4,128)S(1)} %get-tuple-element.94.one_ref), channel_id=1, source_target_pairs={{0,1},{1,0},{2,3},{3,2},{4,5},{5,4},{6,7},{7,6},{8,9},{9,8},{10,11... | collective-permute-start | bytes 24584 | tf_op jit(solution)/shard_map/ppermute | solution.py:627
  33.6 3.7 %collective-permute-start.15 = (f32[4,512]{1,0:T(4,128)S(1)}, f32[4,512]{1,0:T(4,128)S(1)}, u32[]{:S(2)}, u32[]{:S(2)}) collective-permute-start(f32[4,512]{1,0:T(4,128)S(1)} %shard_map.74.one_ref), channel_id=1, source_target_pairs={{0,4},{1,5},{2,6},{3,7},{4,0},{5,1},{6,2},{7,3},{8,12},{9,13},{10,... | collective-permute-start | bytes 24584 | tf_op jit(solution)/shard_map/ppermute | solution.py:627
  37.3 4.9 %collective-permute-start.18 = (f32[4,512]{1,0:T(4,128)S(1)}, f32[4,512]{1,0:T(4,128)S(1)}, u32[]{:S(2)}, u32[]{:S(2)}) collective-permute-start(f32[4,512]{1,0:T(4,128)S(1)} %shard_map.76.one_ref), channel_id=1, source_target_pairs={{0,8},{1,9},{2,10},{3,11},{4,12},{5,13},{6,14},{7,15},{8,0},{9,1},... | collective-permute-start | bytes 24584 | tf_op jit(solution)/shard_map/ppermute | solution.py:627
  42.1 3.7 %collective-permute-start.19 = (f32[4,512]{1,0:T(4,128)S(1)}, f32[4,512]{1,0:T(4,128)S(1)}, u32[]{:S(2)}, u32[]{:S(2)}) collective-permute-start(f32[4,512]{1,0:T(4,128)S(1)} %shard_map.78.one_ref), channel_id=1, source_target_pairs={{0,2},{1,3},{2,0},{3,1},{4,6},{5,7},{6,4},{7,5},{8,10},{9,11},{10,... | collective-permute-start | bytes 24584 | tf_op jit(solution)/shard_map/ppermute | solution.py:627
  47.6 1.2 %collective-permute-start.20 = (f32[4,512]{1,0:T(4,128)S(1)}, f32[4,512]{1,0:T(4,128)S(1)}, u32[]{:S(2)}, u32[]{:S(2)}) collective-permute-start(f32[4,512]{1,0:T(4,128)S(1)} %get-tuple-element.115), channel_id=1, source_target_pairs={{1,0},{0,1},{3,2},{2,3},{5,4},{4,5},{7,6},{6,7},{9,8},{8,9},{11,10... | collective-permute-start | bytes 24584 | tf_op jit(solution)/shard_map/ppermute | solution.py:25

commit v6 on v5

--- a/solution.py
+++ b/solution.py
@@ -161,8 +161,16 @@
     out_ref[...] = one_ref[...] + two_ref[...]
 
 
-def divide_kernel(cells, kept_ref, arrived_ref, one_ref, two_ref, out_ref):
-    out_ref[...] = (kept_ref[...] + arrived_ref[...]) * (cells / (one_ref[...] + two_ref[...]))
+def join_kernel(sent_ref, one_ref, two_ref, out_ref):
+    planes = sent_ref.shape[0]
+    out_ref[:planes] = sent_ref[...]
+    out_ref[planes:] = one_ref[...] + two_ref[...]
+
+
+def divide_kernel(cells, kept_ref, mine_ref, arrived_ref, out_ref):
+    planes = kept_ref.shape[0]
+    total = mine_ref[planes:] + arrived_ref[planes:]
+    out_ref[...] = (kept_ref[...] + arrived_ref[:planes]) * (cells / total)
 
 
 def message_kernel(*refs):
@@ -611,9 +619,8 @@
         )
     )
     arrived1, second_state, partner_inner = lax.optimization_barrier((arrived[0], second_state, partner_inner))
-    *moving, _ = lax.optimization_barrier((*sent_half, *faces, arrived1))
-    partner_faces = [swap_species(block) for block in moving[2:]]
-    *partner_half, crossed1 = lax.optimization_barrier((*map(swap_species, moving[:2]), swap_species(arrived1)))
+    *moving, _ = lax.optimization_barrier((*sent_half, arrived1))
+    *partner_half, crossed1 = lax.optimization_barrier((*map(swap_species, moving), swap_species(arrived1)))
     density = jax.ShapeDtypeStruct((planes, cells), F32)
     met, partition = kernel_call(
         middle_kernel,
@@ -631,8 +638,8 @@
         block, after = received(value, distance, after)
         return kernel_call(add_kernel, density, (), (value, block)), after
 
-    partition, second_state = gathered(partition, 1, second_state)
-    second_state, _ = lax.optimization_barrier((second_state, partition))
+    *faces, second_state, _ = lax.optimization_barrier((*faces, second_state, met))
+    partner_faces = [swap_species(block) for block in faces]
     third_state = kernel_call(
         third_step_kernel,
         wide(2),
@@ -647,12 +654,11 @@
         (),
         (third_state, partner, spread, weights, partner_faces[0], partner_inner, partner_faces[1]),
     )
-    arrived2, shared = lax.optimization_barrier((arrived[1], shared))
     distance = 8
     while distance < count:
         partition, shared = gathered(partition, distance, shared)
         distance *= 2
-    beside, shared = received(partition, 2, shared)
+    arrived2, shared, _ = lax.optimization_barrier((arrived[1], shared, partition))
     sent, kept = kernel_call(
         last_kernel,
         (density, density),
@@ -662,11 +668,15 @@
             own, partner, spread, matrix,
         ),
     )
+    beside, sent = received(partition, 2, sent)
+    joined = kernel_call(
+        join_kernel, jax.ShapeDtypeStruct((2 * planes, cells), F32), (), (sent, partition, beside)
+    )
     return kernel_call(
         functools.partial(divide_kernel, count // 2 * planes * cells),
         density,
         (),
-        (kept, swap_species(sent), partition, beside),
+        (kept, joined, swap_species(joined)),
     )
 
 

time: 49.6 us -> 46.4 us (0.935)
  starting transfers between devices: 14.6 us -> 11 us
  waiting for transfers between devices: 14 us -> 14.6 us
    ppermute x4 -> x3, starting transfers between devices: 3.32 us -> 1.31 us  [received(): lax.ppermute(value, 'space', [(i, i ^ distance) for i in range(count)])]
    ppermute x14, starting transfers between devices: 8.41 us -> 6.75 us  [swap_species(): return lax.ppermute(block, 'space', [(i ^ 1, i) for i in range(count)])]
    ppermute x14, waiting for transfers between devices: 5.89 us -> 6.65 us  [swap_species(): return lax.ppermute(block, 'space', [(i ^ 1, i) for i in range(count)])]
    ppermute x4 -> x3, waiting for transfers between devices: 2.87 us -> 2.16 us  [received(): lax.ppermute(value, 'space', [(i, i ^ distance) for i in range(count)])]
    ppermute x3, waiting for transfers between devices: 5.27 us -> 5.77 us  [exchange_faces(): return lax.ppermute(block, 'space', route)]
  transfers between devices with their start and end apart: 21 -> 20, of which waited for: 12 -> 12; matrix products, arithmetic and copies ran while one was open for 3% -> 3% of each run, Pallas kernels for 33% -> 39%
where the time goes in v6:
time: 46.4 us; the launch traced here: 46.3 us
  Pallas kernels  19.1 us (41%)
  waiting for transfers between devices  14.6 us (31%)
  starting transfers between devices  11 us (24%)
  local copies, waits for them, and re-layouts  1.44 us (3%)
    pallas_call x17, Pallas kernels, kernel_call(): pl.pallas_call(kernel, out_shape=outs, in_specs=[smem if arg.dtype == jnp...  19.1 us
    ppermute x14, starting transfers between devices, swap_species(): return lax.ppermute(block, 'space', [(i ^ 1, i) for i in range(count)])  6.75 us
    ppermute x14, waiting for transfers between devices, swap_species(): return lax.ppermute(block, 'space', [(i ^ 1, i) for i in range(count)])  6.65 us
    ppermute x3, waiting for transfers between devices, exchange_faces(): return lax.ppermute(block, 'space', route)  5.77 us
    ppermute x3, starting transfers between devices, exchange_faces(): return lax.ppermute(block, 'space', route)  2.89 us
    ppermute x3, waiting for transfers between devices, received(): lax.ppermute(value, 'space', [(i, i ^ distance) for i in range(count)])  2.16 us
    unnamed x11, local copies, waits for them, and re-layouts  1.44 us
    ppermute x3, starting transfers between devices, received(): lax.ppermute(value, 'space', [(i, i ^ distance) for i in range(count)])  1.31 us
  transfers between devices with their start and end apart: 20, of which 12 were waited for; matrix products, arithmetic and copies ran while one was open for 3% of the time, Pallas kernels for 39%

profile of v6, /device:TPU:0, one launch (start us, length us, event | category | flops | bytes accessed | tf_op | source)
XLA Modules:
  0.0 46.3 jit_solution(1320917111842974502)
XLA Ops:
  0.0 0.5 %collective-permute-start = (f32[4,512]{1,0:T(4,128)}, f32[4,512]{1,0:T(4,128)S(1)}, u32[]{:S(2)}, u32[]{:S(2)}) collective-permute-start(f32[4,512]{1,0:T(4,128)} %param.6), channel_id=1, source_target_pairs={{1,0},{0,1},{3,2},{2,3},{5,4},{4,5},{7,6},{6,7},{9,8},{8,9},{11,10... | collective-permute-start | bytes 24584 | tf_op jit(solution)/shard_map/ppermute | solution.py:25
  0.6 1.4 %copy.9 = bf16[256,4,512]{2,0,1:T(8,128)(2,1)S(1)} copy(bf16[256,4,512]{2,1,0:T(4,128)(2,1)} %param.7) | data formatting | bytes 2097152 | tf_op args[1]
  2.1 0.4 shard_map.64
  2.6 0.3 shard_map.65
  3.0 1.1 %collective-permute-done.1.other_ref = bf16[1,256,512]{2,1,0:T(8,128)(2,1)S(1)} collective-permute-done((bf16[1,256,512]{2,1,0:T(8,128)(2,1)S(1)}, bf16[1,256,512]{2,1,0:T(8,128)(2,1)S(1)}, u32[]{:S(2)}, u32[]{:S(2)}) %collective-permute-start.1) | collective-permute-done | bytes 262176 | tf_op jit(solution)/shard_map/ppermute | solution.py:25
  4.3 2.9 %collective-permute-start.4 = (bf16[1,272,512]{2,1,0:T(8,128)(2,1)S(1)}, bf16[1,272,512]{2,1,0:T(8,128)(2,1)S(1)}, u32[]{:S(2)}, u32[]{:S(2)}) collective-permute-start(bf16[1,272,512]{2,1,0:T(8,128)(2,1)S(1)} %shard_map.66), channel_id=1, source_target_pairs={{0,2},{1,15},{2,0},{3,5},{4,6},{5,3},{6,4},{7,9},{8,10},{9,7},{10,... | collective-permute-start | bytes 835592 | tf_op jit(solution)/shard_map/ppermute | solution.py:34
  7.2 2.3 %shard_map.67 = (bf16[4,256,512]{2,1,0:T(8,128)(2,1)S(1)}, bf16[2,256,512]{2,1,0:T(8,128)(2,1)S(1)}, bf16[1,256,512]{2,1,0:T(8,128)(2,1)S(1)}) custom-call(bf16[4,256,512]{2,1,0:T(8,128)(2,1)S(1)} %bitcast.8, f32[4,512]{1,0:T(4,128)S(1)} %get-tuple-element.114.fields_ref.first_ref.own_ref, f32[4,256,128]{2,1,0:T(8,128)S(1)} %get-tuple-element.63.v_ref.refs_2_.refs_4_, ...), custom_call_target="tpu_custom_call" | custom-call | tf_op jit(solution)/shard_map/pallas_call | solution.py:539
  9.5 3.0 %collective-permute-start.2 = (bf16[1,256,512]{2,1,0:T(8,128)(2,1)S(1)}, bf16[1,256,512]{2,1,0:T(8,128)(2,1)S(1)}, u32[]{:S(2)}, u32[]{:S(2)}) collective-permute-start(bf16[1,256,512]{2,1,0:T(8,128)(2,1)S(1)} %get-tuple-element.67.refs_0_), channel_id=1, source_target_pairs={{1,0},{0,1},{3,2},{2,3},{5,4},{4,5},{7,6},{6,7},{9,8},{8,9},{11,10... | collective-permute-start | bytes 786440 | tf_op jit(solution)/shard_map/ppermute | solution.py:25
  12.5 0.6 %shard_map.68 = (bf16[4,256,512]{2,1,0:T(8,128)(2,1)S(1)}, bf16[2,256,512]{2,1,0:T(8,128)(2,1)S(1)}) custom-call(s32[1]{0:T(128)} %bitcast.core_ref, bf16[4,256,512]{2,1,0:T(8,128)(2,1)S(1)} %collective-permute-done.3.partner_ref, bf16[4,256,512]{2,1,0:T(8,128)(2,1)S(1)} %bitcast.9, bf16[256,256]{1,0:T(8,128)(2,1)S(1)} %get-tuple-element.68.turned_ref), custom_call_target="tpu_custom_call" | custom-call | tf_op jit(solution)/shard_map/pallas_call | solution.py:539
  13.0 0.6 %collective-permute-done.2.refs_1_ = bf16[1,256,512]{2,1,0:T(8,128)(2,1)S(1)} collective-permute-done((bf16[1,256,512]{2,1,0:T(8,128)(2,1)S(1)}, bf16[1,256,512]{2,1,0:T(8,128)(2,1)S(1)}, u32[]{:S(2)}, u32[]{:S(2)}) %collective-permute-start.2) | collective-permute-done | bytes 262176 | tf_op jit(solution)/shard_map/ppermute | solution.py:25
  13.7 3.3 %shard_map.70 = (bf16[1,256,512]{2,1,0:T(8,128)(2,1)S(1)}, bf16[1,256,512]{2,1,0:T(8,128)(2,1)S(1)}) custom-call(bf16[4,256,512]{2,1,0:T(8,128)(2,1)S(1)} %get-tuple-element.77.state_ref.alone_ref, f32[4,512]{1,0:T(4,128)S(1)} %get-tuple-element.114.fields_ref.first_ref.own_ref, f32[4,512]{1,0:T(4,128)S(1)} %get-tuple-element.113.partner_ref.second_ref, ...), custom_call_target="tpu_custom_call" | custom-call | tf_op jit(solution)/shard_map/pallas_call | solution.py:539
  17.1 0.4 collective-permute-start.10
  17.6 0.4 collective-permute-start.5
  18.1 1.7 %collective-permute-done.5.refs_2_ = bf16[1,256,512]{2,1,0:T(8,128)(2,1)S(1)} collective-permute-done((bf16[1,256,512]{2,1,0:T(8,128)(2,1)S(1)}, bf16[1,256,512]{2,1,0:T(8,128)(2,1)S(1)}, u32[]{:S(2)}, u32[]{:S(2)}) %collective-permute-start.5) | collective-permute-done | bytes 262176 | tf_op jit(solution)/shard_map/ppermute | solution.py:25
  19.8 0.4 collective-permute-done.6.refs_3_
  20.3 3.8 %shard_map.72 = (bf16[1,256,512]{2,1,0:T(8,128)(2,1)S(1)}, bf16[1,256,512]{2,1,0:T(8,128)(2,1)S(1)}, bf16[8,256,512]{2,1,0:T(8,128)(2,1)S(1)}, bf16[1,256,512]{2...) custom-call(s32[1]{0:T(128)} %bitcast.core_ref, ...), custom_call_target="tpu_custom_call" | custom-call | tf_op jit(solution)/shard_map/pallas_call | solution.py:539
  24.2 3.2 %collective-permute-done.9.message_ref.mine_ref = bf16[1,256,512]{2,1,0:T(8,128)(2,1)S(1)} collective-permute-done((bf16[1,256,512]{2,1,0:T(8,128)(2,1)S(1)}, bf16[1,256,512]{2,1,0:T(8,128)(2,1)S(1)}, u32[]{:S(2)}, u32[]{:S(2)}) %collective-permute-start.9) | collective-permute-done | bytes 262176 | tf_op jit(solution)/shard_map/ppermute | solution.py:34
  27.3 0.5 %collective-permute-start.12 = (bf16[1,256,512]{2,1,0:T(8,128)(2,1)S(1)}, bf16[1,256,512]{2,1,0:T(8,128)(2,1)S(1)}, u32[]{:S(2)}, u32[]{:S(2)}) collective-permute-start(bf16[1,256,512]{2,1,0:T(8,128)(2,1)S(1)} %get-tuple-element.87), channel_id=1, source_target_pairs={{1,0},{0,1},{3,2},{2,3},{5,4},{4,5},{7,6},{6,7},{9,8},{8,9},{11,10... | collective-permute-start | bytes 786440 | tf_op jit(solution)/shard_map/ppermute | solution.py:25
  27.8 1.0 %collective-permute-done.11.near_ref = bf16[1,256,512]{2,1,0:T(8,128)(2,1)S(1)} collective-permute-done((bf16[1,256,512]{2,1,0:T(8,128)(2,1)S(1)}, bf16[1,256,512]{2,1,0:T(8,128)(2,1)S(1)}, u32[]{:S(2)}, u32[]{:S(2)}) %collective-permute-start.11) | collective-permute-done | bytes 262176 | tf_op jit(solution)/shard_map/ppermute | solution.py:25
  28.9 0.4 collective-permute-done.12.far_ref
  29.2 0.4 collective-permute-done.13.other_ref
  29.6 0.6 %shard_map.73 = (f32[2,512]{1,0:T(2,128)S(1)}, f32[4,512]{1,0:T(4,128)S(1)}) custom-call(s32[1]{0:T(128)} %bitcast.core_ref, bf16[2,256,512]{2,1,0:T(8,128)(2,1)S(1)} %get-tuple-element.79.own_ref, bf16[1,256,512]{2,1,0:T(8,128)(2,1)S(1)} %collective-permute-done.11.near_ref, bf16[1,256,512]{2,1,0:T(8,128)(2,1)S(1)} %collective-permute-done.12.far_ref, ...), custom_call_target="tpu_custom_call" | custom-call | tf_op jit(solution)/shard_map/pallas_call | solution.py:539
  30.2 1.2 %collective-permute-start.16 = (bf16[1,256,512]{2,1,0:T(8,128)(2,1)S(1)}, bf16[1,256,512]{2,1,0:T(8,128)(2,1)S(1)}, u32[]{:S(2)}, u32[]{:S(2)}) collective-permute-start(bf16[1,256,512]{2,1,0:T(8,128)(2,1)S(1)} %get-tuple-element.101.own_low_ref), channel_id=1, source_target_pairs={{1,0},{0,1},{3,2},{2,3},{5,4},{4,5},{7,6},{6,7},{9,8},{8,9},{11,10... | collective-permute-start | bytes 786440 | tf_op jit(solution)/shard_map/ppermute | solution.py:25
  31.5 3.3 %shard_map.74.held_ref = bf16[6,256,512]{2,1,0:T(8,128)(2,1)S(1)} custom-call(bf16[8,256,512]{2,1,0:T(8,128)(2,1)S(1)} %get-tuple-element.95.held_ref, bf16[1,256,512]{2,1,0:T(8,128)(2,1)S(1)} %collective-permute-done.9.message_ref.mine_ref, bf16[1,256,512]{2,1,0:T(8,128)(2,1)S(1)} %collective-permute-done.13.other_ref, ...), custom_call_target="tpu_custom_call" | custom-call | tf_op jit(solution)/shard_map/pallas_call | solution.py:539
  34.8 0.5 %collective-permute-done.14.two_ref = f32[4,512]{1,0:T(4,128)S(1)} collective-permute-done((f32[4,512]{1,0:T(4,128)S(1)}, f32[4,512]{1,0:T(4,128)S(1)}, u32[]{:S(2)}, u32[]{:S(2)}) %collective-permute-start.14) | collective-permute-done | bytes 8224 | tf_op jit(solution)/shard_map/ppermute | solution.py:634
  35.3 1.1 %collective-permute-start.15 = (f32[4,512]{1,0:T(4,128)S(1)}, f32[4,512]{1,0:T(4,128)S(1)}, u32[]{:S(2)}, u32[]{:S(2)}) collective-permute-start(f32[4,512]{1,0:T(4,128)S(1)} %shard_map.75.one_ref), channel_id=1, source_target_pairs={{0,8},{1,9},{2,10},{3,11},{4,12},{5,13},{6,14},{7,15},{8,0},{9,1},... | collective-permute-start | bytes 24584 | tf_op jit(solution)/shard_map/ppermute | solution.py:634
  36.4 1.8 %shard_map.76.shared_ref = f32[4,512]{1,0:T(4,128)S(1)} custom-call(bf16[6,256,512]{2,1,0:T(8,128)(2,1)S(1)} %shard_map.74.held_ref, f32[4,512]{1,0:T(4,128)S(1)} %get-tuple-element.113.partner_ref.second_ref, f32[4,256,128]{2,1,0:T(8,128)S(1)} %get-tuple-element.63.v_ref.refs_2_.refs_4_, bf16[4,256,512]{2,1,0:T(8,128)(2,1)S(1)} %get-tuple-element.71.weight_ref, ...), custom_call_target="tpu_custom_call" | custom-call | tf_op jit(solution)/shard_map/pallas_call | solution.py:539
  38.2 1.7 %collective-permute-done.15.two_ref = f32[4,512]{1,0:T(4,128)S(1)} collective-permute-done((f32[4,512]{1,0:T(4,128)S(1)}, f32[4,512]{1,0:T(4,128)S(1)}, u32[]{:S(2)}, u32[]{:S(2)}) %collective-permute-start.15) | collective-permute-done | bytes 8224 | tf_op jit(solution)/shard_map/ppermute | solution.py:634
  40.0 2.6 %collective-permute-done.7.message_ref = bf16[2,256,512]{2,1,0:T(8,128)(2,1)S(1)} collective-permute-done((bf16[2,256,512]{2,1,0:T(8,128)(2,1)S(1)}, bf16[2,256,512]{2,1,0:T(8,128)(2,1)S(1)}, u32[]{:S(2)}, u32[]{:S(2)}) %collective-permute-start.7) | collective-permute-done | bytes 524320 | tf_op jit(solution)/shard_map/ppermute | solution.py:34
  42.6 1.8 %shard_map.78 = (f32[4,512]{1,0:T(4,128)S(1)}, f32[4,512]{1,0:T(4,128)S(1)}) custom-call(s32[1]{0:T(128)} %bitcast.core_ref, bf16[2,256,512]{2,1,0:T(8,128)(2,1)S(1)} %collective-permute-done.7.message_ref, bf16[4,256,512]{2,1,0:T(8,128)(2,1)S(1)} %get-tuple-element.71.weight_ref, bf16[2,256,512]{2,1,0:T(8,128)(2,1)S(1)} %get-tuple-element.107.own_weight_ref, ...), custom_call_target="tpu_custom_call" | custom-call | tf_op jit(solution)/shard_map/pallas_call | solution.py:539
  44.5 1.2 %collective-permute-done.19.arrived_ref = f32[8,512]{1,0:T(8,128)S(1)} collective-permute-done((f32[8,512]{1,0:T(8,128)S(1)}, f32[8,512]{1,0:T(8,128)S(1)}, u32[]{:S(2)}, u32[]{:S(2)}) %collective-permute-start.19) | collective-permute-done | bytes 16416 | tf_op jit(solution)/shard_map/ppermute | solution.py:25
  45.7 0.6 %shard_map.80 = f32[4,512]{1,0:T(4,128)} custom-call(f32[4,512]{1,0:T(4,128)S(1)} %get-tuple-element.109.kept_ref, f32[8,512]{1,0:T(8,128)S(1)} %shard_map.79.mine_ref, f32[8,512]{1,0:T(8,128)S(1)} %collective-permute-done.19.arrived_ref), custom_call_target="tpu_custom_call" | custom-call | tf_op jit(solution)/shard_map/pallas_call | solution.py:539
  (38 shorter events, 1.4 us)
Async XLA Ops:
  0.0 2.0 %copy-start.4 = (f32[4,512]{1,0:T(4,128)S(1)}, f32[4,512]{1,0:T(4,128)}, u32[]{:S(2)}) copy-start(f32[4,512]{1,0:T(4,128)} %param.6) | copy-start | bytes 24580
  0.0 2.1 %copy-start.2 = (f32[3,256]{1,0:T(4,128)S(1)}, f32[3,256]{1,0:T(4,128)}, u32[]{:S(2)}) copy-start(f32[3,256]{1,0:T(4,128)} %directions_ref.1) | copy-start | bytes 9220
  0.0 2.6 %copy-start.3 = (f32[256]{0:T(256)S(1)}, f32[256]{0:T(256)}, u32[]{:S(2)}) copy-start(f32[256]{0:T(256)} %param.11) | copy-start | bytes 3076
  0.0 2.6 %copy-start = (bf16[256,256]{1,0:T(8,128)(2,1)S(1)}, bf16[256,256]{1,0:T(8,128)(2,1)}, u32[]{:S(2)}) copy-start(bf16[256,256]{1,0:T(8,128)(2,1)} %synthesis_ref.1) | copy-start | bytes 393220
  0.0 2.6 %copy-start.1 = (bf16[256,256]{1,0:T(8,128)(2,1)S(1)}, bf16[256,256]{1,0:T(8,128)(2,1)}, u32[]{:S(2)}) copy-start(bf16[256,256]{1,0:T(8,128)(2,1)} %analysis_ref.1) | copy-start | bytes 393220
  0.0 2.0 %collective-permute-start = (f32[4,512]{1,0:T(4,128)}, f32[4,512]{1,0:T(4,128)S(1)}, u32[]{:S(2)}, u32[]{:S(2)}) collective-permute-start(f32[4,512]{1,0:T(4,128)} %param.6), channel_id=1, source_target_pairs={{1,0},{0,1},{3,2},{2,3},{5,4},{4,5},{7,6},{6,7},{9,8},{8,9},{11,10... | collective-permute-start | bytes 24584 | tf_op jit(solution)/shard_map/ppermute | solution.py:25
  2.5 1.6 %collective-permute-start.1 = (bf16[1,256,512]{2,1,0:T(8,128)(2,1)S(1)}, bf16[1,256,512]{2,1,0:T(8,128)(2,1)S(1)}, u32[]{:S(2)}, u32[]{:S(2)}) collective-permute-start(bf16[1,256,512]{2,1,0:T(8,128)(2,1)S(1)} %get-tuple-element.59.mine_ref.edge_ref), channel_id=1, source_target_pairs={{1,0},{0,1},{3,2},{2,3},{5,4},{4,5},{7,6},{6,7},{9,8},{8,9},{11,10... | collective-permute-start | bytes 786440 | tf_op jit(solution)/shard_map/ppermute | solution.py:25
  4.1 8.3 %collective-permute-start.3 = (bf16[4,256,512]{2,1,0:T(8,128)(2,1)S(1)}, bf16[4,256,512]{2,1,0:T(8,128)(2,1)S(1)}, u32[]{:S(2)}, u32[]{:S(2)}) collective-permute-start(bf16[4,256,512]{2,1,0:T(8,128)(2,1)S(1)} %bitcast.7), channel_id=1, source_target_pairs={{1,0},{0,1},{3,2},{2,3},{5,4},{4,5},{7,6},{6,7},{9,8},{8,9},{11,10... | collective-permute-start | bytes 3145736 | tf_op jit(solution)/shard_map/ppermute | solution.py:25
  4.3 12.7 %collective-permute-start.4 = (bf16[1,272,512]{2,1,0:T(8,128)(2,1)S(1)}, bf16[1,272,512]{2,1,0:T(8,128)(2,1)S(1)}, u32[]{:S(2)}, u32[]{:S(2)}) collective-permute-start(bf16[1,272,512]{2,1,0:T(8,128)(2,1)S(1)} %shard_map.66), channel_id=1, source_target_pairs={{0,2},{1,15},{2,0},{3,5},{4,6},{5,3},{6,4},{7,9},{8,10},{9,7},{10,... | collective-permute-start | bytes 835592 | tf_op jit(solution)/shard_map/ppermute | solution.py:34
  9.5 4.1 %collective-permute-start.2 = (bf16[1,256,512]{2,1,0:T(8,128)(2,1)S(1)}, bf16[1,256,512]{2,1,0:T(8,128)(2,1)S(1)}, u32[]{:S(2)}, u32[]{:S(2)}) collective-permute-start(bf16[1,256,512]{2,1,0:T(8,128)(2,1)S(1)} %get-tuple-element.67.refs_0_), channel_id=1, source_target_pairs={{1,0},{0,1},{3,2},{2,3},{5,4},{4,5},{7,6},{6,7},{9,8},{8,9},{11,10... | collective-permute-start | bytes 786440 | tf_op jit(solution)/shard_map/ppermute | solution.py:25
  17.1 10.3 %collective-permute-start.10 = (bf16[2,256,512]{2,1,0:T(8,128)(2,1)S(1)}, bf16[2,256,512]{2,1,0:T(8,128)(2,1)S(1)}, u32[]{:S(2)}, u32[]{:S(2)}) collective-permute-start(bf16[2,256,512]{2,1,0:T(8,128)(2,1)S(1)} %get-tuple-element.84), channel_id=1, source_target_pairs={{1,0},{0,1},{3,2},{2,3},{5,4},{4,5},{7,6},{6,7},{9,8},{8,9},{11,10... | collective-permute-start | bytes 1572872 | tf_op jit(solution)/shard_map/ppermute | solution.py:25
  17.5 2.8 %collective-permute-start.8 = (bf16[1,272,512]{2,1,0:T(8,128)(2,1)S(1)}, bf16[1,272,512]{2,1,0:T(8,128)(2,1)S(1)}, u32[]{:S(2)}, u32[]{:S(2)}) collective-permute-start(bf16[1,272,512]{2,1,0:T(8,128)(2,1)S(1)} %collective-permute-done.4.mine_ref), channel_id=1, source_target_pairs={{1,0},{0,1},{3,2},{2,3},{5,4},{4,5},{7,6},{6,7},{9,8},{8,9},{11,10... | collective-permute-start | bytes 835592 | tf_op jit(solution)/shard_map/ppermute | solution.py:25
  17.6 2.2 %collective-permute-start.5 = (bf16[1,256,512]{2,1,0:T(8,128)(2,1)S(1)}, bf16[1,256,512]{2,1,0:T(8,128)(2,1)S(1)}, u32[]{:S(2)}, u32[]{:S(2)}) collective-permute-start(bf16[1,256,512]{2,1,0:T(8,128)(2,1)S(1)} %get-tuple-element.75.refs_0_), channel_id=1, source_target_pairs={{1,0},{0,1},{3,2},{2,3},{5,4},{4,5},{7,6},{6,7},{9,8},{8,9},{11,10... | collective-permute-start | bytes 786440 | tf_op jit(solution)/shard_map/ppermute | solution.py:25
  18.0 2.2 %collective-permute-start.6 = (bf16[1,256,512]{2,1,0:T(8,128)(2,1)S(1)}, bf16[1,256,512]{2,1,0:T(8,128)(2,1)S(1)}, u32[]{:S(2)}, u32[]{:S(2)}) collective-permute-start(bf16[1,256,512]{2,1,0:T(8,128)(2,1)S(1)} %get-tuple-element.76.refs_1_), channel_id=1, source_target_pairs={{1,0},{0,1},{3,2},{2,3},{5,4},{4,5},{7,6},{6,7},{9,8},{8,9},{11,10... | collective-permute-start | bytes 786440 | tf_op jit(solution)/shard_map/ppermute | solution.py:25
  18.1 9.2 %collective-permute-start.9 = (bf16[1,256,512]{2,1,0:T(8,128)(2,1)S(1)}, bf16[1,256,512]{2,1,0:T(8,128)(2,1)S(1)}, u32[]{:S(2)}, u32[]{:S(2)}) collective-permute-start(bf16[1,256,512]{2,1,0:T(8,128)(2,1)S(1)} %shard_map.69), channel_id=1, source_target_pairs={{0,2},{1,15},{2,0},{3,5},{4,6},{5,3},{6,4},{7,9},{8,10},{9,7},{10,... | collective-permute-start | bytes 786440 | tf_op jit(solution)/shard_map/ppermute | solution.py:34
  27.3 1.5 %collective-permute-start.11 = (bf16[1,256,512]{2,1,0:T(8,128)(2,1)S(1)}, bf16[1,256,512]{2,1,0:T(8,128)(2,1)S(1)}, u32[]{:S(2)}, u32[]{:S(2)}) collective-permute-start(bf16[1,256,512]{2,1,0:T(8,128)(2,1)S(1)} %get-tuple-element.86), channel_id=1, source_target_pairs={{1,0},{0,1},{3,2},{2,3},{5,4},{4,5},{7,6},{6,7},{9,8},{8,9},{11,10... | collective-permute-start | bytes 786440 | tf_op jit(solution)/shard_map/ppermute | solution.py:25
  27.3 1.9 %collective-permute-start.12 = (bf16[1,256,512]{2,1,0:T(8,128)(2,1)S(1)}, bf16[1,256,512]{2,1,0:T(8,128)(2,1)S(1)}, u32[]{:S(2)}, u32[]{:S(2)}) collective-permute-start(bf16[1,256,512]{2,1,0:T(8,128)(2,1)S(1)} %get-tuple-element.87), channel_id=1, source_target_pairs={{1,0},{0,1},{3,2},{2,3},{5,4},{4,5},{7,6},{6,7},{9,8},{8,9},{11,10... | collective-permute-start | bytes 786440 | tf_op jit(solution)/shard_map/ppermute | solution.py:25
  27.8 1.8 %collective-permute-start.13 = (bf16[1,256,512]{2,1,0:T(8,128)(2,1)S(1)}, bf16[1,256,512]{2,1,0:T(8,128)(2,1)S(1)}, u32[]{:S(2)}, u32[]{:S(2)}) collective-permute-start(bf16[1,256,512]{2,1,0:T(8,128)(2,1)S(1)} %collective-permute-done.9.message_ref.mine_ref), channel_id=1, source_target_pairs={{1,0},{0,1},{3,2},{2,3},{5,4},{4,5},{7,6},{6,7},{9,8},{8,9},{11,10... | collective-permute-start | bytes 786440 | tf_op jit(solution)/shard_map/ppermute | solution.py:25
  27.8 14.8 %collective-permute-start.7 = (bf16[2,256,512]{2,1,0:T(8,128)(2,1)S(1)}, bf16[2,256,512]{2,1,0:T(8,128)(2,1)S(1)}, u32[]{:S(2)}, u32[]{:S(2)}) collective-permute-start(bf16[2,256,512]{2,1,0:T(8,128)(2,1)S(1)} %shard_map.71), channel_id=1, source_target_pairs={{0,2},{1,15},{2,0},{3,5},{4,6},{5,3},{6,4},{7,9},{8,10},{9,7},{10,... | collective-permute-start | bytes 1572872 | tf_op jit(solution)/shard_map/ppermute | solution.py:34
  30.2 6.1 %collective-permute-start.16 = (bf16[1,256,512]{2,1,0:T(8,128)(2,1)S(1)}, bf16[1,256,512]{2,1,0:T(8,128)(2,1)S(1)}, u32[]{:S(2)}, u32[]{:S(2)}) collective-permute-start(bf16[1,256,512]{2,1,0:T(8,128)(2,1)S(1)} %get-tuple-element.101.own_low_ref), channel_id=1, source_target_pairs={{1,0},{0,1},{3,2},{2,3},{5,4},{4,5},{7,6},{6,7},{9,8},{8,9},{11,10... | collective-permute-start | bytes 786440 | tf_op jit(solution)/shard_map/ppermute | solution.py:25
  31.4 5.0 %collective-permute-start.17 = (bf16[1,256,512]{2,1,0:T(8,128)(2,1)S(1)}, bf16[1,256,512]{2,1,0:T(8,128)(2,1)S(1)}, u32[]{:S(2)}, u32[]{:S(2)}) collective-permute-start(bf16[1,256,512]{2,1,0:T(8,128)(2,1)S(1)} %get-tuple-element.103.own_high_ref), channel_id=1, source_target_pairs={{1,0},{0,1},{3,2},{2,3},{5,4},{4,5},{7,6},{6,7},{9,8},{8,9},{11,10... | collective-permute-start | bytes 786440 | tf_op jit(solution)/shard_map/ppermute | solution.py:25
  31.5 3.8 %collective-permute-start.14 = (f32[4,512]{1,0:T(4,128)S(1)}, f32[4,512]{1,0:T(4,128)S(1)}, u32[]{:S(2)}, u32[]{:S(2)}) collective-permute-start(f32[4,512]{1,0:T(4,128)S(1)} %get-tuple-element.90.one_ref), channel_id=1, source_target_pairs={{0,4},{1,5},{2,6},{3,7},{4,0},{5,1},{6,2},{7,3},{8,12},{9,13},{10,... | collective-permute-start | bytes 24584 | tf_op jit(solution)/shard_map/ppermute | solution.py:634
  35.3 4.5 %collective-permute-start.15 = (f32[4,512]{1,0:T(4,128)S(1)}, f32[4,512]{1,0:T(4,128)S(1)}, u32[]{:S(2)}, u32[]{:S(2)}) collective-permute-start(f32[4,512]{1,0:T(4,128)S(1)} %shard_map.75.one_ref), channel_id=1, source_target_pairs={{0,8},{1,9},{2,10},{3,11},{4,12},{5,13},{6,14},{7,15},{8,0},{9,1},... | collective-permute-start | bytes 24584 | tf_op jit(solution)/shard_map/ppermute | solution.py:634
  39.8 4.6 %collective-permute-start.18 = (f32[4,512]{1,0:T(4,128)S(1)}, f32[4,512]{1,0:T(4,128)S(1)}, u32[]{:S(2)}, u32[]{:S(2)}) collective-permute-start(f32[4,512]{1,0:T(4,128)S(1)} %shard_map.77.one_ref), channel_id=1, source_target_pairs={{0,2},{1,3},{2,0},{3,1},{4,6},{5,7},{6,4},{7,5},{8,10},{9,11},{10,... | collective-permute-start | bytes 24584 | tf_op jit(solution)/shard_map/ppermute | solution.py:634
  44.4 1.2 %collective-permute-start.19 = (f32[8,512]{1,0:T(8,128)S(1)}, f32[8,512]{1,0:T(8,128)S(1)}, u32[]{:S(2)}, u32[]{:S(2)}) collective-permute-start(f32[8,512]{1,0:T(8,128)S(1)} %shard_map.79.mine_ref), channel_id=1, source_target_pairs={{1,0},{0,1},{3,2},{2,3},{5,4},{4,5},{7,6},{6,7},{9,8},{8,9},{11,10... | collective-permute-start | bytes 49160 | tf_op jit(solution)/shard_map/ppermute | solution.py:25

commit v7 on v6

--- a/solution.py
+++ b/solution.py
@@ -12,6 +12,7 @@
 LANES = 128
 ROWS = 16
 UNROLL = 4
+PAD = 2
 
 courant = 0.3
 slope = 0.6
@@ -189,10 +190,12 @@
                 out_ref[p, rows, columns(t)] = jnp.where(leaves, refs[p][at], refs[count + p][at])
 
 
-def first_message_kernel(mine_ref, other_ref, coded_ref, v_ref, out_ref):
+def first_message_kernel(mine_ref, other_ref, *refs):
+    *coded_refs, v_ref, out_ref = refs
     message_kernel(mine_ref, other_ref, v_ref, out_ref)
     orient = mine_ref.shape[1]
-    out_ref[0, orient:] = coded_ref[...]
+    for k, ref in enumerate(coded_refs):
+        out_ref[0, orient + 16 * k : orient + 16 * (k + 1)] = ref[...]
 
 
 def write_edge(edges_ref, step, faces, rows, v_ref):
@@ -218,7 +221,8 @@
             store_plane(moved, p, rows, drift(loaded[p], before, after, geo))
 
 
-def first_alone_kernel(start_ref, first_ref, v_ref, m_ref, out_ref, inner_ref, edges_ref, held, moved):
+def first_alone_kernel(start_ref, first_ref, v_ref, m_ref, out_ref, edges_ref, *refs):
+    *inner_refs, held, moved = refs
     planes, orient, _ = start_ref.shape
     first = boltzmann(first_ref[...])
     for p in range(planes):
@@ -228,7 +232,7 @@
         state = (first[p : p + 1] * first[p : p + 1] * mix(m_ref[...], moved[p])).astype(BF16)
         out_ref[p] = state
         if 0 < p < planes - 1:
-            inner_ref[p - 1] = state
+            inner_refs[p - 1][0] = state
 
     @each_row_block(orient)
     def _(index):
@@ -417,7 +421,8 @@
     return jnp.sum(value.reshape(ROWS // 8, 8, LANES), axis=0)
 
 
-def pairing_kernel(held_ref, second_ref, v_ref, weight_ref, low_ref, inner_ref, high_ref, out_ref):
+def pairing_kernel(held_ref, second_ref, v_ref, weight_ref, *refs):
+    *partner_refs, out_ref = refs
     planes, orient, cells = weight_ref.shape
     second = boltzmann(second_ref[...])
     tiles = cells // LANES
@@ -430,8 +435,7 @@
         for p in range(planes):
             moved_tiles = drift(loaded[p + 1], loaded[p], loaded[p + 2], geo)
             weights = load_plane(weight_ref, p, rows)
-            partner_refs = [(low_ref, 0)] + [(inner_ref, k) for k in range(planes - 2)] + [(high_ref, 0)]
-            partner = load_plane(*partner_refs[p], rows)
+            partner = load_plane(partner_refs[p], 0, rows)
             for t in range(tiles):
                 last, third = sums[2 * (p * tiles + t)], sums[2 * (p * tiles + t) + 1]
                 new.append(last + fold(moved_tiles[t] * weights[t].astype(F32)))
@@ -589,14 +593,24 @@
 
     start, _ = lax.optimization_barrier((start, message0))
     arrived0 = exchange_faces(message0)
-    alone, inner, edges1 = kernel_call(
-        first_alone_kernel, (slab, wide(-2), plane), (slab.shape, slab.shape), (start, own, spread, matrix)
+    alone, edges1, *inner = kernel_call(
+        first_alone_kernel,
+        (slab, plane) + (plane,) * (planes - 2),
+        (slab.shape, slab.shape),
+        (start, own, spread, matrix),
     )
     weights, own_weights = kernel_call(
         weight_kernel, (slab, wide(2 - planes)), (), (core_word, swap_species(start), start, turned)
     )
-    others1, weights = lax.optimization_barrier((swap_species(edges1), weights))
-    message1 = message([edges1], [others1])
+    others1, weights, *partner_inner = lax.optimization_barrier(
+        (swap_species(edges1), weights, *map(swap_species, inner))
+    )
+    message1 = kernel_call(
+        first_message_kernel,
+        jax.ShapeDtypeStruct((1, orient + 16 * PAD, cells), BF16),
+        (),
+        (edges1, others1, *[coded] * PAD, spread),
+    )
     state, *_ = lax.optimization_barrier((alone, message1, weights))
     edges2, edges3 = kernel_call(
         next_alone_kernel, (plane, plane), (slab.shape, slab.shape), (state, own, partner, spread, matrix)
@@ -605,8 +619,6 @@
     message2 = message([edges2, edges3], [swap_species(edges2), swap_species(edges3)])
     arrived = [exchange_faces(message1), exchange_faces(message2)]
     crossed0 = swap_species(arrived0)
-    inner, _ = lax.optimization_barrier((inner, arrived0))
-    partner_inner = swap_species(inner)
 
     alone, *_ = lax.optimization_barrier((alone, message1, message2))
     half = planes // 2
@@ -618,7 +630,7 @@
             (core_word, alone, edge0, arrived0, crossed0, own, partner, spread, matrix),
         )
     )
-    arrived1, second_state, partner_inner = lax.optimization_barrier((arrived[0], second_state, partner_inner))
+    arrived1, second_state = lax.optimization_barrier((arrived[0], second_state))
     *moving, _ = lax.optimization_barrier((*sent_half, arrived1))
     *partner_half, crossed1 = lax.optimization_barrier((*map(swap_species, moving), swap_species(arrived1)))
     density = jax.ShapeDtypeStruct((planes, cells), F32)
@@ -652,7 +664,7 @@
         pairing_kernel,
         density,
         (),
-        (third_state, partner, spread, weights, partner_faces[0], partner_inner, partner_faces[1]),
+        (third_state, partner, spread, weights, partner_faces[0], *partner_inner, partner_faces[1]),
     )
     distance = 8
     while distance < count:

time: 46.4 us -> 45.8 us (0.987)
  waiting for transfers between devices: 14.6 us -> 6.64 us
  starting transfers between devices: 11 us -> 18.3 us
    ppermute x3, waiting for transfers between devices: 5.77 us -> 0.01 us  [exchange_faces(): return lax.ppermute(block, 'space', route)]
    ppermute x3, starting transfers between devices: 1.31 us -> 4.76 us  [received(): lax.ppermute(value, 'space', [(i, i ^ distance) for i in range(count)])]
    ppermute x14 -> x15, starting transfers between devices: 6.75 us -> 9.26 us  [swap_species(): return lax.ppermute(block, 'space', [(i ^ 1, i) for i in range(count)])]
    ppermute x14 -> x15, waiting for transfers between devices: 6.65 us -> 4.68 us  [swap_species(): return lax.ppermute(block, 'space', [(i ^ 1, i) for i in range(count)])]
    ppermute x3, starting transfers between devices: 2.89 us -> 4.24 us  [exchange_faces(): return lax.ppermute(block, 'space', route)]
  transfers between devices with their start and end apart: 20 -> 21, of which waited for: 12 -> 10; matrix products, arithmetic and copies ran while one was open for 3% -> 3% of each run, Pallas kernels for 39% -> 39%
where the time goes in v7:
time: 45.8 us; the launch traced here: 45.7 us
  Pallas kernels  19.1 us (42%)
  starting transfers between devices  18.3 us (40%)
  waiting for transfers between devices  6.64 us (14%)
  local copies, waits for them, and re-layouts  1.44 us (3%)
    pallas_call x17, Pallas kernels, kernel_call(): pl.pallas_call(kernel, out_shape=outs, in_specs=[smem if arg.dtype == jnp...  19.1 us
    ppermute x15, starting transfers between devices, swap_species(): return lax.ppermute(block, 'space', [(i ^ 1, i) for i in range(count)])  9.26 us
    ppermute x3, starting transfers between devices, received(): lax.ppermute(value, 'space', [(i, i ^ distance) for i in range(count)])  4.76 us
    ppermute x15, waiting for transfers between devices, swap_species(): return lax.ppermute(block, 'space', [(i ^ 1, i) for i in range(count)])  4.68 us
    ppermute x3, starting transfers between devices, exchange_faces(): return lax.ppermute(block, 'space', route)  4.24 us
    ppermute x3, waiting for transfers between devices, received(): lax.ppermute(value, 'space', [(i, i ^ distance) for i in range(count)])  1.96 us
    unnamed x11, local copies, waits for them, and re-layouts  1.44 us
  transfers between devices with their start and end apart: 21, of which 10 were waited for; matrix products, arithmetic and copies ran while one was open for 3% of the time, Pallas kernels for 39%

profile of v7, /device:TPU:0, one launch (start us, length us, event | category | flops | bytes accessed | tf_op | source)
XLA Modules:
  0.0 45.7 jit_solution(16141859389484053034)
XLA Ops:
  0.0 0.5 %collective-permute-start = (f32[4,512]{1,0:T(4,128)}, f32[4,512]{1,0:T(4,128)S(1)}, u32[]{:S(2)}, u32[]{:S(2)}) collective-permute-start(f32[4,512]{1,0:T(4,128)} %param.6), channel_id=1, source_target_pairs={{1,0},{0,1},{3,2},{2,3},{5,4},{4,5},{7,6},{6,7},{9,8},{8,9},{11,10... | collective-permute-start | bytes 24584 | tf_op jit(solution)/shard_map/ppermute | solution.py:26
  0.6 1.4 %copy.9 = bf16[256,4,512]{2,0,1:T(8,128)(2,1)S(1)} copy(bf16[256,4,512]{2,1,0:T(4,128)(2,1)} %param.7) | data formatting | bytes 2097152 | tf_op args[1]
  2.1 0.4 shard_map.64
  2.6 0.3 shard_map.65
  3.0 1.1 %collective-permute-done.1.other_ref = bf16[1,256,512]{2,1,0:T(8,128)(2,1)S(1)} collective-permute-done((bf16[1,256,512]{2,1,0:T(8,128)(2,1)S(1)}, bf16[1,256,512]{2,1,0:T(8,128)(2,1)S(1)}, u32[]{:S(2)}, u32[]{:S(2)}) %collective-permute-start.1) | collective-permute-done | bytes 262176 | tf_op jit(solution)/shard_map/ppermute | solution.py:26
  4.3 2.9 %collective-permute-start.6 = (bf16[1,272,512]{2,1,0:T(8,128)(2,1)S(1)}, bf16[1,272,512]{2,1,0:T(8,128)(2,1)S(1)}, u32[]{:S(2)}, u32[]{:S(2)}) collective-permute-start(bf16[1,272,512]{2,1,0:T(8,128)(2,1)S(1)} %shard_map.66), channel_id=1, source_target_pairs={{0,2},{1,15},{2,0},{3,5},{4,6},{5,3},{6,4},{7,9},{8,10},{9,7},{10,... | collective-permute-start | bytes 835592 | tf_op jit(solution)/shard_map/ppermute | solution.py:35
  7.2 2.3 %shard_map.67 = (bf16[4,256,512]{2,1,0:T(8,128)(2,1)S(1)}, bf16[1,256,512]{2,1,0:T(8,128)(2,1)S(1)}, bf16[1,256,512]{2,1,0:T(8,128)(2,1)S(1)}, bf16[1,256,512]{2,1,0:T(8,128)(2,1)S(1)}) custom-call(bf16[4,256,512]{2,1,0:T(8,128)(2,1)S(1)} %bitcast.8, f32[4,512]{1,0:T(4,128)S(1)} %get-tuple-element.116.fields_ref.first_ref.own_ref, ...), custom_call_target="tpu_custom_call" | custom-call | tf_op jit(solution)/shard_map/pallas_call | solution.py:543
  9.5 3.0 %collective-permute-start.4 = (bf16[1,256,512]{2,1,0:T(8,128)(2,1)S(1)}, bf16[1,256,512]{2,1,0:T(8,128)(2,1)S(1)}, u32[]{:S(2)}, u32[]{:S(2)}) collective-permute-start(bf16[1,256,512]{2,1,0:T(8,128)(2,1)S(1)} %get-tuple-element.71), channel_id=1, source_target_pairs={{1,0},{0,1},{3,2},{2,3},{5,4},{4,5},{7,6},{6,7},{9,8},{8,9},{11,10... | collective-permute-start | bytes 786440 | tf_op jit(solution)/shard_map/ppermute | solution.py:26
  12.5 0.4 collective-permute-start.2
  13.0 0.6 %shard_map.68 = (bf16[4,256,512]{2,1,0:T(8,128)(2,1)S(1)}, bf16[2,256,512]{2,1,0:T(8,128)(2,1)S(1)}) custom-call(s32[1]{0:T(128)} %bitcast.core_ref, bf16[4,256,512]{2,1,0:T(8,128)(2,1)S(1)} %collective-permute-done.3.partner_ref, bf16[4,256,512]{2,1,0:T(8,128)(2,1)S(1)} %bitcast.9, bf16[256,256]{1,0:T(8,128)(2,1)S(1)} %get-tuple-element.69.turned_ref), custom_call_target="tpu_custom_call" | custom-call | tf_op jit(solution)/shard_map/pallas_call | solution.py:543
  13.6 0.4 collective-permute-done.5.refs_2_
  14.0 0.4 collective-permute-done.2.other_ref
  14.5 3.3 %shard_map.70 = (bf16[1,256,512]{2,1,0:T(8,128)(2,1)S(1)}, bf16[1,256,512]{2,1,0:T(8,128)(2,1)S(1)}) custom-call(bf16[4,256,512]{2,1,0:T(8,128)(2,1)S(1)} %get-tuple-element.80.state_ref.alone_ref, f32[4,512]{1,0:T(4,128)S(1)} %get-tuple-element.116.fields_ref.first_ref.own_ref, f32[4,512]{1,0:T(4,128)S(1)} %get-tuple-element.115.partner_ref.second_ref, ...), custom_call_target="tpu_custom_call" | custom-call | tf_op jit(solution)/shard_map/pallas_call | solution.py:543
  17.9 0.9 %collective-permute-start.10 = (bf16[1,272,512]{2,1,0:T(8,128)(2,1)S(1)}, bf16[1,272,512]{2,1,0:T(8,128)(2,1)S(1)}, u32[]{:S(2)}, u32[]{:S(2)}) collective-permute-start(bf16[1,272,512]{2,1,0:T(8,128)(2,1)S(1)} %collective-permute-done.6.mine_ref), channel_id=1, source_target_pairs={{1,0},{0,1},{3,2},{2,3},{5,4},{4,5},{7,6},{6,7},{9,8},{8,9},{11,10... | collective-permute-start | bytes 835592 | tf_op jit(solution)/shard_map/ppermute | solution.py:26
  18.9 0.4 collective-permute-start.8
  19.3 1.0 %collective-permute-done.7.refs_2_ = bf16[1,256,512]{2,1,0:T(8,128)(2,1)S(1)} collective-permute-done((bf16[1,256,512]{2,1,0:T(8,128)(2,1)S(1)}, bf16[1,256,512]{2,1,0:T(8,128)(2,1)S(1)}, u32[]{:S(2)}, u32[]{:S(2)}) %collective-permute-start.7) | collective-permute-done | bytes 262176 | tf_op jit(solution)/shard_map/ppermute | solution.py:26
  20.4 0.4 collective-permute-done.8.refs_3_
  20.9 3.8 %shard_map.72 = (bf16[1,256,512]{2,1,0:T(8,128)(2,1)S(1)}, bf16[1,256,512]{2,1,0:T(8,128)(2,1)S(1)}, bf16[8,256,512]{2,1,0:T(8,128)(2,1)S(1)}, bf16[1,256,512]{2...) custom-call(s32[1]{0:T(128)} %bitcast.core_ref, ...), custom_call_target="tpu_custom_call" | custom-call | tf_op jit(solution)/shard_map/pallas_call | solution.py:543
  24.7 0.4 collective-permute-start.14
  25.3 0.4 collective-permute-start.13
  25.7 1.3 %collective-permute-start.9 = (bf16[2,256,512]{2,1,0:T(8,128)(2,1)S(1)}, bf16[2,256,512]{2,1,0:T(8,128)(2,1)S(1)}, u32[]{:S(2)}, u32[]{:S(2)}) collective-permute-start(bf16[2,256,512]{2,1,0:T(8,128)(2,1)S(1)} %shard_map.71), channel_id=1, source_target_pairs={{0,2},{1,15},{2,0},{3,5},{4,6},{5,3},{6,4},{7,9},{8,10},{9,7},{10,... | collective-permute-start | bytes 1572872 | tf_op jit(solution)/shard_map/ppermute | solution.py:35
  27.1 0.6 %shard_map.73 = (f32[2,512]{1,0:T(2,128)S(1)}, f32[4,512]{1,0:T(4,128)S(1)}) custom-call(s32[1]{0:T(128)} %bitcast.core_ref, bf16[2,256,512]{2,1,0:T(8,128)(2,1)S(1)} %get-tuple-element.82.own_ref, bf16[1,256,512]{2,1,0:T(8,128)(2,1)S(1)} %collective-permute-done.12.near_ref, bf16[1,256,512]{2,1,0:T(8,128)(2,1)S(1)} %collective-permute-done.13.far_ref, ...), custom_call_target="tpu_custom_call" | custom-call | tf_op jit(solution)/shard_map/pallas_call | solution.py:543
  27.8 2.4 %collective-permute-start.17 = (bf16[1,256,512]{2,1,0:T(8,128)(2,1)S(1)}, bf16[1,256,512]{2,1,0:T(8,128)(2,1)S(1)}, u32[]{:S(2)}, u32[]{:S(2)}) collective-permute-start(bf16[1,256,512]{2,1,0:T(8,128)(2,1)S(1)} %get-tuple-element.102.own_low_ref), channel_id=1, source_target_pairs={{1,0},{0,1},{3,2},{2,3},{5,4},{4,5},{7,6},{6,7},{9,8},{8,9},{11,10... | collective-permute-start | bytes 786440 | tf_op jit(solution)/shard_map/ppermute | solution.py:26
  30.2 3.3 %shard_map.74.held_ref = bf16[6,256,512]{2,1,0:T(8,128)(2,1)S(1)} custom-call(bf16[8,256,512]{2,1,0:T(8,128)(2,1)S(1)} %get-tuple-element.96.held_ref, bf16[1,288,512]{2,1,0:T(8,128)(2,1)S(1)} %collective-permute-done.11.message_ref.mine_ref, bf16[1,288,512]{2,1,0:T(8,128)(2,1)S(1)} %collective-permute-done.14.other_ref, ...), custom_call_target="tpu_custom_call" | custom-call | tf_op jit(solution)/shard_map/pallas_call | solution.py:543
  33.5 0.5 %collective-permute-done.15.two_ref = f32[4,512]{1,0:T(4,128)S(1)} collective-permute-done((f32[4,512]{1,0:T(4,128)S(1)}, f32[4,512]{1,0:T(4,128)S(1)}, u32[]{:S(2)}, u32[]{:S(2)}) %collective-permute-start.15) | collective-permute-done | bytes 8224 | tf_op jit(solution)/shard_map/ppermute | solution.py:646
  34.0 1.3 %collective-permute-start.16 = (f32[4,512]{1,0:T(4,128)S(1)}, f32[4,512]{1,0:T(4,128)S(1)}, u32[]{:S(2)}, u32[]{:S(2)}) collective-permute-start(f32[4,512]{1,0:T(4,128)S(1)} %shard_map.75.one_ref), channel_id=1, source_target_pairs={{0,8},{1,9},{2,10},{3,11},{4,12},{5,13},{6,14},{7,15},{8,0},{9,1},... | collective-permute-start | bytes 24584 | tf_op jit(solution)/shard_map/ppermute | solution.py:646
  35.3 1.8 %shard_map.76.shared_ref = f32[4,512]{1,0:T(4,128)S(1)} custom-call(bf16[6,256,512]{2,1,0:T(8,128)(2,1)S(1)} %shard_map.74.held_ref, f32[4,512]{1,0:T(4,128)S(1)} %get-tuple-element.115.partner_ref.second_ref, f32[4,256,128]{2,1,0:T(8,128)S(1)} %get-tuple-element.64.refs_1_.v_ref.refs_2_.refs_4_, bf16[4,256,512]{2,1,0:T(8,128)(2,1)S(1)} %get-tuple-element.74.weight_ref, ...), custom_call_target="tpu_custom_call" | custom-call | tf_op jit(solution)/shard_map/pallas_call | solution.py:543
  37.1 1.5 %collective-permute-done.16.two_ref = f32[4,512]{1,0:T(4,128)S(1)} collective-permute-done((f32[4,512]{1,0:T(4,128)S(1)}, f32[4,512]{1,0:T(4,128)S(1)}, u32[]{:S(2)}, u32[]{:S(2)}) %collective-permute-start.16) | collective-permute-done | bytes 8224 | tf_op jit(solution)/shard_map/ppermute | solution.py:646
  38.6 3.5 %collective-permute-start.19 = (f32[4,512]{1,0:T(4,128)S(1)}, f32[4,512]{1,0:T(4,128)S(1)}, u32[]{:S(2)}, u32[]{:S(2)}) collective-permute-start(f32[4,512]{1,0:T(4,128)S(1)} %shard_map.77.one_ref), channel_id=1, source_target_pairs={{0,2},{1,3},{2,0},{3,1},{4,6},{5,7},{6,4},{7,5},{8,10},{9,11},{10,... | collective-permute-start | bytes 24584 | tf_op jit(solution)/shard_map/ppermute | solution.py:646
  42.0 1.8 %shard_map.78 = (f32[4,512]{1,0:T(4,128)S(1)}, f32[4,512]{1,0:T(4,128)S(1)}) custom-call(s32[1]{0:T(128)} %bitcast.core_ref, bf16[2,256,512]{2,1,0:T(8,128)(2,1)S(1)} %collective-permute-done.9.message_ref, bf16[4,256,512]{2,1,0:T(8,128)(2,1)S(1)} %get-tuple-element.74.weight_ref, bf16[2,256,512]{2,1,0:T(8,128)(2,1)S(1)} %get-tuple-element.109.own_weight_ref, ...), custom_call_target="tpu_custom_call" | custom-call | tf_op jit(solution)/shard_map/pallas_call | solution.py:543
  43.9 1.2 %collective-permute-done.20.arrived_ref = f32[8,512]{1,0:T(8,128)S(1)} collective-permute-done((f32[8,512]{1,0:T(8,128)S(1)}, f32[8,512]{1,0:T(8,128)S(1)}, u32[]{:S(2)}, u32[]{:S(2)}) %collective-permute-start.20) | collective-permute-done | bytes 16416 | tf_op jit(solution)/shard_map/ppermute | solution.py:26
  45.1 0.6 %shard_map.80 = f32[4,512]{1,0:T(4,128)} custom-call(f32[4,512]{1,0:T(4,128)S(1)} %get-tuple-element.111.kept_ref, f32[8,512]{1,0:T(8,128)S(1)} %shard_map.79.mine_ref, f32[8,512]{1,0:T(8,128)S(1)} %collective-permute-done.20.arrived_ref), custom_call_target="tpu_custom_call" | custom-call | tf_op jit(solution)/shard_map/pallas_call | solution.py:543
  (40 shorter events, 1.5 us)
Async XLA Ops:
  0.0 2.0 %copy-start.4 = (f32[4,512]{1,0:T(4,128)S(1)}, f32[4,512]{1,0:T(4,128)}, u32[]{:S(2)}) copy-start(f32[4,512]{1,0:T(4,128)} %param.6) | copy-start | bytes 24580
  0.0 2.1 %copy-start.2 = (f32[3,256]{1,0:T(4,128)S(1)}, f32[3,256]{1,0:T(4,128)}, u32[]{:S(2)}) copy-start(f32[3,256]{1,0:T(4,128)} %directions_ref.1) | copy-start | bytes 9220
  0.0 2.6 %copy-start.3 = (f32[256]{0:T(256)S(1)}, f32[256]{0:T(256)}, u32[]{:S(2)}) copy-start(f32[256]{0:T(256)} %param.11) | copy-start | bytes 3076
  0.0 2.6 %copy-start = (bf16[256,256]{1,0:T(8,128)(2,1)S(1)}, bf16[256,256]{1,0:T(8,128)(2,1)}, u32[]{:S(2)}) copy-start(bf16[256,256]{1,0:T(8,128)(2,1)} %synthesis_ref.1) | copy-start | bytes 393220
  0.0 2.6 %copy-start.1 = (bf16[256,256]{1,0:T(8,128)(2,1)S(1)}, bf16[256,256]{1,0:T(8,128)(2,1)}, u32[]{:S(2)}) copy-start(bf16[256,256]{1,0:T(8,128)(2,1)} %analysis_ref.1) | copy-start | bytes 393220
  0.0 2.0 %collective-permute-start = (f32[4,512]{1,0:T(4,128)}, f32[4,512]{1,0:T(4,128)S(1)}, u32[]{:S(2)}, u32[]{:S(2)}) collective-permute-start(f32[4,512]{1,0:T(4,128)} %param.6), channel_id=1, source_target_pairs={{1,0},{0,1},{3,2},{2,3},{5,4},{4,5},{7,6},{6,7},{9,8},{8,9},{11,10... | collective-permute-start | bytes 24584 | tf_op jit(solution)/shard_map/ppermute | solution.py:26
  2.5 1.6 %collective-permute-start.1 = (bf16[1,256,512]{2,1,0:T(8,128)(2,1)S(1)}, bf16[1,256,512]{2,1,0:T(8,128)(2,1)S(1)}, u32[]{:S(2)}, u32[]{:S(2)}) collective-permute-start(bf16[1,256,512]{2,1,0:T(8,128)(2,1)S(1)} %get-tuple-element.60.mine_ref.edge_ref), channel_id=1, source_target_pairs={{1,0},{0,1},{3,2},{2,3},{5,4},{4,5},{7,6},{6,7},{9,8},{8,9},{11,10... | collective-permute-start | bytes 786440 | tf_op jit(solution)/shard_map/ppermute | solution.py:26
  4.1 8.8 %collective-permute-start.3 = (bf16[4,256,512]{2,1,0:T(8,128)(2,1)S(1)}, bf16[4,256,512]{2,1,0:T(8,128)(2,1)S(1)}, u32[]{:S(2)}, u32[]{:S(2)}) collective-permute-start(bf16[4,256,512]{2,1,0:T(8,128)(2,1)S(1)} %bitcast.7), channel_id=1, source_target_pairs={{1,0},{0,1},{3,2},{2,3},{5,4},{4,5},{7,6},{6,7},{9,8},{8,9},{11,10... | collective-permute-start | bytes 3145736 | tf_op jit(solution)/shard_map/ppermute | solution.py:26
  4.3 13.5 %collective-permute-start.6 = (bf16[1,272,512]{2,1,0:T(8,128)(2,1)S(1)}, bf16[1,272,512]{2,1,0:T(8,128)(2,1)S(1)}, u32[]{:S(2)}, u32[]{:S(2)}) collective-permute-start(bf16[1,272,512]{2,1,0:T(8,128)(2,1)S(1)} %shard_map.66), channel_id=1, source_target_pairs={{0,2},{1,15},{2,0},{3,5},{4,6},{5,3},{6,4},{7,9},{8,10},{9,7},{10,... | collective-permute-start | bytes 835592 | tf_op jit(solution)/shard_map/ppermute | solution.py:35
  9.5 4.1 %collective-permute-start.4 = (bf16[1,256,512]{2,1,0:T(8,128)(2,1)S(1)}, bf16[1,256,512]{2,1,0:T(8,128)(2,1)S(1)}, u32[]{:S(2)}, u32[]{:S(2)}) collective-permute-start(bf16[1,256,512]{2,1,0:T(8,128)(2,1)S(1)} %get-tuple-element.71), channel_id=1, source_target_pairs={{1,0},{0,1},{3,2},{2,3},{5,4},{4,5},{7,6},{6,7},{9,8},{8,9},{11,10... | collective-permute-start | bytes 786440 | tf_op jit(solution)/shard_map/ppermute | solution.py:26
  12.4 1.5 %collective-permute-start.5 = (bf16[1,256,512]{2,1,0:T(8,128)(2,1)S(1)}, bf16[1,256,512]{2,1,0:T(8,128)(2,1)S(1)}, u32[]{:S(2)}, u32[]{:S(2)}) collective-permute-start(bf16[1,256,512]{2,1,0:T(8,128)(2,1)S(1)} %get-tuple-element.72), channel_id=1, source_target_pairs={{1,0},{0,1},{3,2},{2,3},{5,4},{4,5},{7,6},{6,7},{9,8},{8,9},{11,10... | collective-permute-start | bytes 786440 | tf_op jit(solution)/shard_map/ppermute | solution.py:26
  12.5 1.8 %collective-permute-start.2 = (bf16[1,256,512]{2,1,0:T(8,128)(2,1)S(1)}, bf16[1,256,512]{2,1,0:T(8,128)(2,1)S(1)}, u32[]{:S(2)}, u32[]{:S(2)}) collective-permute-start(bf16[1,256,512]{2,1,0:T(8,128)(2,1)S(1)} %get-tuple-element.68.mine_ref), channel_id=1, source_target_pairs={{1,0},{0,1},{3,2},{2,3},{5,4},{4,5},{7,6},{6,7},{9,8},{8,9},{11,10... | collective-permute-start | bytes 786440 | tf_op jit(solution)/shard_map/ppermute | solution.py:26
  14.4 10.3 %collective-permute-start.11 = (bf16[1,288,512]{2,1,0:T(8,128)(2,1)S(1)}, bf16[1,288,512]{2,1,0:T(8,128)(2,1)S(1)}, u32[]{:S(2)}, u32[]{:S(2)}) collective-permute-start(bf16[1,288,512]{2,1,0:T(8,128)(2,1)S(1)} %shard_map.69), channel_id=1, source_target_pairs={{0,2},{1,15},{2,0},{3,5},{4,6},{5,3},{6,4},{7,9},{8,10},{9,7},{10,... | collective-permute-start | bytes 884744 | tf_op jit(solution)/shard_map/ppermute | solution.py:35
  17.9 3.0 %collective-permute-start.10 = (bf16[1,272,512]{2,1,0:T(8,128)(2,1)S(1)}, bf16[1,272,512]{2,1,0:T(8,128)(2,1)S(1)}, u32[]{:S(2)}, u32[]{:S(2)}) collective-permute-start(bf16[1,272,512]{2,1,0:T(8,128)(2,1)S(1)} %collective-permute-done.6.mine_ref), channel_id=1, source_target_pairs={{1,0},{0,1},{3,2},{2,3},{5,4},{4,5},{7,6},{6,7},{9,8},{8,9},{11,10... | collective-permute-start | bytes 835592 | tf_op jit(solution)/shard_map/ppermute | solution.py:26
  18.8 1.6 %collective-permute-start.7 = (bf16[1,256,512]{2,1,0:T(8,128)(2,1)S(1)}, bf16[1,256,512]{2,1,0:T(8,128)(2,1)S(1)}, u32[]{:S(2)}, u32[]{:S(2)}) collective-permute-start(bf16[1,256,512]{2,1,0:T(8,128)(2,1)S(1)} %get-tuple-element.78.refs_0_), channel_id=1, source_target_pairs={{1,0},{0,1},{3,2},{2,3},{5,4},{4,5},{7,6},{6,7},{9,8},{8,9},{11,10... | collective-permute-start | bytes 786440 | tf_op jit(solution)/shard_map/ppermute | solution.py:26
  18.9 1.9 %collective-permute-start.8 = (bf16[1,256,512]{2,1,0:T(8,128)(2,1)S(1)}, bf16[1,256,512]{2,1,0:T(8,128)(2,1)S(1)}, u32[]{:S(2)}, u32[]{:S(2)}) collective-permute-start(bf16[1,256,512]{2,1,0:T(8,128)(2,1)S(1)} %get-tuple-element.79.refs_1_), channel_id=1, source_target_pairs={{1,0},{0,1},{3,2},{2,3},{5,4},{4,5},{7,6},{6,7},{9,8},{8,9},{11,10... | collective-permute-start | bytes 786440 | tf_op jit(solution)/shard_map/ppermute | solution.py:26
  24.7 2.4 %collective-permute-start.14 = (bf16[1,288,512]{2,1,0:T(8,128)(2,1)S(1)}, bf16[1,288,512]{2,1,0:T(8,128)(2,1)S(1)}, u32[]{:S(2)}, u32[]{:S(2)}) collective-permute-start(bf16[1,288,512]{2,1,0:T(8,128)(2,1)S(1)} %collective-permute-done.11.message_ref.mine_ref), channel_id=1, source_target_pairs={{1,0},{0,1},{3,2},{2,3},{5,4},{4,5},{7,6},{6,7},{9,8},{8,9},{11,10... | collective-permute-start | bytes 884744 | tf_op jit(solution)/shard_map/ppermute | solution.py:26
  25.2 1.8 %collective-permute-start.12 = (bf16[1,256,512]{2,1,0:T(8,128)(2,1)S(1)}, bf16[1,256,512]{2,1,0:T(8,128)(2,1)S(1)}, u32[]{:S(2)}, u32[]{:S(2)}) collective-permute-start(bf16[1,256,512]{2,1,0:T(8,128)(2,1)S(1)} %get-tuple-element.87), channel_id=1, source_target_pairs={{1,0},{0,1},{3,2},{2,3},{5,4},{4,5},{7,6},{6,7},{9,8},{8,9},{11,10... | collective-permute-start | bytes 786440 | tf_op jit(solution)/shard_map/ppermute | solution.py:26
  25.3 1.8 %collective-permute-start.13 = (bf16[1,256,512]{2,1,0:T(8,128)(2,1)S(1)}, bf16[1,256,512]{2,1,0:T(8,128)(2,1)S(1)}, u32[]{:S(2)}, u32[]{:S(2)}) collective-permute-start(bf16[1,256,512]{2,1,0:T(8,128)(2,1)S(1)} %get-tuple-element.88), channel_id=1, source_target_pairs={{1,0},{0,1},{3,2},{2,3},{5,4},{4,5},{7,6},{6,7},{9,8},{8,9},{11,10... | collective-permute-start | bytes 786440 | tf_op jit(solution)/shard_map/ppermute | solution.py:26
  25.7 16.3 %collective-permute-start.9 = (bf16[2,256,512]{2,1,0:T(8,128)(2,1)S(1)}, bf16[2,256,512]{2,1,0:T(8,128)(2,1)S(1)}, u32[]{:S(2)}, u32[]{:S(2)}) collective-permute-start(bf16[2,256,512]{2,1,0:T(8,128)(2,1)S(1)} %shard_map.71), channel_id=1, source_target_pairs={{0,2},{1,15},{2,0},{3,5},{4,6},{5,3},{6,4},{7,9},{8,10},{9,7},{10,... | collective-permute-start | bytes 1572872 | tf_op jit(solution)/shard_map/ppermute | solution.py:35
  27.8 7.5 %collective-permute-start.17 = (bf16[1,256,512]{2,1,0:T(8,128)(2,1)S(1)}, bf16[1,256,512]{2,1,0:T(8,128)(2,1)S(1)}, u32[]{:S(2)}, u32[]{:S(2)}) collective-permute-start(bf16[1,256,512]{2,1,0:T(8,128)(2,1)S(1)} %get-tuple-element.102.own_low_ref), channel_id=1, source_target_pairs={{1,0},{0,1},{3,2},{2,3},{5,4},{4,5},{7,6},{6,7},{9,8},{8,9},{11,10... | collective-permute-start | bytes 786440 | tf_op jit(solution)/shard_map/ppermute | solution.py:26
  30.1 5.2 %collective-permute-start.18 = (bf16[1,256,512]{2,1,0:T(8,128)(2,1)S(1)}, bf16[1,256,512]{2,1,0:T(8,128)(2,1)S(1)}, u32[]{:S(2)}, u32[]{:S(2)}) collective-permute-start(bf16[1,256,512]{2,1,0:T(8,128)(2,1)S(1)} %get-tuple-element.105.own_high_ref), channel_id=1, source_target_pairs={{1,0},{0,1},{3,2},{2,3},{5,4},{4,5},{7,6},{6,7},{9,8},{8,9},{11,10... | collective-permute-start | bytes 786440 | tf_op jit(solution)/shard_map/ppermute | solution.py:26
  30.2 3.8 %collective-permute-start.15 = (f32[4,512]{1,0:T(4,128)S(1)}, f32[4,512]{1,0:T(4,128)S(1)}, u32[]{:S(2)}, u32[]{:S(2)}) collective-permute-start(f32[4,512]{1,0:T(4,128)S(1)} %get-tuple-element.91.one_ref), channel_id=1, source_target_pairs={{0,4},{1,5},{2,6},{3,7},{4,0},{5,1},{6,2},{7,3},{8,12},{9,13},{10,... | collective-permute-start | bytes 24584 | tf_op jit(solution)/shard_map/ppermute | solution.py:646
  34.0 4.5 %collective-permute-start.16 = (f32[4,512]{1,0:T(4,128)S(1)}, f32[4,512]{1,0:T(4,128)S(1)}, u32[]{:S(2)}, u32[]{:S(2)}) collective-permute-start(f32[4,512]{1,0:T(4,128)S(1)} %shard_map.75.one_ref), channel_id=1, source_target_pairs={{0,8},{1,9},{2,10},{3,11},{4,12},{5,13},{6,14},{7,15},{8,0},{9,1},... | collective-permute-start | bytes 24584 | tf_op jit(solution)/shard_map/ppermute | solution.py:646
  38.6 5.2 %collective-permute-start.19 = (f32[4,512]{1,0:T(4,128)S(1)}, f32[4,512]{1,0:T(4,128)S(1)}, u32[]{:S(2)}, u32[]{:S(2)}) collective-permute-start(f32[4,512]{1,0:T(4,128)S(1)} %shard_map.77.one_ref), channel_id=1, source_target_pairs={{0,2},{1,3},{2,0},{3,1},{4,6},{5,7},{6,4},{7,5},{8,10},{9,11},{10,... | collective-permute-start | bytes 24584 | tf_op jit(solution)/shard_map/ppermute | solution.py:646
  43.8 1.2 %collective-permute-start.20 = (f32[8,512]{1,0:T(8,128)S(1)}, f32[8,512]{1,0:T(8,128)S(1)}, u32[]{:S(2)}, u32[]{:S(2)}) collective-permute-start(f32[8,512]{1,0:T(8,128)S(1)} %shard_map.79.mine_ref), channel_id=1, source_target_pairs={{1,0},{0,1},{3,2},{2,3},{5,4},{4,5},{7,6},{6,7},{9,8},{8,9},{11,10... | collective-permute-start | bytes 49160 | tf_op jit(solution)/shard_map/ppermute | solution.py:26

commit v8 on v7

--- a/solution.py
+++ b/solution.py
@@ -11,7 +11,7 @@
 STEPS = 4
 LANES = 128
 ROWS = 16
-UNROLL = 4
+UNROLL = 16
 PAD = 2
 
 courant = 0.3
@@ -546,7 +546,7 @@
         in_specs=[smem if arg.dtype == jnp.int32 else vmem for arg in args],
         out_specs=jax.tree.map(lambda _: vmem, outs),
         scratch_shapes=[pltpu.VMEM(*s) if len(s) == 2 else pltpu.VMEM(s, BF16) for s in scratch],
-        compiler_params=pltpu.CompilerParams(vmem_limit_bytes=7 << 20),
+        compiler_params=pltpu.CompilerParams(vmem_limit_bytes=12 << 20),
         cost_estimate=pl.CostEstimate(flops=0, bytes_accessed=0, transcendentals=0),
     )(*args)
 

time: 45.8 us -> 44.8 us (0.978)
  Pallas kernels: 19.1 us -> 16.8 us
  starting transfers between devices: 18.3 us -> 19.1 us
  waiting for transfers between devices: 6.64 us -> 7.11 us
    pallas_call x17, Pallas kernels: 19.1 us -> 16.8 us  [kernel_call(): pl.pallas_call(kernel, out_shape=outs, in_specs=[smem if arg.dtype == jnp...]
    ppermute x3, starting transfers between devices: 4.76 us -> 6.24 us  [received(): lax.ppermute(value, 'space', [(i, i ^ distance) for i in range(count)])]
    ppermute x15, starting transfers between devices: 9.26 us -> 8.12 us  [swap_species(): return lax.ppermute(block, 'space', [(i ^ 1, i) for i in range(count)])]
    ppermute x3, waiting for transfers between devices: 0.01 us -> 0.8 us  [exchange_faces(): return lax.ppermute(block, 'space', route)]
    ppermute x3, starting transfers between devices: 4.24 us -> 4.71 us  [exchange_faces(): return lax.ppermute(block, 'space', route)]
  transfers between devices with their start and end apart: 21 -> 21, of which waited for: 10 -> 11; matrix products, arithmetic and copies ran while one was open for 3% -> 3% of each run, Pallas kernels for 39% -> 36%
where the time goes in v8:
time: 44.8 us; the launch traced here: 44.7 us
  starting transfers between devices  19.1 us (43%)
  Pallas kernels  16.8 us (38%)
  waiting for transfers between devices  7.11 us (16%)
  local copies, waits for them, and re-layouts  1.44 us (3%)
    pallas_call x17, Pallas kernels, kernel_call(): pl.pallas_call(kernel, out_shape=outs, in_specs=[smem if arg.dtype == jnp...  16.8 us
    ppermute x15, starting transfers between devices, swap_species(): return lax.ppermute(block, 'space', [(i ^ 1, i) for i in range(count)])  8.12 us
    ppermute x3, starting transfers between devices, received(): lax.ppermute(value, 'space', [(i, i ^ distance) for i in range(count)])  6.24 us
    ppermute x3, starting transfers between devices, exchange_faces(): return lax.ppermute(block, 'space', route)  4.71 us
    ppermute x15, waiting for transfers between devices, swap_species(): return lax.ppermute(block, 'space', [(i ^ 1, i) for i in range(count)])  4.58 us
    ppermute x3, waiting for transfers between devices, received(): lax.ppermute(value, 'space', [(i, i ^ distance) for i in range(count)])  1.73 us
    unnamed x11, local copies, waits for them, and re-layouts  1.44 us
  transfers between devices with their start and end apart: 21, of which 11 were waited for; matrix products, arithmetic and copies ran while one was open for 3% of the time, Pallas kernels for 36%

profile of v8, /device:TPU:0, one launch (start us, length us, event | category | flops | bytes accessed | tf_op | source)
XLA Modules:
  0.0 44.7 jit_solution(29602349804635465)
XLA Ops:
  0.0 0.5 %collective-permute-start = (f32[4,512]{1,0:T(4,128)}, f32[4,512]{1,0:T(4,128)S(1)}, u32[]{:S(2)}, u32[]{:S(2)}) collective-permute-start(f32[4,512]{1,0:T(4,128)} %param.6), channel_id=1, source_target_pairs={{1,0},{0,1},{3,2},{2,3},{5,4},{4,5},{7,6},{6,7},{9,8},{8,9},{11,10... | collective-permute-start | bytes 24584 | tf_op jit(solution)/shard_map/ppermute | solution.py:26
  0.6 1.4 %copy.9 = bf16[256,4,512]{2,0,1:T(8,128)(2,1)S(1)} copy(bf16[256,4,512]{2,1,0:T(4,128)(2,1)} %param.7) | data formatting | bytes 2097152 | tf_op args[1]
  2.5 0.3 shard_map.65
  2.8 1.1 %collective-permute-done.1.other_ref = bf16[1,256,512]{2,1,0:T(8,128)(2,1)S(1)} collective-permute-done((bf16[1,256,512]{2,1,0:T(8,128)(2,1)S(1)}, bf16[1,256,512]{2,1,0:T(8,128)(2,1)S(1)}, u32[]{:S(2)}, u32[]{:S(2)}) %collective-permute-start.1) | collective-permute-done | bytes 262176 | tf_op jit(solution)/shard_map/ppermute | solution.py:26
  4.2 2.9 %collective-permute-start.6 = (bf16[1,272,512]{2,1,0:T(8,128)(2,1)S(1)}, bf16[1,272,512]{2,1,0:T(8,128)(2,1)S(1)}, u32[]{:S(2)}, u32[]{:S(2)}) collective-permute-start(bf16[1,272,512]{2,1,0:T(8,128)(2,1)S(1)} %shard_map.66), channel_id=1, source_target_pairs={{0,2},{1,15},{2,0},{3,5},{4,6},{5,3},{6,4},{7,9},{8,10},{9,7},{10,... | collective-permute-start | bytes 835592 | tf_op jit(solution)/shard_map/ppermute | solution.py:35
  7.1 2.0 %shard_map.67 = (bf16[4,256,512]{2,1,0:T(8,128)(2,1)S(1)}, bf16[1,256,512]{2,1,0:T(8,128)(2,1)S(1)}, bf16[1,256,512]{2,1,0:T(8,128)(2,1)S(1)}, bf16[1,256,512]{2,1,0:T(8,128)(2,1)S(1)}) custom-call(bf16[4,256,512]{2,1,0:T(8,128)(2,1)S(1)} %bitcast.8, f32[4,512]{1,0:T(4,128)S(1)} %get-tuple-element.116.fields_ref.first_ref.own_ref, ...), custom_call_target="tpu_custom_call" | custom-call | tf_op jit(solution)/shard_map/pallas_call | solution.py:543
  9.0 3.0 %collective-permute-start.4 = (bf16[1,256,512]{2,1,0:T(8,128)(2,1)S(1)}, bf16[1,256,512]{2,1,0:T(8,128)(2,1)S(1)}, u32[]{:S(2)}, u32[]{:S(2)}) collective-permute-start(bf16[1,256,512]{2,1,0:T(8,128)(2,1)S(1)} %get-tuple-element.71), channel_id=1, source_target_pairs={{1,0},{0,1},{3,2},{2,3},{5,4},{4,5},{7,6},{6,7},{9,8},{8,9},{11,10... | collective-permute-start | bytes 786440 | tf_op jit(solution)/shard_map/ppermute | solution.py:26
  12.1 0.4 collective-permute-start.2
  12.5 0.6 %shard_map.68 = (bf16[4,256,512]{2,1,0:T(8,128)(2,1)S(1)}, bf16[2,256,512]{2,1,0:T(8,128)(2,1)S(1)}) custom-call(s32[1]{0:T(128)} %bitcast.core_ref, bf16[4,256,512]{2,1,0:T(8,128)(2,1)S(1)} %collective-permute-done.3.partner_ref, bf16[4,256,512]{2,1,0:T(8,128)(2,1)S(1)} %bitcast.9, bf16[256,256]{1,0:T(8,128)(2,1)S(1)} %get-tuple-element.69.turned_ref), custom_call_target="tpu_custom_call" | custom-call | tf_op jit(solution)/shard_map/pallas_call | solution.py:543
  13.2 0.4 collective-permute-done.5.refs_2_
  13.5 0.4 collective-permute-done.2.other_ref
  14.1 2.8 %shard_map.70 = (bf16[1,256,512]{2,1,0:T(8,128)(2,1)S(1)}, bf16[1,256,512]{2,1,0:T(8,128)(2,1)S(1)}) custom-call(bf16[4,256,512]{2,1,0:T(8,128)(2,1)S(1)} %get-tuple-element.80.state_ref.alone_ref, f32[4,512]{1,0:T(4,128)S(1)} %get-tuple-element.116.fields_ref.first_ref.own_ref, f32[4,512]{1,0:T(4,128)S(1)} %get-tuple-element.115.partner_ref.second_ref, ...), custom_call_target="tpu_custom_call" | custom-call | tf_op jit(solution)/shard_map/pallas_call | solution.py:543
  16.9 0.9 %collective-permute-start.10 = (bf16[1,272,512]{2,1,0:T(8,128)(2,1)S(1)}, bf16[1,272,512]{2,1,0:T(8,128)(2,1)S(1)}, u32[]{:S(2)}, u32[]{:S(2)}) collective-permute-start(bf16[1,272,512]{2,1,0:T(8,128)(2,1)S(1)} %collective-permute-done.6.mine_ref), channel_id=1, source_target_pairs={{1,0},{0,1},{3,2},{2,3},{5,4},{4,5},{7,6},{6,7},{9,8},{8,9},{11,10... | collective-permute-start | bytes 835592 | tf_op jit(solution)/shard_map/ppermute | solution.py:26
  17.9 0.4 collective-permute-start.8
  18.3 1.0 %collective-permute-done.7.refs_2_ = bf16[1,256,512]{2,1,0:T(8,128)(2,1)S(1)} collective-permute-done((bf16[1,256,512]{2,1,0:T(8,128)(2,1)S(1)}, bf16[1,256,512]{2,1,0:T(8,128)(2,1)S(1)}, u32[]{:S(2)}, u32[]{:S(2)}) %collective-permute-start.7) | collective-permute-done | bytes 262176 | tf_op jit(solution)/shard_map/ppermute | solution.py:26
  19.3 0.4 collective-permute-done.8.refs_3_
  19.8 3.3 %shard_map.72 = (bf16[1,256,512]{2,1,0:T(8,128)(2,1)S(1)}, bf16[1,256,512]{2,1,0:T(8,128)(2,1)S(1)}, bf16[8,256,512]{2,1,0:T(8,128)(2,1)S(1)}, bf16[1,256,512]{2...) custom-call(s32[1]{0:T(128)} %bitcast.core_ref, ...), custom_call_target="tpu_custom_call" | custom-call | tf_op jit(solution)/shard_map/pallas_call | solution.py:543
  23.1 0.8 %collective-permute-done.11.message_ref.mine_ref = bf16[1,288,512]{2,1,0:T(8,128)(2,1)S(1)} collective-permute-done((bf16[1,288,512]{2,1,0:T(8,128)(2,1)S(1)}, bf16[1,288,512]{2,1,0:T(8,128)(2,1)S(1)}, u32[]{:S(2)}, u32[]{:S(2)}) %collective-permute-start.11) | collective-permute-done | bytes 294944 | tf_op jit(solution)/shard_map/ppermute | solution.py:35
  23.9 0.5 %collective-permute-start.12 = (bf16[1,256,512]{2,1,0:T(8,128)(2,1)S(1)}, bf16[1,256,512]{2,1,0:T(8,128)(2,1)S(1)}, u32[]{:S(2)}, u32[]{:S(2)}) collective-permute-start(bf16[1,256,512]{2,1,0:T(8,128)(2,1)S(1)} %get-tuple-element.87), channel_id=1, source_target_pairs={{1,0},{0,1},{3,2},{2,3},{5,4},{4,5},{7,6},{6,7},{9,8},{8,9},{11,10... | collective-permute-start | bytes 786440 | tf_op jit(solution)/shard_map/ppermute | solution.py:26
  24.4 1.8 %collective-permute-start.9 = (bf16[2,256,512]{2,1,0:T(8,128)(2,1)S(1)}, bf16[2,256,512]{2,1,0:T(8,128)(2,1)S(1)}, u32[]{:S(2)}, u32[]{:S(2)}) collective-permute-start(bf16[2,256,512]{2,1,0:T(8,128)(2,1)S(1)} %shard_map.71), channel_id=1, source_target_pairs={{0,2},{1,15},{2,0},{3,5},{4,6},{5,3},{6,4},{7,9},{8,10},{9,7},{10,... | collective-permute-start | bytes 1572872 | tf_op jit(solution)/shard_map/ppermute | solution.py:35
  26.3 0.6 %shard_map.73 = (f32[2,512]{1,0:T(2,128)S(1)}, f32[4,512]{1,0:T(4,128)S(1)}) custom-call(s32[1]{0:T(128)} %bitcast.core_ref, bf16[2,256,512]{2,1,0:T(8,128)(2,1)S(1)} %get-tuple-element.82.own_ref, bf16[1,256,512]{2,1,0:T(8,128)(2,1)S(1)} %collective-permute-done.12.near_ref, bf16[1,256,512]{2,1,0:T(8,128)(2,1)S(1)} %collective-permute-done.13.far_ref, ...), custom_call_target="tpu_custom_call" | custom-call | tf_op jit(solution)/shard_map/pallas_call | solution.py:543
  26.8 1.7 %collective-permute-start.17 = (bf16[1,256,512]{2,1,0:T(8,128)(2,1)S(1)}, bf16[1,256,512]{2,1,0:T(8,128)(2,1)S(1)}, u32[]{:S(2)}, u32[]{:S(2)}) collective-permute-start(bf16[1,256,512]{2,1,0:T(8,128)(2,1)S(1)} %get-tuple-element.102.own_low_ref), channel_id=1, source_target_pairs={{1,0},{0,1},{3,2},{2,3},{5,4},{4,5},{7,6},{6,7},{9,8},{8,9},{11,10... | collective-permute-start | bytes 786440 | tf_op jit(solution)/shard_map/ppermute | solution.py:26
  28.6 0.3 collective-permute-start.15
  28.9 3.0 %shard_map.74.held_ref = bf16[6,256,512]{2,1,0:T(8,128)(2,1)S(1)} custom-call(bf16[8,256,512]{2,1,0:T(8,128)(2,1)S(1)} %get-tuple-element.96.held_ref, bf16[1,288,512]{2,1,0:T(8,128)(2,1)S(1)} %collective-permute-done.11.message_ref.mine_ref, bf16[1,288,512]{2,1,0:T(8,128)(2,1)S(1)} %collective-permute-done.14.other_ref, ...), custom_call_target="tpu_custom_call" | custom-call | tf_op jit(solution)/shard_map/pallas_call | solution.py:543
  31.9 0.5 %collective-permute-done.15.two_ref = f32[4,512]{1,0:T(4,128)S(1)} collective-permute-done((f32[4,512]{1,0:T(4,128)S(1)}, f32[4,512]{1,0:T(4,128)S(1)}, u32[]{:S(2)}, u32[]{:S(2)}) %collective-permute-start.15) | collective-permute-done | bytes 8224 | tf_op jit(solution)/shard_map/ppermute | solution.py:646
  32.4 1.7 %collective-permute-start.16 = (f32[4,512]{1,0:T(4,128)S(1)}, f32[4,512]{1,0:T(4,128)S(1)}, u32[]{:S(2)}, u32[]{:S(2)}) collective-permute-start(f32[4,512]{1,0:T(4,128)S(1)} %shard_map.75.one_ref), channel_id=1, source_target_pairs={{0,8},{1,9},{2,10},{3,11},{4,12},{5,13},{6,14},{7,15},{8,0},{9,1},... | collective-permute-start | bytes 24584 | tf_op jit(solution)/shard_map/ppermute | solution.py:646
  34.1 1.6 %shard_map.76.shared_ref = f32[4,512]{1,0:T(4,128)S(1)} custom-call(bf16[6,256,512]{2,1,0:T(8,128)(2,1)S(1)} %shard_map.74.held_ref, f32[4,512]{1,0:T(4,128)S(1)} %get-tuple-element.115.partner_ref.second_ref, f32[4,256,128]{2,1,0:T(8,128)S(1)} %get-tuple-element.64.refs_1_.v_ref.refs_2_.refs_4_, bf16[4,256,512]{2,1,0:T(8,128)(2,1)S(1)} %get-tuple-element.74.weight_ref, ...), custom_call_target="tpu_custom_call" | custom-call | tf_op jit(solution)/shard_map/pallas_call | solution.py:543
  35.7 1.2 %collective-permute-done.16.two_ref = f32[4,512]{1,0:T(4,128)S(1)} collective-permute-done((f32[4,512]{1,0:T(4,128)S(1)}, f32[4,512]{1,0:T(4,128)S(1)}, u32[]{:S(2)}, u32[]{:S(2)}) %collective-permute-start.16) | collective-permute-done | bytes 8224 | tf_op jit(solution)/shard_map/ppermute | solution.py:646
  36.9 4.2 %collective-permute-start.19 = (f32[4,512]{1,0:T(4,128)S(1)}, f32[4,512]{1,0:T(4,128)S(1)}, u32[]{:S(2)}, u32[]{:S(2)}) collective-permute-start(f32[4,512]{1,0:T(4,128)S(1)} %shard_map.77.one_ref), channel_id=1, source_target_pairs={{0,2},{1,3},{2,0},{3,1},{4,6},{5,7},{6,4},{7,5},{8,10},{9,11},{10,... | collective-permute-start | bytes 24584 | tf_op jit(solution)/shard_map/ppermute | solution.py:646
  41.2 1.6 %shard_map.78 = (f32[4,512]{1,0:T(4,128)S(1)}, f32[4,512]{1,0:T(4,128)S(1)}) custom-call(s32[1]{0:T(128)} %bitcast.core_ref, bf16[2,256,512]{2,1,0:T(8,128)(2,1)S(1)} %collective-permute-done.9.message_ref, bf16[4,256,512]{2,1,0:T(8,128)(2,1)S(1)} %get-tuple-element.74.weight_ref, bf16[2,256,512]{2,1,0:T(8,128)(2,1)S(1)} %get-tuple-element.109.own_weight_ref, ...), custom_call_target="tpu_custom_call" | custom-call | tf_op jit(solution)/shard_map/pallas_call | solution.py:543
  42.9 1.2 %collective-permute-done.20.arrived_ref = f32[8,512]{1,0:T(8,128)S(1)} collective-permute-done((f32[8,512]{1,0:T(8,128)S(1)}, f32[8,512]{1,0:T(8,128)S(1)}, u32[]{:S(2)}, u32[]{:S(2)}) %collective-permute-start.20) | collective-permute-done | bytes 16416 | tf_op jit(solution)/shard_map/ppermute | solution.py:26
  44.1 0.6 %shard_map.80 = f32[4,512]{1,0:T(4,128)} custom-call(f32[4,512]{1,0:T(4,128)S(1)} %get-tuple-element.111.kept_ref, f32[8,512]{1,0:T(8,128)S(1)} %shard_map.79.mine_ref, f32[8,512]{1,0:T(8,128)S(1)} %collective-permute-done.20.arrived_ref), custom_call_target="tpu_custom_call" | custom-call | tf_op jit(solution)/shard_map/pallas_call | solution.py:543
  (40 shorter events, 1.4 us)
Async XLA Ops:
  0.0 2.0 %copy-start.4 = (f32[4,512]{1,0:T(4,128)S(1)}, f32[4,512]{1,0:T(4,128)}, u32[]{:S(2)}) copy-start(f32[4,512]{1,0:T(4,128)} %param.6) | copy-start | bytes 24580
  0.0 2.1 %copy-start.2 = (f32[3,256]{1,0:T(4,128)S(1)}, f32[3,256]{1,0:T(4,128)}, u32[]{:S(2)}) copy-start(f32[3,256]{1,0:T(4,128)} %directions_ref.1) | copy-start | bytes 9220
  0.0 2.5 %copy-start.3 = (f32[256]{0:T(256)S(1)}, f32[256]{0:T(256)}, u32[]{:S(2)}) copy-start(f32[256]{0:T(256)} %param.11) | copy-start | bytes 3076
  0.0 2.5 %copy-start = (bf16[256,256]{1,0:T(8,128)(2,1)S(1)}, bf16[256,256]{1,0:T(8,128)(2,1)}, u32[]{:S(2)}) copy-start(bf16[256,256]{1,0:T(8,128)(2,1)} %synthesis_ref.1) | copy-start | bytes 393220
  0.0 2.5 %copy-start.1 = (bf16[256,256]{1,0:T(8,128)(2,1)S(1)}, bf16[256,256]{1,0:T(8,128)(2,1)}, u32[]{:S(2)}) copy-start(bf16[256,256]{1,0:T(8,128)(2,1)} %analysis_ref.1) | copy-start | bytes 393220
  0.0 2.0 %collective-permute-start = (f32[4,512]{1,0:T(4,128)}, f32[4,512]{1,0:T(4,128)S(1)}, u32[]{:S(2)}, u32[]{:S(2)}) collective-permute-start(f32[4,512]{1,0:T(4,128)} %param.6), channel_id=1, source_target_pairs={{1,0},{0,1},{3,2},{2,3},{5,4},{4,5},{7,6},{6,7},{9,8},{8,9},{11,10... | collective-permute-start | bytes 24584 | tf_op jit(solution)/shard_map/ppermute | solution.py:26
  2.3 1.6 %collective-permute-start.1 = (bf16[1,256,512]{2,1,0:T(8,128)(2,1)S(1)}, bf16[1,256,512]{2,1,0:T(8,128)(2,1)S(1)}, u32[]{:S(2)}, u32[]{:S(2)}) collective-permute-start(bf16[1,256,512]{2,1,0:T(8,128)(2,1)S(1)} %get-tuple-element.60.mine_ref.edge_ref), channel_id=1, source_target_pairs={{1,0},{0,1},{3,2},{2,3},{5,4},{4,5},{7,6},{6,7},{9,8},{8,9},{11,10... | collective-permute-start | bytes 786440 | tf_op jit(solution)/shard_map/ppermute | solution.py:26
  4.0 8.5 %collective-permute-start.3 = (bf16[4,256,512]{2,1,0:T(8,128)(2,1)S(1)}, bf16[4,256,512]{2,1,0:T(8,128)(2,1)S(1)}, u32[]{:S(2)}, u32[]{:S(2)}) collective-permute-start(bf16[4,256,512]{2,1,0:T(8,128)(2,1)S(1)} %bitcast.7), channel_id=1, source_target_pairs={{1,0},{0,1},{3,2},{2,3},{5,4},{4,5},{7,6},{6,7},{9,8},{8,9},{11,10... | collective-permute-start | bytes 3145736 | tf_op jit(solution)/shard_map/ppermute | solution.py:26
  4.2 12.7 %collective-permute-start.6 = (bf16[1,272,512]{2,1,0:T(8,128)(2,1)S(1)}, bf16[1,272,512]{2,1,0:T(8,128)(2,1)S(1)}, u32[]{:S(2)}, u32[]{:S(2)}) collective-permute-start(bf16[1,272,512]{2,1,0:T(8,128)(2,1)S(1)} %shard_map.66), channel_id=1, source_target_pairs={{0,2},{1,15},{2,0},{3,5},{4,6},{5,3},{6,4},{7,9},{8,10},{9,7},{10,... | collective-permute-start | bytes 835592 | tf_op jit(solution)/shard_map/ppermute | solution.py:35
  9.0 4.1 %collective-permute-start.4 = (bf16[1,256,512]{2,1,0:T(8,128)(2,1)S(1)}, bf16[1,256,512]{2,1,0:T(8,128)(2,1)S(1)}, u32[]{:S(2)}, u32[]{:S(2)}) collective-permute-start(bf16[1,256,512]{2,1,0:T(8,128)(2,1)S(1)} %get-tuple-element.71), channel_id=1, source_target_pairs={{1,0},{0,1},{3,2},{2,3},{5,4},{4,5},{7,6},{6,7},{9,8},{8,9},{11,10... | collective-permute-start | bytes 786440 | tf_op jit(solution)/shard_map/ppermute | solution.py:26
  12.0 1.5 %collective-permute-start.5 = (bf16[1,256,512]{2,1,0:T(8,128)(2,1)S(1)}, bf16[1,256,512]{2,1,0:T(8,128)(2,1)S(1)}, u32[]{:S(2)}, u32[]{:S(2)}) collective-permute-start(bf16[1,256,512]{2,1,0:T(8,128)(2,1)S(1)} %get-tuple-element.72), channel_id=1, source_target_pairs={{1,0},{0,1},{3,2},{2,3},{5,4},{4,5},{7,6},{6,7},{9,8},{8,9},{11,10... | collective-permute-start | bytes 786440 | tf_op jit(solution)/shard_map/ppermute | solution.py:26
  12.1 1.8 %collective-permute-start.2 = (bf16[1,256,512]{2,1,0:T(8,128)(2,1)S(1)}, bf16[1,256,512]{2,1,0:T(8,128)(2,1)S(1)}, u32[]{:S(2)}, u32[]{:S(2)}) collective-permute-start(bf16[1,256,512]{2,1,0:T(8,128)(2,1)S(1)} %get-tuple-element.68.mine_ref), channel_id=1, source_target_pairs={{1,0},{0,1},{3,2},{2,3},{5,4},{4,5},{7,6},{6,7},{9,8},{8,9},{11,10... | collective-permute-start | bytes 786440 | tf_op jit(solution)/shard_map/ppermute | solution.py:26
  14.0 9.9 %collective-permute-start.11 = (bf16[1,288,512]{2,1,0:T(8,128)(2,1)S(1)}, bf16[1,288,512]{2,1,0:T(8,128)(2,1)S(1)}, u32[]{:S(2)}, u32[]{:S(2)}) collective-permute-start(bf16[1,288,512]{2,1,0:T(8,128)(2,1)S(1)} %shard_map.69), channel_id=1, source_target_pairs={{0,2},{1,15},{2,0},{3,5},{4,6},{5,3},{6,4},{7,9},{8,10},{9,7},{10,... | collective-permute-start | bytes 884744 | tf_op jit(solution)/shard_map/ppermute | solution.py:35
  16.9 3.0 %collective-permute-start.10 = (bf16[1,272,512]{2,1,0:T(8,128)(2,1)S(1)}, bf16[1,272,512]{2,1,0:T(8,128)(2,1)S(1)}, u32[]{:S(2)}, u32[]{:S(2)}) collective-permute-start(bf16[1,272,512]{2,1,0:T(8,128)(2,1)S(1)} %collective-permute-done.6.mine_ref), channel_id=1, source_target_pairs={{1,0},{0,1},{3,2},{2,3},{5,4},{4,5},{7,6},{6,7},{9,8},{8,9},{11,10... | collective-permute-start | bytes 835592 | tf_op jit(solution)/shard_map/ppermute | solution.py:26
  17.8 1.6 %collective-permute-start.7 = (bf16[1,256,512]{2,1,0:T(8,128)(2,1)S(1)}, bf16[1,256,512]{2,1,0:T(8,128)(2,1)S(1)}, u32[]{:S(2)}, u32[]{:S(2)}) collective-permute-start(bf16[1,256,512]{2,1,0:T(8,128)(2,1)S(1)} %get-tuple-element.78.refs_0_), channel_id=1, source_target_pairs={{1,0},{0,1},{3,2},{2,3},{5,4},{4,5},{7,6},{6,7},{9,8},{8,9},{11,10... | collective-permute-start | bytes 786440 | tf_op jit(solution)/shard_map/ppermute | solution.py:26
  17.9 1.9 %collective-permute-start.8 = (bf16[1,256,512]{2,1,0:T(8,128)(2,1)S(1)}, bf16[1,256,512]{2,1,0:T(8,128)(2,1)S(1)}, u32[]{:S(2)}, u32[]{:S(2)}) collective-permute-start(bf16[1,256,512]{2,1,0:T(8,128)(2,1)S(1)} %get-tuple-element.79.refs_1_), channel_id=1, source_target_pairs={{1,0},{0,1},{3,2},{2,3},{5,4},{4,5},{7,6},{6,7},{9,8},{8,9},{11,10... | collective-permute-start | bytes 786440 | tf_op jit(solution)/shard_map/ppermute | solution.py:26
  23.9 2.3 %collective-permute-start.14 = (bf16[1,288,512]{2,1,0:T(8,128)(2,1)S(1)}, bf16[1,288,512]{2,1,0:T(8,128)(2,1)S(1)}, u32[]{:S(2)}, u32[]{:S(2)}) collective-permute-start(bf16[1,288,512]{2,1,0:T(8,128)(2,1)S(1)} %collective-permute-done.11.message_ref.mine_ref), channel_id=1, source_target_pairs={{1,0},{0,1},{3,2},{2,3},{5,4},{4,5},{7,6},{6,7},{9,8},{8,9},{11,10... | collective-permute-start | bytes 884744 | tf_op jit(solution)/shard_map/ppermute | solution.py:26
  23.9 2.3 %collective-permute-start.12 = (bf16[1,256,512]{2,1,0:T(8,128)(2,1)S(1)}, bf16[1,256,512]{2,1,0:T(8,128)(2,1)S(1)}, u32[]{:S(2)}, u32[]{:S(2)}) collective-permute-start(bf16[1,256,512]{2,1,0:T(8,128)(2,1)S(1)} %get-tuple-element.87), channel_id=1, source_target_pairs={{1,0},{0,1},{3,2},{2,3},{5,4},{4,5},{7,6},{6,7},{9,8},{8,9},{11,10... | collective-permute-start | bytes 786440 | tf_op jit(solution)/shard_map/ppermute | solution.py:26
  24.4 1.8 %collective-permute-start.13 = (bf16[1,256,512]{2,1,0:T(8,128)(2,1)S(1)}, bf16[1,256,512]{2,1,0:T(8,128)(2,1)S(1)}, u32[]{:S(2)}, u32[]{:S(2)}) collective-permute-start(bf16[1,256,512]{2,1,0:T(8,128)(2,1)S(1)} %get-tuple-element.88), channel_id=1, source_target_pairs={{1,0},{0,1},{3,2},{2,3},{5,4},{4,5},{7,6},{6,7},{9,8},{8,9},{11,10... | collective-permute-start | bytes 786440 | tf_op jit(solution)/shard_map/ppermute | solution.py:26
  24.4 16.7 %collective-permute-start.9 = (bf16[2,256,512]{2,1,0:T(8,128)(2,1)S(1)}, bf16[2,256,512]{2,1,0:T(8,128)(2,1)S(1)}, u32[]{:S(2)}, u32[]{:S(2)}) collective-permute-start(bf16[2,256,512]{2,1,0:T(8,128)(2,1)S(1)} %shard_map.71), channel_id=1, source_target_pairs={{0,2},{1,15},{2,0},{3,5},{4,6},{5,3},{6,4},{7,9},{8,10},{9,7},{10,... | collective-permute-start | bytes 1572872 | tf_op jit(solution)/shard_map/ppermute | solution.py:35
  26.8 7.2 %collective-permute-start.17 = (bf16[1,256,512]{2,1,0:T(8,128)(2,1)S(1)}, bf16[1,256,512]{2,1,0:T(8,128)(2,1)S(1)}, u32[]{:S(2)}, u32[]{:S(2)}) collective-permute-start(bf16[1,256,512]{2,1,0:T(8,128)(2,1)S(1)} %get-tuple-element.102.own_low_ref), channel_id=1, source_target_pairs={{1,0},{0,1},{3,2},{2,3},{5,4},{4,5},{7,6},{6,7},{9,8},{8,9},{11,10... | collective-permute-start | bytes 786440 | tf_op jit(solution)/shard_map/ppermute | solution.py:26
  28.5 5.6 %collective-permute-start.18 = (bf16[1,256,512]{2,1,0:T(8,128)(2,1)S(1)}, bf16[1,256,512]{2,1,0:T(8,128)(2,1)S(1)}, u32[]{:S(2)}, u32[]{:S(2)}) collective-permute-start(bf16[1,256,512]{2,1,0:T(8,128)(2,1)S(1)} %get-tuple-element.105.own_high_ref), channel_id=1, source_target_pairs={{1,0},{0,1},{3,2},{2,3},{5,4},{4,5},{7,6},{6,7},{9,8},{8,9},{11,10... | collective-permute-start | bytes 786440 | tf_op jit(solution)/shard_map/ppermute | solution.py:26
  28.6 3.8 %collective-permute-start.15 = (f32[4,512]{1,0:T(4,128)S(1)}, f32[4,512]{1,0:T(4,128)S(1)}, u32[]{:S(2)}, u32[]{:S(2)}) collective-permute-start(f32[4,512]{1,0:T(4,128)S(1)} %get-tuple-element.91.one_ref), channel_id=1, source_target_pairs={{0,4},{1,5},{2,6},{3,7},{4,0},{5,1},{6,2},{7,3},{8,12},{9,13},{10,... | collective-permute-start | bytes 24584 | tf_op jit(solution)/shard_map/ppermute | solution.py:646
  32.4 4.5 %collective-permute-start.16 = (f32[4,512]{1,0:T(4,128)S(1)}, f32[4,512]{1,0:T(4,128)S(1)}, u32[]{:S(2)}, u32[]{:S(2)}) collective-permute-start(f32[4,512]{1,0:T(4,128)S(1)} %shard_map.75.one_ref), channel_id=1, source_target_pairs={{0,8},{1,9},{2,10},{3,11},{4,12},{5,13},{6,14},{7,15},{8,0},{9,1},... | collective-permute-start | bytes 24584 | tf_op jit(solution)/shard_map/ppermute | solution.py:646
  36.9 5.9 %collective-permute-start.19 = (f32[4,512]{1,0:T(4,128)S(1)}, f32[4,512]{1,0:T(4,128)S(1)}, u32[]{:S(2)}, u32[]{:S(2)}) collective-permute-start(f32[4,512]{1,0:T(4,128)S(1)} %shard_map.77.one_ref), channel_id=1, source_target_pairs={{0,2},{1,3},{2,0},{3,1},{4,6},{5,7},{6,4},{7,5},{8,10},{9,11},{10,... | collective-permute-start | bytes 24584 | tf_op jit(solution)/shard_map/ppermute | solution.py:646
  42.8 1.2 %collective-permute-start.20 = (f32[8,512]{1,0:T(8,128)S(1)}, f32[8,512]{1,0:T(8,128)S(1)}, u32[]{:S(2)}, u32[]{:S(2)}) collective-permute-start(f32[8,512]{1,0:T(8,128)S(1)} %shard_map.79.mine_ref), channel_id=1, source_target_pairs={{1,0},{0,1},{3,2},{2,3},{5,4},{4,5},{7,6},{6,7},{9,8},{8,9},{11,10... | collective-permute-start | bytes 49160 | tf_op jit(solution)/shard_map/ppermute | solution.py:26

commit v9 on v8

--- a/solution.py
+++ b/solution.py
@@ -13,6 +13,7 @@
 ROWS = 16
 UNROLL = 16
 PAD = 2
+PAD_ROWS = 32
 
 courant = 0.3
 slope = 0.6
@@ -188,6 +189,9 @@
             for t in range(cells // LANES):
                 at = 0, rows, columns(t)
                 out_ref[p, rows, columns(t)] = jnp.where(leaves, refs[p][at], refs[count + p][at])
+
+    if count > 1:
+        out_ref[:, orient:] = jnp.zeros_like(out_ref[:, orient:])
 
 
 def first_message_kernel(mine_ref, other_ref, *refs):
@@ -588,7 +592,7 @@
     )
 
     def message(blocks, others):
-        shape = jax.ShapeDtypeStruct((len(blocks),) + blocks[0].shape[1:], BF16)
+        shape = jax.ShapeDtypeStruct((len(blocks), orient + PAD_ROWS, cells), BF16)
         return kernel_call(message_kernel, shape, (), (*blocks, *others, spread))
 
     start, _ = lax.optimization_barrier((start, message0))

time: 44.8 us -> 43.8 us (0.978)
  starting transfers between devices: 19.1 us -> 15.8 us
  waiting for transfers between devices: 7.11 us -> 9.37 us
    ppermute x3, starting transfers between devices: 6.24 us -> 1.88 us  [received(): lax.ppermute(value, 'space', [(i, i ^ distance) for i in range(count)])]
    ppermute x3, waiting for transfers between devices: 1.73 us -> 3.79 us  [received(): lax.ppermute(value, 'space', [(i, i ^ distance) for i in range(count)])]
    ppermute x15, waiting for transfers between devices: 4.58 us -> 5.57 us  [swap_species(): return lax.ppermute(block, 'space', [(i ^ 1, i) for i in range(count)])]
    ppermute x3, waiting for transfers between devices: 0.8 us -> 0.01 us  [exchange_faces(): return lax.ppermute(block, 'space', route)]
    ppermute x3, starting transfers between devices: 4.71 us -> 5.36 us  [exchange_faces(): return lax.ppermute(block, 'space', route)]
    ppermute x15, starting transfers between devices: 8.12 us -> 8.59 us  [swap_species(): return lax.ppermute(block, 'space', [(i ^ 1, i) for i in range(count)])]
  transfers between devices with their start and end apart: 21 -> 21, of which waited for: 11 -> 12; matrix products, arithmetic and copies ran while one was open for 3% -> 3% of each run, Pallas kernels for 36% -> 36%
where the time goes in v9:
time: 43.8 us; the launch traced here: 43.7 us
  Pallas kernels  16.8 us (38%)
  starting transfers between devices  15.8 us (36%)
  waiting for transfers between devices  9.37 us (21%)
  local copies, waits for them, and re-layouts  1.44 us (3%)
    pallas_call x17, Pallas kernels, kernel_call(): pl.pallas_call(kernel, out_shape=outs, in_specs=[smem if arg.dtype == jnp...  16.8 us
    ppermute x15, starting transfers between devices, swap_species(): return lax.ppermute(block, 'space', [(i ^ 1, i) for i in range(count)])  8.59 us
    ppermute x15, waiting for transfers between devices, swap_species(): return lax.ppermute(block, 'space', [(i ^ 1, i) for i in range(count)])  5.57 us
    ppermute x3, starting transfers between devices, exchange_faces(): return lax.ppermute(block, 'space', route)  5.36 us
    ppermute x3, waiting for transfers between devices, received(): lax.ppermute(value, 'space', [(i, i ^ distance) for i in range(count)])  3.79 us
    ppermute x3, starting transfers between devices, received(): lax.ppermute(value, 'space', [(i, i ^ distance) for i in range(count)])  1.88 us
    unnamed x11, local copies, waits for them, and re-layouts  1.44 us
  transfers between devices with their start and end apart: 21, of which 12 were waited for; matrix products, arithmetic and copies ran while one was open for 3% of the time, Pallas kernels for 36%

profile of v9, /device:TPU:0, one launch (start us, length us, event | category | flops | bytes accessed | tf_op | source)
XLA Modules:
  0.0 43.7 jit_solution(8926010962993690536)
XLA Ops:
  0.0 0.5 %collective-permute-start = (f32[4,512]{1,0:T(4,128)}, f32[4,512]{1,0:T(4,128)S(1)}, u32[]{:S(2)}, u32[]{:S(2)}) collective-permute-start(f32[4,512]{1,0:T(4,128)} %param.6), channel_id=1, source_target_pairs={{1,0},{0,1},{3,2},{2,3},{5,4},{4,5},{7,6},{6,7},{9,8},{8,9},{11,10... | collective-permute-start | bytes 24584 | tf_op jit(solution)/shard_map/ppermute | solution.py:27
  0.6 1.4 %copy.9 = bf16[256,4,512]{2,0,1:T(8,128)(2,1)S(1)} copy(bf16[256,4,512]{2,1,0:T(4,128)(2,1)} %param.7) | data formatting | bytes 2097152 | tf_op args[1]
  2.8 1.1 %collective-permute-done.1.other_ref = bf16[1,256,512]{2,1,0:T(8,128)(2,1)S(1)} collective-permute-done((bf16[1,256,512]{2,1,0:T(8,128)(2,1)S(1)}, bf16[1,256,512]{2,1,0:T(8,128)(2,1)S(1)}, u32[]{:S(2)}, u32[]{:S(2)}) %collective-permute-start.1) | collective-permute-done | bytes 262176 | tf_op jit(solution)/shard_map/ppermute | solution.py:27
  4.2 2.9 %collective-permute-start.6 = (bf16[1,272,512]{2,1,0:T(8,128)(2,1)S(1)}, bf16[1,272,512]{2,1,0:T(8,128)(2,1)S(1)}, u32[]{:S(2)}, u32[]{:S(2)}) collective-permute-start(bf16[1,272,512]{2,1,0:T(8,128)(2,1)S(1)} %shard_map.66), channel_id=1, source_target_pairs={{0,2},{1,15},{2,0},{3,5},{4,6},{5,3},{6,4},{7,9},{8,10},{9,7},{10,... | collective-permute-start | bytes 835592 | tf_op jit(solution)/shard_map/ppermute | solution.py:36
  7.1 2.0 %shard_map.67 = (bf16[4,256,512]{2,1,0:T(8,128)(2,1)S(1)}, bf16[1,256,512]{2,1,0:T(8,128)(2,1)S(1)}, bf16[1,256,512]{2,1,0:T(8,128)(2,1)S(1)}, bf16[1,256,512]{2,1,0:T(8,128)(2,1)S(1)}) custom-call(bf16[4,256,512]{2,1,0:T(8,128)(2,1)S(1)} %bitcast.8, f32[4,512]{1,0:T(4,128)S(1)} %get-tuple-element.116.fields_ref.first_ref.own_ref, ...), custom_call_target="tpu_custom_call" | custom-call | tf_op jit(solution)/shard_map/pallas_call | solution.py:547
  9.0 3.0 %collective-permute-start.4 = (bf16[1,256,512]{2,1,0:T(8,128)(2,1)S(1)}, bf16[1,256,512]{2,1,0:T(8,128)(2,1)S(1)}, u32[]{:S(2)}, u32[]{:S(2)}) collective-permute-start(bf16[1,256,512]{2,1,0:T(8,128)(2,1)S(1)} %get-tuple-element.71), channel_id=1, source_target_pairs={{1,0},{0,1},{3,2},{2,3},{5,4},{4,5},{7,6},{6,7},{9,8},{8,9},{11,10... | collective-permute-start | bytes 786440 | tf_op jit(solution)/shard_map/ppermute | solution.py:27
  12.1 0.4 collective-permute-start.2
  12.5 0.6 %shard_map.68 = (bf16[4,256,512]{2,1,0:T(8,128)(2,1)S(1)}, bf16[2,256,512]{2,1,0:T(8,128)(2,1)S(1)}) custom-call(s32[1]{0:T(128)} %bitcast.core_ref, bf16[4,256,512]{2,1,0:T(8,128)(2,1)S(1)} %collective-permute-done.3.partner_ref, bf16[4,256,512]{2,1,0:T(8,128)(2,1)S(1)} %bitcast.9, bf16[256,256]{1,0:T(8,128)(2,1)S(1)} %get-tuple-element.69.turned_ref), custom_call_target="tpu_custom_call" | custom-call | tf_op jit(solution)/shard_map/pallas_call | solution.py:547
  13.2 0.4 collective-permute-done.5.refs_2_
  13.5 0.4 collective-permute-done.2.other_ref
  14.1 2.8 %shard_map.70 = (bf16[1,256,512]{2,1,0:T(8,128)(2,1)S(1)}, bf16[1,256,512]{2,1,0:T(8,128)(2,1)S(1)}) custom-call(bf16[4,256,512]{2,1,0:T(8,128)(2,1)S(1)} %get-tuple-element.80.state_ref.alone_ref, f32[4,512]{1,0:T(4,128)S(1)} %get-tuple-element.116.fields_ref.first_ref.own_ref, f32[4,512]{1,0:T(4,128)S(1)} %get-tuple-element.115.partner_ref.second_ref, ...), custom_call_target="tpu_custom_call" | custom-call | tf_op jit(solution)/shard_map/pallas_call | solution.py:547
  16.9 0.9 %collective-permute-start.7 = (bf16[1,256,512]{2,1,0:T(8,128)(2,1)S(1)}, bf16[1,256,512]{2,1,0:T(8,128)(2,1)S(1)}, u32[]{:S(2)}, u32[]{:S(2)}) collective-permute-start(bf16[1,256,512]{2,1,0:T(8,128)(2,1)S(1)} %get-tuple-element.78.refs_0_), channel_id=1, source_target_pairs={{1,0},{0,1},{3,2},{2,3},{5,4},{4,5},{7,6},{6,7},{9,8},{8,9},{11,10... | collective-permute-start | bytes 786440 | tf_op jit(solution)/shard_map/ppermute | solution.py:27
  17.9 0.4 collective-permute-start.10
  18.3 0.7 %collective-permute-done.7.refs_2_ = bf16[1,256,512]{2,1,0:T(8,128)(2,1)S(1)} collective-permute-done((bf16[1,256,512]{2,1,0:T(8,128)(2,1)S(1)}, bf16[1,256,512]{2,1,0:T(8,128)(2,1)S(1)}, u32[]{:S(2)}, u32[]{:S(2)}) %collective-permute-start.7) | collective-permute-done | bytes 262176 | tf_op jit(solution)/shard_map/ppermute | solution.py:27
  18.9 0.4 collective-permute-done.8.refs_3_
  19.4 2.4 %collective-permute-start.9 = (bf16[2,288,512]{2,1,0:T(8,128)(2,1)S(1)}, bf16[2,288,512]{2,1,0:T(8,128)(2,1)S(1)}, u32[]{:S(2)}, u32[]{:S(2)}) collective-permute-start(bf16[2,288,512]{2,1,0:T(8,128)(2,1)S(1)} %shard_map.71), channel_id=1, source_target_pairs={{0,2},{1,15},{2,0},{3,5},{4,6},{5,3},{6,4},{7,9},{8,10},{9,7},{10,... | collective-permute-start | bytes 1769480 | tf_op jit(solution)/shard_map/ppermute | solution.py:36
  21.8 3.3 %shard_map.72 = (bf16[1,256,512]{2,1,0:T(8,128)(2,1)S(1)}, bf16[1,256,512]{2,1,0:T(8,128)(2,1)S(1)}, bf16[8,256,512]{2,1,0:T(8,128)(2,1)S(1)}, bf16[1,256,512]{2...) custom-call(s32[1]{0:T(128)} %bitcast.core_ref, ...), custom_call_target="tpu_custom_call" | custom-call | tf_op jit(solution)/shard_map/pallas_call | solution.py:547
  25.1 1.7 %collective-permute-start.14 = (bf16[1,288,512]{2,1,0:T(8,128)(2,1)S(1)}, bf16[1,288,512]{2,1,0:T(8,128)(2,1)S(1)}, u32[]{:S(2)}, u32[]{:S(2)}) collective-permute-start(bf16[1,288,512]{2,1,0:T(8,128)(2,1)S(1)} %collective-permute-done.11.message_ref.mine_ref), channel_id=1, source_target_pairs={{1,0},{0,1},{3,2},{2,3},{5,4},{4,5},{7,6},{6,7},{9,8},{8,9},{11,10... | collective-permute-start | bytes 884744 | tf_op jit(solution)/shard_map/ppermute | solution.py:27
  27.0 0.4 collective-permute-start.13
  27.4 1.1 %collective-permute-done.12.near_ref = bf16[1,256,512]{2,1,0:T(8,128)(2,1)S(1)} collective-permute-done((bf16[1,256,512]{2,1,0:T(8,128)(2,1)S(1)}, bf16[1,256,512]{2,1,0:T(8,128)(2,1)S(1)}, u32[]{:S(2)}, u32[]{:S(2)}) %collective-permute-start.12) | collective-permute-done | bytes 262176 | tf_op jit(solution)/shard_map/ppermute | solution.py:27
  28.5 0.4 collective-permute-done.13.far_ref
  28.9 0.6 %shard_map.73 = (f32[2,512]{1,0:T(2,128)S(1)}, f32[4,512]{1,0:T(4,128)S(1)}) custom-call(s32[1]{0:T(128)} %bitcast.core_ref, bf16[2,256,512]{2,1,0:T(8,128)(2,1)S(1)} %get-tuple-element.82.own_ref, bf16[1,256,512]{2,1,0:T(8,128)(2,1)S(1)} %collective-permute-done.12.near_ref, bf16[1,256,512]{2,1,0:T(8,128)(2,1)S(1)} %collective-permute-done.13.far_ref, ...), custom_call_target="tpu_custom_call" | custom-call | tf_op jit(solution)/shard_map/pallas_call | solution.py:547
  29.4 0.4 collective-permute-start.17
  30.2 3.0 %shard_map.74.held_ref = bf16[6,256,512]{2,1,0:T(8,128)(2,1)S(1)} custom-call(bf16[8,256,512]{2,1,0:T(8,128)(2,1)S(1)} %get-tuple-element.96.held_ref, bf16[1,288,512]{2,1,0:T(8,128)(2,1)S(1)} %collective-permute-done.11.message_ref.mine_ref, bf16[1,288,512]{2,1,0:T(8,128)(2,1)S(1)} %collective-permute-done.14.other_ref, ...), custom_call_target="tpu_custom_call" | custom-call | tf_op jit(solution)/shard_map/pallas_call | solution.py:547
  33.2 0.4 %collective-permute-done.15.two_ref = f32[4,512]{1,0:T(4,128)S(1)} collective-permute-done((f32[4,512]{1,0:T(4,128)S(1)}, f32[4,512]{1,0:T(4,128)S(1)}, u32[]{:S(2)}, u32[]{:S(2)}) %collective-permute-start.15) | collective-permute-done | bytes 8224 | tf_op jit(solution)/shard_map/ppermute | solution.py:650
  33.6 1.6 %collective-permute-start.16 = (f32[4,512]{1,0:T(4,128)S(1)}, f32[4,512]{1,0:T(4,128)S(1)}, u32[]{:S(2)}, u32[]{:S(2)}) collective-permute-start(f32[4,512]{1,0:T(4,128)S(1)} %shard_map.75.one_ref), channel_id=1, source_target_pairs={{0,8},{1,9},{2,10},{3,11},{4,12},{5,13},{6,14},{7,15},{8,0},{9,1},... | collective-permute-start | bytes 24584 | tf_op jit(solution)/shard_map/ppermute | solution.py:650
  35.3 1.6 %shard_map.76.shared_ref = f32[4,512]{1,0:T(4,128)S(1)} custom-call(bf16[6,256,512]{2,1,0:T(8,128)(2,1)S(1)} %shard_map.74.held_ref, f32[4,512]{1,0:T(4,128)S(1)} %get-tuple-element.115.partner_ref.second_ref, f32[4,256,128]{2,1,0:T(8,128)S(1)} %get-tuple-element.64.refs_1_.v_ref.refs_2_.refs_4_, bf16[4,256,512]{2,1,0:T(8,128)(2,1)S(1)} %get-tuple-element.74.weight_ref, ...), custom_call_target="tpu_custom_call" | custom-call | tf_op jit(solution)/shard_map/pallas_call | solution.py:547
  36.9 1.4 %collective-permute-done.16.two_ref = f32[4,512]{1,0:T(4,128)S(1)} collective-permute-done((f32[4,512]{1,0:T(4,128)S(1)}, f32[4,512]{1,0:T(4,128)S(1)}, u32[]{:S(2)}, u32[]{:S(2)}) %collective-permute-start.16) | collective-permute-done | bytes 8224 | tf_op jit(solution)/shard_map/ppermute | solution.py:650
  38.3 1.6 %shard_map.78 = (f32[4,512]{1,0:T(4,128)S(1)}, f32[4,512]{1,0:T(4,128)S(1)}) custom-call(s32[1]{0:T(128)} %bitcast.core_ref, bf16[2,288,512]{2,1,0:T(8,128)(2,1)S(1)} %collective-permute-done.9.message_ref, bf16[4,256,512]{2,1,0:T(8,128)(2,1)S(1)} %get-tuple-element.74.weight_ref, bf16[2,256,512]{2,1,0:T(8,128)(2,1)S(1)} %get-tuple-element.109.own_weight_ref, ...), custom_call_target="tpu_custom_call" | custom-call | tf_op jit(solution)/shard_map/pallas_call | solution.py:547
  39.9 2.0 %collective-permute-done.19.two_ref = f32[4,512]{1,0:T(4,128)S(1)} collective-permute-done((f32[4,512]{1,0:T(4,128)S(1)}, f32[4,512]{1,0:T(4,128)S(1)}, u32[]{:S(2)}, u32[]{:S(2)}) %collective-permute-start.19) | collective-permute-done | bytes 8224 | tf_op jit(solution)/shard_map/ppermute | solution.py:650
  41.9 1.2 %collective-permute-done.20.arrived_ref = f32[8,512]{1,0:T(8,128)S(1)} collective-permute-done((f32[8,512]{1,0:T(8,128)S(1)}, f32[8,512]{1,0:T(8,128)S(1)}, u32[]{:S(2)}, u32[]{:S(2)}) %collective-permute-start.20) | collective-permute-done | bytes 16416 | tf_op jit(solution)/shard_map/ppermute | solution.py:27
  43.1 0.6 %shard_map.80 = f32[4,512]{1,0:T(4,128)} custom-call(f32[4,512]{1,0:T(4,128)S(1)} %get-tuple-element.111.kept_ref, f32[8,512]{1,0:T(8,128)S(1)} %shard_map.79.mine_ref, f32[8,512]{1,0:T(8,128)S(1)} %collective-permute-done.20.arrived_ref), custom_call_target="tpu_custom_call" | custom-call | tf_op jit(solution)/shard_map/pallas_call | solution.py:547
  (40 shorter events, 2.1 us)
Async XLA Ops:
  0.0 2.0 %copy-start.4 = (f32[4,512]{1,0:T(4,128)S(1)}, f32[4,512]{1,0:T(4,128)}, u32[]{:S(2)}) copy-start(f32[4,512]{1,0:T(4,128)} %param.6) | copy-start | bytes 24580
  0.0 2.1 %copy-start.2 = (f32[3,256]{1,0:T(4,128)S(1)}, f32[3,256]{1,0:T(4,128)}, u32[]{:S(2)}) copy-start(f32[3,256]{1,0:T(4,128)} %directions_ref.1) | copy-start | bytes 9220
  0.0 2.5 %copy-start.3 = (f32[256]{0:T(256)S(1)}, f32[256]{0:T(256)}, u32[]{:S(2)}) copy-start(f32[256]{0:T(256)} %param.11) | copy-start | bytes 3076
  0.0 2.5 %copy-start = (bf16[256,256]{1,0:T(8,128)(2,1)S(1)}, bf16[256,256]{1,0:T(8,128)(2,1)}, u32[]{:S(2)}) copy-start(bf16[256,256]{1,0:T(8,128)(2,1)} %synthesis_ref.1) | copy-start | bytes 393220
  0.0 2.5 %copy-start.1 = (bf16[256,256]{1,0:T(8,128)(2,1)S(1)}, bf16[256,256]{1,0:T(8,128)(2,1)}, u32[]{:S(2)}) copy-start(bf16[256,256]{1,0:T(8,128)(2,1)} %analysis_ref.1) | copy-start | bytes 393220
  0.0 2.0 %collective-permute-start = (f32[4,512]{1,0:T(4,128)}, f32[4,512]{1,0:T(4,128)S(1)}, u32[]{:S(2)}, u32[]{:S(2)}) collective-permute-start(f32[4,512]{1,0:T(4,128)} %param.6), channel_id=1, source_target_pairs={{1,0},{0,1},{3,2},{2,3},{5,4},{4,5},{7,6},{6,7},{9,8},{8,9},{11,10... | collective-permute-start | bytes 24584 | tf_op jit(solution)/shard_map/ppermute | solution.py:27
  2.3 1.6 %collective-permute-start.1 = (bf16[1,256,512]{2,1,0:T(8,128)(2,1)S(1)}, bf16[1,256,512]{2,1,0:T(8,128)(2,1)S(1)}, u32[]{:S(2)}, u32[]{:S(2)}) collective-permute-start(bf16[1,256,512]{2,1,0:T(8,128)(2,1)S(1)} %get-tuple-element.60.mine_ref.edge_ref), channel_id=1, source_target_pairs={{1,0},{0,1},{3,2},{2,3},{5,4},{4,5},{7,6},{6,7},{9,8},{8,9},{11,10... | collective-permute-start | bytes 786440 | tf_op jit(solution)/shard_map/ppermute | solution.py:27
  4.0 8.5 %collective-permute-start.3 = (bf16[4,256,512]{2,1,0:T(8,128)(2,1)S(1)}, bf16[4,256,512]{2,1,0:T(8,128)(2,1)S(1)}, u32[]{:S(2)}, u32[]{:S(2)}) collective-permute-start(bf16[4,256,512]{2,1,0:T(8,128)(2,1)S(1)} %bitcast.7), channel_id=1, source_target_pairs={{1,0},{0,1},{3,2},{2,3},{5,4},{4,5},{7,6},{6,7},{9,8},{8,9},{11,10... | collective-permute-start | bytes 3145736 | tf_op jit(solution)/shard_map/ppermute | solution.py:27
  4.2 12.7 %collective-permute-start.6 = (bf16[1,272,512]{2,1,0:T(8,128)(2,1)S(1)}, bf16[1,272,512]{2,1,0:T(8,128)(2,1)S(1)}, u32[]{:S(2)}, u32[]{:S(2)}) collective-permute-start(bf16[1,272,512]{2,1,0:T(8,128)(2,1)S(1)} %shard_map.66), channel_id=1, source_target_pairs={{0,2},{1,15},{2,0},{3,5},{4,6},{5,3},{6,4},{7,9},{8,10},{9,7},{10,... | collective-permute-start | bytes 835592 | tf_op jit(solution)/shard_map/ppermute | solution.py:36
  9.0 4.1 %collective-permute-start.4 = (bf16[1,256,512]{2,1,0:T(8,128)(2,1)S(1)}, bf16[1,256,512]{2,1,0:T(8,128)(2,1)S(1)}, u32[]{:S(2)}, u32[]{:S(2)}) collective-permute-start(bf16[1,256,512]{2,1,0:T(8,128)(2,1)S(1)} %get-tuple-element.71), channel_id=1, source_target_pairs={{1,0},{0,1},{3,2},{2,3},{5,4},{4,5},{7,6},{6,7},{9,8},{8,9},{11,10... | collective-permute-start | bytes 786440 | tf_op jit(solution)/shard_map/ppermute | solution.py:27
  12.0 1.5 %collective-permute-start.5 = (bf16[1,256,512]{2,1,0:T(8,128)(2,1)S(1)}, bf16[1,256,512]{2,1,0:T(8,128)(2,1)S(1)}, u32[]{:S(2)}, u32[]{:S(2)}) collective-permute-start(bf16[1,256,512]{2,1,0:T(8,128)(2,1)S(1)} %get-tuple-element.72), channel_id=1, source_target_pairs={{1,0},{0,1},{3,2},{2,3},{5,4},{4,5},{7,6},{6,7},{9,8},{8,9},{11,10... | collective-permute-start | bytes 786440 | tf_op jit(solution)/shard_map/ppermute | solution.py:27
  12.1 1.8 %collective-permute-start.2 = (bf16[1,256,512]{2,1,0:T(8,128)(2,1)S(1)}, bf16[1,256,512]{2,1,0:T(8,128)(2,1)S(1)}, u32[]{:S(2)}, u32[]{:S(2)}) collective-permute-start(bf16[1,256,512]{2,1,0:T(8,128)(2,1)S(1)} %get-tuple-element.68.mine_ref), channel_id=1, source_target_pairs={{1,0},{0,1},{3,2},{2,3},{5,4},{4,5},{7,6},{6,7},{9,8},{8,9},{11,10... | collective-permute-start | bytes 786440 | tf_op jit(solution)/shard_map/ppermute | solution.py:27
  14.0 11.2 %collective-permute-start.11 = (bf16[1,288,512]{2,1,0:T(8,128)(2,1)S(1)}, bf16[1,288,512]{2,1,0:T(8,128)(2,1)S(1)}, u32[]{:S(2)}, u32[]{:S(2)}) collective-permute-start(bf16[1,288,512]{2,1,0:T(8,128)(2,1)S(1)} %shard_map.69), channel_id=1, source_target_pairs={{0,2},{1,15},{2,0},{3,5},{4,6},{5,3},{6,4},{7,9},{8,10},{9,7},{10,... | collective-permute-start | bytes 884744 | tf_op jit(solution)/shard_map/ppermute | solution.py:36
  16.9 2.1 %collective-permute-start.7 = (bf16[1,256,512]{2,1,0:T(8,128)(2,1)S(1)}, bf16[1,256,512]{2,1,0:T(8,128)(2,1)S(1)}, u32[]{:S(2)}, u32[]{:S(2)}) collective-permute-start(bf16[1,256,512]{2,1,0:T(8,128)(2,1)S(1)} %get-tuple-element.78.refs_0_), channel_id=1, source_target_pairs={{1,0},{0,1},{3,2},{2,3},{5,4},{4,5},{7,6},{6,7},{9,8},{8,9},{11,10... | collective-permute-start | bytes 786440 | tf_op jit(solution)/shard_map/ppermute | solution.py:27
  17.8 1.5 %collective-permute-start.8 = (bf16[1,256,512]{2,1,0:T(8,128)(2,1)S(1)}, bf16[1,256,512]{2,1,0:T(8,128)(2,1)S(1)}, u32[]{:S(2)}, u32[]{:S(2)}) collective-permute-start(bf16[1,256,512]{2,1,0:T(8,128)(2,1)S(1)} %get-tuple-element.79.refs_1_), channel_id=1, source_target_pairs={{1,0},{0,1},{3,2},{2,3},{5,4},{4,5},{7,6},{6,7},{9,8},{8,9},{11,10... | collective-permute-start | bytes 786440 | tf_op jit(solution)/shard_map/ppermute | solution.py:27
  17.9 4.0 %collective-permute-start.10 = (bf16[1,272,512]{2,1,0:T(8,128)(2,1)S(1)}, bf16[1,272,512]{2,1,0:T(8,128)(2,1)S(1)}, u32[]{:S(2)}, u32[]{:S(2)}) collective-permute-start(bf16[1,272,512]{2,1,0:T(8,128)(2,1)S(1)} %collective-permute-done.6.mine_ref), channel_id=1, source_target_pairs={{1,0},{0,1},{3,2},{2,3},{5,4},{4,5},{7,6},{6,7},{9,8},{8,9},{11,10... | collective-permute-start | bytes 835592 | tf_op jit(solution)/shard_map/ppermute | solution.py:27
  19.4 18.8 %collective-permute-start.9 = (bf16[2,288,512]{2,1,0:T(8,128)(2,1)S(1)}, bf16[2,288,512]{2,1,0:T(8,128)(2,1)S(1)}, u32[]{:S(2)}, u32[]{:S(2)}) collective-permute-start(bf16[2,288,512]{2,1,0:T(8,128)(2,1)S(1)} %shard_map.71), channel_id=1, source_target_pairs={{0,2},{1,15},{2,0},{3,5},{4,6},{5,3},{6,4},{7,9},{8,10},{9,7},{10,... | collective-permute-start | bytes 1769480 | tf_op jit(solution)/shard_map/ppermute | solution.py:36
  25.1 3.7 %collective-permute-start.14 = (bf16[1,288,512]{2,1,0:T(8,128)(2,1)S(1)}, bf16[1,288,512]{2,1,0:T(8,128)(2,1)S(1)}, u32[]{:S(2)}, u32[]{:S(2)}) collective-permute-start(bf16[1,288,512]{2,1,0:T(8,128)(2,1)S(1)} %collective-permute-done.11.message_ref.mine_ref), channel_id=1, source_target_pairs={{1,0},{0,1},{3,2},{2,3},{5,4},{4,5},{7,6},{6,7},{9,8},{8,9},{11,10... | collective-permute-start | bytes 884744 | tf_op jit(solution)/shard_map/ppermute | solution.py:27
  26.9 1.6 %collective-permute-start.12 = (bf16[1,256,512]{2,1,0:T(8,128)(2,1)S(1)}, bf16[1,256,512]{2,1,0:T(8,128)(2,1)S(1)}, u32[]{:S(2)}, u32[]{:S(2)}) collective-permute-start(bf16[1,256,512]{2,1,0:T(8,128)(2,1)S(1)} %get-tuple-element.87), channel_id=1, source_target_pairs={{1,0},{0,1},{3,2},{2,3},{5,4},{4,5},{7,6},{6,7},{9,8},{8,9},{11,10... | collective-permute-start | bytes 786440 | tf_op jit(solution)/shard_map/ppermute | solution.py:27
  27.0 1.9 %collective-permute-start.13 = (bf16[1,256,512]{2,1,0:T(8,128)(2,1)S(1)}, bf16[1,256,512]{2,1,0:T(8,128)(2,1)S(1)}, u32[]{:S(2)}, u32[]{:S(2)}) collective-permute-start(bf16[1,256,512]{2,1,0:T(8,128)(2,1)S(1)} %get-tuple-element.88), channel_id=1, source_target_pairs={{1,0},{0,1},{3,2},{2,3},{5,4},{4,5},{7,6},{6,7},{9,8},{8,9},{11,10... | collective-permute-start | bytes 786440 | tf_op jit(solution)/shard_map/ppermute | solution.py:27
  29.4 5.8 %collective-permute-start.17 = (bf16[1,256,512]{2,1,0:T(8,128)(2,1)S(1)}, bf16[1,256,512]{2,1,0:T(8,128)(2,1)S(1)}, u32[]{:S(2)}, u32[]{:S(2)}) collective-permute-start(bf16[1,256,512]{2,1,0:T(8,128)(2,1)S(1)} %get-tuple-element.102.own_low_ref), channel_id=1, source_target_pairs={{1,0},{0,1},{3,2},{2,3},{5,4},{4,5},{7,6},{6,7},{9,8},{8,9},{11,10... | collective-permute-start | bytes 786440 | tf_op jit(solution)/shard_map/ppermute | solution.py:27
  29.8 5.4 %collective-permute-start.18 = (bf16[1,256,512]{2,1,0:T(8,128)(2,1)S(1)}, bf16[1,256,512]{2,1,0:T(8,128)(2,1)S(1)}, u32[]{:S(2)}, u32[]{:S(2)}) collective-permute-start(bf16[1,256,512]{2,1,0:T(8,128)(2,1)S(1)} %get-tuple-element.105.own_high_ref), channel_id=1, source_target_pairs={{1,0},{0,1},{3,2},{2,3},{5,4},{4,5},{7,6},{6,7},{9,8},{8,9},{11,10... | collective-permute-start | bytes 786440 | tf_op jit(solution)/shard_map/ppermute | solution.py:27
  30.0 3.7 %collective-permute-start.15 = (f32[4,512]{1,0:T(4,128)S(1)}, f32[4,512]{1,0:T(4,128)S(1)}, u32[]{:S(2)}, u32[]{:S(2)}) collective-permute-start(f32[4,512]{1,0:T(4,128)S(1)} %get-tuple-element.91.one_ref), channel_id=1, source_target_pairs={{0,4},{1,5},{2,6},{3,7},{4,0},{5,1},{6,2},{7,3},{8,12},{9,13},{10,... | collective-permute-start | bytes 24584 | tf_op jit(solution)/shard_map/ppermute | solution.py:650
  33.6 4.6 %collective-permute-start.16 = (f32[4,512]{1,0:T(4,128)S(1)}, f32[4,512]{1,0:T(4,128)S(1)}, u32[]{:S(2)}, u32[]{:S(2)}) collective-permute-start(f32[4,512]{1,0:T(4,128)S(1)} %shard_map.75.one_ref), channel_id=1, source_target_pairs={{0,8},{1,9},{2,10},{3,11},{4,12},{5,13},{6,14},{7,15},{8,0},{9,1},... | collective-permute-start | bytes 24584 | tf_op jit(solution)/shard_map/ppermute | solution.py:650
  38.3 3.7 %collective-permute-start.19 = (f32[4,512]{1,0:T(4,128)S(1)}, f32[4,512]{1,0:T(4,128)S(1)}, u32[]{:S(2)}, u32[]{:S(2)}) collective-permute-start(f32[4,512]{1,0:T(4,128)S(1)} %shard_map.77.one_ref), channel_id=1, source_target_pairs={{0,2},{1,3},{2,0},{3,1},{4,6},{5,7},{6,4},{7,5},{8,10},{9,11},{10,... | collective-permute-start | bytes 24584 | tf_op jit(solution)/shard_map/ppermute | solution.py:650
  41.9 1.2 %collective-permute-start.20 = (f32[8,512]{1,0:T(8,128)S(1)}, f32[8,512]{1,0:T(8,128)S(1)}, u32[]{:S(2)}, u32[]{:S(2)}) collective-permute-start(f32[8,512]{1,0:T(8,128)S(1)} %shard_map.79.mine_ref), channel_id=1, source_target_pairs={{1,0},{0,1},{3,2},{2,3},{5,4},{4,5},{7,6},{6,7},{9,8},{8,9},{11,10... | collective-permute-start | bytes 49160 | tf_op jit(solution)/shard_map/ppermute | solution.py:27

commit v10 on v9

--- a/solution.py
+++ b/solution.py
@@ -244,14 +244,16 @@
         write_edge(edges_ref, 0, [load_plane(out_ref, p, rows) for p in (0, planes - 1)], rows, v_ref)
 
 
-def next_alone_kernel(state_ref, first_ref, second_ref, v_ref, m_ref, edges2_ref, edges3_ref, held, moved):
+def next_alone_kernel(
+    state_ref, first_ref, second_ref, v_ref, m_ref, out_ref, edges2_ref, edges3_ref, held, moved
+):
     planes, orient, _ = state_ref.shape
     first = boltzmann(first_ref[...])
     second = boltzmann(second_ref[...])
     alone_step(state_ref, moved, range(planes), v_ref, None, 0)
     for p in range(planes):
-        held[p] = (first[p : p + 1] * second[p : p + 1] * mix(m_ref[...], moved[p])).astype(BF16)
-    alone_step(held, moved, (0, planes - 1), v_ref, edges2_ref, 0)
+        out_ref[p] = (first[p : p + 1] * second[p : p + 1] * mix(m_ref[...], moved[p])).astype(BF16)
+    alone_step(out_ref, moved, (0, planes - 1), v_ref, edges2_ref, 0)
     for p in (0, planes - 1):
         held[p] = (second[p : p + 1] * second[p : p + 1] * mix(m_ref[...], moved[p])).astype(BF16)
 
@@ -281,7 +283,7 @@
 
 
 def second_step_kernel(
-    core_ref, alone_ref, edge_ref, mine_ref, other_ref, first_ref, second_ref, v_ref, m_ref,
+    core_ref, alone_ref, later_ref, edge_ref, mine_ref, other_ref, first_ref, second_ref, v_ref, m_ref,
     face_low_ref, face_high_ref, next_ref, sent_near_ref, sent_far_ref, kept_ref, outer_ref, held, moved,
 ):
     planes, orient, _ = alone_ref.shape
@@ -306,36 +308,44 @@
             moved[3, rows, columns(t)] = (rate_plus * edge).astype(BF16)
 
     squared = first * first
-    for p in range(planes):
-        kept = alone_ref[p]
-        if p in (0, planes - 1):
-            arrived = squared[p : p + 1] * mix(matrix, moved[min(p, 1)])
-            kept = (kept.astype(F32) + arrived).astype(BF16)
-            (face_high_ref if p else face_low_ref)[0] = kept
-        held[p + 1] = kept
+    for p, slot, face_ref in ((0, 1, face_low_ref), (planes - 1, 2, face_high_ref)):
+        arrived = squared[p : p + 1] * mix(matrix, moved[slot - 1])
+        held[slot] = arrived.astype(BF16)
+        face_ref[0] = (alone_ref[p].astype(F32) + arrived).astype(BF16)
     held[0] = (beyond[0] * beyond[0] * mix(matrix, moved[2])).astype(BF16)
-    held[planes + 1] = (beyond[2] * beyond[2] * mix(matrix, moved[3])).astype(BF16)
-    count = planes + 2
+    held[3] = (beyond[2] * beyond[2] * mix(matrix, moved[3])).astype(BF16)
 
     @each_row_block(orient)
     def _(index):
         rows = rows_of(index)
         geo = geometry(v_ref, rows)
         _, rate_plus, rate_minus = face_parts(v_ref, rows)
-        loaded = [load_plane(held, p, rows) for p in range(count)]
-        for p in range(count):
-            before = loaded[p - 1] if p > 0 else None
-            after = loaded[p + 1] if p < count - 1 else None
-            store_plane(moved, p + 1, rows, drift(loaded[p], before, after, geo))
-        store_plane(moved, 0, rows, [rate_minus * tile.astype(F32) for tile in loaded[0]])
-        store_plane(moved, count + 1, rows, [rate_plus * tile.astype(F32) for tile in loaded[-1]])
+        below, low, high, above = (load_plane(held, p, rows) for p in range(4))
+        face_low, face_high = (load_plane(ref, 0, rows) for ref in (face_low_ref, face_high_ref))
+
+        def onward(rate, tiles):
+            return [rate * tile.astype(F32) for tile in tiles]
+
+        store_plane(moved, 0, rows, onward(rate_minus, below))
+        store_plane(moved, 1, rows, drift(below, None, face_low, geo))
+        store_plane(moved, 2, rows, drift(low, below, None, geo))
+        store_plane(moved, 3, rows, onward(rate_plus, low))
+        store_plane(moved, 4, rows, onward(rate_minus, high))
+        store_plane(moved, 5, rows, drift(high, None, above, geo))
+        store_plane(moved, 6, rows, drift(above, face_high, None, geo))
+        store_plane(moved, 7, rows, onward(rate_plus, above))
 
     cross = first * second
-    factors = [beyond[1] * beyond[5], beyond[0] * beyond[4]]
-    factors += [cross[p : p + 1] for p in range(planes)]
-    factors += [beyond[2] * beyond[6], beyond[3] * beyond[7]]
-    for p, factor in enumerate(factors):
-        next_ref[p] = (factor * mix(matrix, moved[p])).astype(BF16)
+    outer = ((0, 0, beyond[1] * beyond[5]), (1, 1, beyond[0] * beyond[4]))
+    outer += ((planes + 2, 6, beyond[2] * beyond[6]), (planes + 3, 7, beyond[3] * beyond[7]))
+    for p, slot, factor in outer:
+        next_ref[p] = (factor * mix(matrix, moved[slot])).astype(BF16)
+    slots = {0: 2, 1: 3, planes - 2: 4, planes - 1: 5}
+    for p in range(planes):
+        kept = later_ref[p]
+        if p in slots:
+            kept = (kept.astype(F32) + cross[p : p + 1] * mix(matrix, moved[slots[p]])).astype(BF16)
+        next_ref[p + 2] = kept
     for p in range(planes // 2):
         sent_ref = (sent_near_ref, sent_far_ref)[p]
         sent_ref[0] = next_ref[2 + (planes - 1) * (1 - core) + (2 * core - 1) * p]
@@ -616,8 +626,8 @@
         (edges1, others1, *[coded] * PAD, spread),
     )
     state, *_ = lax.optimization_barrier((alone, message1, weights))
-    edges2, edges3 = kernel_call(
-        next_alone_kernel, (plane, plane), (slab.shape, slab.shape), (state, own, partner, spread, matrix)
+    later, edges2, edges3 = kernel_call(
+        next_alone_kernel, (slab, plane, plane), (slab.shape, slab.shape), (state, own, partner, spread, matrix)
     )
     edges2, edges3, arrived0 = lax.optimization_barrier((edges2, edges3, arrived0))
     message2 = message([edges2, edges3], [swap_species(edges2), swap_species(edges3)])
@@ -630,8 +640,8 @@
         kernel_call(
             second_step_kernel,
             (plane, plane, wide(4), plane, plane, wide(half - planes), jax.ShapeDtypeStruct((2, cells), F32)),
-            (wide(2).shape, wide(4).shape),
-            (core_word, alone, edge0, arrived0, crossed0, own, partner, spread, matrix),
+            ((4, orient, cells), (8, orient, cells)),
+            (core_word, alone, later, edge0, arrived0, crossed0, own, partner, spread, matrix),
         )
     )
     arrived1, second_state = lax.optimization_barrier((arrived[0], second_state))

time: 43.8 us -> 43.3 us (0.989)
  Pallas kernels: 16.8 us -> 16.3 us
    pallas_call x17, Pallas kernels: 16.8 us -> 16.3 us  [kernel_call(): pl.pallas_call(kernel, out_shape=outs, in_specs=[smem if arg.dtype == jnp...]
where the time goes in v10:
time: 43.3 us; the launch traced here: 43.1 us
  Pallas kernels  16.3 us (38%)
  starting transfers between devices  15.7 us (36%)
  waiting for transfers between devices  9.46 us (22%)
  local copies, waits for them, and re-layouts  1.44 us (3%)
    pallas_call x17, Pallas kernels, kernel_call(): pl.pallas_call(kernel, out_shape=outs, in_specs=[smem if arg.dtype == jnp...  16.3 us
    ppermute x15, starting transfers between devices, swap_species(): return lax.ppermute(block, 'space', [(i ^ 1, i) for i in range(count)])  8.65 us
    ppermute x15, waiting for transfers between devices, swap_species(): return lax.ppermute(block, 'space', [(i ^ 1, i) for i in range(count)])  5.57 us
    ppermute x3, starting transfers between devices, exchange_faces(): return lax.ppermute(block, 'space', route)  5.31 us
    ppermute x3, waiting for transfers between devices, received(): lax.ppermute(value, 'space', [(i, i ^ distance) for i in range(count)])  3.88 us
    ppermute x3, starting transfers between devices, received(): lax.ppermute(value, 'space', [(i, i ^ distance) for i in range(count)])  1.77 us
    unnamed x11, local copies, waits for them, and re-layouts  1.44 us
  transfers between devices with their start and end apart: 21, of which 12 were waited for; matrix products, arithmetic and copies ran while one was open for 3% of the time, Pallas kernels for 36%

profile of v10, /device:TPU:0, one launch (start us, length us, event | category | flops | bytes accessed | tf_op | source)
XLA Modules:
  0.0 43.1 jit_solution(7264076206514488864)
XLA Ops:
  0.0 0.5 %collective-permute-start = (f32[4,512]{1,0:T(4,128)}, f32[4,512]{1,0:T(4,128)S(1)}, u32[]{:S(2)}, u32[]{:S(2)}) collective-permute-start(f32[4,512]{1,0:T(4,128)} %param.6), channel_id=1, source_target_pairs={{1,0},{0,1},{3,2},{2,3},{5,4},{4,5},{7,6},{6,7},{9,8},{8,9},{11,10... | collective-permute-start | bytes 24584 | tf_op jit(solution)/shard_map/ppermute | solution.py:27
  0.6 1.4 %copy.9 = bf16[256,4,512]{2,0,1:T(8,128)(2,1)S(1)} copy(bf16[256,4,512]{2,1,0:T(4,128)(2,1)} %param.7) | data formatting | bytes 2097152 | tf_op args[1]
  2.8 1.1 %collective-permute-done.1.other_ref = bf16[1,256,512]{2,1,0:T(8,128)(2,1)S(1)} collective-permute-done((bf16[1,256,512]{2,1,0:T(8,128)(2,1)S(1)}, bf16[1,256,512]{2,1,0:T(8,128)(2,1)S(1)}, u32[]{:S(2)}, u32[]{:S(2)}) %collective-permute-start.1) | collective-permute-done | bytes 262176 | tf_op jit(solution)/shard_map/ppermute | solution.py:27
  4.2 2.9 %collective-permute-start.6 = (bf16[1,272,512]{2,1,0:T(8,128)(2,1)S(1)}, bf16[1,272,512]{2,1,0:T(8,128)(2,1)S(1)}, u32[]{:S(2)}, u32[]{:S(2)}) collective-permute-start(bf16[1,272,512]{2,1,0:T(8,128)(2,1)S(1)} %shard_map.66), channel_id=1, source_target_pairs={{0,2},{1,15},{2,0},{3,5},{4,6},{5,3},{6,4},{7,9},{8,10},{9,7},{10,... | collective-permute-start | bytes 835592 | tf_op jit(solution)/shard_map/ppermute | solution.py:36
  7.1 2.0 %shard_map.67 = (bf16[4,256,512]{2,1,0:T(8,128)(2,1)S(1)}, bf16[1,256,512]{2,1,0:T(8,128)(2,1)S(1)}, bf16[1,256,512]{2,1,0:T(8,128)(2,1)S(1)}, bf16[1,256,512]{2,1,0:T(8,128)(2,1)S(1)}) custom-call(bf16[4,256,512]{2,1,0:T(8,128)(2,1)S(1)} %bitcast.8, f32[4,512]{1,0:T(4,128)S(1)} %get-tuple-element.118.fields_ref.first_ref.own_ref, ...), custom_call_target="tpu_custom_call" | custom-call | tf_op jit(solution)/shard_map/pallas_call | solution.py:557
  9.0 3.0 %collective-permute-start.4 = (bf16[1,256,512]{2,1,0:T(8,128)(2,1)S(1)}, bf16[1,256,512]{2,1,0:T(8,128)(2,1)S(1)}, u32[]{:S(2)}, u32[]{:S(2)}) collective-permute-start(bf16[1,256,512]{2,1,0:T(8,128)(2,1)S(1)} %get-tuple-element.72), channel_id=1, source_target_pairs={{1,0},{0,1},{3,2},{2,3},{5,4},{4,5},{7,6},{6,7},{9,8},{8,9},{11,10... | collective-permute-start | bytes 786440 | tf_op jit(solution)/shard_map/ppermute | solution.py:27
  12.1 0.4 %collective-permute-start.2 = (bf16[1,256,512]{2,1,0:T(8,128)(2,1)S(1)}, bf16[1,256,512]{2,1,0:T(8,128)(2,1)S(1)}, u32[]{:S(2)}, u32[]{:S(2)}) collective-permute-start(bf16[1,256,512]{2,1,0:T(8,128)(2,1)S(1)} %get-tuple-element.69.mine_ref), channel_id=1, source_target_pairs={{1,0},{0,1},{3,2},{2,3},{5,4},{4,5},{7,6},{6,7},{9,8},{8,9},{11,10... | collective-permute-start | bytes 786440 | tf_op jit(solution)/shard_map/ppermute | solution.py:27
  12.5 0.6 %shard_map.68 = (bf16[4,256,512]{2,1,0:T(8,128)(2,1)S(1)}, bf16[2,256,512]{2,1,0:T(8,128)(2,1)S(1)}) custom-call(s32[1]{0:T(128)} %bitcast.core_ref, bf16[4,256,512]{2,1,0:T(8,128)(2,1)S(1)} %collective-permute-done.3.partner_ref, bf16[4,256,512]{2,1,0:T(8,128)(2,1)S(1)} %bitcast.9, bf16[256,256]{1,0:T(8,128)(2,1)S(1)} %get-tuple-element.70.turned_ref), custom_call_target="tpu_custom_call" | custom-call | tf_op jit(solution)/shard_map/pallas_call | solution.py:557
  13.2 0.4 collective-permute-done.5.refs_2_
  13.5 0.4 collective-permute-done.2.other_ref
  14.1 2.8 %shard_map.70 = (bf16[4,256,512]{2,1,0:T(8,128)(2,1)S(1)}, bf16[1,256,512]{2,1,0:T(8,128)(2,1)S(1)}, bf16[1,256,512]{2,1,0:T(8,128)(2,1)S(1)}) custom-call(bf16[4,256,512]{2,1,0:T(8,128)(2,1)S(1)} %get-tuple-element.81.state_ref.alone_ref, f32[4,512]{1,0:T(4,128)S(1)} %get-tuple-element.118.fields_ref.first_ref.own_ref, ...), custom_call_target="tpu_custom_call" | custom-call | tf_op jit(solution)/shard_map/pallas_call | solution.py:557
  16.9 0.9 %collective-permute-start.7 = (bf16[1,256,512]{2,1,0:T(8,128)(2,1)S(1)}, bf16[1,256,512]{2,1,0:T(8,128)(2,1)S(1)}, u32[]{:S(2)}, u32[]{:S(2)}) collective-permute-start(bf16[1,256,512]{2,1,0:T(8,128)(2,1)S(1)} %get-tuple-element.79.refs_0_), channel_id=1, source_target_pairs={{1,0},{0,1},{3,2},{2,3},{5,4},{4,5},{7,6},{6,7},{9,8},{8,9},{11,10... | collective-permute-start | bytes 786440 | tf_op jit(solution)/shard_map/ppermute | solution.py:27
  17.9 0.4 %collective-permute-start.10 = (bf16[1,272,512]{2,1,0:T(8,128)(2,1)S(1)}, bf16[1,272,512]{2,1,0:T(8,128)(2,1)S(1)}, u32[]{:S(2)}, u32[]{:S(2)}) collective-permute-start(bf16[1,272,512]{2,1,0:T(8,128)(2,1)S(1)} %collective-permute-done.6.mine_ref), channel_id=1, source_target_pairs={{1,0},{0,1},{3,2},{2,3},{5,4},{4,5},{7,6},{6,7},{9,8},{8,9},{11,10... | collective-permute-start | bytes 835592 | tf_op jit(solution)/shard_map/ppermute | solution.py:27
  18.4 0.7 %collective-permute-done.7.refs_2_ = bf16[1,256,512]{2,1,0:T(8,128)(2,1)S(1)} collective-permute-done((bf16[1,256,512]{2,1,0:T(8,128)(2,1)S(1)}, bf16[1,256,512]{2,1,0:T(8,128)(2,1)S(1)}, u32[]{:S(2)}, u32[]{:S(2)}) %collective-permute-start.7) | collective-permute-done | bytes 262176 | tf_op jit(solution)/shard_map/ppermute | solution.py:27
  19.0 0.4 collective-permute-done.8.refs_3_
  19.5 2.4 %collective-permute-start.9 = (bf16[2,288,512]{2,1,0:T(8,128)(2,1)S(1)}, bf16[2,288,512]{2,1,0:T(8,128)(2,1)S(1)}, u32[]{:S(2)}, u32[]{:S(2)}) collective-permute-start(bf16[2,288,512]{2,1,0:T(8,128)(2,1)S(1)} %shard_map.71), channel_id=1, source_target_pairs={{0,2},{1,15},{2,0},{3,5},{4,6},{5,3},{6,4},{7,9},{8,10},{9,7},{10,... | collective-permute-start | bytes 1769480 | tf_op jit(solution)/shard_map/ppermute | solution.py:36
  21.8 2.7 %shard_map.72 = (bf16[1,256,512]{2,1,0:T(8,128)(2,1)S(1)}, bf16[1,256,512]{2,1,0:T(8,128)(2,1)S(1)}, bf16[8,256,512]{2,1,0:T(8,128)(2,1)S(1)}, bf16[1,256,512]{2...) custom-call(s32[1]{0:T(128)} %bitcast.core_ref, ...), custom_call_target="tpu_custom_call" | custom-call | tf_op jit(solution)/shard_map/pallas_call | solution.py:557
  24.5 1.8 %collective-permute-start.14 = (bf16[1,288,512]{2,1,0:T(8,128)(2,1)S(1)}, bf16[1,288,512]{2,1,0:T(8,128)(2,1)S(1)}, u32[]{:S(2)}, u32[]{:S(2)}) collective-permute-start(bf16[1,288,512]{2,1,0:T(8,128)(2,1)S(1)} %collective-permute-done.11.message_ref.mine_ref), channel_id=1, source_target_pairs={{1,0},{0,1},{3,2},{2,3},{5,4},{4,5},{7,6},{6,7},{9,8},{8,9},{11,10... | collective-permute-start | bytes 884744 | tf_op jit(solution)/shard_map/ppermute | solution.py:27
  26.4 0.4 %collective-permute-start.13 = (bf16[1,256,512]{2,1,0:T(8,128)(2,1)S(1)}, bf16[1,256,512]{2,1,0:T(8,128)(2,1)S(1)}, u32[]{:S(2)}, u32[]{:S(2)}) collective-permute-start(bf16[1,256,512]{2,1,0:T(8,128)(2,1)S(1)} %get-tuple-element.90), channel_id=1, source_target_pairs={{1,0},{0,1},{3,2},{2,3},{5,4},{4,5},{7,6},{6,7},{9,8},{8,9},{11,10... | collective-permute-start | bytes 786440 | tf_op jit(solution)/shard_map/ppermute | solution.py:27
  26.9 1.1 %collective-permute-done.12.near_ref = bf16[1,256,512]{2,1,0:T(8,128)(2,1)S(1)} collective-permute-done((bf16[1,256,512]{2,1,0:T(8,128)(2,1)S(1)}, bf16[1,256,512]{2,1,0:T(8,128)(2,1)S(1)}, u32[]{:S(2)}, u32[]{:S(2)}) %collective-permute-start.12) | collective-permute-done | bytes 262176 | tf_op jit(solution)/shard_map/ppermute | solution.py:27
  27.9 0.4 collective-permute-done.13.far_ref
  28.3 0.6 %shard_map.73 = (f32[2,512]{1,0:T(2,128)S(1)}, f32[4,512]{1,0:T(4,128)S(1)}) custom-call(s32[1]{0:T(128)} %bitcast.core_ref, bf16[2,256,512]{2,1,0:T(8,128)(2,1)S(1)} %get-tuple-element.84.own_ref, bf16[1,256,512]{2,1,0:T(8,128)(2,1)S(1)} %collective-permute-done.12.near_ref, bf16[1,256,512]{2,1,0:T(8,128)(2,1)S(1)} %collective-permute-done.13.far_ref, ...), custom_call_target="tpu_custom_call" | custom-call | tf_op jit(solution)/shard_map/pallas_call | solution.py:557
  28.9 0.4 collective-permute-start.17
  29.6 3.0 %shard_map.74.held_ref = bf16[6,256,512]{2,1,0:T(8,128)(2,1)S(1)} custom-call(bf16[8,256,512]{2,1,0:T(8,128)(2,1)S(1)} %get-tuple-element.98.held_ref, bf16[1,288,512]{2,1,0:T(8,128)(2,1)S(1)} %collective-permute-done.11.message_ref.mine_ref, bf16[1,288,512]{2,1,0:T(8,128)(2,1)S(1)} %collective-permute-done.14.other_ref, ...), custom_call_target="tpu_custom_call" | custom-call | tf_op jit(solution)/shard_map/pallas_call | solution.py:557
  32.6 0.5 %collective-permute-done.15.two_ref = f32[4,512]{1,0:T(4,128)S(1)} collective-permute-done((f32[4,512]{1,0:T(4,128)S(1)}, f32[4,512]{1,0:T(4,128)S(1)}, u32[]{:S(2)}, u32[]{:S(2)}) %collective-permute-start.15) | collective-permute-done | bytes 8224 | tf_op jit(solution)/shard_map/ppermute | solution.py:660
  33.1 1.6 %collective-permute-start.16 = (f32[4,512]{1,0:T(4,128)S(1)}, f32[4,512]{1,0:T(4,128)S(1)}, u32[]{:S(2)}, u32[]{:S(2)}) collective-permute-start(f32[4,512]{1,0:T(4,128)S(1)} %shard_map.75.one_ref), channel_id=1, source_target_pairs={{0,8},{1,9},{2,10},{3,11},{4,12},{5,13},{6,14},{7,15},{8,0},{9,1},... | collective-permute-start | bytes 24584 | tf_op jit(solution)/shard_map/ppermute | solution.py:660
  34.6 1.6 %shard_map.76.shared_ref = f32[4,512]{1,0:T(4,128)S(1)} custom-call(bf16[6,256,512]{2,1,0:T(8,128)(2,1)S(1)} %shard_map.74.held_ref, f32[4,512]{1,0:T(4,128)S(1)} %get-tuple-element.117.partner_ref.second_ref, f32[4,256,128]{2,1,0:T(8,128)S(1)} %get-tuple-element.65.refs_1_.v_ref.refs_2_.refs_4_, bf16[4,256,512]{2,1,0:T(8,128)(2,1)S(1)} %get-tuple-element.75.weight_ref, ...), custom_call_target="tpu_custom_call" | custom-call | tf_op jit(solution)/shard_map/pallas_call | solution.py:557
  36.3 1.4 %collective-permute-done.16.two_ref = f32[4,512]{1,0:T(4,128)S(1)} collective-permute-done((f32[4,512]{1,0:T(4,128)S(1)}, f32[4,512]{1,0:T(4,128)S(1)}, u32[]{:S(2)}, u32[]{:S(2)}) %collective-permute-start.16) | collective-permute-done | bytes 8224 | tf_op jit(solution)/shard_map/ppermute | solution.py:660
  37.7 1.6 %shard_map.78 = (f32[4,512]{1,0:T(4,128)S(1)}, f32[4,512]{1,0:T(4,128)S(1)}) custom-call(s32[1]{0:T(128)} %bitcast.core_ref, bf16[2,288,512]{2,1,0:T(8,128)(2,1)S(1)} %collective-permute-done.9.message_ref, bf16[4,256,512]{2,1,0:T(8,128)(2,1)S(1)} %get-tuple-element.75.weight_ref, bf16[2,256,512]{2,1,0:T(8,128)(2,1)S(1)} %get-tuple-element.111.own_weight_ref, ...), custom_call_target="tpu_custom_call" | custom-call | tf_op jit(solution)/shard_map/pallas_call | solution.py:557
  39.4 2.0 %collective-permute-done.19.two_ref = f32[4,512]{1,0:T(4,128)S(1)} collective-permute-done((f32[4,512]{1,0:T(4,128)S(1)}, f32[4,512]{1,0:T(4,128)S(1)}, u32[]{:S(2)}, u32[]{:S(2)}) %collective-permute-start.19) | collective-permute-done | bytes 8224 | tf_op jit(solution)/shard_map/ppermute | solution.py:660
  41.3 1.2 %collective-permute-done.20.arrived_ref = f32[8,512]{1,0:T(8,128)S(1)} collective-permute-done((f32[8,512]{1,0:T(8,128)S(1)}, f32[8,512]{1,0:T(8,128)S(1)}, u32[]{:S(2)}, u32[]{:S(2)}) %collective-permute-start.20) | collective-permute-done | bytes 16416 | tf_op jit(solution)/shard_map/ppermute | solution.py:27
  42.5 0.6 %shard_map.80 = f32[4,512]{1,0:T(4,128)} custom-call(f32[4,512]{1,0:T(4,128)S(1)} %get-tuple-element.113.kept_ref, f32[8,512]{1,0:T(8,128)S(1)} %shard_map.79.mine_ref, f32[8,512]{1,0:T(8,128)S(1)} %collective-permute-done.20.arrived_ref), custom_call_target="tpu_custom_call" | custom-call | tf_op jit(solution)/shard_map/pallas_call | solution.py:557
  (40 shorter events, 2.0 us)
Async XLA Ops:
  0.0 2.0 %copy-start.4 = (f32[4,512]{1,0:T(4,128)S(1)}, f32[4,512]{1,0:T(4,128)}, u32[]{:S(2)}) copy-start(f32[4,512]{1,0:T(4,128)} %param.6) | copy-start | bytes 24580
  0.0 2.1 %copy-start.2 = (f32[3,256]{1,0:T(4,128)S(1)}, f32[3,256]{1,0:T(4,128)}, u32[]{:S(2)}) copy-start(f32[3,256]{1,0:T(4,128)} %directions_ref.1) | copy-start | bytes 9220
  0.0 2.5 %copy-start.3 = (f32[256]{0:T(256)S(1)}, f32[256]{0:T(256)}, u32[]{:S(2)}) copy-start(f32[256]{0:T(256)} %param.11) | copy-start | bytes 3076
  0.0 2.5 %copy-start = (bf16[256,256]{1,0:T(8,128)(2,1)S(1)}, bf16[256,256]{1,0:T(8,128)(2,1)}, u32[]{:S(2)}) copy-start(bf16[256,256]{1,0:T(8,128)(2,1)} %synthesis_ref.1) | copy-start | bytes 393220
  0.0 2.5 %copy-start.1 = (bf16[256,256]{1,0:T(8,128)(2,1)S(1)}, bf16[256,256]{1,0:T(8,128)(2,1)}, u32[]{:S(2)}) copy-start(bf16[256,256]{1,0:T(8,128)(2,1)} %analysis_ref.1) | copy-start | bytes 393220
  0.0 2.0 %collective-permute-start = (f32[4,512]{1,0:T(4,128)}, f32[4,512]{1,0:T(4,128)S(1)}, u32[]{:S(2)}, u32[]{:S(2)}) collective-permute-start(f32[4,512]{1,0:T(4,128)} %param.6), channel_id=1, source_target_pairs={{1,0},{0,1},{3,2},{2,3},{5,4},{4,5},{7,6},{6,7},{9,8},{8,9},{11,10... | collective-permute-start | bytes 24584 | tf_op jit(solution)/shard_map/ppermute | solution.py:27
  2.3 1.6 %collective-permute-start.1 = (bf16[1,256,512]{2,1,0:T(8,128)(2,1)S(1)}, bf16[1,256,512]{2,1,0:T(8,128)(2,1)S(1)}, u32[]{:S(2)}, u32[]{:S(2)}) collective-permute-start(bf16[1,256,512]{2,1,0:T(8,128)(2,1)S(1)} %get-tuple-element.61.mine_ref.edge_ref), channel_id=1, source_target_pairs={{1,0},{0,1},{3,2},{2,3},{5,4},{4,5},{7,6},{6,7},{9,8},{8,9},{11,10... | collective-permute-start | bytes 786440 | tf_op jit(solution)/shard_map/ppermute | solution.py:27
  4.0 8.5 %collective-permute-start.3 = (bf16[4,256,512]{2,1,0:T(8,128)(2,1)S(1)}, bf16[4,256,512]{2,1,0:T(8,128)(2,1)S(1)}, u32[]{:S(2)}, u32[]{:S(2)}) collective-permute-start(bf16[4,256,512]{2,1,0:T(8,128)(2,1)S(1)} %bitcast.7), channel_id=1, source_target_pairs={{1,0},{0,1},{3,2},{2,3},{5,4},{4,5},{7,6},{6,7},{9,8},{8,9},{11,10... | collective-permute-start | bytes 3145736 | tf_op jit(solution)/shard_map/ppermute | solution.py:27
  4.2 12.7 %collective-permute-start.6 = (bf16[1,272,512]{2,1,0:T(8,128)(2,1)S(1)}, bf16[1,272,512]{2,1,0:T(8,128)(2,1)S(1)}, u32[]{:S(2)}, u32[]{:S(2)}) collective-permute-start(bf16[1,272,512]{2,1,0:T(8,128)(2,1)S(1)} %shard_map.66), channel_id=1, source_target_pairs={{0,2},{1,15},{2,0},{3,5},{4,6},{5,3},{6,4},{7,9},{8,10},{9,7},{10,... | collective-permute-start | bytes 835592 | tf_op jit(solution)/shard_map/ppermute | solution.py:36
  9.0 4.1 %collective-permute-start.4 = (bf16[1,256,512]{2,1,0:T(8,128)(2,1)S(1)}, bf16[1,256,512]{2,1,0:T(8,128)(2,1)S(1)}, u32[]{:S(2)}, u32[]{:S(2)}) collective-permute-start(bf16[1,256,512]{2,1,0:T(8,128)(2,1)S(1)} %get-tuple-element.72), channel_id=1, source_target_pairs={{1,0},{0,1},{3,2},{2,3},{5,4},{4,5},{7,6},{6,7},{9,8},{8,9},{11,10... | collective-permute-start | bytes 786440 | tf_op jit(solution)/shard_map/ppermute | solution.py:27
  12.0 1.5 %collective-permute-start.5 = (bf16[1,256,512]{2,1,0:T(8,128)(2,1)S(1)}, bf16[1,256,512]{2,1,0:T(8,128)(2,1)S(1)}, u32[]{:S(2)}, u32[]{:S(2)}) collective-permute-start(bf16[1,256,512]{2,1,0:T(8,128)(2,1)S(1)} %get-tuple-element.73), channel_id=1, source_target_pairs={{1,0},{0,1},{3,2},{2,3},{5,4},{4,5},{7,6},{6,7},{9,8},{8,9},{11,10... | collective-permute-start | bytes 786440 | tf_op jit(solution)/shard_map/ppermute | solution.py:27
  12.1 1.8 %collective-permute-start.2 = (bf16[1,256,512]{2,1,0:T(8,128)(2,1)S(1)}, bf16[1,256,512]{2,1,0:T(8,128)(2,1)S(1)}, u32[]{:S(2)}, u32[]{:S(2)}) collective-permute-start(bf16[1,256,512]{2,1,0:T(8,128)(2,1)S(1)} %get-tuple-element.69.mine_ref), channel_id=1, source_target_pairs={{1,0},{0,1},{3,2},{2,3},{5,4},{4,5},{7,6},{6,7},{9,8},{8,9},{11,10... | collective-permute-start | bytes 786440 | tf_op jit(solution)/shard_map/ppermute | solution.py:27
  14.0 10.6 %collective-permute-start.11 = (bf16[1,288,512]{2,1,0:T(8,128)(2,1)S(1)}, bf16[1,288,512]{2,1,0:T(8,128)(2,1)S(1)}, u32[]{:S(2)}, u32[]{:S(2)}) collective-permute-start(bf16[1,288,512]{2,1,0:T(8,128)(2,1)S(1)} %shard_map.69), channel_id=1, source_target_pairs={{0,2},{1,15},{2,0},{3,5},{4,6},{5,3},{6,4},{7,9},{8,10},{9,7},{10,... | collective-permute-start | bytes 884744 | tf_op jit(solution)/shard_map/ppermute | solution.py:36
  16.9 2.1 %collective-permute-start.7 = (bf16[1,256,512]{2,1,0:T(8,128)(2,1)S(1)}, bf16[1,256,512]{2,1,0:T(8,128)(2,1)S(1)}, u32[]{:S(2)}, u32[]{:S(2)}) collective-permute-start(bf16[1,256,512]{2,1,0:T(8,128)(2,1)S(1)} %get-tuple-element.79.refs_0_), channel_id=1, source_target_pairs={{1,0},{0,1},{3,2},{2,3},{5,4},{4,5},{7,6},{6,7},{9,8},{8,9},{11,10... | collective-permute-start | bytes 786440 | tf_op jit(solution)/shard_map/ppermute | solution.py:27
  17.8 1.5 %collective-permute-start.8 = (bf16[1,256,512]{2,1,0:T(8,128)(2,1)S(1)}, bf16[1,256,512]{2,1,0:T(8,128)(2,1)S(1)}, u32[]{:S(2)}, u32[]{:S(2)}) collective-permute-start(bf16[1,256,512]{2,1,0:T(8,128)(2,1)S(1)} %get-tuple-element.80.refs_1_), channel_id=1, source_target_pairs={{1,0},{0,1},{3,2},{2,3},{5,4},{4,5},{7,6},{6,7},{9,8},{8,9},{11,10... | collective-permute-start | bytes 786440 | tf_op jit(solution)/shard_map/ppermute | solution.py:27
  17.9 3.9 %collective-permute-start.10 = (bf16[1,272,512]{2,1,0:T(8,128)(2,1)S(1)}, bf16[1,272,512]{2,1,0:T(8,128)(2,1)S(1)}, u32[]{:S(2)}, u32[]{:S(2)}) collective-permute-start(bf16[1,272,512]{2,1,0:T(8,128)(2,1)S(1)} %collective-permute-done.6.mine_ref), channel_id=1, source_target_pairs={{1,0},{0,1},{3,2},{2,3},{5,4},{4,5},{7,6},{6,7},{9,8},{8,9},{11,10... | collective-permute-start | bytes 835592 | tf_op jit(solution)/shard_map/ppermute | solution.py:27
  19.5 18.2 %collective-permute-start.9 = (bf16[2,288,512]{2,1,0:T(8,128)(2,1)S(1)}, bf16[2,288,512]{2,1,0:T(8,128)(2,1)S(1)}, u32[]{:S(2)}, u32[]{:S(2)}) collective-permute-start(bf16[2,288,512]{2,1,0:T(8,128)(2,1)S(1)} %shard_map.71), channel_id=1, source_target_pairs={{0,2},{1,15},{2,0},{3,5},{4,6},{5,3},{6,4},{7,9},{8,10},{9,7},{10,... | collective-permute-start | bytes 1769480 | tf_op jit(solution)/shard_map/ppermute | solution.py:36
  24.5 3.8 %collective-permute-start.14 = (bf16[1,288,512]{2,1,0:T(8,128)(2,1)S(1)}, bf16[1,288,512]{2,1,0:T(8,128)(2,1)S(1)}, u32[]{:S(2)}, u32[]{:S(2)}) collective-permute-start(bf16[1,288,512]{2,1,0:T(8,128)(2,1)S(1)} %collective-permute-done.11.message_ref.mine_ref), channel_id=1, source_target_pairs={{1,0},{0,1},{3,2},{2,3},{5,4},{4,5},{7,6},{6,7},{9,8},{8,9},{11,10... | collective-permute-start | bytes 884744 | tf_op jit(solution)/shard_map/ppermute | solution.py:27
  26.3 1.6 %collective-permute-start.12 = (bf16[1,256,512]{2,1,0:T(8,128)(2,1)S(1)}, bf16[1,256,512]{2,1,0:T(8,128)(2,1)S(1)}, u32[]{:S(2)}, u32[]{:S(2)}) collective-permute-start(bf16[1,256,512]{2,1,0:T(8,128)(2,1)S(1)} %get-tuple-element.89), channel_id=1, source_target_pairs={{1,0},{0,1},{3,2},{2,3},{5,4},{4,5},{7,6},{6,7},{9,8},{8,9},{11,10... | collective-permute-start | bytes 786440 | tf_op jit(solution)/shard_map/ppermute | solution.py:27
  26.4 1.9 %collective-permute-start.13 = (bf16[1,256,512]{2,1,0:T(8,128)(2,1)S(1)}, bf16[1,256,512]{2,1,0:T(8,128)(2,1)S(1)}, u32[]{:S(2)}, u32[]{:S(2)}) collective-permute-start(bf16[1,256,512]{2,1,0:T(8,128)(2,1)S(1)} %get-tuple-element.90), channel_id=1, source_target_pairs={{1,0},{0,1},{3,2},{2,3},{5,4},{4,5},{7,6},{6,7},{9,8},{8,9},{11,10... | collective-permute-start | bytes 786440 | tf_op jit(solution)/shard_map/ppermute | solution.py:27
  28.9 5.8 %collective-permute-start.17 = (bf16[1,256,512]{2,1,0:T(8,128)(2,1)S(1)}, bf16[1,256,512]{2,1,0:T(8,128)(2,1)S(1)}, u32[]{:S(2)}, u32[]{:S(2)}) collective-permute-start(bf16[1,256,512]{2,1,0:T(8,128)(2,1)S(1)} %get-tuple-element.104.own_low_ref), channel_id=1, source_target_pairs={{1,0},{0,1},{3,2},{2,3},{5,4},{4,5},{7,6},{6,7},{9,8},{8,9},{11,10... | collective-permute-start | bytes 786440 | tf_op jit(solution)/shard_map/ppermute | solution.py:27
  29.3 5.4 %collective-permute-start.18 = (bf16[1,256,512]{2,1,0:T(8,128)(2,1)S(1)}, bf16[1,256,512]{2,1,0:T(8,128)(2,1)S(1)}, u32[]{:S(2)}, u32[]{:S(2)}) collective-permute-start(bf16[1,256,512]{2,1,0:T(8,128)(2,1)S(1)} %get-tuple-element.107.own_high_ref), channel_id=1, source_target_pairs={{1,0},{0,1},{3,2},{2,3},{5,4},{4,5},{7,6},{6,7},{9,8},{8,9},{11,10... | collective-permute-start | bytes 786440 | tf_op jit(solution)/shard_map/ppermute | solution.py:27
  29.4 3.7 %collective-permute-start.15 = (f32[4,512]{1,0:T(4,128)S(1)}, f32[4,512]{1,0:T(4,128)S(1)}, u32[]{:S(2)}, u32[]{:S(2)}) collective-permute-start(f32[4,512]{1,0:T(4,128)S(1)} %get-tuple-element.93.one_ref), channel_id=1, source_target_pairs={{0,4},{1,5},{2,6},{3,7},{4,0},{5,1},{6,2},{7,3},{8,12},{9,13},{10,... | collective-permute-start | bytes 24584 | tf_op jit(solution)/shard_map/ppermute | solution.py:660
  33.1 4.6 %collective-permute-start.16 = (f32[4,512]{1,0:T(4,128)S(1)}, f32[4,512]{1,0:T(4,128)S(1)}, u32[]{:S(2)}, u32[]{:S(2)}) collective-permute-start(f32[4,512]{1,0:T(4,128)S(1)} %shard_map.75.one_ref), channel_id=1, source_target_pairs={{0,8},{1,9},{2,10},{3,11},{4,12},{5,13},{6,14},{7,15},{8,0},{9,1},... | collective-permute-start | bytes 24584 | tf_op jit(solution)/shard_map/ppermute | solution.py:660
  37.7 3.7 %collective-permute-start.19 = (f32[4,512]{1,0:T(4,128)S(1)}, f32[4,512]{1,0:T(4,128)S(1)}, u32[]{:S(2)}, u32[]{:S(2)}) collective-permute-start(f32[4,512]{1,0:T(4,128)S(1)} %shard_map.77.one_ref), channel_id=1, source_target_pairs={{0,2},{1,3},{2,0},{3,1},{4,6},{5,7},{6,4},{7,5},{8,10},{9,11},{10,... | collective-permute-start | bytes 24584 | tf_op jit(solution)/shard_map/ppermute | solution.py:660
  41.3 1.2 %collective-permute-start.20 = (f32[8,512]{1,0:T(8,128)S(1)}, f32[8,512]{1,0:T(8,128)S(1)}, u32[]{:S(2)}, u32[]{:S(2)}) collective-permute-start(f32[8,512]{1,0:T(8,128)S(1)} %shard_map.79.mine_ref), channel_id=1, source_target_pairs={{1,0},{0,1},{3,2},{2,3},{5,4},{4,5},{7,6},{6,7},{9,8},{8,9},{11,10... | collective-permute-start | bytes 49160 | tf_op jit(solution)/shard_map/ppermute | solution.py:27

commit v11 on v10

--- a/solution.py
+++ b/solution.py
@@ -616,22 +616,20 @@
     weights, own_weights = kernel_call(
         weight_kernel, (slab, wide(2 - planes)), (), (core_word, swap_species(start), start, turned)
     )
-    others1, weights, *partner_inner = lax.optimization_barrier(
-        (swap_species(edges1), weights, *map(swap_species, inner))
-    )
+    later, edges2, edges3 = kernel_call(
+        next_alone_kernel, (slab, plane, plane), (slab.shape, slab.shape), (alone, own, partner, spread, matrix)
+    )
+    edges1, edges2 = lax.optimization_barrier((edges1, edges2))
+    others1, weights = lax.optimization_barrier((swap_species(edges1), weights))
     message1 = kernel_call(
         first_message_kernel,
         jax.ShapeDtypeStruct((1, orient + 16 * PAD, cells), BF16),
         (),
         (edges1, others1, *[coded] * PAD, spread),
     )
-    state, *_ = lax.optimization_barrier((alone, message1, weights))
-    later, edges2, edges3 = kernel_call(
-        next_alone_kernel, (slab, plane, plane), (slab.shape, slab.shape), (state, own, partner, spread, matrix)
-    )
-    edges2, edges3, arrived0 = lax.optimization_barrier((edges2, edges3, arrived0))
     message2 = message([edges2, edges3], [swap_species(edges2), swap_species(edges3)])
     arrived = [exchange_faces(message1), exchange_faces(message2)]
+    arrived0, _ = lax.optimization_barrier((arrived0, message2))
     crossed0 = swap_species(arrived0)
 
     alone, *_ = lax.optimization_barrier((alone, message1, message2))
@@ -645,8 +643,10 @@
         )
     )
     arrived1, second_state = lax.optimization_barrier((arrived[0], second_state))
-    *moving, _ = lax.optimization_barrier((*sent_half, arrived1))
-    *partner_half, crossed1 = lax.optimization_barrier((*map(swap_species, moving), swap_species(arrived1)))
+    *moving, first_inner, _ = lax.optimization_barrier((*sent_half, inner[0], arrived1))
+    *partner_half, partner_first, crossed1 = lax.optimization_barrier(
+        (*map(swap_species, moving), swap_species(first_inner), swap_species(arrived1))
+    )
     density = jax.ShapeDtypeStruct((planes, cells), F32)
     met, partition = kernel_call(
         middle_kernel,
@@ -664,7 +664,9 @@
         block, after = received(value, distance, after)
         return kernel_call(add_kernel, density, (), (value, block)), after
 
-    *faces, second_state, _ = lax.optimization_barrier((*faces, second_state, met))
+    second_state, _, *moving = lax.optimization_barrier((second_state, met, *faces, *inner[1:]))
+    faces, inner = moving[:2], moving[2:]
+    partner_inner = [partner_first] + [swap_species(block) for block in inner]
     partner_faces = [swap_species(block) for block in faces]
     third_state = kernel_call(
         third_step_kernel,

time: 43.3 us -> 50.1 us (1.16)
  waiting for transfers between devices: 9.46 us -> 20.5 us
  starting transfers between devices: 15.7 us -> 11.6 us
    ppermute x3, waiting for transfers between devices: 0.01 us -> 11.1 us  [exchange_faces(): return lax.ppermute(block, 'space', route)]
    ppermute x15, starting transfers between devices: 8.65 us -> 6.49 us  [swap_species(): return lax.ppermute(block, 'space', [(i ^ 1, i) for i in range(count)])]
    ppermute x3, starting transfers between devices: 5.31 us -> 4.07 us  [exchange_faces(): return lax.ppermute(block, 'space', route)]
    ppermute x15, waiting for transfers between devices: 5.57 us -> 4.72 us  [swap_species(): return lax.ppermute(block, 'space', [(i ^ 1, i) for i in range(count)])]
    ppermute x3, starting transfers between devices: 1.77 us -> 1.05 us  [received(): lax.ppermute(value, 'space', [(i, i ^ distance) for i in range(count)])]
    ppermute x3, waiting for transfers between devices: 3.88 us -> 4.6 us  [received(): lax.ppermute(value, 'space', [(i, i ^ distance) for i in range(count)])]
  transfers between devices with their start and end apart: 21 -> 21, of which waited for: 12 -> 13; matrix products, arithmetic and copies ran while one was open for 3% -> 3% of each run, Pallas kernels for 36% -> 31%
where the time goes in v11:
time: 50.1 us; the launch traced here: 50 us
  waiting for transfers between devices  20.5 us (41%)
  Pallas kernels  16.3 us (33%)
  starting transfers between devices  11.6 us (23%)
  local copies, waits for them, and re-layouts  1.44 us (3%)
    pallas_call x17, Pallas kernels, kernel_call(): pl.pallas_call(kernel, out_shape=outs, in_specs=[smem if arg.dtype == jnp...  16.3 us
    ppermute x3, waiting for transfers between devices, exchange_faces(): return lax.ppermute(block, 'space', route)  11.1 us
    ppermute x15, starting transfers between devices, swap_species(): return lax.ppermute(block, 'space', [(i ^ 1, i) for i in range(count)])  6.49 us
    ppermute x15, waiting for transfers between devices, swap_species(): return lax.ppermute(block, 'space', [(i ^ 1, i) for i in range(count)])  4.72 us
    ppermute x3, waiting for transfers between devices, received(): lax.ppermute(value, 'space', [(i, i ^ distance) for i in range(count)])  4.6 us
    ppermute x3, starting transfers between devices, exchange_faces(): return lax.ppermute(block, 'space', route)  4.07 us
    unnamed x11, local copies, waits for them, and re-layouts  1.44 us
    ppermute x3, starting transfers between devices, received(): lax.ppermute(value, 'space', [(i, i ^ distance) for i in range(count)])  1.05 us
  transfers between devices with their start and end apart: 21, of which 13 were waited for; matrix products, arithmetic and copies ran while one was open for 3% of the time, Pallas kernels for 31%

profile of v11, /device:TPU:0, one launch (start us, length us, event | category | flops | bytes accessed | tf_op | source)
XLA Modules:
  0.0 50.0 jit_solution(10641417418012145877)
XLA Ops:
  0.0 0.5 %collective-permute-start = (f32[4,512]{1,0:T(4,128)}, f32[4,512]{1,0:T(4,128)S(1)}, u32[]{:S(2)}, u32[]{:S(2)}) collective-permute-start(f32[4,512]{1,0:T(4,128)} %param.6), channel_id=1, source_target_pairs={{1,0},{0,1},{3,2},{2,3},{5,4},{4,5},{7,6},{6,7},{9,8},{8,9},{11,10... | collective-permute-start | bytes 24584 | tf_op jit(solution)/shard_map/ppermute | solution.py:27
  0.6 1.4 %copy.9 = bf16[256,4,512]{2,0,1:T(8,128)(2,1)S(1)} copy(bf16[256,4,512]{2,1,0:T(4,128)(2,1)} %param.7) | data formatting | bytes 2097152 | tf_op args[1]
  2.5 0.3 shard_map.65
  2.8 1.1 %collective-permute-done.1.other_ref = bf16[1,256,512]{2,1,0:T(8,128)(2,1)S(1)} collective-permute-done((bf16[1,256,512]{2,1,0:T(8,128)(2,1)S(1)}, bf16[1,256,512]{2,1,0:T(8,128)(2,1)S(1)}, u32[]{:S(2)}, u32[]{:S(2)}) %collective-permute-start.1) | collective-permute-done | bytes 262176 | tf_op jit(solution)/shard_map/ppermute | solution.py:27
  4.2 2.9 %collective-permute-start.7 = (bf16[1,272,512]{2,1,0:T(8,128)(2,1)S(1)}, bf16[1,272,512]{2,1,0:T(8,128)(2,1)S(1)}, u32[]{:S(2)}, u32[]{:S(2)}) collective-permute-start(bf16[1,272,512]{2,1,0:T(8,128)(2,1)S(1)} %shard_map.66), channel_id=1, source_target_pairs={{0,2},{1,15},{2,0},{3,5},{4,6},{5,3},{6,4},{7,9},{8,10},{9,7},{10,... | collective-permute-start | bytes 835592 | tf_op jit(solution)/shard_map/ppermute | solution.py:36
  7.1 2.0 %shard_map.67 = (bf16[4,256,512]{2,1,0:T(8,128)(2,1)S(1)}, bf16[1,256,512]{2,1,0:T(8,128)(2,1)S(1)}, bf16[1,256,512]{2,1,0:T(8,128)(2,1)S(1)}, bf16[1,256,512]{2,1,0:T(8,128)(2,1)S(1)}) custom-call(bf16[4,256,512]{2,1,0:T(8,128)(2,1)S(1)} %bitcast.8, f32[4,512]{1,0:T(4,128)S(1)} %get-tuple-element.118.fields_ref.first_ref.own_ref, ...), custom_call_target="tpu_custom_call" | custom-call | tf_op jit(solution)/shard_map/pallas_call | solution.py:557
  9.0 2.8 %shard_map.68 = (bf16[4,256,512]{2,1,0:T(8,128)(2,1)S(1)}, bf16[1,256,512]{2,1,0:T(8,128)(2,1)S(1)}, bf16[1,256,512]{2,1,0:T(8,128)(2,1)S(1)}) custom-call(bf16[4,256,512]{2,1,0:T(8,128)(2,1)S(1)} %get-tuple-element.77.state_ref.alone_ref, f32[4,512]{1,0:T(4,128)S(1)} %get-tuple-element.118.fields_ref.first_ref.own_ref, ...), custom_call_target="tpu_custom_call" | custom-call | tf_op jit(solution)/shard_map/pallas_call | solution.py:557
  11.9 3.0 %collective-permute-start.5 = (bf16[1,256,512]{2,1,0:T(8,128)(2,1)S(1)}, bf16[1,256,512]{2,1,0:T(8,128)(2,1)S(1)}, u32[]{:S(2)}, u32[]{:S(2)}) collective-permute-start(bf16[1,256,512]{2,1,0:T(8,128)(2,1)S(1)} %get-tuple-element.73.mine_ref), channel_id=1, source_target_pairs={{1,0},{0,1},{3,2},{2,3},{5,4},{4,5},{7,6},{6,7},{9,8},{8,9},{11,10... | collective-permute-start | bytes 786440 | tf_op jit(solution)/shard_map/ppermute | solution.py:27
  14.9 0.4 collective-permute-start.3
  15.3 0.6 %shard_map.70 = (bf16[4,256,512]{2,1,0:T(8,128)(2,1)S(1)}, bf16[2,256,512]{2,1,0:T(8,128)(2,1)S(1)}) custom-call(s32[1]{0:T(128)} %bitcast.core_ref, bf16[4,256,512]{2,1,0:T(8,128)(2,1)S(1)} %collective-permute-done.6.partner_ref, bf16[4,256,512]{2,1,0:T(8,128)(2,1)S(1)} %bitcast.9, bf16[256,256]{1,0:T(8,128)(2,1)S(1)} %get-tuple-element.74.turned_ref), custom_call_target="tpu_custom_call" | custom-call | tf_op jit(solution)/shard_map/pallas_call | solution.py:557
  16.1 0.2 collective-permute-done.2.refs_2_
  16.4 0.4 collective-permute-done.3.refs_3_
  16.9 0.4 collective-permute-start.8
  17.3 1.1 %collective-permute-start.4 = (bf16[2,288,512]{2,1,0:T(8,128)(2,1)S(1)}, bf16[2,288,512]{2,1,0:T(8,128)(2,1)S(1)}, u32[]{:S(2)}, u32[]{:S(2)}) collective-permute-start(bf16[2,288,512]{2,1,0:T(8,128)(2,1)S(1)} %shard_map.69), channel_id=1, source_target_pairs={{0,2},{1,15},{2,0},{3,5},{4,6},{5,3},{6,4},{7,9},{8,10},{9,7},{10,... | collective-permute-start | bytes 1769480 | tf_op jit(solution)/shard_map/ppermute | solution.py:36
  18.5 2.7 %shard_map.72 = (bf16[1,256,512]{2,1,0:T(8,128)(2,1)S(1)}, bf16[1,256,512]{2,1,0:T(8,128)(2,1)S(1)}, bf16[8,256,512]{2,1,0:T(8,128)(2,1)S(1)}, bf16[1,256,512]{2...) custom-call(s32[1]{0:T(128)} %bitcast.core_ref, ...), custom_call_target="tpu_custom_call" | custom-call | tf_op jit(solution)/shard_map/pallas_call | solution.py:557
  21.2 11.1 %collective-permute-done.9.message_ref.mine_ref = bf16[1,288,512]{2,1,0:T(8,128)(2,1)S(1)} collective-permute-done((bf16[1,288,512]{2,1,0:T(8,128)(2,1)S(1)}, bf16[1,288,512]{2,1,0:T(8,128)(2,1)S(1)}, u32[]{:S(2)}, u32[]{:S(2)}) %collective-permute-start.9) | collective-permute-done | bytes 294944 | tf_op jit(solution)/shard_map/ppermute | solution.py:36
  32.3 0.5 %collective-permute-start.10 = (bf16[1,256,512]{2,1,0:T(8,128)(2,1)S(1)}, bf16[1,256,512]{2,1,0:T(8,128)(2,1)S(1)}, u32[]{:S(2)}, u32[]{:S(2)}) collective-permute-start(bf16[1,256,512]{2,1,0:T(8,128)(2,1)S(1)} %get-tuple-element.86), channel_id=1, source_target_pairs={{1,0},{0,1},{3,2},{2,3},{5,4},{4,5},{7,6},{6,7},{9,8},{8,9},{11,10... | collective-permute-start | bytes 786440 | tf_op jit(solution)/shard_map/ppermute | solution.py:27
  32.8 0.5 %collective-permute-start.12 = (bf16[1,256,512]{2,1,0:T(8,128)(2,1)S(1)}, bf16[1,256,512]{2,1,0:T(8,128)(2,1)S(1)}, u32[]{:S(2)}, u32[]{:S(2)}) collective-permute-start(bf16[1,256,512]{2,1,0:T(8,128)(2,1)S(1)} %get-tuple-element.88), channel_id=1, source_target_pairs={{1,0},{0,1},{3,2},{2,3},{5,4},{4,5},{7,6},{6,7},{9,8},{8,9},{11,10... | collective-permute-start | bytes 786440 | tf_op jit(solution)/shard_map/ppermute | solution.py:27
  33.3 0.9 %collective-permute-done.10.near_ref = bf16[1,256,512]{2,1,0:T(8,128)(2,1)S(1)} collective-permute-done((bf16[1,256,512]{2,1,0:T(8,128)(2,1)S(1)}, bf16[1,256,512]{2,1,0:T(8,128)(2,1)S(1)}, u32[]{:S(2)}, u32[]{:S(2)}) %collective-permute-start.10) | collective-permute-done | bytes 262176 | tf_op jit(solution)/shard_map/ppermute | solution.py:27
  34.3 0.4 collective-permute-done.11.far_ref
  34.6 0.4 collective-permute-done.12.refs_1_
  35.0 0.6 %shard_map.73 = (f32[2,512]{1,0:T(2,128)S(1)}, f32[4,512]{1,0:T(4,128)S(1)}) custom-call(s32[1]{0:T(128)} %bitcast.core_ref, bf16[2,256,512]{2,1,0:T(8,128)(2,1)S(1)} %get-tuple-element.80.own_ref, bf16[1,256,512]{2,1,0:T(8,128)(2,1)S(1)} %collective-permute-done.10.near_ref, bf16[1,256,512]{2,1,0:T(8,128)(2,1)S(1)} %collective-permute-done.11.far_ref, ...), custom_call_target="tpu_custom_call" | custom-call | tf_op jit(solution)/shard_map/pallas_call | solution.py:557
  35.8 0.4 collective-permute-start.16
  36.3 3.0 %shard_map.74.held_ref = bf16[6,256,512]{2,1,0:T(8,128)(2,1)S(1)} custom-call(bf16[8,256,512]{2,1,0:T(8,128)(2,1)S(1)} %get-tuple-element.97.held_ref, bf16[1,288,512]{2,1,0:T(8,128)(2,1)S(1)} %collective-permute-done.9.message_ref.mine_ref, bf16[1,288,512]{2,1,0:T(8,128)(2,1)S(1)} %collective-permute-done.13.other_ref, ...), custom_call_target="tpu_custom_call" | custom-call | tf_op jit(solution)/shard_map/pallas_call | solution.py:557
  39.2 0.7 %collective-permute-done.14.two_ref = f32[4,512]{1,0:T(4,128)S(1)} collective-permute-done((f32[4,512]{1,0:T(4,128)S(1)}, f32[4,512]{1,0:T(4,128)S(1)}, u32[]{:S(2)}, u32[]{:S(2)}) %collective-permute-start.14) | collective-permute-done | bytes 8224 | tf_op jit(solution)/shard_map/ppermute | solution.py:660
  39.9 1.0 %collective-permute-start.15 = (f32[4,512]{1,0:T(4,128)S(1)}, f32[4,512]{1,0:T(4,128)S(1)}, u32[]{:S(2)}, u32[]{:S(2)}) collective-permute-start(f32[4,512]{1,0:T(4,128)S(1)} %shard_map.75.one_ref), channel_id=1, source_target_pairs={{0,8},{1,9},{2,10},{3,11},{4,12},{5,13},{6,14},{7,15},{8,0},{9,1},... | collective-permute-start | bytes 24584 | tf_op jit(solution)/shard_map/ppermute | solution.py:660
  41.0 1.6 %shard_map.76.shared_ref = f32[4,512]{1,0:T(4,128)S(1)} custom-call(bf16[6,256,512]{2,1,0:T(8,128)(2,1)S(1)} %shard_map.74.held_ref, f32[4,512]{1,0:T(4,128)S(1)} %get-tuple-element.117.partner_ref.second_ref, f32[4,256,128]{2,1,0:T(8,128)S(1)} %get-tuple-element.65.refs_1_.v_ref.refs_4_.refs_2_, bf16[4,256,512]{2,1,0:T(8,128)(2,1)S(1)} %get-tuple-element.103.weight_ref, ...), custom_call_target="tpu_custom_call" | custom-call | tf_op jit(solution)/shard_map/pallas_call | solution.py:557
  42.6 1.9 %collective-permute-done.15.two_ref = f32[4,512]{1,0:T(4,128)S(1)} collective-permute-done((f32[4,512]{1,0:T(4,128)S(1)}, f32[4,512]{1,0:T(4,128)S(1)}, u32[]{:S(2)}, u32[]{:S(2)}) %collective-permute-start.15) | collective-permute-done | bytes 8224 | tf_op jit(solution)/shard_map/ppermute | solution.py:660
  44.6 1.7 %shard_map.78 = (f32[4,512]{1,0:T(4,128)S(1)}, f32[4,512]{1,0:T(4,128)S(1)}) custom-call(s32[1]{0:T(128)} %bitcast.core_ref, bf16[2,288,512]{2,1,0:T(8,128)(2,1)S(1)} %collective-permute-done.4.message_ref, bf16[4,256,512]{2,1,0:T(8,128)(2,1)S(1)} %get-tuple-element.103.weight_ref, bf16[2,256,512]{2,1,0:T(8,128)(2,1)S(1)} %get-tuple-element.111.own_weight_ref, ...), custom_call_target="tpu_custom_call" | custom-call | tf_op jit(solution)/shard_map/pallas_call | solution.py:557
  46.2 2.0 %collective-permute-done.19.two_ref = f32[4,512]{1,0:T(4,128)S(1)} collective-permute-done((f32[4,512]{1,0:T(4,128)S(1)}, f32[4,512]{1,0:T(4,128)S(1)}, u32[]{:S(2)}, u32[]{:S(2)}) %collective-permute-start.19) | collective-permute-done | bytes 8224 | tf_op jit(solution)/shard_map/ppermute | solution.py:660
  48.2 1.2 %collective-permute-done.20.arrived_ref = f32[8,512]{1,0:T(8,128)S(1)} collective-permute-done((f32[8,512]{1,0:T(8,128)S(1)}, f32[8,512]{1,0:T(8,128)S(1)}, u32[]{:S(2)}, u32[]{:S(2)}) %collective-permute-start.20) | collective-permute-done | bytes 16416 | tf_op jit(solution)/shard_map/ppermute | solution.py:27
  49.4 0.6 %shard_map.80 = f32[4,512]{1,0:T(4,128)} custom-call(f32[4,512]{1,0:T(4,128)S(1)} %get-tuple-element.113.kept_ref, f32[8,512]{1,0:T(8,128)S(1)} %shard_map.79.mine_ref, f32[8,512]{1,0:T(8,128)S(1)} %collective-permute-done.20.arrived_ref), custom_call_target="tpu_custom_call" | custom-call | tf_op jit(solution)/shard_map/pallas_call | solution.py:557
  (40 shorter events, 1.5 us)
Async XLA Ops:
  0.0 2.0 %copy-start.4 = (f32[4,512]{1,0:T(4,128)S(1)}, f32[4,512]{1,0:T(4,128)}, u32[]{:S(2)}) copy-start(f32[4,512]{1,0:T(4,128)} %param.6) | copy-start | bytes 24580
  0.0 2.1 %copy-start.2 = (f32[3,256]{1,0:T(4,128)S(1)}, f32[3,256]{1,0:T(4,128)}, u32[]{:S(2)}) copy-start(f32[3,256]{1,0:T(4,128)} %directions_ref.1) | copy-start | bytes 9220
  0.0 2.5 %copy-start.3 = (f32[256]{0:T(256)S(1)}, f32[256]{0:T(256)}, u32[]{:S(2)}) copy-start(f32[256]{0:T(256)} %param.11) | copy-start | bytes 3076
  0.0 2.5 %copy-start = (bf16[256,256]{1,0:T(8,128)(2,1)S(1)}, bf16[256,256]{1,0:T(8,128)(2,1)}, u32[]{:S(2)}) copy-start(bf16[256,256]{1,0:T(8,128)(2,1)} %synthesis_ref.1) | copy-start | bytes 393220
  0.0 2.5 %copy-start.1 = (bf16[256,256]{1,0:T(8,128)(2,1)S(1)}, bf16[256,256]{1,0:T(8,128)(2,1)}, u32[]{:S(2)}) copy-start(bf16[256,256]{1,0:T(8,128)(2,1)} %analysis_ref.1) | copy-start | bytes 393220
  0.0 2.0 %collective-permute-start = (f32[4,512]{1,0:T(4,128)}, f32[4,512]{1,0:T(4,128)S(1)}, u32[]{:S(2)}, u32[]{:S(2)}) collective-permute-start(f32[4,512]{1,0:T(4,128)} %param.6), channel_id=1, source_target_pairs={{1,0},{0,1},{3,2},{2,3},{5,4},{4,5},{7,6},{6,7},{9,8},{8,9},{11,10... | collective-permute-start | bytes 24584 | tf_op jit(solution)/shard_map/ppermute | solution.py:27
  2.3 1.6 %collective-permute-start.1 = (bf16[1,256,512]{2,1,0:T(8,128)(2,1)S(1)}, bf16[1,256,512]{2,1,0:T(8,128)(2,1)S(1)}, u32[]{:S(2)}, u32[]{:S(2)}) collective-permute-start(bf16[1,256,512]{2,1,0:T(8,128)(2,1)S(1)} %get-tuple-element.61.mine_ref.edge_ref), channel_id=1, source_target_pairs={{1,0},{0,1},{3,2},{2,3},{5,4},{4,5},{7,6},{6,7},{9,8},{8,9},{11,10... | collective-permute-start | bytes 786440 | tf_op jit(solution)/shard_map/ppermute | solution.py:27
  4.0 11.4 %collective-permute-start.6 = (bf16[4,256,512]{2,1,0:T(8,128)(2,1)S(1)}, bf16[4,256,512]{2,1,0:T(8,128)(2,1)S(1)}, u32[]{:S(2)}, u32[]{:S(2)}) collective-permute-start(bf16[4,256,512]{2,1,0:T(8,128)(2,1)S(1)} %bitcast.7), channel_id=1, source_target_pairs={{1,0},{0,1},{3,2},{2,3},{5,4},{4,5},{7,6},{6,7},{9,8},{8,9},{11,10... | collective-permute-start | bytes 3145736 | tf_op jit(solution)/shard_map/ppermute | solution.py:27
  4.2 12.7 %collective-permute-start.7 = (bf16[1,272,512]{2,1,0:T(8,128)(2,1)S(1)}, bf16[1,272,512]{2,1,0:T(8,128)(2,1)S(1)}, u32[]{:S(2)}, u32[]{:S(2)}) collective-permute-start(bf16[1,272,512]{2,1,0:T(8,128)(2,1)S(1)} %shard_map.66), channel_id=1, source_target_pairs={{0,2},{1,15},{2,0},{3,5},{4,6},{5,3},{6,4},{7,9},{8,10},{9,7},{10,... | collective-permute-start | bytes 835592 | tf_op jit(solution)/shard_map/ppermute | solution.py:36
  11.9 4.1 %collective-permute-start.5 = (bf16[1,256,512]{2,1,0:T(8,128)(2,1)S(1)}, bf16[1,256,512]{2,1,0:T(8,128)(2,1)S(1)}, u32[]{:S(2)}, u32[]{:S(2)}) collective-permute-start(bf16[1,256,512]{2,1,0:T(8,128)(2,1)S(1)} %get-tuple-element.73.mine_ref), channel_id=1, source_target_pairs={{1,0},{0,1},{3,2},{2,3},{5,4},{4,5},{7,6},{6,7},{9,8},{8,9},{11,10... | collective-permute-start | bytes 786440 | tf_op jit(solution)/shard_map/ppermute | solution.py:27
  14.8 1.5 %collective-permute-start.2 = (bf16[1,256,512]{2,1,0:T(8,128)(2,1)S(1)}, bf16[1,256,512]{2,1,0:T(8,128)(2,1)S(1)}, u32[]{:S(2)}, u32[]{:S(2)}) collective-permute-start(bf16[1,256,512]{2,1,0:T(8,128)(2,1)S(1)} %get-tuple-element.71.refs_0_), channel_id=1, source_target_pairs={{1,0},{0,1},{3,2},{2,3},{5,4},{4,5},{7,6},{6,7},{9,8},{8,9},{11,10... | collective-permute-start | bytes 786440 | tf_op jit(solution)/shard_map/ppermute | solution.py:27
  14.9 1.8 %collective-permute-start.3 = (bf16[1,256,512]{2,1,0:T(8,128)(2,1)S(1)}, bf16[1,256,512]{2,1,0:T(8,128)(2,1)S(1)}, u32[]{:S(2)}, u32[]{:S(2)}) collective-permute-start(bf16[1,256,512]{2,1,0:T(8,128)(2,1)S(1)} %get-tuple-element.72.refs_1_), channel_id=1, source_target_pairs={{1,0},{0,1},{3,2},{2,3},{5,4},{4,5},{7,6},{6,7},{9,8},{8,9},{11,10... | collective-permute-start | bytes 786440 | tf_op jit(solution)/shard_map/ppermute | solution.py:27
  16.0 16.3 %collective-permute-start.9 = (bf16[1,288,512]{2,1,0:T(8,128)(2,1)S(1)}, bf16[1,288,512]{2,1,0:T(8,128)(2,1)S(1)}, u32[]{:S(2)}, u32[]{:S(2)}) collective-permute-start(bf16[1,288,512]{2,1,0:T(8,128)(2,1)S(1)} %shard_map.71), channel_id=1, source_target_pairs={{0,2},{1,15},{2,0},{3,5},{4,6},{5,3},{6,4},{7,9},{8,10},{9,7},{10,... | collective-permute-start | bytes 884744 | tf_op jit(solution)/shard_map/ppermute | solution.py:36
  16.9 1.6 %collective-permute-start.8 = (bf16[1,272,512]{2,1,0:T(8,128)(2,1)S(1)}, bf16[1,272,512]{2,1,0:T(8,128)(2,1)S(1)}, u32[]{:S(2)}, u32[]{:S(2)}) collective-permute-start(bf16[1,272,512]{2,1,0:T(8,128)(2,1)S(1)} %collective-permute-done.7.mine_ref), channel_id=1, source_target_pairs={{1,0},{0,1},{3,2},{2,3},{5,4},{4,5},{7,6},{6,7},{9,8},{8,9},{11,10... | collective-permute-start | bytes 835592 | tf_op jit(solution)/shard_map/ppermute | solution.py:27
  17.3 27.2 %collective-permute-start.4 = (bf16[2,288,512]{2,1,0:T(8,128)(2,1)S(1)}, bf16[2,288,512]{2,1,0:T(8,128)(2,1)S(1)}, u32[]{:S(2)}, u32[]{:S(2)}) collective-permute-start(bf16[2,288,512]{2,1,0:T(8,128)(2,1)S(1)} %shard_map.69), channel_id=1, source_target_pairs={{0,2},{1,15},{2,0},{3,5},{4,6},{5,3},{6,4},{7,9},{8,10},{9,7},{10,... | collective-permute-start | bytes 1769480 | tf_op jit(solution)/shard_map/ppermute | solution.py:36
  32.3 2.7 %collective-permute-start.13 = (bf16[1,288,512]{2,1,0:T(8,128)(2,1)S(1)}, bf16[1,288,512]{2,1,0:T(8,128)(2,1)S(1)}, u32[]{:S(2)}, u32[]{:S(2)}) collective-permute-start(bf16[1,288,512]{2,1,0:T(8,128)(2,1)S(1)} %collective-permute-done.9.message_ref.mine_ref), channel_id=1, source_target_pairs={{1,0},{0,1},{3,2},{2,3},{5,4},{4,5},{7,6},{6,7},{9,8},{8,9},{11,10... | collective-permute-start | bytes 884744 | tf_op jit(solution)/shard_map/ppermute | solution.py:27
  32.3 2.0 %collective-permute-start.10 = (bf16[1,256,512]{2,1,0:T(8,128)(2,1)S(1)}, bf16[1,256,512]{2,1,0:T(8,128)(2,1)S(1)}, u32[]{:S(2)}, u32[]{:S(2)}) collective-permute-start(bf16[1,256,512]{2,1,0:T(8,128)(2,1)S(1)} %get-tuple-element.86), channel_id=1, source_target_pairs={{1,0},{0,1},{3,2},{2,3},{5,4},{4,5},{7,6},{6,7},{9,8},{8,9},{11,10... | collective-permute-start | bytes 786440 | tf_op jit(solution)/shard_map/ppermute | solution.py:27
  32.8 1.8 %collective-permute-start.11 = (bf16[1,256,512]{2,1,0:T(8,128)(2,1)S(1)}, bf16[1,256,512]{2,1,0:T(8,128)(2,1)S(1)}, u32[]{:S(2)}, u32[]{:S(2)}) collective-permute-start(bf16[1,256,512]{2,1,0:T(8,128)(2,1)S(1)} %get-tuple-element.87), channel_id=1, source_target_pairs={{1,0},{0,1},{3,2},{2,3},{5,4},{4,5},{7,6},{6,7},{9,8},{8,9},{11,10... | collective-permute-start | bytes 786440 | tf_op jit(solution)/shard_map/ppermute | solution.py:27
  32.8 2.2 %collective-permute-start.12 = (bf16[1,256,512]{2,1,0:T(8,128)(2,1)S(1)}, bf16[1,256,512]{2,1,0:T(8,128)(2,1)S(1)}, u32[]{:S(2)}, u32[]{:S(2)}) collective-permute-start(bf16[1,256,512]{2,1,0:T(8,128)(2,1)S(1)} %get-tuple-element.88), channel_id=1, source_target_pairs={{1,0},{0,1},{3,2},{2,3},{5,4},{4,5},{7,6},{6,7},{9,8},{8,9},{11,10... | collective-permute-start | bytes 786440 | tf_op jit(solution)/shard_map/ppermute | solution.py:27
  35.6 5.4 %collective-permute-start.17 = (bf16[1,256,512]{2,1,0:T(8,128)(2,1)S(1)}, bf16[1,256,512]{2,1,0:T(8,128)(2,1)S(1)}, u32[]{:S(2)}, u32[]{:S(2)}) collective-permute-start(bf16[1,256,512]{2,1,0:T(8,128)(2,1)S(1)} %get-tuple-element.106), channel_id=1, source_target_pairs={{1,0},{0,1},{3,2},{2,3},{5,4},{4,5},{7,6},{6,7},{9,8},{8,9},{11,10... | collective-permute-start | bytes 786440 | tf_op jit(solution)/shard_map/ppermute | solution.py:27
  35.8 5.2 %collective-permute-start.16 = (bf16[1,256,512]{2,1,0:T(8,128)(2,1)S(1)}, bf16[1,256,512]{2,1,0:T(8,128)(2,1)S(1)}, u32[]{:S(2)}, u32[]{:S(2)}) collective-permute-start(bf16[1,256,512]{2,1,0:T(8,128)(2,1)S(1)} %get-tuple-element.104.own_low_ref), channel_id=1, source_target_pairs={{1,0},{0,1},{3,2},{2,3},{5,4},{4,5},{7,6},{6,7},{9,8},{8,9},{11,10... | collective-permute-start | bytes 786440 | tf_op jit(solution)/shard_map/ppermute | solution.py:27
  36.1 4.9 %collective-permute-start.18 = (bf16[1,256,512]{2,1,0:T(8,128)(2,1)S(1)}, bf16[1,256,512]{2,1,0:T(8,128)(2,1)S(1)}, u32[]{:S(2)}, u32[]{:S(2)}) collective-permute-start(bf16[1,256,512]{2,1,0:T(8,128)(2,1)S(1)} %get-tuple-element.107.own_high_ref), channel_id=1, source_target_pairs={{1,0},{0,1},{3,2},{2,3},{5,4},{4,5},{7,6},{6,7},{9,8},{8,9},{11,10... | collective-permute-start | bytes 786440 | tf_op jit(solution)/shard_map/ppermute | solution.py:27
  36.3 3.7 %collective-permute-start.14 = (f32[4,512]{1,0:T(4,128)S(1)}, f32[4,512]{1,0:T(4,128)S(1)}, u32[]{:S(2)}, u32[]{:S(2)}) collective-permute-start(f32[4,512]{1,0:T(4,128)S(1)} %get-tuple-element.91.one_ref), channel_id=1, source_target_pairs={{0,4},{1,5},{2,6},{3,7},{4,0},{5,1},{6,2},{7,3},{8,12},{9,13},{10,... | collective-permute-start | bytes 24584 | tf_op jit(solution)/shard_map/ppermute | solution.py:660
  39.9 4.6 %collective-permute-start.15 = (f32[4,512]{1,0:T(4,128)S(1)}, f32[4,512]{1,0:T(4,128)S(1)}, u32[]{:S(2)}, u32[]{:S(2)}) collective-permute-start(f32[4,512]{1,0:T(4,128)S(1)} %shard_map.75.one_ref), channel_id=1, source_target_pairs={{0,8},{1,9},{2,10},{3,11},{4,12},{5,13},{6,14},{7,15},{8,0},{9,1},... | collective-permute-start | bytes 24584 | tf_op jit(solution)/shard_map/ppermute | solution.py:660
  44.5 3.7 %collective-permute-start.19 = (f32[4,512]{1,0:T(4,128)S(1)}, f32[4,512]{1,0:T(4,128)S(1)}, u32[]{:S(2)}, u32[]{:S(2)}) collective-permute-start(f32[4,512]{1,0:T(4,128)S(1)} %shard_map.77.one_ref), channel_id=1, source_target_pairs={{0,2},{1,3},{2,0},{3,1},{4,6},{5,7},{6,4},{7,5},{8,10},{9,11},{10,... | collective-permute-start | bytes 24584 | tf_op jit(solution)/shard_map/ppermute | solution.py:660
  48.2 1.2 %collective-permute-start.20 = (f32[8,512]{1,0:T(8,128)S(1)}, f32[8,512]{1,0:T(8,128)S(1)}, u32[]{:S(2)}, u32[]{:S(2)}) collective-permute-start(f32[8,512]{1,0:T(8,128)S(1)} %shard_map.79.mine_ref), channel_id=1, source_target_pairs={{1,0},{0,1},{3,2},{2,3},{5,4},{4,5},{7,6},{6,7},{9,8},{8,9},{11,10... | collective-permute-start | bytes 49160 | tf_op jit(solution)/shard_map/ppermute | solution.py:27

commit v12 on v10

--- a/solution.py
+++ b/solution.py
@@ -159,8 +159,9 @@
     turned_ref[...] = total.T.astype(BF16)
 
 
-def add_kernel(one_ref, two_ref, out_ref):
-    out_ref[...] = one_ref[...] + two_ref[...]
+def add_kernel(*refs):
+    *value_refs, out_ref = refs
+    out_ref[...] = functools.reduce(jnp.add, [ref[...] for ref in value_refs])
 
 
 def join_kernel(sent_ref, one_ref, two_ref, out_ref):
@@ -645,8 +646,10 @@
         )
     )
     arrived1, second_state = lax.optimization_barrier((arrived[0], second_state))
-    *moving, _ = lax.optimization_barrier((*sent_half, arrived1))
-    *partner_half, crossed1 = lax.optimization_barrier((*map(swap_species, moving), swap_species(arrived1)))
+    *moving, low_face, _ = lax.optimization_barrier((*sent_half, faces[0], arrived1))
+    *partner_half, partner_low, crossed1 = lax.optimization_barrier(
+        (*map(swap_species, moving), swap_species(low_face), swap_species(arrived1))
+    )
     density = jax.ShapeDtypeStruct((planes, cells), F32)
     met, partition = kernel_call(
         middle_kernel,
@@ -664,23 +667,24 @@
         block, after = received(value, distance, after)
         return kernel_call(add_kernel, density, (), (value, block)), after
 
-    *faces, second_state, _ = lax.optimization_barrier((*faces, second_state, met))
-    partner_faces = [swap_species(block) for block in faces]
+    high_face, second_state, _ = lax.optimization_barrier((faces[1], second_state, met))
+    partner_faces = [partner_low, swap_species(high_face)]
     third_state = kernel_call(
         third_step_kernel,
         wide(2),
         (slab.shape, wide(2).shape),
         (second_state, arrived1, crossed1, own, partner, outer, spread, matrix),
     )
-    partition, third_state = gathered(partition, 4, third_state)
-    third_state, _ = lax.optimization_barrier((third_state, partition))
     shared = kernel_call(
         pairing_kernel,
         density,
         (),
         (third_state, partner, spread, weights, partner_faces[0], *partner_inner, partner_faces[1]),
     )
-    distance = 8
+    blocks = [lax.ppermute(partition, "space", [(i, i ^ far) for i in range(count)]) for far in (4, 8, 12)]
+    *blocks, shared = lax.optimization_barrier((*blocks, shared))
+    partition = kernel_call(add_kernel, density, (), (partition, *blocks))
+    distance = 16
     while distance < count:
         partition, shared = gathered(partition, distance, shared)
         distance *= 2

time: 43.3 us -> 44.3 us (1.023)
  starting transfers between devices: 15.7 us -> 18.4 us
  waiting for transfers between devices: 9.46 us -> 7.85 us
    ppermute x0 -> x3, starting transfers between devices: none -> 4.39 us  [shards(): lax.ppermute(partition, 'space', [(i, i ^ far) for i in range(count)])]
    ppermute x3 -> x1, waiting for transfers between devices: 3.88 us -> 1.97 us  [received(): lax.ppermute(value, 'space', [(i, i ^ distance) for i in range(count)])]
    ppermute x3 -> x1, starting transfers between devices: 1.77 us -> 0.07 us  [received(): lax.ppermute(value, 'space', [(i, i ^ distance) for i in range(count)])]
    pallas_call x17 -> x16, Pallas kernels: 16.3 us -> 16.3 us  [kernel_call(): pl.pallas_call(kernel, out_shape=outs, in_specs=[smem if arg.dtype == jnp...]
  transfers between devices with their start and end apart: 21 -> 22, of which waited for: 12 -> 11; matrix products, arithmetic and copies ran while one was open for 3% -> 3% of each run, Pallas kernels for 36% -> 35%
where the time goes in v12:
time: 44.3 us; the launch traced here: 44.2 us
  starting transfers between devices  18.4 us (42%)
  Pallas kernels  16.3 us (37%)
  waiting for transfers between devices  7.85 us (18%)
  local copies, waits for them, and re-layouts  1.44 us (3%)
    pallas_call x16, Pallas kernels, kernel_call(): pl.pallas_call(kernel, out_shape=outs, in_specs=[smem if arg.dtype == jnp...  16.3 us
    ppermute x15, starting transfers between devices, swap_species(): return lax.ppermute(block, 'space', [(i ^ 1, i) for i in range(count)])  8.59 us
    ppermute x15, waiting for transfers between devices, swap_species(): return lax.ppermute(block, 'space', [(i ^ 1, i) for i in range(count)])  5.86 us
    ppermute x3, starting transfers between devices, exchange_faces(): return lax.ppermute(block, 'space', route)  5.32 us
    ppermute x3, starting transfers between devices, shards(): lax.ppermute(partition, 'space', [(i, i ^ far) for i in range(count)])  4.39 us
    ppermute x1, waiting for transfers between devices, received(): lax.ppermute(value, 'space', [(i, i ^ distance) for i in range(count)])  1.97 us
    unnamed x11, local copies, waits for them, and re-layouts  1.44 us
  transfers between devices with their start and end apart: 22, of which 11 were waited for; matrix products, arithmetic and copies ran while one was open for 3% of the time, Pallas kernels for 35%

profile of v12, /device:TPU:0, one launch (start us, length us, event | category | flops | bytes accessed | tf_op | source)
XLA Modules:
  0.0 44.2 jit_solution(10751546105648966332)
XLA Ops:
  0.0 0.5 %collective-permute-start = (f32[4,512]{1,0:T(4,128)}, f32[4,512]{1,0:T(4,128)S(1)}, u32[]{:S(2)}, u32[]{:S(2)}) collective-permute-start(f32[4,512]{1,0:T(4,128)} %param.6), channel_id=1, source_target_pairs={{1,0},{0,1},{3,2},{2,3},{5,4},{4,5},{7,6},{6,7},{9,8},{8,9},{11,10... | collective-permute-start | bytes 24584 | tf_op jit(solution)/shard_map/ppermute | solution.py:27
  0.6 1.4 %copy.9 = bf16[256,4,512]{2,0,1:T(8,128)(2,1)S(1)} copy(bf16[256,4,512]{2,1,0:T(4,128)(2,1)} %param.7) | data formatting | bytes 2097152 | tf_op args[1]
  2.8 1.1 %collective-permute-done.1.other_ref = bf16[1,256,512]{2,1,0:T(8,128)(2,1)S(1)} collective-permute-done((bf16[1,256,512]{2,1,0:T(8,128)(2,1)S(1)}, bf16[1,256,512]{2,1,0:T(8,128)(2,1)S(1)}, u32[]{:S(2)}, u32[]{:S(2)}) %collective-permute-start.1) | collective-permute-done | bytes 262176 | tf_op jit(solution)/shard_map/ppermute | solution.py:27
  4.2 2.9 %collective-permute-start.6 = (bf16[1,272,512]{2,1,0:T(8,128)(2,1)S(1)}, bf16[1,272,512]{2,1,0:T(8,128)(2,1)S(1)}, u32[]{:S(2)}, u32[]{:S(2)}) collective-permute-start(bf16[1,272,512]{2,1,0:T(8,128)(2,1)S(1)} %shard_map.66), channel_id=1, source_target_pairs={{0,2},{1,15},{2,0},{3,5},{4,6},{5,3},{6,4},{7,9},{8,10},{9,7},{10,... | collective-permute-start | bytes 835592 | tf_op jit(solution)/shard_map/ppermute | solution.py:36
  7.1 2.0 %shard_map.67 = (bf16[4,256,512]{2,1,0:T(8,128)(2,1)S(1)}, bf16[1,256,512]{2,1,0:T(8,128)(2,1)S(1)}, bf16[1,256,512]{2,1,0:T(8,128)(2,1)S(1)}, bf16[1,256,512]{2,1,0:T(8,128)(2,1)S(1)}) custom-call(bf16[4,256,512]{2,1,0:T(8,128)(2,1)S(1)} %bitcast.8, f32[4,512]{1,0:T(4,128)S(1)} %get-tuple-element.118.fields_ref.first_ref.own_ref, ...), custom_call_target="tpu_custom_call" | custom-call | tf_op jit(solution)/shard_map/pallas_call | solution.py:558
  9.0 3.0 %collective-permute-start.4 = (bf16[1,256,512]{2,1,0:T(8,128)(2,1)S(1)}, bf16[1,256,512]{2,1,0:T(8,128)(2,1)S(1)}, u32[]{:S(2)}, u32[]{:S(2)}) collective-permute-start(bf16[1,256,512]{2,1,0:T(8,128)(2,1)S(1)} %get-tuple-element.72), channel_id=1, source_target_pairs={{1,0},{0,1},{3,2},{2,3},{5,4},{4,5},{7,6},{6,7},{9,8},{8,9},{11,10... | collective-permute-start | bytes 786440 | tf_op jit(solution)/shard_map/ppermute | solution.py:27
  12.1 0.4 collective-permute-start.2
  12.5 0.6 %shard_map.68 = (bf16[4,256,512]{2,1,0:T(8,128)(2,1)S(1)}, bf16[2,256,512]{2,1,0:T(8,128)(2,1)S(1)}) custom-call(s32[1]{0:T(128)} %bitcast.core_ref, bf16[4,256,512]{2,1,0:T(8,128)(2,1)S(1)} %collective-permute-done.3.partner_ref, bf16[4,256,512]{2,1,0:T(8,128)(2,1)S(1)} %bitcast.9, bf16[256,256]{1,0:T(8,128)(2,1)S(1)} %get-tuple-element.70.turned_ref), custom_call_target="tpu_custom_call" | custom-call | tf_op jit(solution)/shard_map/pallas_call | solution.py:558
  13.2 0.4 collective-permute-done.5.refs_2_
  13.5 0.4 collective-permute-done.2.other_ref
  14.1 2.8 %shard_map.70 = (bf16[4,256,512]{2,1,0:T(8,128)(2,1)S(1)}, bf16[1,256,512]{2,1,0:T(8,128)(2,1)S(1)}, bf16[1,256,512]{2,1,0:T(8,128)(2,1)S(1)}) custom-call(bf16[4,256,512]{2,1,0:T(8,128)(2,1)S(1)} %get-tuple-element.81.state_ref.alone_ref, f32[4,512]{1,0:T(4,128)S(1)} %get-tuple-element.118.fields_ref.first_ref.own_ref, ...), custom_call_target="tpu_custom_call" | custom-call | tf_op jit(solution)/shard_map/pallas_call | solution.py:558
  16.9 0.9 %collective-permute-start.7 = (bf16[1,256,512]{2,1,0:T(8,128)(2,1)S(1)}, bf16[1,256,512]{2,1,0:T(8,128)(2,1)S(1)}, u32[]{:S(2)}, u32[]{:S(2)}) collective-permute-start(bf16[1,256,512]{2,1,0:T(8,128)(2,1)S(1)} %get-tuple-element.79.refs_0_), channel_id=1, source_target_pairs={{1,0},{0,1},{3,2},{2,3},{5,4},{4,5},{7,6},{6,7},{9,8},{8,9},{11,10... | collective-permute-start | bytes 786440 | tf_op jit(solution)/shard_map/ppermute | solution.py:27
  17.9 0.4 collective-permute-start.10
  18.3 0.7 %collective-permute-done.7.refs_2_ = bf16[1,256,512]{2,1,0:T(8,128)(2,1)S(1)} collective-permute-done((bf16[1,256,512]{2,1,0:T(8,128)(2,1)S(1)}, bf16[1,256,512]{2,1,0:T(8,128)(2,1)S(1)}, u32[]{:S(2)}, u32[]{:S(2)}) %collective-permute-start.7) | collective-permute-done | bytes 262176 | tf_op jit(solution)/shard_map/ppermute | solution.py:27
  19.0 0.4 collective-permute-done.8.refs_3_
  19.5 2.4 %collective-permute-start.9 = (bf16[2,288,512]{2,1,0:T(8,128)(2,1)S(1)}, bf16[2,288,512]{2,1,0:T(8,128)(2,1)S(1)}, u32[]{:S(2)}, u32[]{:S(2)}) collective-permute-start(bf16[2,288,512]{2,1,0:T(8,128)(2,1)S(1)} %shard_map.71), channel_id=1, source_target_pairs={{0,2},{1,15},{2,0},{3,5},{4,6},{5,3},{6,4},{7,9},{8,10},{9,7},{10,... | collective-permute-start | bytes 1769480 | tf_op jit(solution)/shard_map/ppermute | solution.py:36
  21.8 2.7 %shard_map.72 = (bf16[1,256,512]{2,1,0:T(8,128)(2,1)S(1)}, bf16[1,256,512]{2,1,0:T(8,128)(2,1)S(1)}, bf16[8,256,512]{2,1,0:T(8,128)(2,1)S(1)}, bf16[1,256,512]{2...) custom-call(s32[1]{0:T(128)} %bitcast.core_ref, ...), custom_call_target="tpu_custom_call" | custom-call | tf_op jit(solution)/shard_map/pallas_call | solution.py:558
  24.5 1.8 %collective-permute-start.15 = (bf16[1,288,512]{2,1,0:T(8,128)(2,1)S(1)}, bf16[1,288,512]{2,1,0:T(8,128)(2,1)S(1)}, u32[]{:S(2)}, u32[]{:S(2)}) collective-permute-start(bf16[1,288,512]{2,1,0:T(8,128)(2,1)S(1)} %collective-permute-done.11.message_ref.mine_ref), channel_id=1, source_target_pairs={{1,0},{0,1},{3,2},{2,3},{5,4},{4,5},{7,6},{6,7},{9,8},{8,9},{11,10... | collective-permute-start | bytes 884744 | tf_op jit(solution)/shard_map/ppermute | solution.py:27
  26.4 0.4 collective-permute-start.13
  26.9 1.0 %collective-permute-done.12.near_ref = bf16[1,256,512]{2,1,0:T(8,128)(2,1)S(1)} collective-permute-done((bf16[1,256,512]{2,1,0:T(8,128)(2,1)S(1)}, bf16[1,256,512]{2,1,0:T(8,128)(2,1)S(1)}, u32[]{:S(2)}, u32[]{:S(2)}) %collective-permute-start.12) | collective-permute-done | bytes 262176 | tf_op jit(solution)/shard_map/ppermute | solution.py:27
  27.9 0.4 collective-permute-done.13.far_ref
  28.3 0.4 collective-permute-done.14.refs_0_.partner_low_ref
  28.7 0.6 %shard_map.73 = (f32[2,512]{1,0:T(2,128)S(1)}, f32[4,512]{1,0:T(4,128)S(1)}) custom-call(s32[1]{0:T(128)} %bitcast.core_ref, bf16[2,256,512]{2,1,0:T(8,128)(2,1)S(1)} %get-tuple-element.84.own_ref, bf16[1,256,512]{2,1,0:T(8,128)(2,1)S(1)} %collective-permute-done.12.near_ref, bf16[1,256,512]{2,1,0:T(8,128)(2,1)S(1)} %collective-permute-done.13.far_ref, ...), custom_call_target="tpu_custom_call" | custom-call | tf_op jit(solution)/shard_map/pallas_call | solution.py:558
  29.2 0.4 collective-permute-start.19
  29.6 1.6 %collective-permute-start.18 = (f32[4,512]{1,0:T(4,128)S(1)}, f32[4,512]{1,0:T(4,128)S(1)}, u32[]{:S(2)}, u32[]{:S(2)}) collective-permute-start(f32[4,512]{1,0:T(4,128)S(1)} %get-tuple-element.95.refs_0_), channel_id=1, source_target_pairs={{0,12},{1,13},{2,14},{3,15},{4,8},{5,9},{6,10},{7,11},{8,4},{9,5},... | collective-permute-start | bytes 24584 | tf_op jit(solution)/shard_map/ppermute | solution.py:684
  31.3 2.8 %collective-permute-start.16 = (f32[4,512]{1,0:T(4,128)S(1)}, f32[4,512]{1,0:T(4,128)S(1)}, u32[]{:S(2)}, u32[]{:S(2)}) collective-permute-start(f32[4,512]{1,0:T(4,128)S(1)} %get-tuple-element.95.refs_0_), channel_id=1, source_target_pairs={{0,4},{1,5},{2,6},{3,7},{4,0},{5,1},{6,2},{7,3},{8,12},{9,13},{10,... | collective-permute-start | bytes 24584 | tf_op jit(solution)/shard_map/ppermute | solution.py:684
  34.0 2.9 %shard_map.74.held_ref = bf16[6,256,512]{2,1,0:T(8,128)(2,1)S(1)} custom-call(bf16[8,256,512]{2,1,0:T(8,128)(2,1)S(1)} %get-tuple-element.99.held_ref, bf16[1,288,512]{2,1,0:T(8,128)(2,1)S(1)} %collective-permute-done.11.message_ref.mine_ref, bf16[1,288,512]{2,1,0:T(8,128)(2,1)S(1)} %collective-permute-done.15.other_ref, ...), custom_call_target="tpu_custom_call" | custom-call | tf_op jit(solution)/shard_map/pallas_call | solution.py:558
  37.0 1.6 %shard_map.75.shared_ref = f32[4,512]{1,0:T(4,128)S(1)} custom-call(bf16[6,256,512]{2,1,0:T(8,128)(2,1)S(1)} %shard_map.74.held_ref, f32[4,512]{1,0:T(4,128)S(1)} %get-tuple-element.117.partner_ref.second_ref, f32[4,256,128]{2,1,0:T(8,128)S(1)} %get-tuple-element.65.refs_1_.v_ref.refs_2_.refs_4_, bf16[4,256,512]{2,1,0:T(8,128)(2,1)S(1)} %get-tuple-element.75.weight_ref, ...), custom_call_target="tpu_custom_call" | custom-call | tf_op jit(solution)/shard_map/pallas_call | solution.py:558
  38.8 1.6 %shard_map.77 = (f32[4,512]{1,0:T(4,128)S(1)}, f32[4,512]{1,0:T(4,128)S(1)}) custom-call(s32[1]{0:T(128)} %bitcast.core_ref, bf16[2,288,512]{2,1,0:T(8,128)(2,1)S(1)} %collective-permute-done.9.message_ref, bf16[4,256,512]{2,1,0:T(8,128)(2,1)S(1)} %get-tuple-element.75.weight_ref, bf16[2,256,512]{2,1,0:T(8,128)(2,1)S(1)} %get-tuple-element.111.own_weight_ref, ...), custom_call_target="tpu_custom_call" | custom-call | tf_op jit(solution)/shard_map/pallas_call | solution.py:558
  40.4 2.0 %collective-permute-done.20.two_ref = f32[4,512]{1,0:T(4,128)S(1)} collective-permute-done((f32[4,512]{1,0:T(4,128)S(1)}, f32[4,512]{1,0:T(4,128)S(1)}, u32[]{:S(2)}, u32[]{:S(2)}) %collective-permute-start.20) | collective-permute-done | bytes 8224 | tf_op jit(solution)/shard_map/ppermute | solution.py:663
  42.4 1.2 %collective-permute-done.21.arrived_ref = f32[8,512]{1,0:T(8,128)S(1)} collective-permute-done((f32[8,512]{1,0:T(8,128)S(1)}, f32[8,512]{1,0:T(8,128)S(1)}, u32[]{:S(2)}, u32[]{:S(2)}) %collective-permute-start.21) | collective-permute-done | bytes 16416 | tf_op jit(solution)/shard_map/ppermute | solution.py:27
  43.6 0.6 %shard_map.79 = f32[4,512]{1,0:T(4,128)} custom-call(f32[4,512]{1,0:T(4,128)S(1)} %get-tuple-element.113.kept_ref, f32[8,512]{1,0:T(8,128)S(1)} %shard_map.78.mine_ref, f32[8,512]{1,0:T(8,128)S(1)} %collective-permute-done.21.arrived_ref), custom_call_target="tpu_custom_call" | custom-call | tf_op jit(solution)/shard_map/pallas_call | solution.py:558
  (41 shorter events, 1.8 us)
Async XLA Ops:
  0.0 2.0 %copy-start.4 = (f32[4,512]{1,0:T(4,128)S(1)}, f32[4,512]{1,0:T(4,128)}, u32[]{:S(2)}) copy-start(f32[4,512]{1,0:T(4,128)} %param.6) | copy-start | bytes 24580
  0.0 2.1 %copy-start.2 = (f32[3,256]{1,0:T(4,128)S(1)}, f32[3,256]{1,0:T(4,128)}, u32[]{:S(2)}) copy-start(f32[3,256]{1,0:T(4,128)} %directions_ref.1) | copy-start | bytes 9220
  0.0 2.5 %copy-start.3 = (f32[256]{0:T(256)S(1)}, f32[256]{0:T(256)}, u32[]{:S(2)}) copy-start(f32[256]{0:T(256)} %param.11) | copy-start | bytes 3076
  0.0 2.5 %copy-start = (bf16[256,256]{1,0:T(8,128)(2,1)S(1)}, bf16[256,256]{1,0:T(8,128)(2,1)}, u32[]{:S(2)}) copy-start(bf16[256,256]{1,0:T(8,128)(2,1)} %synthesis_ref.1) | copy-start | bytes 393220
  0.0 2.5 %copy-start.1 = (bf16[256,256]{1,0:T(8,128)(2,1)S(1)}, bf16[256,256]{1,0:T(8,128)(2,1)}, u32[]{:S(2)}) copy-start(bf16[256,256]{1,0:T(8,128)(2,1)} %analysis_ref.1) | copy-start | bytes 393220
  0.0 2.0 %collective-permute-start = (f32[4,512]{1,0:T(4,128)}, f32[4,512]{1,0:T(4,128)S(1)}, u32[]{:S(2)}, u32[]{:S(2)}) collective-permute-start(f32[4,512]{1,0:T(4,128)} %param.6), channel_id=1, source_target_pairs={{1,0},{0,1},{3,2},{2,3},{5,4},{4,5},{7,6},{6,7},{9,8},{8,9},{11,10... | collective-permute-start | bytes 24584 | tf_op jit(solution)/shard_map/ppermute | solution.py:27
  2.3 1.6 %collective-permute-start.1 = (bf16[1,256,512]{2,1,0:T(8,128)(2,1)S(1)}, bf16[1,256,512]{2,1,0:T(8,128)(2,1)S(1)}, u32[]{:S(2)}, u32[]{:S(2)}) collective-permute-start(bf16[1,256,512]{2,1,0:T(8,128)(2,1)S(1)} %get-tuple-element.61.mine_ref.edge_ref), channel_id=1, source_target_pairs={{1,0},{0,1},{3,2},{2,3},{5,4},{4,5},{7,6},{6,7},{9,8},{8,9},{11,10... | collective-permute-start | bytes 786440 | tf_op jit(solution)/shard_map/ppermute | solution.py:27
  4.0 8.5 %collective-permute-start.3 = (bf16[4,256,512]{2,1,0:T(8,128)(2,1)S(1)}, bf16[4,256,512]{2,1,0:T(8,128)(2,1)S(1)}, u32[]{:S(2)}, u32[]{:S(2)}) collective-permute-start(bf16[4,256,512]{2,1,0:T(8,128)(2,1)S(1)} %bitcast.7), channel_id=1, source_target_pairs={{1,0},{0,1},{3,2},{2,3},{5,4},{4,5},{7,6},{6,7},{9,8},{8,9},{11,10... | collective-permute-start | bytes 3145736 | tf_op jit(solution)/shard_map/ppermute | solution.py:27
  4.2 12.7 %collective-permute-start.6 = (bf16[1,272,512]{2,1,0:T(8,128)(2,1)S(1)}, bf16[1,272,512]{2,1,0:T(8,128)(2,1)S(1)}, u32[]{:S(2)}, u32[]{:S(2)}) collective-permute-start(bf16[1,272,512]{2,1,0:T(8,128)(2,1)S(1)} %shard_map.66), channel_id=1, source_target_pairs={{0,2},{1,15},{2,0},{3,5},{4,6},{5,3},{6,4},{7,9},{8,10},{9,7},{10,... | collective-permute-start | bytes 835592 | tf_op jit(solution)/shard_map/ppermute | solution.py:36
  9.0 4.1 %collective-permute-start.4 = (bf16[1,256,512]{2,1,0:T(8,128)(2,1)S(1)}, bf16[1,256,512]{2,1,0:T(8,128)(2,1)S(1)}, u32[]{:S(2)}, u32[]{:S(2)}) collective-permute-start(bf16[1,256,512]{2,1,0:T(8,128)(2,1)S(1)} %get-tuple-element.72), channel_id=1, source_target_pairs={{1,0},{0,1},{3,2},{2,3},{5,4},{4,5},{7,6},{6,7},{9,8},{8,9},{11,10... | collective-permute-start | bytes 786440 | tf_op jit(solution)/shard_map/ppermute | solution.py:27
  12.0 1.5 %collective-permute-start.5 = (bf16[1,256,512]{2,1,0:T(8,128)(2,1)S(1)}, bf16[1,256,512]{2,1,0:T(8,128)(2,1)S(1)}, u32[]{:S(2)}, u32[]{:S(2)}) collective-permute-start(bf16[1,256,512]{2,1,0:T(8,128)(2,1)S(1)} %get-tuple-element.73), channel_id=1, source_target_pairs={{1,0},{0,1},{3,2},{2,3},{5,4},{4,5},{7,6},{6,7},{9,8},{8,9},{11,10... | collective-permute-start | bytes 786440 | tf_op jit(solution)/shard_map/ppermute | solution.py:27
  12.1 1.8 %collective-permute-start.2 = (bf16[1,256,512]{2,1,0:T(8,128)(2,1)S(1)}, bf16[1,256,512]{2,1,0:T(8,128)(2,1)S(1)}, u32[]{:S(2)}, u32[]{:S(2)}) collective-permute-start(bf16[1,256,512]{2,1,0:T(8,128)(2,1)S(1)} %get-tuple-element.69.mine_ref), channel_id=1, source_target_pairs={{1,0},{0,1},{3,2},{2,3},{5,4},{4,5},{7,6},{6,7},{9,8},{8,9},{11,10... | collective-permute-start | bytes 786440 | tf_op jit(solution)/shard_map/ppermute | solution.py:27
  14.0 10.6 %collective-permute-start.11 = (bf16[1,288,512]{2,1,0:T(8,128)(2,1)S(1)}, bf16[1,288,512]{2,1,0:T(8,128)(2,1)S(1)}, u32[]{:S(2)}, u32[]{:S(2)}) collective-permute-start(bf16[1,288,512]{2,1,0:T(8,128)(2,1)S(1)} %shard_map.69), channel_id=1, source_target_pairs={{0,2},{1,15},{2,0},{3,5},{4,6},{5,3},{6,4},{7,9},{8,10},{9,7},{10,... | collective-permute-start | bytes 884744 | tf_op jit(solution)/shard_map/ppermute | solution.py:36
  16.9 2.1 %collective-permute-start.7 = (bf16[1,256,512]{2,1,0:T(8,128)(2,1)S(1)}, bf16[1,256,512]{2,1,0:T(8,128)(2,1)S(1)}, u32[]{:S(2)}, u32[]{:S(2)}) collective-permute-start(bf16[1,256,512]{2,1,0:T(8,128)(2,1)S(1)} %get-tuple-element.79.refs_0_), channel_id=1, source_target_pairs={{1,0},{0,1},{3,2},{2,3},{5,4},{4,5},{7,6},{6,7},{9,8},{8,9},{11,10... | collective-permute-start | bytes 786440 | tf_op jit(solution)/shard_map/ppermute | solution.py:27
  17.8 1.5 %collective-permute-start.8 = (bf16[1,256,512]{2,1,0:T(8,128)(2,1)S(1)}, bf16[1,256,512]{2,1,0:T(8,128)(2,1)S(1)}, u32[]{:S(2)}, u32[]{:S(2)}) collective-permute-start(bf16[1,256,512]{2,1,0:T(8,128)(2,1)S(1)} %get-tuple-element.80.refs_1_), channel_id=1, source_target_pairs={{1,0},{0,1},{3,2},{2,3},{5,4},{4,5},{7,6},{6,7},{9,8},{8,9},{11,10... | collective-permute-start | bytes 786440 | tf_op jit(solution)/shard_map/ppermute | solution.py:27
  17.9 3.9 %collective-permute-start.10 = (bf16[1,272,512]{2,1,0:T(8,128)(2,1)S(1)}, bf16[1,272,512]{2,1,0:T(8,128)(2,1)S(1)}, u32[]{:S(2)}, u32[]{:S(2)}) collective-permute-start(bf16[1,272,512]{2,1,0:T(8,128)(2,1)S(1)} %collective-permute-done.6.mine_ref), channel_id=1, source_target_pairs={{1,0},{0,1},{3,2},{2,3},{5,4},{4,5},{7,6},{6,7},{9,8},{8,9},{11,10... | collective-permute-start | bytes 835592 | tf_op jit(solution)/shard_map/ppermute | solution.py:27
  19.5 19.3 %collective-permute-start.9 = (bf16[2,288,512]{2,1,0:T(8,128)(2,1)S(1)}, bf16[2,288,512]{2,1,0:T(8,128)(2,1)S(1)}, u32[]{:S(2)}, u32[]{:S(2)}) collective-permute-start(bf16[2,288,512]{2,1,0:T(8,128)(2,1)S(1)} %shard_map.71), channel_id=1, source_target_pairs={{0,2},{1,15},{2,0},{3,5},{4,6},{5,3},{6,4},{7,9},{8,10},{9,7},{10,... | collective-permute-start | bytes 1769480 | tf_op jit(solution)/shard_map/ppermute | solution.py:36
  24.5 4.1 %collective-permute-start.15 = (bf16[1,288,512]{2,1,0:T(8,128)(2,1)S(1)}, bf16[1,288,512]{2,1,0:T(8,128)(2,1)S(1)}, u32[]{:S(2)}, u32[]{:S(2)}) collective-permute-start(bf16[1,288,512]{2,1,0:T(8,128)(2,1)S(1)} %collective-permute-done.11.message_ref.mine_ref), channel_id=1, source_target_pairs={{1,0},{0,1},{3,2},{2,3},{5,4},{4,5},{7,6},{6,7},{9,8},{8,9},{11,10... | collective-permute-start | bytes 884744 | tf_op jit(solution)/shard_map/ppermute | solution.py:27
  26.3 1.6 %collective-permute-start.12 = (bf16[1,256,512]{2,1,0:T(8,128)(2,1)S(1)}, bf16[1,256,512]{2,1,0:T(8,128)(2,1)S(1)}, u32[]{:S(2)}, u32[]{:S(2)}) collective-permute-start(bf16[1,256,512]{2,1,0:T(8,128)(2,1)S(1)} %get-tuple-element.90), channel_id=1, source_target_pairs={{1,0},{0,1},{3,2},{2,3},{5,4},{4,5},{7,6},{6,7},{9,8},{8,9},{11,10... | collective-permute-start | bytes 786440 | tf_op jit(solution)/shard_map/ppermute | solution.py:27
  26.4 1.9 %collective-permute-start.13 = (bf16[1,256,512]{2,1,0:T(8,128)(2,1)S(1)}, bf16[1,256,512]{2,1,0:T(8,128)(2,1)S(1)}, u32[]{:S(2)}, u32[]{:S(2)}) collective-permute-start(bf16[1,256,512]{2,1,0:T(8,128)(2,1)S(1)} %get-tuple-element.91), channel_id=1, source_target_pairs={{1,0},{0,1},{3,2},{2,3},{5,4},{4,5},{7,6},{6,7},{9,8},{8,9},{11,10... | collective-permute-start | bytes 786440 | tf_op jit(solution)/shard_map/ppermute | solution.py:27
  26.9 1.8 %collective-permute-start.14 = (bf16[1,256,512]{2,1,0:T(8,128)(2,1)S(1)}, bf16[1,256,512]{2,1,0:T(8,128)(2,1)S(1)}, u32[]{:S(2)}, u32[]{:S(2)}) collective-permute-start(bf16[1,256,512]{2,1,0:T(8,128)(2,1)S(1)} %get-tuple-element.92.own_low_ref), channel_id=1, source_target_pairs={{1,0},{0,1},{3,2},{2,3},{5,4},{4,5},{7,6},{6,7},{9,8},{8,9},{11,10... | collective-permute-start | bytes 786440 | tf_op jit(solution)/shard_map/ppermute | solution.py:27
  29.2 7.7 %collective-permute-start.19 = (bf16[1,256,512]{2,1,0:T(8,128)(2,1)S(1)}, bf16[1,256,512]{2,1,0:T(8,128)(2,1)S(1)}, u32[]{:S(2)}, u32[]{:S(2)}) collective-permute-start(bf16[1,256,512]{2,1,0:T(8,128)(2,1)S(1)} %get-tuple-element.105.own_high_ref), channel_id=1, source_target_pairs={{1,0},{0,1},{3,2},{2,3},{5,4},{4,5},{7,6},{6,7},{9,8},{8,9},{11,10... | collective-permute-start | bytes 786440 | tf_op jit(solution)/shard_map/ppermute | solution.py:27
  29.6 9.0 %collective-permute-start.18 = (f32[4,512]{1,0:T(4,128)S(1)}, f32[4,512]{1,0:T(4,128)S(1)}, u32[]{:S(2)}, u32[]{:S(2)}) collective-permute-start(f32[4,512]{1,0:T(4,128)S(1)} %get-tuple-element.95.refs_0_), channel_id=1, source_target_pairs={{0,12},{1,13},{2,14},{3,15},{4,8},{5,9},{6,10},{7,11},{8,4},{9,5},... | collective-permute-start | bytes 24584 | tf_op jit(solution)/shard_map/ppermute | solution.py:684
  31.2 7.4 %collective-permute-start.17 = (f32[4,512]{1,0:T(4,128)S(1)}, f32[4,512]{1,0:T(4,128)S(1)}, u32[]{:S(2)}, u32[]{:S(2)}) collective-permute-start(f32[4,512]{1,0:T(4,128)S(1)} %get-tuple-element.95.refs_0_), channel_id=1, source_target_pairs={{0,8},{1,9},{2,10},{3,11},{4,12},{5,13},{6,14},{7,15},{8,0},{9,1},... | collective-permute-start | bytes 24584 | tf_op jit(solution)/shard_map/ppermute | solution.py:684
  31.3 7.4 %collective-permute-start.16 = (f32[4,512]{1,0:T(4,128)S(1)}, f32[4,512]{1,0:T(4,128)S(1)}, u32[]{:S(2)}, u32[]{:S(2)}) collective-permute-start(f32[4,512]{1,0:T(4,128)S(1)} %get-tuple-element.95.refs_0_), channel_id=1, source_target_pairs={{0,4},{1,5},{2,6},{3,7},{4,0},{5,1},{6,2},{7,3},{8,12},{9,13},{10,... | collective-permute-start | bytes 24584 | tf_op jit(solution)/shard_map/ppermute | solution.py:684
  38.7 3.7 %collective-permute-start.20 = (f32[4,512]{1,0:T(4,128)S(1)}, f32[4,512]{1,0:T(4,128)S(1)}, u32[]{:S(2)}, u32[]{:S(2)}) collective-permute-start(f32[4,512]{1,0:T(4,128)S(1)} %shard_map.76.one_ref), channel_id=1, source_target_pairs={{0,2},{1,3},{2,0},{3,1},{4,6},{5,7},{6,4},{7,5},{8,10},{9,11},{10,... | collective-permute-start | bytes 24584 | tf_op jit(solution)/shard_map/ppermute | solution.py:663
  42.4 1.2 %collective-permute-start.21 = (f32[8,512]{1,0:T(8,128)S(1)}, f32[8,512]{1,0:T(8,128)S(1)}, u32[]{:S(2)}, u32[]{:S(2)}) collective-permute-start(f32[8,512]{1,0:T(8,128)S(1)} %shard_map.78.mine_ref), channel_id=1, source_target_pairs={{1,0},{0,1},{3,2},{2,3},{5,4},{4,5},{7,6},{6,7},{9,8},{8,9},{11,10... | collective-permute-start | bytes 49160 | tf_op jit(solution)/shard_map/ppermute | solution.py:27

commit v13 on v10

--- a/solution.py
+++ b/solution.py
@@ -163,16 +163,17 @@
     out_ref[...] = one_ref[...] + two_ref[...]
 
 
-def join_kernel(sent_ref, one_ref, two_ref, out_ref):
-    planes = sent_ref.shape[0]
-    out_ref[:planes] = sent_ref[...]
-    out_ref[planes:] = one_ref[...] + two_ref[...]
-
-
-def divide_kernel(cells, kept_ref, mine_ref, arrived_ref, out_ref):
+def add_wide_kernel(one_ref, two_ref, out_ref):
+    planes = one_ref.shape[0]
+    for k in range(out_ref.shape[0] // planes):
+        out_ref[k * planes : (k + 1) * planes] = one_ref[...] + two_ref[...]
+
+
+def divide_kernel(cells, kept_ref, arrived_ref, *refs):
+    *total_refs, out_ref = refs
     planes = kept_ref.shape[0]
-    total = mine_ref[planes:] + arrived_ref[planes:]
-    out_ref[...] = (kept_ref[...] + arrived_ref[:planes]) * (cells / total)
+    total = functools.reduce(jnp.add, [ref[:planes] for ref in total_refs])
+    out_ref[...] = (kept_ref[...] + arrived_ref[...]) * (cells / total)
 
 
 def message_kernel(*refs):
@@ -681,10 +682,14 @@
         (third_state, partner, spread, weights, partner_faces[0], *partner_inner, partner_faces[1]),
     )
     distance = 8
-    while distance < count:
+    while distance < count // 2:
         partition, shared = gathered(partition, distance, shared)
         distance *= 2
+    block, shared = received(partition, distance, shared)
+    triple = jax.ShapeDtypeStruct((3 * planes, cells), F32)
+    partition = kernel_call(add_wide_kernel, triple, (), (partition, block))
     arrived2, shared, _ = lax.optimization_barrier((arrived[1], shared, partition))
+    beside = [lax.ppermute(partition, "space", [(i, i ^ near) for i in range(count)]) for near in (2, 3, 1)]
     sent, kept = kernel_call(
         last_kernel,
         (density, density),
@@ -694,15 +699,11 @@
             own, partner, spread, matrix,
         ),
     )
-    beside, sent = received(partition, 2, sent)
-    joined = kernel_call(
-        join_kernel, jax.ShapeDtypeStruct((2 * planes, cells), F32), (), (sent, partition, beside)
-    )
     return kernel_call(
         functools.partial(divide_kernel, count // 2 * planes * cells),
         density,
         (),
-        (kept, joined, swap_species(joined)),
+        (kept, swap_species(sent), partition, *beside),
     )
 
 

time: 43.3 us -> 43.9 us (1.014)
  starting transfers between devices: 15.7 us -> 17.9 us
  waiting for transfers between devices: 9.46 us -> 7.88 us
    ppermute x0 -> x3, starting transfers between devices: none -> 2.13 us  [shards(): lax.ppermute(partition, 'space', [(i, i ^ near) for i in range(count)])]
    ppermute x3 -> x2, waiting for transfers between devices: 3.88 us -> 1.91 us  [received(): lax.ppermute(value, 'space', [(i, i ^ distance) for i in range(count)])]
    ppermute x3 -> x2, starting transfers between devices: 1.77 us -> 1.76 us  [received(): lax.ppermute(value, 'space', [(i, i ^ distance) for i in range(count)])]
    pallas_call x17 -> x16, Pallas kernels: 16.3 us -> 16.3 us  [kernel_call(): pl.pallas_call(kernel, out_shape=outs, in_specs=[smem if arg.dtype == jnp...]
  transfers between devices with their start and end apart: 21 -> 23, of which waited for: 12 -> 11; matrix products, arithmetic and copies ran while one was open for 3% -> 3% of each run, Pallas kernels for 36% -> 35%
where the time goes in v13:
time: 43.9 us; the launch traced here: 43.8 us
  starting transfers between devices  17.9 us (41%)
  Pallas kernels  16.3 us (37%)
  waiting for transfers between devices  7.88 us (18%)
  local copies, waits for them, and re-layouts  1.44 us (3%)
    pallas_call x16, Pallas kernels, kernel_call(): pl.pallas_call(kernel, out_shape=outs, in_specs=[smem if arg.dtype == jnp...  16.3 us
    ppermute x15, starting transfers between devices, swap_species(): return lax.ppermute(block, 'space', [(i ^ 1, i) for i in range(count)])  8.72 us
    ppermute x15, waiting for transfers between devices, swap_species(): return lax.ppermute(block, 'space', [(i ^ 1, i) for i in range(count)])  5.95 us
    ppermute x3, starting transfers between devices, exchange_faces(): return lax.ppermute(block, 'space', route)  5.31 us
    ppermute x3, starting transfers between devices, shards(): lax.ppermute(partition, 'space', [(i, i ^ near) for i in range(count)])  2.13 us
    ppermute x2, waiting for transfers between devices, received(): lax.ppermute(value, 'space', [(i, i ^ distance) for i in range(count)])  1.91 us
    ppermute x2, starting transfers between devices, received(): lax.ppermute(value, 'space', [(i, i ^ distance) for i in range(count)])  1.76 us
    unnamed x11, local copies, waits for them, and re-layouts  1.44 us
  transfers between devices with their start and end apart: 23, of which 11 were waited for; matrix products, arithmetic and copies ran while one was open for 3% of the time, Pallas kernels for 35%

profile of v13, /device:TPU:0, one launch (start us, length us, event | category | flops | bytes accessed | tf_op | source)
XLA Modules:
  0.0 43.8 jit_solution(2269384825011077654)
XLA Ops:
  0.0 0.5 %collective-permute-start = (f32[4,512]{1,0:T(4,128)}, f32[4,512]{1,0:T(4,128)S(1)}, u32[]{:S(2)}, u32[]{:S(2)}) collective-permute-start(f32[4,512]{1,0:T(4,128)} %param.6), channel_id=1, source_target_pairs={{1,0},{0,1},{3,2},{2,3},{5,4},{4,5},{7,6},{6,7},{9,8},{8,9},{11,10... | collective-permute-start | bytes 24584 | tf_op jit(solution)/shard_map/ppermute | solution.py:27
  0.6 1.4 %copy.9 = bf16[256,4,512]{2,0,1:T(8,128)(2,1)S(1)} copy(bf16[256,4,512]{2,1,0:T(4,128)(2,1)} %param.7) | data formatting | bytes 2097152 | tf_op args[1]
  2.8 1.1 %collective-permute-done.1.other_ref = bf16[1,256,512]{2,1,0:T(8,128)(2,1)S(1)} collective-permute-done((bf16[1,256,512]{2,1,0:T(8,128)(2,1)S(1)}, bf16[1,256,512]{2,1,0:T(8,128)(2,1)S(1)}, u32[]{:S(2)}, u32[]{:S(2)}) %collective-permute-start.1) | collective-permute-done | bytes 262176 | tf_op jit(solution)/shard_map/ppermute | solution.py:27
  4.2 2.9 %collective-permute-start.6 = (bf16[1,272,512]{2,1,0:T(8,128)(2,1)S(1)}, bf16[1,272,512]{2,1,0:T(8,128)(2,1)S(1)}, u32[]{:S(2)}, u32[]{:S(2)}) collective-permute-start(bf16[1,272,512]{2,1,0:T(8,128)(2,1)S(1)} %shard_map.66), channel_id=1, source_target_pairs={{0,2},{1,15},{2,0},{3,5},{4,6},{5,3},{6,4},{7,9},{8,10},{9,7},{10,... | collective-permute-start | bytes 835592 | tf_op jit(solution)/shard_map/ppermute | solution.py:36
  7.1 2.0 %shard_map.67 = (bf16[4,256,512]{2,1,0:T(8,128)(2,1)S(1)}, bf16[1,256,512]{2,1,0:T(8,128)(2,1)S(1)}, bf16[1,256,512]{2,1,0:T(8,128)(2,1)S(1)}, bf16[1,256,512]{2,1,0:T(8,128)(2,1)S(1)}) custom-call(bf16[4,256,512]{2,1,0:T(8,128)(2,1)S(1)} %bitcast.8, f32[4,512]{1,0:T(4,128)S(1)} %get-tuple-element.114.fields_ref.first_ref.own_ref, ...), custom_call_target="tpu_custom_call" | custom-call | tf_op jit(solution)/shard_map/pallas_call | solution.py:558
  9.0 3.0 %collective-permute-start.4 = (bf16[1,256,512]{2,1,0:T(8,128)(2,1)S(1)}, bf16[1,256,512]{2,1,0:T(8,128)(2,1)S(1)}, u32[]{:S(2)}, u32[]{:S(2)}) collective-permute-start(bf16[1,256,512]{2,1,0:T(8,128)(2,1)S(1)} %get-tuple-element.70), channel_id=1, source_target_pairs={{1,0},{0,1},{3,2},{2,3},{5,4},{4,5},{7,6},{6,7},{9,8},{8,9},{11,10... | collective-permute-start | bytes 786440 | tf_op jit(solution)/shard_map/ppermute | solution.py:27
  12.1 0.4 collective-permute-start.2
  12.5 0.6 %shard_map.68 = (bf16[4,256,512]{2,1,0:T(8,128)(2,1)S(1)}, bf16[2,256,512]{2,1,0:T(8,128)(2,1)S(1)}) custom-call(s32[1]{0:T(128)} %bitcast.core_ref, bf16[4,256,512]{2,1,0:T(8,128)(2,1)S(1)} %collective-permute-done.3.partner_ref, bf16[4,256,512]{2,1,0:T(8,128)(2,1)S(1)} %bitcast.9, bf16[256,256]{1,0:T(8,128)(2,1)S(1)} %get-tuple-element.68.turned_ref), custom_call_target="tpu_custom_call" | custom-call | tf_op jit(solution)/shard_map/pallas_call | solution.py:558
  13.2 0.4 collective-permute-done.5.refs_2_
  13.5 0.4 collective-permute-done.2.other_ref
  14.1 2.8 %shard_map.70 = (bf16[4,256,512]{2,1,0:T(8,128)(2,1)S(1)}, bf16[1,256,512]{2,1,0:T(8,128)(2,1)S(1)}, bf16[1,256,512]{2,1,0:T(8,128)(2,1)S(1)}) custom-call(bf16[4,256,512]{2,1,0:T(8,128)(2,1)S(1)} %get-tuple-element.79.state_ref.alone_ref, f32[4,512]{1,0:T(4,128)S(1)} %get-tuple-element.114.fields_ref.first_ref.own_ref, ...), custom_call_target="tpu_custom_call" | custom-call | tf_op jit(solution)/shard_map/pallas_call | solution.py:558
  16.9 0.9 %collective-permute-start.10 = (bf16[1,272,512]{2,1,0:T(8,128)(2,1)S(1)}, bf16[1,272,512]{2,1,0:T(8,128)(2,1)S(1)}, u32[]{:S(2)}, u32[]{:S(2)}) collective-permute-start(bf16[1,272,512]{2,1,0:T(8,128)(2,1)S(1)} %collective-permute-done.6.mine_ref), channel_id=1, source_target_pairs={{1,0},{0,1},{3,2},{2,3},{5,4},{4,5},{7,6},{6,7},{9,8},{8,9},{11,10... | collective-permute-start | bytes 835592 | tf_op jit(solution)/shard_map/ppermute | solution.py:27
  17.9 0.4 collective-permute-start.8
  18.4 1.0 %collective-permute-done.7.refs_2_ = bf16[1,256,512]{2,1,0:T(8,128)(2,1)S(1)} collective-permute-done((bf16[1,256,512]{2,1,0:T(8,128)(2,1)S(1)}, bf16[1,256,512]{2,1,0:T(8,128)(2,1)S(1)}, u32[]{:S(2)}, u32[]{:S(2)}) %collective-permute-start.7) | collective-permute-done | bytes 262176 | tf_op jit(solution)/shard_map/ppermute | solution.py:27
  19.4 0.4 collective-permute-done.8.refs_3_
  19.9 2.4 %collective-permute-start.9 = (bf16[2,288,512]{2,1,0:T(8,128)(2,1)S(1)}, bf16[2,288,512]{2,1,0:T(8,128)(2,1)S(1)}, u32[]{:S(2)}, u32[]{:S(2)}) collective-permute-start(bf16[2,288,512]{2,1,0:T(8,128)(2,1)S(1)} %shard_map.71), channel_id=1, source_target_pairs={{0,2},{1,15},{2,0},{3,5},{4,6},{5,3},{6,4},{7,9},{8,10},{9,7},{10,... | collective-permute-start | bytes 1769480 | tf_op jit(solution)/shard_map/ppermute | solution.py:36
  22.2 2.7 %shard_map.72 = (bf16[1,256,512]{2,1,0:T(8,128)(2,1)S(1)}, bf16[1,256,512]{2,1,0:T(8,128)(2,1)S(1)}, bf16[8,256,512]{2,1,0:T(8,128)(2,1)S(1)}, bf16[1,256,512]{2...) custom-call(s32[1]{0:T(128)} %bitcast.core_ref, ...), custom_call_target="tpu_custom_call" | custom-call | tf_op jit(solution)/shard_map/pallas_call | solution.py:558
  24.9 1.8 %collective-permute-start.14 = (bf16[1,288,512]{2,1,0:T(8,128)(2,1)S(1)}, bf16[1,288,512]{2,1,0:T(8,128)(2,1)S(1)}, u32[]{:S(2)}, u32[]{:S(2)}) collective-permute-start(bf16[1,288,512]{2,1,0:T(8,128)(2,1)S(1)} %collective-permute-done.11.message_ref.mine_ref), channel_id=1, source_target_pairs={{1,0},{0,1},{3,2},{2,3},{5,4},{4,5},{7,6},{6,7},{9,8},{8,9},{11,10... | collective-permute-start | bytes 884744 | tf_op jit(solution)/shard_map/ppermute | solution.py:27
  26.8 0.4 collective-permute-start.13
  27.3 1.1 %collective-permute-done.12.near_ref = bf16[1,256,512]{2,1,0:T(8,128)(2,1)S(1)} collective-permute-done((bf16[1,256,512]{2,1,0:T(8,128)(2,1)S(1)}, bf16[1,256,512]{2,1,0:T(8,128)(2,1)S(1)}, u32[]{:S(2)}, u32[]{:S(2)}) %collective-permute-start.12) | collective-permute-done | bytes 262176 | tf_op jit(solution)/shard_map/ppermute | solution.py:27
  28.3 0.4 collective-permute-done.13.far_ref
  28.7 0.6 %shard_map.73 = (f32[2,512]{1,0:T(2,128)S(1)}, f32[4,512]{1,0:T(4,128)S(1)}) custom-call(s32[1]{0:T(128)} %bitcast.core_ref, bf16[2,256,512]{2,1,0:T(8,128)(2,1)S(1)} %get-tuple-element.82.own_ref, bf16[1,256,512]{2,1,0:T(8,128)(2,1)S(1)} %collective-permute-done.12.near_ref, bf16[1,256,512]{2,1,0:T(8,128)(2,1)S(1)} %collective-permute-done.13.far_ref, ...), custom_call_target="tpu_custom_call" | custom-call | tf_op jit(solution)/shard_map/pallas_call | solution.py:558
  29.3 0.4 collective-permute-start.17
  30.0 3.0 %shard_map.74.held_ref = bf16[6,256,512]{2,1,0:T(8,128)(2,1)S(1)} custom-call(bf16[8,256,512]{2,1,0:T(8,128)(2,1)S(1)} %get-tuple-element.96.held_ref, bf16[1,288,512]{2,1,0:T(8,128)(2,1)S(1)} %collective-permute-done.11.message_ref.mine_ref, bf16[1,288,512]{2,1,0:T(8,128)(2,1)S(1)} %collective-permute-done.14.other_ref, ...), custom_call_target="tpu_custom_call" | custom-call | tf_op jit(solution)/shard_map/pallas_call | solution.py:558
  33.0 0.5 %collective-permute-done.15.two_ref = f32[4,512]{1,0:T(4,128)S(1)} collective-permute-done((f32[4,512]{1,0:T(4,128)S(1)}, f32[4,512]{1,0:T(4,128)S(1)}, u32[]{:S(2)}, u32[]{:S(2)}) %collective-permute-start.15) | collective-permute-done | bytes 8224 | tf_op jit(solution)/shard_map/ppermute | solution.py:661
  33.5 1.6 %collective-permute-start.16 = (f32[4,512]{1,0:T(4,128)S(1)}, f32[4,512]{1,0:T(4,128)S(1)}, u32[]{:S(2)}, u32[]{:S(2)}) collective-permute-start(f32[4,512]{1,0:T(4,128)S(1)} %shard_map.75.one_ref), channel_id=1, source_target_pairs={{0,8},{1,9},{2,10},{3,11},{4,12},{5,13},{6,14},{7,15},{8,0},{9,1},... | collective-permute-start | bytes 24584 | tf_op jit(solution)/shard_map/ppermute | solution.py:661
  35.1 1.6 %shard_map.76.shared_ref = f32[4,512]{1,0:T(4,128)S(1)} custom-call(bf16[6,256,512]{2,1,0:T(8,128)(2,1)S(1)} %shard_map.74.held_ref, f32[4,512]{1,0:T(4,128)S(1)} %get-tuple-element.113.partner_ref.second_ref, f32[4,256,128]{2,1,0:T(8,128)S(1)} %get-tuple-element.63.refs_1_.v_ref.refs_2_.refs_4_, bf16[4,256,512]{2,1,0:T(8,128)(2,1)S(1)} %get-tuple-element.73.weight_ref, ...), custom_call_target="tpu_custom_call" | custom-call | tf_op jit(solution)/shard_map/pallas_call | solution.py:558
  36.7 1.4 %collective-permute-done.16.two_ref = f32[4,512]{1,0:T(4,128)S(1)} collective-permute-done((f32[4,512]{1,0:T(4,128)S(1)}, f32[4,512]{1,0:T(4,128)S(1)}, u32[]{:S(2)}, u32[]{:S(2)}) %collective-permute-start.16) | collective-permute-done | bytes 8224 | tf_op jit(solution)/shard_map/ppermute | solution.py:661
  38.2 2.1 %collective-permute-start.20 = (f32[12,512]{1,0:T(8,128)S(1)}, f32[12,512]{1,0:T(8,128)S(1)}, u32[]{:S(2)}, u32[]{:S(2)}) collective-permute-start(f32[12,512]{1,0:T(8,128)S(1)} %shard_map.77.refs_0_), channel_id=1, source_target_pairs={{0,2},{1,3},{2,0},{3,1},{4,6},{5,7},{6,4},{7,5},{8,10},{9,11},{10,... | collective-permute-start | bytes 73736 | tf_op jit(solution)/shard_map/ppermute | solution.py:692
  40.2 1.6 %shard_map.78 = (f32[4,512]{1,0:T(4,128)S(1)}, f32[4,512]{1,0:T(4,128)S(1)}) custom-call(s32[1]{0:T(128)} %bitcast.core_ref, bf16[2,288,512]{2,1,0:T(8,128)(2,1)S(1)} %collective-permute-done.9.message_ref, bf16[4,256,512]{2,1,0:T(8,128)(2,1)S(1)} %get-tuple-element.73.weight_ref, bf16[2,256,512]{2,1,0:T(8,128)(2,1)S(1)} %get-tuple-element.109.own_weight_ref, ...), custom_call_target="tpu_custom_call" | custom-call | tf_op jit(solution)/shard_map/pallas_call | solution.py:558
  42.0 1.2 %collective-permute-done.19.arrived_ref = f32[4,512]{1,0:T(4,128)S(1)} collective-permute-done((f32[4,512]{1,0:T(4,128)S(1)}, f32[4,512]{1,0:T(4,128)S(1)}, u32[]{:S(2)}, u32[]{:S(2)}) %collective-permute-start.19) | collective-permute-done | bytes 8224 | tf_op jit(solution)/shard_map/ppermute | solution.py:27
  43.1 0.6 %shard_map.79 = f32[4,512]{1,0:T(4,128)} custom-call(f32[4,512]{1,0:T(4,128)S(1)} %get-tuple-element.111.kept_ref, f32[4,512]{1,0:T(4,128)S(1)} %collective-permute-done.19.arrived_ref, f32[12,512]{1,0:T(8,128)S(1)} %shard_map.77.refs_0_, f32[12,512]{1,0:T(8,128)S(1)} %collective-permute-done.20.refs_1_, f32[12,512]{1,0:T(8,128)S(1)} %collective-permute-done.21.refs_2_, ...), custom_call_target="tpu_custom_call" | custom-call | tf_op jit(solution)/shard_map/pallas_call | solution.py:558
  (43 shorter events, 2.2 us)
Async XLA Ops:
  0.0 2.0 %copy-start.4 = (f32[4,512]{1,0:T(4,128)S(1)}, f32[4,512]{1,0:T(4,128)}, u32[]{:S(2)}) copy-start(f32[4,512]{1,0:T(4,128)} %param.6) | copy-start | bytes 24580
  0.0 2.1 %copy-start.2 = (f32[3,256]{1,0:T(4,128)S(1)}, f32[3,256]{1,0:T(4,128)}, u32[]{:S(2)}) copy-start(f32[3,256]{1,0:T(4,128)} %directions_ref.1) | copy-start | bytes 9220
  0.0 2.5 %copy-start.3 = (f32[256]{0:T(256)S(1)}, f32[256]{0:T(256)}, u32[]{:S(2)}) copy-start(f32[256]{0:T(256)} %param.11) | copy-start | bytes 3076
  0.0 2.5 %copy-start = (bf16[256,256]{1,0:T(8,128)(2,1)S(1)}, bf16[256,256]{1,0:T(8,128)(2,1)}, u32[]{:S(2)}) copy-start(bf16[256,256]{1,0:T(8,128)(2,1)} %synthesis_ref.1) | copy-start | bytes 393220
  0.0 2.5 %copy-start.1 = (bf16[256,256]{1,0:T(8,128)(2,1)S(1)}, bf16[256,256]{1,0:T(8,128)(2,1)}, u32[]{:S(2)}) copy-start(bf16[256,256]{1,0:T(8,128)(2,1)} %analysis_ref.1) | copy-start | bytes 393220
  0.0 2.0 %collective-permute-start = (f32[4,512]{1,0:T(4,128)}, f32[4,512]{1,0:T(4,128)S(1)}, u32[]{:S(2)}, u32[]{:S(2)}) collective-permute-start(f32[4,512]{1,0:T(4,128)} %param.6), channel_id=1, source_target_pairs={{1,0},{0,1},{3,2},{2,3},{5,4},{4,5},{7,6},{6,7},{9,8},{8,9},{11,10... | collective-permute-start | bytes 24584 | tf_op jit(solution)/shard_map/ppermute | solution.py:27
  2.3 1.6 %collective-permute-start.1 = (bf16[1,256,512]{2,1,0:T(8,128)(2,1)S(1)}, bf16[1,256,512]{2,1,0:T(8,128)(2,1)S(1)}, u32[]{:S(2)}, u32[]{:S(2)}) collective-permute-start(bf16[1,256,512]{2,1,0:T(8,128)(2,1)S(1)} %get-tuple-element.59.mine_ref.edge_ref), channel_id=1, source_target_pairs={{1,0},{0,1},{3,2},{2,3},{5,4},{4,5},{7,6},{6,7},{9,8},{8,9},{11,10... | collective-permute-start | bytes 786440 | tf_op jit(solution)/shard_map/ppermute | solution.py:27
  4.0 8.5 %collective-permute-start.3 = (bf16[4,256,512]{2,1,0:T(8,128)(2,1)S(1)}, bf16[4,256,512]{2,1,0:T(8,128)(2,1)S(1)}, u32[]{:S(2)}, u32[]{:S(2)}) collective-permute-start(bf16[4,256,512]{2,1,0:T(8,128)(2,1)S(1)} %bitcast.7), channel_id=1, source_target_pairs={{1,0},{0,1},{3,2},{2,3},{5,4},{4,5},{7,6},{6,7},{9,8},{8,9},{11,10... | collective-permute-start | bytes 3145736 | tf_op jit(solution)/shard_map/ppermute | solution.py:27
  4.2 12.7 %collective-permute-start.6 = (bf16[1,272,512]{2,1,0:T(8,128)(2,1)S(1)}, bf16[1,272,512]{2,1,0:T(8,128)(2,1)S(1)}, u32[]{:S(2)}, u32[]{:S(2)}) collective-permute-start(bf16[1,272,512]{2,1,0:T(8,128)(2,1)S(1)} %shard_map.66), channel_id=1, source_target_pairs={{0,2},{1,15},{2,0},{3,5},{4,6},{5,3},{6,4},{7,9},{8,10},{9,7},{10,... | collective-permute-start | bytes 835592 | tf_op jit(solution)/shard_map/ppermute | solution.py:36
  9.0 4.1 %collective-permute-start.4 = (bf16[1,256,512]{2,1,0:T(8,128)(2,1)S(1)}, bf16[1,256,512]{2,1,0:T(8,128)(2,1)S(1)}, u32[]{:S(2)}, u32[]{:S(2)}) collective-permute-start(bf16[1,256,512]{2,1,0:T(8,128)(2,1)S(1)} %get-tuple-element.70), channel_id=1, source_target_pairs={{1,0},{0,1},{3,2},{2,3},{5,4},{4,5},{7,6},{6,7},{9,8},{8,9},{11,10... | collective-permute-start | bytes 786440 | tf_op jit(solution)/shard_map/ppermute | solution.py:27
  12.0 1.5 %collective-permute-start.5 = (bf16[1,256,512]{2,1,0:T(8,128)(2,1)S(1)}, bf16[1,256,512]{2,1,0:T(8,128)(2,1)S(1)}, u32[]{:S(2)}, u32[]{:S(2)}) collective-permute-start(bf16[1,256,512]{2,1,0:T(8,128)(2,1)S(1)} %get-tuple-element.71), channel_id=1, source_target_pairs={{1,0},{0,1},{3,2},{2,3},{5,4},{4,5},{7,6},{6,7},{9,8},{8,9},{11,10... | collective-permute-start | bytes 786440 | tf_op jit(solution)/shard_map/ppermute | solution.py:27
  12.1 1.8 %collective-permute-start.2 = (bf16[1,256,512]{2,1,0:T(8,128)(2,1)S(1)}, bf16[1,256,512]{2,1,0:T(8,128)(2,1)S(1)}, u32[]{:S(2)}, u32[]{:S(2)}) collective-permute-start(bf16[1,256,512]{2,1,0:T(8,128)(2,1)S(1)} %get-tuple-element.67.mine_ref), channel_id=1, source_target_pairs={{1,0},{0,1},{3,2},{2,3},{5,4},{4,5},{7,6},{6,7},{9,8},{8,9},{11,10... | collective-permute-start | bytes 786440 | tf_op jit(solution)/shard_map/ppermute | solution.py:27
  14.0 10.9 %collective-permute-start.11 = (bf16[1,288,512]{2,1,0:T(8,128)(2,1)S(1)}, bf16[1,288,512]{2,1,0:T(8,128)(2,1)S(1)}, u32[]{:S(2)}, u32[]{:S(2)}) collective-permute-start(bf16[1,288,512]{2,1,0:T(8,128)(2,1)S(1)} %shard_map.69), channel_id=1, source_target_pairs={{0,2},{1,15},{2,0},{3,5},{4,6},{5,3},{6,4},{7,9},{8,10},{9,7},{10,... | collective-permute-start | bytes 884744 | tf_op jit(solution)/shard_map/ppermute | solution.py:36
  16.9 5.3 %collective-permute-start.10 = (bf16[1,272,512]{2,1,0:T(8,128)(2,1)S(1)}, bf16[1,272,512]{2,1,0:T(8,128)(2,1)S(1)}, u32[]{:S(2)}, u32[]{:S(2)}) collective-permute-start(bf16[1,272,512]{2,1,0:T(8,128)(2,1)S(1)} %collective-permute-done.6.mine_ref), channel_id=1, source_target_pairs={{1,0},{0,1},{3,2},{2,3},{5,4},{4,5},{7,6},{6,7},{9,8},{8,9},{11,10... | collective-permute-start | bytes 835592 | tf_op jit(solution)/shard_map/ppermute | solution.py:27
  17.8 1.6 %collective-permute-start.7 = (bf16[1,256,512]{2,1,0:T(8,128)(2,1)S(1)}, bf16[1,256,512]{2,1,0:T(8,128)(2,1)S(1)}, u32[]{:S(2)}, u32[]{:S(2)}) collective-permute-start(bf16[1,256,512]{2,1,0:T(8,128)(2,1)S(1)} %get-tuple-element.77.refs_0_), channel_id=1, source_target_pairs={{1,0},{0,1},{3,2},{2,3},{5,4},{4,5},{7,6},{6,7},{9,8},{8,9},{11,10... | collective-permute-start | bytes 786440 | tf_op jit(solution)/shard_map/ppermute | solution.py:27
  17.9 1.9 %collective-permute-start.8 = (bf16[1,256,512]{2,1,0:T(8,128)(2,1)S(1)}, bf16[1,256,512]{2,1,0:T(8,128)(2,1)S(1)}, u32[]{:S(2)}, u32[]{:S(2)}) collective-permute-start(bf16[1,256,512]{2,1,0:T(8,128)(2,1)S(1)} %get-tuple-element.78.refs_1_), channel_id=1, source_target_pairs={{1,0},{0,1},{3,2},{2,3},{5,4},{4,5},{7,6},{6,7},{9,8},{8,9},{11,10... | collective-permute-start | bytes 786440 | tf_op jit(solution)/shard_map/ppermute | solution.py:27
  19.9 20.4 %collective-permute-start.9 = (bf16[2,288,512]{2,1,0:T(8,128)(2,1)S(1)}, bf16[2,288,512]{2,1,0:T(8,128)(2,1)S(1)}, u32[]{:S(2)}, u32[]{:S(2)}) collective-permute-start(bf16[2,288,512]{2,1,0:T(8,128)(2,1)S(1)} %shard_map.71), channel_id=1, source_target_pairs={{0,2},{1,15},{2,0},{3,5},{4,6},{5,3},{6,4},{7,9},{8,10},{9,7},{10,... | collective-permute-start | bytes 1769480 | tf_op jit(solution)/shard_map/ppermute | solution.py:36
  24.9 3.8 %collective-permute-start.14 = (bf16[1,288,512]{2,1,0:T(8,128)(2,1)S(1)}, bf16[1,288,512]{2,1,0:T(8,128)(2,1)S(1)}, u32[]{:S(2)}, u32[]{:S(2)}) collective-permute-start(bf16[1,288,512]{2,1,0:T(8,128)(2,1)S(1)} %collective-permute-done.11.message_ref.mine_ref), channel_id=1, source_target_pairs={{1,0},{0,1},{3,2},{2,3},{5,4},{4,5},{7,6},{6,7},{9,8},{8,9},{11,10... | collective-permute-start | bytes 884744 | tf_op jit(solution)/shard_map/ppermute | solution.py:27
  26.8 1.6 %collective-permute-start.12 = (bf16[1,256,512]{2,1,0:T(8,128)(2,1)S(1)}, bf16[1,256,512]{2,1,0:T(8,128)(2,1)S(1)}, u32[]{:S(2)}, u32[]{:S(2)}) collective-permute-start(bf16[1,256,512]{2,1,0:T(8,128)(2,1)S(1)} %get-tuple-element.87), channel_id=1, source_target_pairs={{1,0},{0,1},{3,2},{2,3},{5,4},{4,5},{7,6},{6,7},{9,8},{8,9},{11,10... | collective-permute-start | bytes 786440 | tf_op jit(solution)/shard_map/ppermute | solution.py:27
  26.8 1.9 %collective-permute-start.13 = (bf16[1,256,512]{2,1,0:T(8,128)(2,1)S(1)}, bf16[1,256,512]{2,1,0:T(8,128)(2,1)S(1)}, u32[]{:S(2)}, u32[]{:S(2)}) collective-permute-start(bf16[1,256,512]{2,1,0:T(8,128)(2,1)S(1)} %get-tuple-element.88), channel_id=1, source_target_pairs={{1,0},{0,1},{3,2},{2,3},{5,4},{4,5},{7,6},{6,7},{9,8},{8,9},{11,10... | collective-permute-start | bytes 786440 | tf_op jit(solution)/shard_map/ppermute | solution.py:27
  29.3 5.8 %collective-permute-start.17 = (bf16[1,256,512]{2,1,0:T(8,128)(2,1)S(1)}, bf16[1,256,512]{2,1,0:T(8,128)(2,1)S(1)}, u32[]{:S(2)}, u32[]{:S(2)}) collective-permute-start(bf16[1,256,512]{2,1,0:T(8,128)(2,1)S(1)} %get-tuple-element.102.own_low_ref), channel_id=1, source_target_pairs={{1,0},{0,1},{3,2},{2,3},{5,4},{4,5},{7,6},{6,7},{9,8},{8,9},{11,10... | collective-permute-start | bytes 786440 | tf_op jit(solution)/shard_map/ppermute | solution.py:27
  29.7 5.4 %collective-permute-start.18 = (bf16[1,256,512]{2,1,0:T(8,128)(2,1)S(1)}, bf16[1,256,512]{2,1,0:T(8,128)(2,1)S(1)}, u32[]{:S(2)}, u32[]{:S(2)}) collective-permute-start(bf16[1,256,512]{2,1,0:T(8,128)(2,1)S(1)} %get-tuple-element.105.own_high_ref), channel_id=1, source_target_pairs={{1,0},{0,1},{3,2},{2,3},{5,4},{4,5},{7,6},{6,7},{9,8},{8,9},{11,10... | collective-permute-start | bytes 786440 | tf_op jit(solution)/shard_map/ppermute | solution.py:27
  29.8 3.7 %collective-permute-start.15 = (f32[4,512]{1,0:T(4,128)S(1)}, f32[4,512]{1,0:T(4,128)S(1)}, u32[]{:S(2)}, u32[]{:S(2)}) collective-permute-start(f32[4,512]{1,0:T(4,128)S(1)} %get-tuple-element.91.one_ref), channel_id=1, source_target_pairs={{0,4},{1,5},{2,6},{3,7},{4,0},{5,1},{6,2},{7,3},{8,12},{9,13},{10,... | collective-permute-start | bytes 24584 | tf_op jit(solution)/shard_map/ppermute | solution.py:661
  33.5 4.6 %collective-permute-start.16 = (f32[4,512]{1,0:T(4,128)S(1)}, f32[4,512]{1,0:T(4,128)S(1)}, u32[]{:S(2)}, u32[]{:S(2)}) collective-permute-start(f32[4,512]{1,0:T(4,128)S(1)} %shard_map.75.one_ref), channel_id=1, source_target_pairs={{0,8},{1,9},{2,10},{3,11},{4,12},{5,13},{6,14},{7,15},{8,0},{9,1},... | collective-permute-start | bytes 24584 | tf_op jit(solution)/shard_map/ppermute | solution.py:661
  38.1 5.0 %collective-permute-start.22 = (f32[12,512]{1,0:T(8,128)S(1)}, f32[12,512]{1,0:T(8,128)S(1)}, u32[]{:S(2)}, u32[]{:S(2)}) collective-permute-start(f32[12,512]{1,0:T(8,128)S(1)} %shard_map.77.refs_0_), channel_id=1, source_target_pairs={{0,1},{1,0},{2,3},{3,2},{4,5},{5,4},{6,7},{7,6},{8,9},{9,8},{10,11... | collective-permute-start | bytes 73736 | tf_op jit(solution)/shard_map/ppermute | solution.py:692
  38.1 5.0 %collective-permute-start.21 = (f32[12,512]{1,0:T(8,128)S(1)}, f32[12,512]{1,0:T(8,128)S(1)}, u32[]{:S(2)}, u32[]{:S(2)}) collective-permute-start(f32[12,512]{1,0:T(8,128)S(1)} %shard_map.77.refs_0_), channel_id=1, source_target_pairs={{0,3},{1,2},{2,1},{3,0},{4,7},{5,6},{6,5},{7,4},{8,11},{9,10},{10,... | collective-permute-start | bytes 73736 | tf_op jit(solution)/shard_map/ppermute | solution.py:692
  38.2 5.0 %collective-permute-start.20 = (f32[12,512]{1,0:T(8,128)S(1)}, f32[12,512]{1,0:T(8,128)S(1)}, u32[]{:S(2)}, u32[]{:S(2)}) collective-permute-start(f32[12,512]{1,0:T(8,128)S(1)} %shard_map.77.refs_0_), channel_id=1, source_target_pairs={{0,2},{1,3},{2,0},{3,1},{4,6},{5,7},{6,4},{7,5},{8,10},{9,11},{10,... | collective-permute-start | bytes 73736 | tf_op jit(solution)/shard_map/ppermute | solution.py:692
  41.9 1.2 %collective-permute-start.19 = (f32[4,512]{1,0:T(4,128)S(1)}, f32[4,512]{1,0:T(4,128)S(1)}, u32[]{:S(2)}, u32[]{:S(2)}) collective-permute-start(f32[4,512]{1,0:T(4,128)S(1)} %get-tuple-element.112), channel_id=1, source_target_pairs={{1,0},{0,1},{3,2},{2,3},{5,4},{4,5},{7,6},{6,7},{9,8},{8,9},{11,10... | collective-permute-start | bytes 24584 | tf_op jit(solution)/shard_map/ppermute | solution.py:27

commit v14 on v10

--- a/solution.py
+++ b/solution.py
@@ -646,7 +646,7 @@
     )
     arrived1, second_state = lax.optimization_barrier((arrived[0], second_state))
     *moving, _ = lax.optimization_barrier((*sent_half, arrived1))
-    *partner_half, crossed1 = lax.optimization_barrier((*map(swap_species, moving), swap_species(arrived1)))
+    partner_half = [swap_species(block) for block in moving]
     density = jax.ShapeDtypeStruct((planes, cells), F32)
     met, partition = kernel_call(
         middle_kernel,
@@ -664,7 +664,8 @@
         block, after = received(value, distance, after)
         return kernel_call(add_kernel, density, (), (value, block)), after
 
-    *faces, second_state, _ = lax.optimization_barrier((*faces, second_state, met))
+    *faces, second_state, late, _ = lax.optimization_barrier((*faces, second_state, arrived1, met))
+    crossed1 = swap_species(late)
     partner_faces = [swap_species(block) for block in faces]
     third_state = kernel_call(
         third_step_kernel,

time: 43.3 us -> 43.7 us (level)
  waiting for transfers between devices: 9.46 us -> 10.1 us
    ppermute x15, waiting for transfers between devices: 5.57 us -> 6.67 us  [swap_species(): return lax.ppermute(block, 'space', [(i ^ 1, i) for i in range(count)])]
  transfers between devices with their start and end apart: 21 -> 21, of which waited for: 12 -> 12; matrix products, arithmetic and copies ran while one was open for 3% -> 3% of each run, Pallas kernels for 36% -> 35%
where the time goes in v14:
time: 43.7 us; the launch traced here: 43.5 us
  Pallas kernels  16.3 us (37%)
  starting transfers between devices  15.4 us (35%)
  waiting for transfers between devices  10.1 us (23%)
  local copies, waits for them, and re-layouts  1.44 us (3%)
    pallas_call x17, Pallas kernels, kernel_call(): pl.pallas_call(kernel, out_shape=outs, in_specs=[smem if arg.dtype == jnp...  16.3 us
    ppermute x15, starting transfers between devices, swap_species(): return lax.ppermute(block, 'space', [(i ^ 1, i) for i in range(count)])  8.6 us
    ppermute x15, waiting for transfers between devices, swap_species(): return lax.ppermute(block, 'space', [(i ^ 1, i) for i in range(count)])  6.67 us
    ppermute x3, starting transfers between devices, exchange_faces(): return lax.ppermute(block, 'space', route)  5.31 us
    ppermute x3, waiting for transfers between devices, received(): lax.ppermute(value, 'space', [(i, i ^ distance) for i in range(count)])  3.45 us
    ppermute x3, starting transfers between devices, received(): lax.ppermute(value, 'space', [(i, i ^ distance) for i in range(count)])  1.54 us
    unnamed x11, local copies, waits for them, and re-layouts  1.44 us
  transfers between devices with their start and end apart: 21, of which 12 were waited for; matrix products, arithmetic and copies ran while one was open for 3% of the time, Pallas kernels for 35%

profile of v14, /device:TPU:0, one launch (start us, length us, event | category | flops | bytes accessed | tf_op | source)
XLA Modules:
  0.0 43.5 jit_solution(17858793640004400008)
XLA Ops:
  0.0 0.5 %collective-permute-start = (f32[4,512]{1,0:T(4,128)}, f32[4,512]{1,0:T(4,128)S(1)}, u32[]{:S(2)}, u32[]{:S(2)}) collective-permute-start(f32[4,512]{1,0:T(4,128)} %param.6), channel_id=1, source_target_pairs={{1,0},{0,1},{3,2},{2,3},{5,4},{4,5},{7,6},{6,7},{9,8},{8,9},{11,10... | collective-permute-start | bytes 24584 | tf_op jit(solution)/shard_map/ppermute | solution.py:27
  0.6 1.4 %copy.9 = bf16[256,4,512]{2,0,1:T(8,128)(2,1)S(1)} copy(bf16[256,4,512]{2,1,0:T(4,128)(2,1)} %param.7) | data formatting | bytes 2097152 | tf_op args[1]
  2.8 1.1 %collective-permute-done.1.other_ref = bf16[1,256,512]{2,1,0:T(8,128)(2,1)S(1)} collective-permute-done((bf16[1,256,512]{2,1,0:T(8,128)(2,1)S(1)}, bf16[1,256,512]{2,1,0:T(8,128)(2,1)S(1)}, u32[]{:S(2)}, u32[]{:S(2)}) %collective-permute-start.1) | collective-permute-done | bytes 262176 | tf_op jit(solution)/shard_map/ppermute | solution.py:27
  4.2 2.9 %collective-permute-start.6 = (bf16[1,272,512]{2,1,0:T(8,128)(2,1)S(1)}, bf16[1,272,512]{2,1,0:T(8,128)(2,1)S(1)}, u32[]{:S(2)}, u32[]{:S(2)}) collective-permute-start(bf16[1,272,512]{2,1,0:T(8,128)(2,1)S(1)} %shard_map.66), channel_id=1, source_target_pairs={{0,2},{1,15},{2,0},{3,5},{4,6},{5,3},{6,4},{7,9},{8,10},{9,7},{10,... | collective-permute-start | bytes 835592 | tf_op jit(solution)/shard_map/ppermute | solution.py:36
  7.1 2.0 %shard_map.67 = (bf16[4,256,512]{2,1,0:T(8,128)(2,1)S(1)}, bf16[1,256,512]{2,1,0:T(8,128)(2,1)S(1)}, bf16[1,256,512]{2,1,0:T(8,128)(2,1)S(1)}, bf16[1,256,512]{2,1,0:T(8,128)(2,1)S(1)}) custom-call(bf16[4,256,512]{2,1,0:T(8,128)(2,1)S(1)} %bitcast.8, f32[4,512]{1,0:T(4,128)S(1)} %get-tuple-element.114.fields_ref.first_ref.own_ref, ...), custom_call_target="tpu_custom_call" | custom-call | tf_op jit(solution)/shard_map/pallas_call | solution.py:557
  9.0 3.0 %collective-permute-start.4 = (bf16[1,256,512]{2,1,0:T(8,128)(2,1)S(1)}, bf16[1,256,512]{2,1,0:T(8,128)(2,1)S(1)}, u32[]{:S(2)}, u32[]{:S(2)}) collective-permute-start(bf16[1,256,512]{2,1,0:T(8,128)(2,1)S(1)} %get-tuple-element.70), channel_id=1, source_target_pairs={{1,0},{0,1},{3,2},{2,3},{5,4},{4,5},{7,6},{6,7},{9,8},{8,9},{11,10... | collective-permute-start | bytes 786440 | tf_op jit(solution)/shard_map/ppermute | solution.py:27
  12.1 0.4 collective-permute-start.2
  12.5 0.6 %shard_map.68 = (bf16[4,256,512]{2,1,0:T(8,128)(2,1)S(1)}, bf16[2,256,512]{2,1,0:T(8,128)(2,1)S(1)}) custom-call(s32[1]{0:T(128)} %bitcast.core_ref, bf16[4,256,512]{2,1,0:T(8,128)(2,1)S(1)} %collective-permute-done.3.partner_ref, bf16[4,256,512]{2,1,0:T(8,128)(2,1)S(1)} %bitcast.9, bf16[256,256]{1,0:T(8,128)(2,1)S(1)} %get-tuple-element.68.turned_ref), custom_call_target="tpu_custom_call" | custom-call | tf_op jit(solution)/shard_map/pallas_call | solution.py:557
  13.2 0.4 collective-permute-done.5.refs_2_
  13.5 0.4 collective-permute-done.2.other_ref
  14.1 2.8 %shard_map.70 = (bf16[4,256,512]{2,1,0:T(8,128)(2,1)S(1)}, bf16[1,256,512]{2,1,0:T(8,128)(2,1)S(1)}, bf16[1,256,512]{2,1,0:T(8,128)(2,1)S(1)}) custom-call(bf16[4,256,512]{2,1,0:T(8,128)(2,1)S(1)} %get-tuple-element.79.state_ref.alone_ref, f32[4,512]{1,0:T(4,128)S(1)} %get-tuple-element.114.fields_ref.first_ref.own_ref, ...), custom_call_target="tpu_custom_call" | custom-call | tf_op jit(solution)/shard_map/pallas_call | solution.py:557
  16.9 0.9 %collective-permute-start.10 = (bf16[1,272,512]{2,1,0:T(8,128)(2,1)S(1)}, bf16[1,272,512]{2,1,0:T(8,128)(2,1)S(1)}, u32[]{:S(2)}, u32[]{:S(2)}) collective-permute-start(bf16[1,272,512]{2,1,0:T(8,128)(2,1)S(1)} %collective-permute-done.6.mine_ref), channel_id=1, source_target_pairs={{1,0},{0,1},{3,2},{2,3},{5,4},{4,5},{7,6},{6,7},{9,8},{8,9},{11,10... | collective-permute-start | bytes 835592 | tf_op jit(solution)/shard_map/ppermute | solution.py:27
  17.9 0.4 collective-permute-start.8
  18.4 1.0 %collective-permute-done.7.refs_2_ = bf16[1,256,512]{2,1,0:T(8,128)(2,1)S(1)} collective-permute-done((bf16[1,256,512]{2,1,0:T(8,128)(2,1)S(1)}, bf16[1,256,512]{2,1,0:T(8,128)(2,1)S(1)}, u32[]{:S(2)}, u32[]{:S(2)}) %collective-permute-start.7) | collective-permute-done | bytes 262176 | tf_op jit(solution)/shard_map/ppermute | solution.py:27
  19.4 0.4 collective-permute-done.8.refs_3_
  19.9 2.4 %collective-permute-start.9 = (bf16[2,288,512]{2,1,0:T(8,128)(2,1)S(1)}, bf16[2,288,512]{2,1,0:T(8,128)(2,1)S(1)}, u32[]{:S(2)}, u32[]{:S(2)}) collective-permute-start(bf16[2,288,512]{2,1,0:T(8,128)(2,1)S(1)} %shard_map.71), channel_id=1, source_target_pairs={{0,2},{1,15},{2,0},{3,5},{4,6},{5,3},{6,4},{7,9},{8,10},{9,7},{10,... | collective-permute-start | bytes 1769480 | tf_op jit(solution)/shard_map/ppermute | solution.py:36
  22.2 2.7 %shard_map.72 = (bf16[1,256,512]{2,1,0:T(8,128)(2,1)S(1)}, bf16[1,256,512]{2,1,0:T(8,128)(2,1)S(1)}, bf16[8,256,512]{2,1,0:T(8,128)(2,1)S(1)}, bf16[1,256,512]{2...) custom-call(s32[1]{0:T(128)} %bitcast.core_ref, ...), custom_call_target="tpu_custom_call" | custom-call | tf_op jit(solution)/shard_map/pallas_call | solution.py:557
  24.9 1.8 %collective-permute-start.12 = (bf16[1,256,512]{2,1,0:T(8,128)(2,1)S(1)}, bf16[1,256,512]{2,1,0:T(8,128)(2,1)S(1)}, u32[]{:S(2)}, u32[]{:S(2)}) collective-permute-start(bf16[1,256,512]{2,1,0:T(8,128)(2,1)S(1)} %get-tuple-element.87), channel_id=1, source_target_pairs={{1,0},{0,1},{3,2},{2,3},{5,4},{4,5},{7,6},{6,7},{9,8},{8,9},{11,10... | collective-permute-start | bytes 786440 | tf_op jit(solution)/shard_map/ppermute | solution.py:27
  26.8 1.1 %collective-permute-done.12.near_ref = bf16[1,256,512]{2,1,0:T(8,128)(2,1)S(1)} collective-permute-done((bf16[1,256,512]{2,1,0:T(8,128)(2,1)S(1)}, bf16[1,256,512]{2,1,0:T(8,128)(2,1)S(1)}, u32[]{:S(2)}, u32[]{:S(2)}) %collective-permute-start.12) | collective-permute-done | bytes 262176 | tf_op jit(solution)/shard_map/ppermute | solution.py:27
  27.9 0.4 collective-permute-done.13.far_ref
  28.3 0.6 %shard_map.73 = (f32[2,512]{1,0:T(2,128)S(1)}, f32[4,512]{1,0:T(4,128)S(1)}) custom-call(s32[1]{0:T(128)} %bitcast.core_ref, bf16[2,256,512]{2,1,0:T(8,128)(2,1)S(1)} %get-tuple-element.82.own_ref, bf16[1,256,512]{2,1,0:T(8,128)(2,1)S(1)} %collective-permute-done.12.near_ref, bf16[1,256,512]{2,1,0:T(8,128)(2,1)S(1)} %collective-permute-done.13.far_ref, ...), custom_call_target="tpu_custom_call" | custom-call | tf_op jit(solution)/shard_map/pallas_call | solution.py:557
  28.9 0.4 collective-permute-start.15
  29.4 0.4 collective-permute-start.18
  29.8 0.7 %collective-permute-done.15.other_ref = bf16[1,288,512]{2,1,0:T(8,128)(2,1)S(1)} collective-permute-done((bf16[1,288,512]{2,1,0:T(8,128)(2,1)S(1)}, bf16[1,288,512]{2,1,0:T(8,128)(2,1)S(1)}, u32[]{:S(2)}, u32[]{:S(2)}) %collective-permute-start.15) | collective-permute-done | bytes 294944 | tf_op jit(solution)/shard_map/ppermute | solution.py:27
  30.5 3.0 %shard_map.74.held_ref = bf16[6,256,512]{2,1,0:T(8,128)(2,1)S(1)} custom-call(bf16[8,256,512]{2,1,0:T(8,128)(2,1)S(1)} %get-tuple-element.94.held_ref, bf16[1,288,512]{2,1,0:T(8,128)(2,1)S(1)} %collective-permute-done.11.message_ref.mine_ref, bf16[1,288,512]{2,1,0:T(8,128)(2,1)S(1)} %collective-permute-done.15.other_ref, ...), custom_call_target="tpu_custom_call" | custom-call | tf_op jit(solution)/shard_map/pallas_call | solution.py:557
  33.5 1.5 %collective-permute-start.16 = (f32[4,512]{1,0:T(4,128)S(1)}, f32[4,512]{1,0:T(4,128)S(1)}, u32[]{:S(2)}, u32[]{:S(2)}) collective-permute-start(f32[4,512]{1,0:T(4,128)S(1)} %shard_map.75.one_ref), channel_id=1, source_target_pairs={{0,8},{1,9},{2,10},{3,11},{4,12},{5,13},{6,14},{7,15},{8,0},{9,1},... | collective-permute-start | bytes 24584 | tf_op jit(solution)/shard_map/ppermute | solution.py:660
  35.0 1.6 %shard_map.76.shared_ref = f32[4,512]{1,0:T(4,128)S(1)} custom-call(bf16[6,256,512]{2,1,0:T(8,128)(2,1)S(1)} %shard_map.74.held_ref, f32[4,512]{1,0:T(4,128)S(1)} %get-tuple-element.113.partner_ref.second_ref, f32[4,256,128]{2,1,0:T(8,128)S(1)} %get-tuple-element.63.refs_1_.v_ref.refs_2_.refs_4_, bf16[4,256,512]{2,1,0:T(8,128)(2,1)S(1)} %get-tuple-element.73.weight_ref, ...), custom_call_target="tpu_custom_call" | custom-call | tf_op jit(solution)/shard_map/pallas_call | solution.py:557
  36.6 1.5 %collective-permute-done.16.two_ref = f32[4,512]{1,0:T(4,128)S(1)} collective-permute-done((f32[4,512]{1,0:T(4,128)S(1)}, f32[4,512]{1,0:T(4,128)S(1)}, u32[]{:S(2)}, u32[]{:S(2)}) %collective-permute-start.16) | collective-permute-done | bytes 8224 | tf_op jit(solution)/shard_map/ppermute | solution.py:660
  38.1 1.6 %shard_map.78 = (f32[4,512]{1,0:T(4,128)S(1)}, f32[4,512]{1,0:T(4,128)S(1)}) custom-call(s32[1]{0:T(128)} %bitcast.core_ref, bf16[2,288,512]{2,1,0:T(8,128)(2,1)S(1)} %collective-permute-done.9.message_ref, bf16[4,256,512]{2,1,0:T(8,128)(2,1)S(1)} %get-tuple-element.73.weight_ref, bf16[2,256,512]{2,1,0:T(8,128)(2,1)S(1)} %get-tuple-element.107.own_weight_ref, ...), custom_call_target="tpu_custom_call" | custom-call | tf_op jit(solution)/shard_map/pallas_call | solution.py:557
  39.7 2.0 %collective-permute-done.19.two_ref = f32[4,512]{1,0:T(4,128)S(1)} collective-permute-done((f32[4,512]{1,0:T(4,128)S(1)}, f32[4,512]{1,0:T(4,128)S(1)}, u32[]{:S(2)}, u32[]{:S(2)}) %collective-permute-start.19) | collective-permute-done | bytes 8224 | tf_op jit(solution)/shard_map/ppermute | solution.py:660
  41.7 1.2 %collective-permute-done.20.arrived_ref = f32[8,512]{1,0:T(8,128)S(1)} collective-permute-done((f32[8,512]{1,0:T(8,128)S(1)}, f32[8,512]{1,0:T(8,128)S(1)}, u32[]{:S(2)}, u32[]{:S(2)}) %collective-permute-start.20) | collective-permute-done | bytes 16416 | tf_op jit(solution)/shard_map/ppermute | solution.py:27
  42.9 0.6 %shard_map.80 = f32[4,512]{1,0:T(4,128)} custom-call(f32[4,512]{1,0:T(4,128)S(1)} %get-tuple-element.109.kept_ref, f32[8,512]{1,0:T(8,128)S(1)} %shard_map.79.mine_ref, f32[8,512]{1,0:T(8,128)S(1)} %collective-permute-done.20.arrived_ref), custom_call_target="tpu_custom_call" | custom-call | tf_op jit(solution)/shard_map/pallas_call | solution.py:557
  (40 shorter events, 1.8 us)
Async XLA Ops:
  0.0 2.0 %copy-start.4 = (f32[4,512]{1,0:T(4,128)S(1)}, f32[4,512]{1,0:T(4,128)}, u32[]{:S(2)}) copy-start(f32[4,512]{1,0:T(4,128)} %param.6) | copy-start | bytes 24580
  0.0 2.1 %copy-start.2 = (f32[3,256]{1,0:T(4,128)S(1)}, f32[3,256]{1,0:T(4,128)}, u32[]{:S(2)}) copy-start(f32[3,256]{1,0:T(4,128)} %directions_ref.1) | copy-start | bytes 9220
  0.0 2.5 %copy-start.3 = (f32[256]{0:T(256)S(1)}, f32[256]{0:T(256)}, u32[]{:S(2)}) copy-start(f32[256]{0:T(256)} %param.11) | copy-start | bytes 3076
  0.0 2.5 %copy-start = (bf16[256,256]{1,0:T(8,128)(2,1)S(1)}, bf16[256,256]{1,0:T(8,128)(2,1)}, u32[]{:S(2)}) copy-start(bf16[256,256]{1,0:T(8,128)(2,1)} %synthesis_ref.1) | copy-start | bytes 393220
  0.0 2.5 %copy-start.1 = (bf16[256,256]{1,0:T(8,128)(2,1)S(1)}, bf16[256,256]{1,0:T(8,128)(2,1)}, u32[]{:S(2)}) copy-start(bf16[256,256]{1,0:T(8,128)(2,1)} %analysis_ref.1) | copy-start | bytes 393220
  0.0 2.0 %collective-permute-start = (f32[4,512]{1,0:T(4,128)}, f32[4,512]{1,0:T(4,128)S(1)}, u32[]{:S(2)}, u32[]{:S(2)}) collective-permute-start(f32[4,512]{1,0:T(4,128)} %param.6), channel_id=1, source_target_pairs={{1,0},{0,1},{3,2},{2,3},{5,4},{4,5},{7,6},{6,7},{9,8},{8,9},{11,10... | collective-permute-start | bytes 24584 | tf_op jit(solution)/shard_map/ppermute | solution.py:27
  2.3 1.6 %collective-permute-start.1 = (bf16[1,256,512]{2,1,0:T(8,128)(2,1)S(1)}, bf16[1,256,512]{2,1,0:T(8,128)(2,1)S(1)}, u32[]{:S(2)}, u32[]{:S(2)}) collective-permute-start(bf16[1,256,512]{2,1,0:T(8,128)(2,1)S(1)} %get-tuple-element.59.mine_ref.edge_ref), channel_id=1, source_target_pairs={{1,0},{0,1},{3,2},{2,3},{5,4},{4,5},{7,6},{6,7},{9,8},{8,9},{11,10... | collective-permute-start | bytes 786440 | tf_op jit(solution)/shard_map/ppermute | solution.py:27
  4.0 8.5 %collective-permute-start.3 = (bf16[4,256,512]{2,1,0:T(8,128)(2,1)S(1)}, bf16[4,256,512]{2,1,0:T(8,128)(2,1)S(1)}, u32[]{:S(2)}, u32[]{:S(2)}) collective-permute-start(bf16[4,256,512]{2,1,0:T(8,128)(2,1)S(1)} %bitcast.7), channel_id=1, source_target_pairs={{1,0},{0,1},{3,2},{2,3},{5,4},{4,5},{7,6},{6,7},{9,8},{8,9},{11,10... | collective-permute-start | bytes 3145736 | tf_op jit(solution)/shard_map/ppermute | solution.py:27
  4.2 12.7 %collective-permute-start.6 = (bf16[1,272,512]{2,1,0:T(8,128)(2,1)S(1)}, bf16[1,272,512]{2,1,0:T(8,128)(2,1)S(1)}, u32[]{:S(2)}, u32[]{:S(2)}) collective-permute-start(bf16[1,272,512]{2,1,0:T(8,128)(2,1)S(1)} %shard_map.66), channel_id=1, source_target_pairs={{0,2},{1,15},{2,0},{3,5},{4,6},{5,3},{6,4},{7,9},{8,10},{9,7},{10,... | collective-permute-start | bytes 835592 | tf_op jit(solution)/shard_map/ppermute | solution.py:36
  9.0 4.1 %collective-permute-start.4 = (bf16[1,256,512]{2,1,0:T(8,128)(2,1)S(1)}, bf16[1,256,512]{2,1,0:T(8,128)(2,1)S(1)}, u32[]{:S(2)}, u32[]{:S(2)}) collective-permute-start(bf16[1,256,512]{2,1,0:T(8,128)(2,1)S(1)} %get-tuple-element.70), channel_id=1, source_target_pairs={{1,0},{0,1},{3,2},{2,3},{5,4},{4,5},{7,6},{6,7},{9,8},{8,9},{11,10... | collective-permute-start | bytes 786440 | tf_op jit(solution)/shard_map/ppermute | solution.py:27
  12.0 1.5 %collective-permute-start.5 = (bf16[1,256,512]{2,1,0:T(8,128)(2,1)S(1)}, bf16[1,256,512]{2,1,0:T(8,128)(2,1)S(1)}, u32[]{:S(2)}, u32[]{:S(2)}) collective-permute-start(bf16[1,256,512]{2,1,0:T(8,128)(2,1)S(1)} %get-tuple-element.71), channel_id=1, source_target_pairs={{1,0},{0,1},{3,2},{2,3},{5,4},{4,5},{7,6},{6,7},{9,8},{8,9},{11,10... | collective-permute-start | bytes 786440 | tf_op jit(solution)/shard_map/ppermute | solution.py:27
  12.1 1.8 %collective-permute-start.2 = (bf16[1,256,512]{2,1,0:T(8,128)(2,1)S(1)}, bf16[1,256,512]{2,1,0:T(8,128)(2,1)S(1)}, u32[]{:S(2)}, u32[]{:S(2)}) collective-permute-start(bf16[1,256,512]{2,1,0:T(8,128)(2,1)S(1)} %get-tuple-element.67.mine_ref), channel_id=1, source_target_pairs={{1,0},{0,1},{3,2},{2,3},{5,4},{4,5},{7,6},{6,7},{9,8},{8,9},{11,10... | collective-permute-start | bytes 786440 | tf_op jit(solution)/shard_map/ppermute | solution.py:27
  14.0 10.9 %collective-permute-start.11 = (bf16[1,288,512]{2,1,0:T(8,128)(2,1)S(1)}, bf16[1,288,512]{2,1,0:T(8,128)(2,1)S(1)}, u32[]{:S(2)}, u32[]{:S(2)}) collective-permute-start(bf16[1,288,512]{2,1,0:T(8,128)(2,1)S(1)} %shard_map.69), channel_id=1, source_target_pairs={{0,2},{1,15},{2,0},{3,5},{4,6},{5,3},{6,4},{7,9},{8,10},{9,7},{10,... | collective-permute-start | bytes 884744 | tf_op jit(solution)/shard_map/ppermute | solution.py:36
  16.9 5.3 %collective-permute-start.10 = (bf16[1,272,512]{2,1,0:T(8,128)(2,1)S(1)}, bf16[1,272,512]{2,1,0:T(8,128)(2,1)S(1)}, u32[]{:S(2)}, u32[]{:S(2)}) collective-permute-start(bf16[1,272,512]{2,1,0:T(8,128)(2,1)S(1)} %collective-permute-done.6.mine_ref), channel_id=1, source_target_pairs={{1,0},{0,1},{3,2},{2,3},{5,4},{4,5},{7,6},{6,7},{9,8},{8,9},{11,10... | collective-permute-start | bytes 835592 | tf_op jit(solution)/shard_map/ppermute | solution.py:27
  17.8 1.6 %collective-permute-start.7 = (bf16[1,256,512]{2,1,0:T(8,128)(2,1)S(1)}, bf16[1,256,512]{2,1,0:T(8,128)(2,1)S(1)}, u32[]{:S(2)}, u32[]{:S(2)}) collective-permute-start(bf16[1,256,512]{2,1,0:T(8,128)(2,1)S(1)} %get-tuple-element.77.refs_0_), channel_id=1, source_target_pairs={{1,0},{0,1},{3,2},{2,3},{5,4},{4,5},{7,6},{6,7},{9,8},{8,9},{11,10... | collective-permute-start | bytes 786440 | tf_op jit(solution)/shard_map/ppermute | solution.py:27
  17.9 1.9 %collective-permute-start.8 = (bf16[1,256,512]{2,1,0:T(8,128)(2,1)S(1)}, bf16[1,256,512]{2,1,0:T(8,128)(2,1)S(1)}, u32[]{:S(2)}, u32[]{:S(2)}) collective-permute-start(bf16[1,256,512]{2,1,0:T(8,128)(2,1)S(1)} %get-tuple-element.78.refs_1_), channel_id=1, source_target_pairs={{1,0},{0,1},{3,2},{2,3},{5,4},{4,5},{7,6},{6,7},{9,8},{8,9},{11,10... | collective-permute-start | bytes 786440 | tf_op jit(solution)/shard_map/ppermute | solution.py:27
  19.9 18.2 %collective-permute-start.9 = (bf16[2,288,512]{2,1,0:T(8,128)(2,1)S(1)}, bf16[2,288,512]{2,1,0:T(8,128)(2,1)S(1)}, u32[]{:S(2)}, u32[]{:S(2)}) collective-permute-start(bf16[2,288,512]{2,1,0:T(8,128)(2,1)S(1)} %shard_map.71), channel_id=1, source_target_pairs={{0,2},{1,15},{2,0},{3,5},{4,6},{5,3},{6,4},{7,9},{8,10},{9,7},{10,... | collective-permute-start | bytes 1769480 | tf_op jit(solution)/shard_map/ppermute | solution.py:36
  24.9 3.0 %collective-permute-start.12 = (bf16[1,256,512]{2,1,0:T(8,128)(2,1)S(1)}, bf16[1,256,512]{2,1,0:T(8,128)(2,1)S(1)}, u32[]{:S(2)}, u32[]{:S(2)}) collective-permute-start(bf16[1,256,512]{2,1,0:T(8,128)(2,1)S(1)} %get-tuple-element.87), channel_id=1, source_target_pairs={{1,0},{0,1},{3,2},{2,3},{5,4},{4,5},{7,6},{6,7},{9,8},{8,9},{11,10... | collective-permute-start | bytes 786440 | tf_op jit(solution)/shard_map/ppermute | solution.py:27
  26.8 1.5 %collective-permute-start.13 = (bf16[1,256,512]{2,1,0:T(8,128)(2,1)S(1)}, bf16[1,256,512]{2,1,0:T(8,128)(2,1)S(1)}, u32[]{:S(2)}, u32[]{:S(2)}) collective-permute-start(bf16[1,256,512]{2,1,0:T(8,128)(2,1)S(1)} %get-tuple-element.88), channel_id=1, source_target_pairs={{1,0},{0,1},{3,2},{2,3},{5,4},{4,5},{7,6},{6,7},{9,8},{8,9},{11,10... | collective-permute-start | bytes 786440 | tf_op jit(solution)/shard_map/ppermute | solution.py:27
  28.9 1.6 %collective-permute-start.15 = (bf16[1,288,512]{2,1,0:T(8,128)(2,1)S(1)}, bf16[1,288,512]{2,1,0:T(8,128)(2,1)S(1)}, u32[]{:S(2)}, u32[]{:S(2)}) collective-permute-start(bf16[1,288,512]{2,1,0:T(8,128)(2,1)S(1)} %collective-permute-done.11.message_ref.mine_ref), channel_id=1, source_target_pairs={{1,0},{0,1},{3,2},{2,3},{5,4},{4,5},{7,6},{6,7},{9,8},{8,9},{11,10... | collective-permute-start | bytes 884744 | tf_op jit(solution)/shard_map/ppermute | solution.py:27
  29.3 5.7 %collective-permute-start.17 = (bf16[1,256,512]{2,1,0:T(8,128)(2,1)S(1)}, bf16[1,256,512]{2,1,0:T(8,128)(2,1)S(1)}, u32[]{:S(2)}, u32[]{:S(2)}) collective-permute-start(bf16[1,256,512]{2,1,0:T(8,128)(2,1)S(1)} %get-tuple-element.100.own_low_ref), channel_id=1, source_target_pairs={{1,0},{0,1},{3,2},{2,3},{5,4},{4,5},{7,6},{6,7},{9,8},{8,9},{11,10... | collective-permute-start | bytes 786440 | tf_op jit(solution)/shard_map/ppermute | solution.py:27
  29.4 5.6 %collective-permute-start.18 = (bf16[1,256,512]{2,1,0:T(8,128)(2,1)S(1)}, bf16[1,256,512]{2,1,0:T(8,128)(2,1)S(1)}, u32[]{:S(2)}, u32[]{:S(2)}) collective-permute-start(bf16[1,256,512]{2,1,0:T(8,128)(2,1)S(1)} %get-tuple-element.103.own_high_ref), channel_id=1, source_target_pairs={{1,0},{0,1},{3,2},{2,3},{5,4},{4,5},{7,6},{6,7},{9,8},{8,9},{11,10... | collective-permute-start | bytes 786440 | tf_op jit(solution)/shard_map/ppermute | solution.py:27
  29.8 3.7 %collective-permute-start.14 = (f32[4,512]{1,0:T(4,128)S(1)}, f32[4,512]{1,0:T(4,128)S(1)}, u32[]{:S(2)}, u32[]{:S(2)}) collective-permute-start(f32[4,512]{1,0:T(4,128)S(1)} %get-tuple-element.89.one_ref), channel_id=1, source_target_pairs={{0,4},{1,5},{2,6},{3,7},{4,0},{5,1},{6,2},{7,3},{8,12},{9,13},{10,... | collective-permute-start | bytes 24584 | tf_op jit(solution)/shard_map/ppermute | solution.py:660
  33.5 4.6 %collective-permute-start.16 = (f32[4,512]{1,0:T(4,128)S(1)}, f32[4,512]{1,0:T(4,128)S(1)}, u32[]{:S(2)}, u32[]{:S(2)}) collective-permute-start(f32[4,512]{1,0:T(4,128)S(1)} %shard_map.75.one_ref), channel_id=1, source_target_pairs={{0,8},{1,9},{2,10},{3,11},{4,12},{5,13},{6,14},{7,15},{8,0},{9,1},... | collective-permute-start | bytes 24584 | tf_op jit(solution)/shard_map/ppermute | solution.py:660
  38.1 3.7 %collective-permute-start.19 = (f32[4,512]{1,0:T(4,128)S(1)}, f32[4,512]{1,0:T(4,128)S(1)}, u32[]{:S(2)}, u32[]{:S(2)}) collective-permute-start(f32[4,512]{1,0:T(4,128)S(1)} %shard_map.77.one_ref), channel_id=1, source_target_pairs={{0,2},{1,3},{2,0},{3,1},{4,6},{5,7},{6,4},{7,5},{8,10},{9,11},{10,... | collective-permute-start | bytes 24584 | tf_op jit(solution)/shard_map/ppermute | solution.py:660
  41.7 1.2 %collective-permute-start.20 = (f32[8,512]{1,0:T(8,128)S(1)}, f32[8,512]{1,0:T(8,128)S(1)}, u32[]{:S(2)}, u32[]{:S(2)}) collective-permute-start(f32[8,512]{1,0:T(8,128)S(1)} %shard_map.79.mine_ref), channel_id=1, source_target_pairs={{1,0},{0,1},{3,2},{2,3},{5,4},{4,5},{7,6},{6,7},{9,8},{8,9},{11,10... | collective-permute-start | bytes 49160 | tf_op jit(solution)/shard_map/ppermute | solution.py:27

commit v15 on v10

--- a/solution.py
+++ b/solution.py
@@ -616,9 +616,8 @@
     weights, own_weights = kernel_call(
         weight_kernel, (slab, wide(2 - planes)), (), (core_word, swap_species(start), start, turned)
     )
-    others1, weights, *partner_inner = lax.optimization_barrier(
-        (swap_species(edges1), weights, *map(swap_species, inner))
-    )
+    others1, weights = lax.optimization_barrier((swap_species(edges1), weights))
+    partner_inner = [swap_species(block) for block in inner]
     message1 = kernel_call(
         first_message_kernel,
         jax.ShapeDtypeStruct((1, orient + 16 * PAD, cells), BF16),
@@ -629,7 +628,7 @@
     later, edges2, edges3 = kernel_call(
         next_alone_kernel, (slab, plane, plane), (slab.shape, slab.shape), (state, own, partner, spread, matrix)
     )
-    edges2, edges3, arrived0 = lax.optimization_barrier((edges2, edges3, arrived0))
+    edges2, edges3, arrived0, *partner_inner = lax.optimization_barrier((edges2, edges3, arrived0, *partner_inner))
     message2 = message([edges2, edges3], [swap_species(edges2), swap_species(edges3)])
     arrived = [exchange_faces(message1), exchange_faces(message2)]
     crossed0 = swap_species(arrived0)

time: 43.3 us -> 42.8 us (0.988)
  waiting for transfers between devices: 9.46 us -> 8.23 us
  starting transfers between devices: 15.7 us -> 16.5 us
    ppermute x3, starting transfers between devices: 1.77 us -> 3.99 us  [received(): lax.ppermute(value, 'space', [(i, i ^ distance) for i in range(count)])]
    ppermute x3, waiting for transfers between devices: 3.88 us -> 1.93 us  [received(): lax.ppermute(value, 'space', [(i, i ^ distance) for i in range(count)])]
    ppermute x15, starting transfers between devices: 8.65 us -> 7 us  [swap_species(): return lax.ppermute(block, 'space', [(i ^ 1, i) for i in range(count)])]
    ppermute x3, waiting for transfers between devices: 0.01 us -> 1.1 us  [exchange_faces(): return lax.ppermute(block, 'space', route)]
  transfers between devices with their start and end apart: 21 -> 21, of which waited for: 12 -> 10; matrix products, arithmetic and copies ran while one was open for 3% -> 3% of each run, Pallas kernels for 36% -> 36%
where the time goes in v15:
time: 42.8 us; the launch traced here: 42.7 us
  starting transfers between devices  16.5 us (39%)
  Pallas kernels  16.3 us (38%)
  waiting for transfers between devices  8.23 us (19%)
  local copies, waits for them, and re-layouts  1.44 us (3%)
    pallas_call x17, Pallas kernels, kernel_call(): pl.pallas_call(kernel, out_shape=outs, in_specs=[smem if arg.dtype == jnp...  16.3 us
    ppermute x15, starting transfers between devices, swap_species(): return lax.ppermute(block, 'space', [(i ^ 1, i) for i in range(count)])  7 us
    ppermute x3, starting transfers between devices, exchange_faces(): return lax.ppermute(block, 'space', route)  5.51 us
    ppermute x15, waiting for transfers between devices, swap_species(): return lax.ppermute(block, 'space', [(i ^ 1, i) for i in range(count)])  5.2 us
    ppermute x3, starting transfers between devices, received(): lax.ppermute(value, 'space', [(i, i ^ distance) for i in range(count)])  3.99 us
    ppermute x3, waiting for transfers between devices, received(): lax.ppermute(value, 'space', [(i, i ^ distance) for i in range(count)])  1.93 us
    unnamed x11, local copies, waits for them, and re-layouts  1.44 us
    ppermute x3, waiting for transfers between devices, exchange_faces(): return lax.ppermute(block, 'space', route)  1.1 us
  transfers between devices with their start and end apart: 21, of which 10 were waited for; matrix products, arithmetic and copies ran while one was open for 3% of the time, Pallas kernels for 36%

profile of v15, /device:TPU:0, one launch (start us, length us, event | category | flops | bytes accessed | tf_op | source)
XLA Modules:
  0.0 42.7 jit_solution(1842408880429727576)
XLA Ops:
  0.0 0.5 %collective-permute-start = (f32[4,512]{1,0:T(4,128)}, f32[4,512]{1,0:T(4,128)S(1)}, u32[]{:S(2)}, u32[]{:S(2)}) collective-permute-start(f32[4,512]{1,0:T(4,128)} %param.6), channel_id=1, source_target_pairs={{1,0},{0,1},{3,2},{2,3},{5,4},{4,5},{7,6},{6,7},{9,8},{8,9},{11,10... | collective-permute-start | bytes 24584 | tf_op jit(solution)/shard_map/ppermute | solution.py:27
  0.6 1.4 %copy.9 = bf16[256,4,512]{2,0,1:T(8,128)(2,1)S(1)} copy(bf16[256,4,512]{2,1,0:T(4,128)(2,1)} %param.7) | data formatting | bytes 2097152 | tf_op args[1]
  2.5 0.3 shard_map.65
  2.8 1.1 %collective-permute-done.1.other_ref = bf16[1,256,512]{2,1,0:T(8,128)(2,1)S(1)} collective-permute-done((bf16[1,256,512]{2,1,0:T(8,128)(2,1)S(1)}, bf16[1,256,512]{2,1,0:T(8,128)(2,1)S(1)}, u32[]{:S(2)}, u32[]{:S(2)}) %collective-permute-start.1) | collective-permute-done | bytes 262176 | tf_op jit(solution)/shard_map/ppermute | solution.py:27
  4.2 2.9 %collective-permute-start.4 = (bf16[1,272,512]{2,1,0:T(8,128)(2,1)S(1)}, bf16[1,272,512]{2,1,0:T(8,128)(2,1)S(1)}, u32[]{:S(2)}, u32[]{:S(2)}) collective-permute-start(bf16[1,272,512]{2,1,0:T(8,128)(2,1)S(1)} %shard_map.66), channel_id=1, source_target_pairs={{0,2},{1,15},{2,0},{3,5},{4,6},{5,3},{6,4},{7,9},{8,10},{9,7},{10,... | collective-permute-start | bytes 835592 | tf_op jit(solution)/shard_map/ppermute | solution.py:36
  7.1 2.0 %shard_map.67 = (bf16[4,256,512]{2,1,0:T(8,128)(2,1)S(1)}, bf16[1,256,512]{2,1,0:T(8,128)(2,1)S(1)}, bf16[1,256,512]{2,1,0:T(8,128)(2,1)S(1)}, bf16[1,256,512]{2,1,0:T(8,128)(2,1)S(1)}) custom-call(bf16[4,256,512]{2,1,0:T(8,128)(2,1)S(1)} %bitcast.8, f32[4,512]{1,0:T(4,128)S(1)} %get-tuple-element.118.fields_ref.first_ref.own_ref, ...), custom_call_target="tpu_custom_call" | custom-call | tf_op jit(solution)/shard_map/pallas_call | solution.py:557
  9.0 3.0 %collective-permute-start.2 = (bf16[1,256,512]{2,1,0:T(8,128)(2,1)S(1)}, bf16[1,256,512]{2,1,0:T(8,128)(2,1)S(1)}, u32[]{:S(2)}, u32[]{:S(2)}) collective-permute-start(bf16[1,256,512]{2,1,0:T(8,128)(2,1)S(1)} %get-tuple-element.69.mine_ref), channel_id=1, source_target_pairs={{1,0},{0,1},{3,2},{2,3},{5,4},{4,5},{7,6},{6,7},{9,8},{8,9},{11,10... | collective-permute-start | bytes 786440 | tf_op jit(solution)/shard_map/ppermute | solution.py:27
  12.1 0.4 %collective-permute-start.6 = (bf16[1,256,512]{2,1,0:T(8,128)(2,1)S(1)}, bf16[1,256,512]{2,1,0:T(8,128)(2,1)S(1)}, u32[]{:S(2)}, u32[]{:S(2)}) collective-permute-start(bf16[1,256,512]{2,1,0:T(8,128)(2,1)S(1)} %get-tuple-element.78), channel_id=1, source_target_pairs={{1,0},{0,1},{3,2},{2,3},{5,4},{4,5},{7,6},{6,7},{9,8},{8,9},{11,10... | collective-permute-start | bytes 786440 | tf_op jit(solution)/shard_map/ppermute | solution.py:27
  12.5 0.6 %shard_map.68 = (bf16[4,256,512]{2,1,0:T(8,128)(2,1)S(1)}, bf16[2,256,512]{2,1,0:T(8,128)(2,1)S(1)}) custom-call(s32[1]{0:T(128)} %bitcast.core_ref, bf16[4,256,512]{2,1,0:T(8,128)(2,1)S(1)} %collective-permute-done.3.partner_ref, bf16[4,256,512]{2,1,0:T(8,128)(2,1)S(1)} %bitcast.9, bf16[256,256]{1,0:T(8,128)(2,1)S(1)} %get-tuple-element.70.turned_ref), custom_call_target="tpu_custom_call" | custom-call | tf_op jit(solution)/shard_map/pallas_call | solution.py:557
  13.3 2.8 %shard_map.70 = (bf16[4,256,512]{2,1,0:T(8,128)(2,1)S(1)}, bf16[1,256,512]{2,1,0:T(8,128)(2,1)S(1)}, bf16[1,256,512]{2,1,0:T(8,128)(2,1)S(1)}) custom-call(bf16[4,256,512]{2,1,0:T(8,128)(2,1)S(1)} %get-tuple-element.81.state_ref.alone_ref, f32[4,512]{1,0:T(4,128)S(1)} %get-tuple-element.118.fields_ref.first_ref.own_ref, ...), custom_call_target="tpu_custom_call" | custom-call | tf_op jit(solution)/shard_map/pallas_call | solution.py:557
  16.2 1.1 %collective-permute-done.4.mine_ref = bf16[1,272,512]{2,1,0:T(8,128)(2,1)S(1)} collective-permute-done((bf16[1,272,512]{2,1,0:T(8,128)(2,1)S(1)}, bf16[1,272,512]{2,1,0:T(8,128)(2,1)S(1)}, u32[]{:S(2)}, u32[]{:S(2)}) %collective-permute-start.4) | collective-permute-done | bytes 278560 | tf_op jit(solution)/shard_map/ppermute | solution.py:36
  17.3 0.5 %collective-permute-start.8 = (bf16[1,256,512]{2,1,0:T(8,128)(2,1)S(1)}, bf16[1,256,512]{2,1,0:T(8,128)(2,1)S(1)}, u32[]{:S(2)}, u32[]{:S(2)}) collective-permute-start(bf16[1,256,512]{2,1,0:T(8,128)(2,1)S(1)} %get-tuple-element.80.refs_1_), channel_id=1, source_target_pairs={{1,0},{0,1},{3,2},{2,3},{5,4},{4,5},{7,6},{6,7},{9,8},{8,9},{11,10... | collective-permute-start | bytes 786440 | tf_op jit(solution)/shard_map/ppermute | solution.py:27
  17.8 1.0 %collective-permute-done.7.refs_2_ = bf16[1,256,512]{2,1,0:T(8,128)(2,1)S(1)} collective-permute-done((bf16[1,256,512]{2,1,0:T(8,128)(2,1)S(1)}, bf16[1,256,512]{2,1,0:T(8,128)(2,1)S(1)}, u32[]{:S(2)}, u32[]{:S(2)}) %collective-permute-start.7) | collective-permute-done | bytes 262176 | tf_op jit(solution)/shard_map/ppermute | solution.py:27
  18.8 0.4 collective-permute-done.8.refs_3_
  19.3 2.5 %collective-permute-start.9 = (bf16[2,288,512]{2,1,0:T(8,128)(2,1)S(1)}, bf16[2,288,512]{2,1,0:T(8,128)(2,1)S(1)}, u32[]{:S(2)}, u32[]{:S(2)}) collective-permute-start(bf16[2,288,512]{2,1,0:T(8,128)(2,1)S(1)} %shard_map.71), channel_id=1, source_target_pairs={{0,2},{1,15},{2,0},{3,5},{4,6},{5,3},{6,4},{7,9},{8,10},{9,7},{10,... | collective-permute-start | bytes 1769480 | tf_op jit(solution)/shard_map/ppermute | solution.py:36
  21.8 2.7 %shard_map.72 = (bf16[1,256,512]{2,1,0:T(8,128)(2,1)S(1)}, bf16[1,256,512]{2,1,0:T(8,128)(2,1)S(1)}, bf16[8,256,512]{2,1,0:T(8,128)(2,1)S(1)}, bf16[1,256,512]{2...) custom-call(s32[1]{0:T(128)} %bitcast.core_ref, ...), custom_call_target="tpu_custom_call" | custom-call | tf_op jit(solution)/shard_map/pallas_call | solution.py:557
  24.5 1.1 %collective-permute-start.14 = (bf16[1,288,512]{2,1,0:T(8,128)(2,1)S(1)}, bf16[1,288,512]{2,1,0:T(8,128)(2,1)S(1)}, u32[]{:S(2)}, u32[]{:S(2)}) collective-permute-start(bf16[1,288,512]{2,1,0:T(8,128)(2,1)S(1)} %collective-permute-done.11.message_ref.mine_ref), channel_id=1, source_target_pairs={{1,0},{0,1},{3,2},{2,3},{5,4},{4,5},{7,6},{6,7},{9,8},{8,9},{11,10... | collective-permute-start | bytes 884744 | tf_op jit(solution)/shard_map/ppermute | solution.py:27
  25.7 0.4 %collective-permute-start.13 = (bf16[1,256,512]{2,1,0:T(8,128)(2,1)S(1)}, bf16[1,256,512]{2,1,0:T(8,128)(2,1)S(1)}, u32[]{:S(2)}, u32[]{:S(2)}) collective-permute-start(bf16[1,256,512]{2,1,0:T(8,128)(2,1)S(1)} %get-tuple-element.90), channel_id=1, source_target_pairs={{1,0},{0,1},{3,2},{2,3},{5,4},{4,5},{7,6},{6,7},{9,8},{8,9},{11,10... | collective-permute-start | bytes 786440 | tf_op jit(solution)/shard_map/ppermute | solution.py:27
  26.1 1.1 %collective-permute-done.12.near_ref = bf16[1,256,512]{2,1,0:T(8,128)(2,1)S(1)} collective-permute-done((bf16[1,256,512]{2,1,0:T(8,128)(2,1)S(1)}, bf16[1,256,512]{2,1,0:T(8,128)(2,1)S(1)}, u32[]{:S(2)}, u32[]{:S(2)}) %collective-permute-start.12) | collective-permute-done | bytes 262176 | tf_op jit(solution)/shard_map/ppermute | solution.py:27
  27.2 0.4 collective-permute-done.13.far_ref
  27.6 0.6 %shard_map.73 = (f32[2,512]{1,0:T(2,128)S(1)}, f32[4,512]{1,0:T(4,128)S(1)}) custom-call(s32[1]{0:T(128)} %bitcast.core_ref, bf16[2,256,512]{2,1,0:T(8,128)(2,1)S(1)} %get-tuple-element.84.own_ref, bf16[1,256,512]{2,1,0:T(8,128)(2,1)S(1)} %collective-permute-done.12.near_ref, bf16[1,256,512]{2,1,0:T(8,128)(2,1)S(1)} %collective-permute-done.13.far_ref, ...), custom_call_target="tpu_custom_call" | custom-call | tf_op jit(solution)/shard_map/pallas_call | solution.py:557
  28.2 0.4 collective-permute-start.17
  28.7 0.9 %collective-permute-start.15 = (f32[4,512]{1,0:T(4,128)S(1)}, f32[4,512]{1,0:T(4,128)S(1)}, u32[]{:S(2)}, u32[]{:S(2)}) collective-permute-start(f32[4,512]{1,0:T(4,128)S(1)} %get-tuple-element.93.one_ref), channel_id=1, source_target_pairs={{0,4},{1,5},{2,6},{3,7},{4,0},{5,1},{6,2},{7,3},{8,12},{9,13},{10,... | collective-permute-start | bytes 24584 | tf_op jit(solution)/shard_map/ppermute | solution.py:659
  29.6 3.0 %shard_map.74.held_ref = bf16[6,256,512]{2,1,0:T(8,128)(2,1)S(1)} custom-call(bf16[8,256,512]{2,1,0:T(8,128)(2,1)S(1)} %get-tuple-element.98.held_ref, bf16[1,288,512]{2,1,0:T(8,128)(2,1)S(1)} %collective-permute-done.11.message_ref.mine_ref, bf16[1,288,512]{2,1,0:T(8,128)(2,1)S(1)} %collective-permute-done.14.other_ref, ...), custom_call_target="tpu_custom_call" | custom-call | tf_op jit(solution)/shard_map/pallas_call | solution.py:557
  32.6 2.0 %collective-permute-start.16 = (f32[4,512]{1,0:T(4,128)S(1)}, f32[4,512]{1,0:T(4,128)S(1)}, u32[]{:S(2)}, u32[]{:S(2)}) collective-permute-start(f32[4,512]{1,0:T(4,128)S(1)} %shard_map.75.one_ref), channel_id=1, source_target_pairs={{0,8},{1,9},{2,10},{3,11},{4,12},{5,13},{6,14},{7,15},{8,0},{9,1},... | collective-permute-start | bytes 24584 | tf_op jit(solution)/shard_map/ppermute | solution.py:659
  34.6 1.6 %shard_map.76.shared_ref = f32[4,512]{1,0:T(4,128)S(1)} custom-call(bf16[6,256,512]{2,1,0:T(8,128)(2,1)S(1)} %shard_map.74.held_ref, f32[4,512]{1,0:T(4,128)S(1)} %get-tuple-element.117.partner_ref.second_ref, f32[4,256,128]{2,1,0:T(8,128)S(1)} %get-tuple-element.65.refs_1_.v_ref.refs_2_.refs_4_, bf16[4,256,512]{2,1,0:T(8,128)(2,1)S(1)} %get-tuple-element.73.weight_ref, ...), custom_call_target="tpu_custom_call" | custom-call | tf_op jit(solution)/shard_map/pallas_call | solution.py:557
  36.3 0.9 %collective-permute-done.16.two_ref = f32[4,512]{1,0:T(4,128)S(1)} collective-permute-done((f32[4,512]{1,0:T(4,128)S(1)}, f32[4,512]{1,0:T(4,128)S(1)}, u32[]{:S(2)}, u32[]{:S(2)}) %collective-permute-start.16) | collective-permute-done | bytes 8224 | tf_op jit(solution)/shard_map/ppermute | solution.py:659
  37.2 1.0 %collective-permute-start.19 = (f32[4,512]{1,0:T(4,128)S(1)}, f32[4,512]{1,0:T(4,128)S(1)}, u32[]{:S(2)}, u32[]{:S(2)}) collective-permute-start(f32[4,512]{1,0:T(4,128)S(1)} %shard_map.77.one_ref), channel_id=1, source_target_pairs={{0,2},{1,3},{2,0},{3,1},{4,6},{5,7},{6,4},{7,5},{8,10},{9,11},{10,... | collective-permute-start | bytes 24584 | tf_op jit(solution)/shard_map/ppermute | solution.py:659
  38.3 1.6 %shard_map.78 = (f32[4,512]{1,0:T(4,128)S(1)}, f32[4,512]{1,0:T(4,128)S(1)}) custom-call(s32[1]{0:T(128)} %bitcast.core_ref, bf16[2,288,512]{2,1,0:T(8,128)(2,1)S(1)} %collective-permute-done.9.message_ref, bf16[4,256,512]{2,1,0:T(8,128)(2,1)S(1)} %get-tuple-element.73.weight_ref, bf16[2,256,512]{2,1,0:T(8,128)(2,1)S(1)} %get-tuple-element.111.own_weight_ref, ...), custom_call_target="tpu_custom_call" | custom-call | tf_op jit(solution)/shard_map/pallas_call | solution.py:557
  39.9 1.0 %collective-permute-done.19.two_ref = f32[4,512]{1,0:T(4,128)S(1)} collective-permute-done((f32[4,512]{1,0:T(4,128)S(1)}, f32[4,512]{1,0:T(4,128)S(1)}, u32[]{:S(2)}, u32[]{:S(2)}) %collective-permute-start.19) | collective-permute-done | bytes 8224 | tf_op jit(solution)/shard_map/ppermute | solution.py:659
  40.9 1.2 %collective-permute-done.20.arrived_ref = f32[8,512]{1,0:T(8,128)S(1)} collective-permute-done((f32[8,512]{1,0:T(8,128)S(1)}, f32[8,512]{1,0:T(8,128)S(1)}, u32[]{:S(2)}, u32[]{:S(2)}) %collective-permute-start.20) | collective-permute-done | bytes 16416 | tf_op jit(solution)/shard_map/ppermute | solution.py:27
  42.1 0.6 %shard_map.80 = f32[4,512]{1,0:T(4,128)} custom-call(f32[4,512]{1,0:T(4,128)S(1)} %get-tuple-element.113.kept_ref, f32[8,512]{1,0:T(8,128)S(1)} %shard_map.79.mine_ref, f32[8,512]{1,0:T(8,128)S(1)} %collective-permute-done.20.arrived_ref), custom_call_target="tpu_custom_call" | custom-call | tf_op jit(solution)/shard_map/pallas_call | solution.py:557
  (40 shorter events, 1.4 us)
Async XLA Ops:
  0.0 2.0 %copy-start.4 = (f32[4,512]{1,0:T(4,128)S(1)}, f32[4,512]{1,0:T(4,128)}, u32[]{:S(2)}) copy-start(f32[4,512]{1,0:T(4,128)} %param.6) | copy-start | bytes 24580
  0.0 2.1 %copy-start.2 = (f32[3,256]{1,0:T(4,128)S(1)}, f32[3,256]{1,0:T(4,128)}, u32[]{:S(2)}) copy-start(f32[3,256]{1,0:T(4,128)} %directions_ref.1) | copy-start | bytes 9220
  0.0 2.5 %copy-start.3 = (f32[256]{0:T(256)S(1)}, f32[256]{0:T(256)}, u32[]{:S(2)}) copy-start(f32[256]{0:T(256)} %param.11) | copy-start | bytes 3076
  0.0 2.5 %copy-start = (bf16[256,256]{1,0:T(8,128)(2,1)S(1)}, bf16[256,256]{1,0:T(8,128)(2,1)}, u32[]{:S(2)}) copy-start(bf16[256,256]{1,0:T(8,128)(2,1)} %synthesis_ref.1) | copy-start | bytes 393220
  0.0 2.5 %copy-start.1 = (bf16[256,256]{1,0:T(8,128)(2,1)S(1)}, bf16[256,256]{1,0:T(8,128)(2,1)}, u32[]{:S(2)}) copy-start(bf16[256,256]{1,0:T(8,128)(2,1)} %analysis_ref.1) | copy-start | bytes 393220
  0.0 2.0 %collective-permute-start = (f32[4,512]{1,0:T(4,128)}, f32[4,512]{1,0:T(4,128)S(1)}, u32[]{:S(2)}, u32[]{:S(2)}) collective-permute-start(f32[4,512]{1,0:T(4,128)} %param.6), channel_id=1, source_target_pairs={{1,0},{0,1},{3,2},{2,3},{5,4},{4,5},{7,6},{6,7},{9,8},{8,9},{11,10... | collective-permute-start | bytes 24584 | tf_op jit(solution)/shard_map/ppermute | solution.py:27
  2.3 1.6 %collective-permute-start.1 = (bf16[1,256,512]{2,1,0:T(8,128)(2,1)S(1)}, bf16[1,256,512]{2,1,0:T(8,128)(2,1)S(1)}, u32[]{:S(2)}, u32[]{:S(2)}) collective-permute-start(bf16[1,256,512]{2,1,0:T(8,128)(2,1)S(1)} %get-tuple-element.61.mine_ref.edge_ref), channel_id=1, source_target_pairs={{1,0},{0,1},{3,2},{2,3},{5,4},{4,5},{7,6},{6,7},{9,8},{8,9},{11,10... | collective-permute-start | bytes 786440 | tf_op jit(solution)/shard_map/ppermute | solution.py:27
  4.0 8.5 %collective-permute-start.3 = (bf16[4,256,512]{2,1,0:T(8,128)(2,1)S(1)}, bf16[4,256,512]{2,1,0:T(8,128)(2,1)S(1)}, u32[]{:S(2)}, u32[]{:S(2)}) collective-permute-start(bf16[4,256,512]{2,1,0:T(8,128)(2,1)S(1)} %bitcast.7), channel_id=1, source_target_pairs={{1,0},{0,1},{3,2},{2,3},{5,4},{4,5},{7,6},{6,7},{9,8},{8,9},{11,10... | collective-permute-start | bytes 3145736 | tf_op jit(solution)/shard_map/ppermute | solution.py:27
  4.2 13.1 %collective-permute-start.4 = (bf16[1,272,512]{2,1,0:T(8,128)(2,1)S(1)}, bf16[1,272,512]{2,1,0:T(8,128)(2,1)S(1)}, u32[]{:S(2)}, u32[]{:S(2)}) collective-permute-start(bf16[1,272,512]{2,1,0:T(8,128)(2,1)S(1)} %shard_map.66), channel_id=1, source_target_pairs={{0,2},{1,15},{2,0},{3,5},{4,6},{5,3},{6,4},{7,9},{8,10},{9,7},{10,... | collective-permute-start | bytes 835592 | tf_op jit(solution)/shard_map/ppermute | solution.py:36
  9.0 4.1 %collective-permute-start.2 = (bf16[1,256,512]{2,1,0:T(8,128)(2,1)S(1)}, bf16[1,256,512]{2,1,0:T(8,128)(2,1)S(1)}, u32[]{:S(2)}, u32[]{:S(2)}) collective-permute-start(bf16[1,256,512]{2,1,0:T(8,128)(2,1)S(1)} %get-tuple-element.69.mine_ref), channel_id=1, source_target_pairs={{1,0},{0,1},{3,2},{2,3},{5,4},{4,5},{7,6},{6,7},{9,8},{8,9},{11,10... | collective-permute-start | bytes 786440 | tf_op jit(solution)/shard_map/ppermute | solution.py:27
  12.0 4.2 %collective-permute-start.5 = (bf16[1,256,512]{2,1,0:T(8,128)(2,1)S(1)}, bf16[1,256,512]{2,1,0:T(8,128)(2,1)S(1)}, u32[]{:S(2)}, u32[]{:S(2)}) collective-permute-start(bf16[1,256,512]{2,1,0:T(8,128)(2,1)S(1)} %get-tuple-element.77), channel_id=1, source_target_pairs={{1,0},{0,1},{3,2},{2,3},{5,4},{4,5},{7,6},{6,7},{9,8},{8,9},{11,10... | collective-permute-start | bytes 786440 | tf_op jit(solution)/shard_map/ppermute | solution.py:27
  12.1 4.1 %collective-permute-start.6 = (bf16[1,256,512]{2,1,0:T(8,128)(2,1)S(1)}, bf16[1,256,512]{2,1,0:T(8,128)(2,1)S(1)}, u32[]{:S(2)}, u32[]{:S(2)}) collective-permute-start(bf16[1,256,512]{2,1,0:T(8,128)(2,1)S(1)} %get-tuple-element.78), channel_id=1, source_target_pairs={{1,0},{0,1},{3,2},{2,3},{5,4},{4,5},{7,6},{6,7},{9,8},{8,9},{11,10... | collective-permute-start | bytes 786440 | tf_op jit(solution)/shard_map/ppermute | solution.py:27
  13.2 11.3 %collective-permute-start.11 = (bf16[1,288,512]{2,1,0:T(8,128)(2,1)S(1)}, bf16[1,288,512]{2,1,0:T(8,128)(2,1)S(1)}, u32[]{:S(2)}, u32[]{:S(2)}) collective-permute-start(bf16[1,288,512]{2,1,0:T(8,128)(2,1)S(1)} %shard_map.69), channel_id=1, source_target_pairs={{0,2},{1,15},{2,0},{3,5},{4,6},{5,3},{6,4},{7,9},{8,10},{9,7},{10,... | collective-permute-start | bytes 884744 | tf_op jit(solution)/shard_map/ppermute | solution.py:36
  17.3 1.5 %collective-permute-start.7 = (bf16[1,256,512]{2,1,0:T(8,128)(2,1)S(1)}, bf16[1,256,512]{2,1,0:T(8,128)(2,1)S(1)}, u32[]{:S(2)}, u32[]{:S(2)}) collective-permute-start(bf16[1,256,512]{2,1,0:T(8,128)(2,1)S(1)} %get-tuple-element.79.refs_0_), channel_id=1, source_target_pairs={{1,0},{0,1},{3,2},{2,3},{5,4},{4,5},{7,6},{6,7},{9,8},{8,9},{11,10... | collective-permute-start | bytes 786440 | tf_op jit(solution)/shard_map/ppermute | solution.py:27
  17.3 1.9 %collective-permute-start.8 = (bf16[1,256,512]{2,1,0:T(8,128)(2,1)S(1)}, bf16[1,256,512]{2,1,0:T(8,128)(2,1)S(1)}, u32[]{:S(2)}, u32[]{:S(2)}) collective-permute-start(bf16[1,256,512]{2,1,0:T(8,128)(2,1)S(1)} %get-tuple-element.80.refs_1_), channel_id=1, source_target_pairs={{1,0},{0,1},{3,2},{2,3},{5,4},{4,5},{7,6},{6,7},{9,8},{8,9},{11,10... | collective-permute-start | bytes 786440 | tf_op jit(solution)/shard_map/ppermute | solution.py:27
  17.8 4.1 %collective-permute-start.10 = (bf16[1,272,512]{2,1,0:T(8,128)(2,1)S(1)}, bf16[1,272,512]{2,1,0:T(8,128)(2,1)S(1)}, u32[]{:S(2)}, u32[]{:S(2)}) collective-permute-start(bf16[1,272,512]{2,1,0:T(8,128)(2,1)S(1)} %collective-permute-done.4.mine_ref), channel_id=1, source_target_pairs={{1,0},{0,1},{3,2},{2,3},{5,4},{4,5},{7,6},{6,7},{9,8},{8,9},{11,10... | collective-permute-start | bytes 835592 | tf_op jit(solution)/shard_map/ppermute | solution.py:27
  19.3 19.0 %collective-permute-start.9 = (bf16[2,288,512]{2,1,0:T(8,128)(2,1)S(1)}, bf16[2,288,512]{2,1,0:T(8,128)(2,1)S(1)}, u32[]{:S(2)}, u32[]{:S(2)}) collective-permute-start(bf16[2,288,512]{2,1,0:T(8,128)(2,1)S(1)} %shard_map.71), channel_id=1, source_target_pairs={{0,2},{1,15},{2,0},{3,5},{4,6},{5,3},{6,4},{7,9},{8,10},{9,7},{10,... | collective-permute-start | bytes 1769480 | tf_op jit(solution)/shard_map/ppermute | solution.py:36
  24.5 3.0 %collective-permute-start.14 = (bf16[1,288,512]{2,1,0:T(8,128)(2,1)S(1)}, bf16[1,288,512]{2,1,0:T(8,128)(2,1)S(1)}, u32[]{:S(2)}, u32[]{:S(2)}) collective-permute-start(bf16[1,288,512]{2,1,0:T(8,128)(2,1)S(1)} %collective-permute-done.11.message_ref.mine_ref), channel_id=1, source_target_pairs={{1,0},{0,1},{3,2},{2,3},{5,4},{4,5},{7,6},{6,7},{9,8},{8,9},{11,10... | collective-permute-start | bytes 884744 | tf_op jit(solution)/shard_map/ppermute | solution.py:27
  25.6 1.6 %collective-permute-start.12 = (bf16[1,256,512]{2,1,0:T(8,128)(2,1)S(1)}, bf16[1,256,512]{2,1,0:T(8,128)(2,1)S(1)}, u32[]{:S(2)}, u32[]{:S(2)}) collective-permute-start(bf16[1,256,512]{2,1,0:T(8,128)(2,1)S(1)} %get-tuple-element.89), channel_id=1, source_target_pairs={{1,0},{0,1},{3,2},{2,3},{5,4},{4,5},{7,6},{6,7},{9,8},{8,9},{11,10... | collective-permute-start | bytes 786440 | tf_op jit(solution)/shard_map/ppermute | solution.py:27
  25.7 1.9 %collective-permute-start.13 = (bf16[1,256,512]{2,1,0:T(8,128)(2,1)S(1)}, bf16[1,256,512]{2,1,0:T(8,128)(2,1)S(1)}, u32[]{:S(2)}, u32[]{:S(2)}) collective-permute-start(bf16[1,256,512]{2,1,0:T(8,128)(2,1)S(1)} %get-tuple-element.90), channel_id=1, source_target_pairs={{1,0},{0,1},{3,2},{2,3},{5,4},{4,5},{7,6},{6,7},{9,8},{8,9},{11,10... | collective-permute-start | bytes 786440 | tf_op jit(solution)/shard_map/ppermute | solution.py:27
  28.2 6.5 %collective-permute-start.17 = (bf16[1,256,512]{2,1,0:T(8,128)(2,1)S(1)}, bf16[1,256,512]{2,1,0:T(8,128)(2,1)S(1)}, u32[]{:S(2)}, u32[]{:S(2)}) collective-permute-start(bf16[1,256,512]{2,1,0:T(8,128)(2,1)S(1)} %get-tuple-element.104.own_low_ref), channel_id=1, source_target_pairs={{1,0},{0,1},{3,2},{2,3},{5,4},{4,5},{7,6},{6,7},{9,8},{8,9},{11,10... | collective-permute-start | bytes 786440 | tf_op jit(solution)/shard_map/ppermute | solution.py:27
  28.6 6.1 %collective-permute-start.18 = (bf16[1,256,512]{2,1,0:T(8,128)(2,1)S(1)}, bf16[1,256,512]{2,1,0:T(8,128)(2,1)S(1)}, u32[]{:S(2)}, u32[]{:S(2)}) collective-permute-start(bf16[1,256,512]{2,1,0:T(8,128)(2,1)S(1)} %get-tuple-element.107.own_high_ref), channel_id=1, source_target_pairs={{1,0},{0,1},{3,2},{2,3},{5,4},{4,5},{7,6},{6,7},{9,8},{8,9},{11,10... | collective-permute-start | bytes 786440 | tf_op jit(solution)/shard_map/ppermute | solution.py:27
  28.7 3.9 %collective-permute-start.15 = (f32[4,512]{1,0:T(4,128)S(1)}, f32[4,512]{1,0:T(4,128)S(1)}, u32[]{:S(2)}, u32[]{:S(2)}) collective-permute-start(f32[4,512]{1,0:T(4,128)S(1)} %get-tuple-element.93.one_ref), channel_id=1, source_target_pairs={{0,4},{1,5},{2,6},{3,7},{4,0},{5,1},{6,2},{7,3},{8,12},{9,13},{10,... | collective-permute-start | bytes 24584 | tf_op jit(solution)/shard_map/ppermute | solution.py:659
  32.6 4.6 %collective-permute-start.16 = (f32[4,512]{1,0:T(4,128)S(1)}, f32[4,512]{1,0:T(4,128)S(1)}, u32[]{:S(2)}, u32[]{:S(2)}) collective-permute-start(f32[4,512]{1,0:T(4,128)S(1)} %shard_map.75.one_ref), channel_id=1, source_target_pairs={{0,8},{1,9},{2,10},{3,11},{4,12},{5,13},{6,14},{7,15},{8,0},{9,1},... | collective-permute-start | bytes 24584 | tf_op jit(solution)/shard_map/ppermute | solution.py:659
  37.2 3.7 %collective-permute-start.19 = (f32[4,512]{1,0:T(4,128)S(1)}, f32[4,512]{1,0:T(4,128)S(1)}, u32[]{:S(2)}, u32[]{:S(2)}) collective-permute-start(f32[4,512]{1,0:T(4,128)S(1)} %shard_map.77.one_ref), channel_id=1, source_target_pairs={{0,2},{1,3},{2,0},{3,1},{4,6},{5,7},{6,4},{7,5},{8,10},{9,11},{10,... | collective-permute-start | bytes 24584 | tf_op jit(solution)/shard_map/ppermute | solution.py:659
  40.9 1.2 %collective-permute-start.20 = (f32[8,512]{1,0:T(8,128)S(1)}, f32[8,512]{1,0:T(8,128)S(1)}, u32[]{:S(2)}, u32[]{:S(2)}) collective-permute-start(f32[8,512]{1,0:T(8,128)S(1)} %shard_map.79.mine_ref), channel_id=1, source_target_pairs={{1,0},{0,1},{3,2},{2,3},{5,4},{4,5},{7,6},{6,7},{9,8},{8,9},{11,10... | collective-permute-start | bytes 49160 | tf_op jit(solution)/shard_map/ppermute | solution.py:27
